TPU v7x, 32 devices: a whole 2x2x4 slice. The times are simulated.
32 devices in a mesh: grp: 2 (over x), src: 8 (over z, y), tgt: 2 (over core).
Axes of the slice: x: 2, y: 2, z: 4, core: 2. Of those that a mesh axis runs over, the one named last changes fastest.
Arguments:
- source_mass: float32 [8192, 1024], P(('grp', 'src'), 'tgt'), parts along dimension 0, may hold values from 0.3 to 3
- target_mass: float32 [2, 1024, 1024], P('tgt', ('grp', 'src')), parts along dimension 1, may hold values from 0.3 to 3
- kernel_tiles: bfloat16 [32, 4, 256, 256], P(('grp', 'src'), 'tgt'), parts along dimension 0, may hold values from 0.00039863586 to 0.0039978027
- tile_cols: int32 [32, 4], P(('grp', 'src'), 'tgt'), parts along dimension 0, may hold values from 0 to 1, as said below
- tile_count: int32 [32, 2], P(('grp', 'src'), 'tgt'), parts along dimension 0, may hold values from 1 to 2, as said below
- source_cotangent: float32 [8192, 1024], P(('grp', 'src'), 'tgt'), parts along dimension 0, may hold values from -6 to 6
- target_cotangent: float32 [2, 1024, 1024], P('tgt', ('grp', 'src')), parts along dimension 1, may hold values from -6 to 6
Outputs:
- source_potential: float32 [8192, 1024], P(('grp', 'src'), 'tgt'), parts along dimension 0
- target_potential: float32 [2, 1024, 1024], P('tgt', ('grp', 'src')), parts along dimension 1
- source_grad: float32 [8192, 1024], P(('grp', 'src'), 'tgt'), parts along dimension 0
- target_grad: float32 [2, 1024, 1024], P('tgt', ('grp', 'src')), parts along dimension 1
There are 2 independent parts, one for each index of `grp`. A program takes and returns all parts, laid end to end along the dimension named above; each array names one. Nothing has to cross between parts.
Inputs may be any that keep to these rules, and one draw needn't show every extreme that they name: `tile_cols`: the live slots of one row block in one set name distinct column blocks, and every column block of every set is named by a live slot of some row block. `tile_count`: every set has a row block with all 2 slots live.
All inputs are finite; a program needn't handle non-finite values.
Results may differ from a plain program's by a relative error of at most 0.0003.
Values may be sent and summed in bfloat16 or wider, within the bound.
No kernel may reach another device: no remote copies, remote signals or barrier semaphores. Data moves between devices by JAX's collectives and lax.ppermute only.
A program may use at most 64 MiB of HBM per device.

v0:
```python
import jax
import jax.numpy as jnp
from jax import lax
from jax.sharding import PartitionSpec as P

TILE = 256
CB_DEV = 2


def dense_blocks(kernel_tiles, tile_cols, tile_count):
    keep = kernel_tiles.shape[1]
    live = jnp.arange(keep, dtype=jnp.int32)[None, :] < tile_count
    hits = (tile_cols[:, :, None] == jnp.arange(CB_DEV, dtype=jnp.int32)) & live[:, :, None]
    blocks = jnp.einsum(
        "rkc,rkab->rcab",
        hits.astype(jnp.bfloat16),
        kernel_tiles,
        preferred_element_type=jnp.float32,
    )
    return blocks.astype(jnp.bfloat16)


def alternate(
    kernel_times,
    kernel_transposed,
    first,
    source_mass,
    target_mass,
    source_cotangent,
    target_cotangent,
):
    left_one = source_mass / first
    col_one = kernel_transposed(left_one.astype(jnp.bfloat16))
    right_one = target_mass / col_one
    row_two = kernel_times(right_one.astype(jnp.bfloat16))
    left_two = source_mass / row_two
    col_two = kernel_transposed(left_two.astype(jnp.bfloat16))
    right_two = target_mass / col_two
    row_three = kernel_times(right_two.astype(jnp.bfloat16))
    left_three = source_mass / row_three
    col_three = kernel_transposed(left_three.astype(jnp.bfloat16))
    right_three = target_mass / col_three
    colgrad_three = -target_cotangent / col_three
    leftgrad_three = source_cotangent / left_three + kernel_times(
        colgrad_three.astype(jnp.bfloat16)
    )
    source_grad = leftgrad_three / row_three
    rowgrad_three = -leftgrad_three * left_three / row_three
    rightgrad_two = kernel_transposed(rowgrad_three.astype(jnp.bfloat16))
    target_grad = target_cotangent / target_mass + rightgrad_two / col_two
    colgrad_two = -rightgrad_two * right_two / col_two
    leftgrad_two = kernel_times(colgrad_two.astype(jnp.bfloat16))
    source_grad = source_grad + leftgrad_two / row_two
    rowgrad_two = -leftgrad_two * left_two / row_two
    rightgrad_one = kernel_transposed(rowgrad_two.astype(jnp.bfloat16))
    target_grad = target_grad + rightgrad_one / col_one
    colgrad_one = -rightgrad_one * right_one / col_one
    leftgrad_one = kernel_times(colgrad_one.astype(jnp.bfloat16))
    source_grad = source_grad + leftgrad_one / first
    return (jnp.log(left_three), jnp.log(right_three), source_grad, target_grad)


def local(
    source_mass,
    target_mass,
    kernel_tiles,
    tile_cols,
    tile_count,
    source_cotangent,
    target_cotangent,
):
    blocks = dense_blocks(kernel_tiles, tile_cols, tile_count)
    rows = blocks.shape[0] * TILE
    flat = blocks.transpose(0, 2, 1, 3).reshape(rows, CB_DEV * TILE)
    target_rows = target_mass[0]
    cot_rows = target_cotangent[0]

    def row_reduce(partial_value):
        return lax.psum_scatter(partial_value, "tgt", scatter_dimension=1, tiled=True)

    def kernel_times(panel):
        return row_reduce(
            jnp.dot(
                flat,
                lax.all_gather(panel, "src", axis=0, tiled=True),
                preferred_element_type=jnp.float32,
            )
        )

    def kernel_transposed(panel):
        whole = lax.all_gather(panel, "tgt", axis=1, tiled=True)
        return lax.psum_scatter(
            lax.dot_general(
                flat, whole, (((0,), (0,)), ((), ())), preferred_element_type=jnp.float32
            ),
            "src",
            scatter_dimension=0,
            tiled=True,
        )

    sums = jnp.sum(flat, axis=1, dtype=jnp.float32)[:, None]
    first = row_reduce(jnp.broadcast_to(sums, (rows, target_rows.shape[1])))
    source_potential, target_potential, source_grad, target_grad = alternate(
        kernel_times, kernel_transposed, first, source_mass, target_rows, source_cotangent, cot_rows
    )
    target_potential = target_potential[None]
    target_grad = target_grad[None]
    return (source_potential, target_potential, source_grad, target_grad)


def solution(mesh):
    return jax.shard_map(
        local,
        mesh=mesh,
        in_specs=(
            P(("grp", "src"), "tgt"),
            P("tgt", ("grp", "src"), None),
            P(("grp", "src"), "tgt", None, None),
            P(("grp", "src"), "tgt"),
            P(("grp", "src"), "tgt"),
            P(("grp", "src"), "tgt"),
            P("tgt", ("grp", "src"), None),
        ),
        out_specs=(
            P(("grp", "src"), "tgt"),
            P("tgt", ("grp", "src"), None),
            P(("grp", "src"), "tgt"),
            P("tgt", ("grp", "src"), None),
        ),
        check_vma=False,
    )
```

profile of v0, /device:TPU:1, one launch (start us, length us, event | category | flops | bytes accessed | tf_op | source)
XLA Modules:
  0.0 734.4 jit_solution(15183016247024782162)
XLA Ops:
  12.5 12.2 %reduce-scatter.12.cloned.1.call-done = f32[512,512]{1,0:T(8,128)} async-done(((f32[512,1024]{1,0:T(8,128)}), f32[512,512]{1,0:T(8,128)}) %reduce-scatter.12.cloned.1.call-update) | async-done | bytes 1048592 | tf_op jit(solution)/shard_map/reduce_scatter | solution.py:79
  27.0 10.2 %all-gather.11.cloned.1.call-done = bf16[512,1024]{1,0:T(8,128)(2,1)} async-done(((bf16[512,512]{1,0:T(8,128)(2,1)}), bf16[512,1024]{1,0:T(8,128)(2,1)}) %all-gather.11.cloned.1.call-update) | async-done | bytes 1048592 | tf_op jit(solution)/shard_map/all_gather | solution.py:91
  37.3 3.4 fusion.16
  40.7 67.4 %reduce-scatter.14.cloned.1.call-done = f32[64,1024]{1,0:T(8,128)} async-done(((f32[512,1024]{1,0:T(8,128)}), f32[64,1024]{1,0:T(8,128)}) %reduce-scatter.14.cloned.1.call-update) | async-done | bytes 262160 | tf_op jit(solution)/shard_map/reduce_scatter | solution.py:92
  109.9 40.9 %all-gather.13.cloned.1.call-done = bf16[512,1024]{1,0:T(8,128)(2,1)} async-done(((bf16[64,1024]{1,0:T(8,128)(2,1)}), bf16[512,1024]{1,0:T(8,128)(2,1)}) %all-gather.13.cloned.1.call-update) | async-done | bytes 1048592 | tf_op jit(solution)/shard_map/all_gather | solution.py:85
  154.1 9.8 %reduce-scatter.16.cloned.1.call-done = f32[512,512]{1,0:T(8,128)} async-done(((f32[512,1024]{1,0:T(8,128)}), f32[512,512]{1,0:T(8,128)}) %reduce-scatter.16.cloned.1.call-update) | async-done | bytes 1048592 | tf_op jit(solution)/shard_map/reduce_scatter | solution.py:79
  166.7 10.3 %all-gather.15.cloned.1.call-done = bf16[512,1024]{1,0:T(8,128)(2,1)} async-done(((bf16[512,512]{1,0:T(8,128)(2,1)}), bf16[512,1024]{1,0:T(8,128)(2,1)}) %all-gather.15.cloned.1.call-update) | async-done | bytes 1048592 | tf_op jit(solution)/shard_map/all_gather | solution.py:91
  180.4 66.7 %reduce-scatter.18.cloned.1.call-done = f32[64,1024]{1,0:T(8,128)} async-done(((f32[512,1024]{1,0:T(8,128)}), f32[64,1024]{1,0:T(8,128)}) %reduce-scatter.18.cloned.1.call-update) | async-done | bytes 262160 | tf_op jit(solution)/shard_map/reduce_scatter | solution.py:92
  248.8 41.0 %all-gather.17.cloned.1.call-done = bf16[512,1024]{1,0:T(8,128)(2,1)} async-done(((bf16[64,1024]{1,0:T(8,128)(2,1)}), bf16[512,1024]{1,0:T(8,128)(2,1)}) %all-gather.17.cloned.1.call-update) | async-done | bytes 1048592 | tf_op jit(solution)/shard_map/all_gather | solution.py:85
  293.2 9.8 %reduce-scatter.20.cloned.1.call-done = f32[512,512]{1,0:T(8,128)} async-done(((f32[512,1024]{1,0:T(8,128)}), f32[512,512]{1,0:T(8,128)}) %reduce-scatter.20.cloned.1.call-update) | async-done | bytes 1048592 | tf_op jit(solution)/shard_map/reduce_scatter | solution.py:79
  305.7 10.3 %all-gather.19.cloned.1.call-done = bf16[512,1024]{1,0:T(8,128)(2,1)} async-done(((bf16[512,512]{1,0:T(8,128)(2,1)}), bf16[512,1024]{1,0:T(8,128)(2,1)}) %all-gather.19.cloned.1.call-update) | async-done | bytes 1048592 | tf_op jit(solution)/shard_map/all_gather | solution.py:91
  319.4 67.5 %reduce-scatter.22.cloned.1.call-done = f32[64,1024]{1,0:T(8,128)} async-done(((f32[512,1024]{1,0:T(8,128)}), f32[64,1024]{1,0:T(8,128)}) %reduce-scatter.22.cloned.1.call-update) | async-done | bytes 262160 | tf_op jit(solution)/shard_map/reduce_scatter | solution.py:92
  388.6 40.9 %all-gather.21.cloned.1.call-done = bf16[512,1024]{1,0:T(8,128)(2,1)} async-done(((bf16[64,1024]{1,0:T(8,128)(2,1)}), bf16[512,1024]{1,0:T(8,128)(2,1)}) %all-gather.21.cloned.1.call-update) | async-done | bytes 1048592 | tf_op jit(solution)/shard_map/all_gather | solution.py:85
  432.9 9.8 %reduce-scatter.24.cloned.1.call-done = f32[512,512]{1,0:T(8,128)} async-done(((f32[512,1024]{1,0:T(8,128)}), f32[512,512]{1,0:T(8,128)}) %reduce-scatter.24.cloned.1.call-update) | async-done | bytes 1048592 | tf_op jit(solution)/shard_map/reduce_scatter | solution.py:79
  442.7 3.7 divide_convert_fusion.1
  446.5 10.3 %all-gather.23.cloned.1.call-done = bf16[512,1024]{1,0:T(8,128)(2,1)} async-done(((bf16[512,512]{1,0:T(8,128)(2,1)}), bf16[512,1024]{1,0:T(8,128)(2,1)}) %all-gather.23.cloned.1.call-update) | async-done | bytes 1048592 | tf_op jit(solution)/shard_map/all_gather | solution.py:91
  460.2 66.9 %reduce-scatter.26.cloned.1.call-done = f32[64,1024]{1,0:T(8,128)} async-done(((f32[512,1024]{1,0:T(8,128)}), f32[64,1024]{1,0:T(8,128)}) %reduce-scatter.26.cloned.1.call-update) | async-done | bytes 262160 | tf_op jit(solution)/shard_map/reduce_scatter | solution.py:92
  528.8 40.8 %all-gather.25.cloned.1.call-done = bf16[512,1024]{1,0:T(8,128)(2,1)} async-done(((bf16[64,1024]{1,0:T(8,128)(2,1)}), bf16[512,1024]{1,0:T(8,128)(2,1)}) %all-gather.25.cloned.1.call-update) | async-done | bytes 1048592 | tf_op jit(solution)/shard_map/all_gather | solution.py:85
  573.1 9.8 %reduce-scatter.28.cloned.1.call-done = f32[512,512]{1,0:T(8,128)} async-done(((f32[512,1024]{1,0:T(8,128)}), f32[512,512]{1,0:T(8,128)}) %reduce-scatter.28.cloned.1.call-update) | async-done | bytes 1048592 | tf_op jit(solution)/shard_map/reduce_scatter | solution.py:79
  585.7 10.3 %all-gather.27.cloned.1.call-done = bf16[512,1024]{1,0:T(8,128)(2,1)} async-done(((bf16[512,512]{1,0:T(8,128)(2,1)}), bf16[512,1024]{1,0:T(8,128)(2,1)}) %all-gather.27.cloned.1.call-update) | async-done | bytes 1048592 | tf_op jit(solution)/shard_map/all_gather | solution.py:91
  599.4 67.5 %reduce-scatter.30.cloned.1.call-done = f32[64,1024]{1,0:T(8,128)} async-done(((f32[512,1024]{1,0:T(8,128)}), f32[64,1024]{1,0:T(8,128)}) %reduce-scatter.30.cloned.1.call-update) | async-done | bytes 262160 | tf_op jit(solution)/shard_map/reduce_scatter | solution.py:92
  669.3 40.2 %all-gather.29.cloned.1.call-done = bf16[512,1024]{1,0:T(8,128)(2,1)} async-done(((bf16[64,1024]{1,0:T(8,128)(2,1)}), bf16[512,1024]{1,0:T(8,128)(2,1)}) %all-gather.29.cloned.1.call-update) | async-done | bytes 1048592 | tf_op jit(solution)/shard_map/all_gather | solution.py:85
  712.9 9.9 %reduce-scatter.32.cloned.1.call-done = f32[512,512]{1,0:T(8,128)} async-done(((f32[512,1024]{1,0:T(8,128)}), f32[512,512]{1,0:T(8,128)}) %reduce-scatter.32.cloned.1.call-update) | async-done | bytes 1048592 | tf_op jit(solution)/shard_map/reduce_scatter | solution.py:79
  722.7 4.8 divide_add_fusion
  (79 shorter events, 55.4 us)
Async XLA Ops:
  7.2 17.5 %reduce-scatter.12.cloned.1.call-start = ((), (), s32[]{:S(2)}) async-start(), calls=%async_computation.11 | async-start | bytes 3145728 | tf_op jit(solution)/shard_map/reduce_scatter | solution.py:79
  12.4 24.8 %all-gather.11.cloned.1.call-start = ((), (), s32[]{:S(2)}) async-start(), calls=%async_computation.12 | async-start | bytes 1572864 | tf_op jit(solution)/shard_map/all_gather | solution.py:91
  26.9 81.2 %reduce-scatter.14.cloned.1.call-start = ((), (), s32[]{:S(2)}) async-start(), calls=%async_computation.13 | async-start | bytes 2359296 | tf_op jit(solution)/shard_map/reduce_scatter | solution.py:92
  37.3 70.9 %copy-start.4 = (f32[1,64,1024]{2,1,0:T(8,128)S(1)}, f32[1,64,1024]{2,1,0:T(8,128)}, u32[]{:S(2)}) copy-start(f32[1,64,1024]{2,1,0:T(8,128)} %param.8) | copy-start | bytes 786436
  40.7 110.1 %all-gather.13.cloned.1.call-start = ((), (), s32[]{:S(2)}) async-start(), calls=%async_computation.14 | async-start | bytes 1179648 | tf_op jit(solution)/shard_map/all_gather | solution.py:85
  109.8 54.2 %reduce-scatter.16.cloned.1.call-start = ((), (), s32[]{:S(2)}) async-start(), calls=%async_computation.15 | async-start | bytes 3145728 | tf_op jit(solution)/shard_map/reduce_scatter | solution.py:79
  154.1 22.9 %all-gather.15.cloned.1.call-start = ((), (), s32[]{:S(2)}) async-start(), calls=%async_computation.16 | async-start | bytes 1572864 | tf_op jit(solution)/shard_map/all_gather | solution.py:91
  166.6 80.5 %reduce-scatter.18.cloned.1.call-start = ((), (), s32[]{:S(2)}) async-start(), calls=%async_computation.17 | async-start | bytes 2359296 | tf_op jit(solution)/shard_map/reduce_scatter | solution.py:92
  180.3 109.5 %all-gather.17.cloned.1.call-start = ((), (), s32[]{:S(2)}) async-start(), calls=%async_computation.18 | async-start | bytes 1179648 | tf_op jit(solution)/shard_map/all_gather | solution.py:85
  248.8 54.3 %reduce-scatter.20.cloned.1.call-start = ((), (), s32[]{:S(2)}) async-start(), calls=%async_computation.19 | async-start | bytes 3145728 | tf_op jit(solution)/shard_map/reduce_scatter | solution.py:79
  293.2 22.9 %all-gather.19.cloned.1.call-start = ((), (), s32[]{:S(2)}) async-start(), calls=%async_computation.20 | async-start | bytes 1572864 | tf_op jit(solution)/shard_map/all_gather | solution.py:91
  305.7 81.2 %copy-start.6 = (f32[1,64,1024]{2,1,0:T(8,128)S(1)}, f32[1,64,1024]{2,1,0:T(8,128)}, u32[]{:S(2)}) copy-start(f32[1,64,1024]{2,1,0:T(8,128)} %param.13) | copy-start | bytes 786436
  305.7 81.2 %reduce-scatter.22.cloned.1.call-start = ((), (), s32[]{:S(2)}) async-start(), calls=%async_computation.21 | async-start | bytes 2359296 | tf_op jit(solution)/shard_map/reduce_scatter | solution.py:92
  319.4 110.2 %all-gather.21.cloned.1.call-start = ((), (), s32[]{:S(2)}) async-start(), calls=%async_computation.22 | async-start | bytes 1179648 | tf_op jit(solution)/shard_map/all_gather | solution.py:85
  388.6 54.2 %reduce-scatter.24.cloned.1.call-start = ((), (), s32[]{:S(2)}) async-start(), calls=%async_computation.23 | async-start | bytes 3145728 | tf_op jit(solution)/shard_map/reduce_scatter | solution.py:79
  432.9 23.9 %all-gather.23.cloned.1.call-start = ((), (), s32[]{:S(2)}) async-start(), calls=%async_computation.24 | async-start | bytes 1572864 | tf_op jit(solution)/shard_map/all_gather | solution.py:91
  446.4 80.7 %copy-start.5 = (f32[64,1024]{1,0:T(8,128)S(1)}, f32[64,1024]{1,0:T(8,128)}, u32[]{:S(2)}) copy-start(f32[64,1024]{1,0:T(8,128)} %reduce-scatter.18.cloned.1.call-done) | copy-start | bytes 786436
  446.4 80.6 %reduce-scatter.26.cloned.1.call-start = ((), (), s32[]{:S(2)}) async-start(), calls=%async_computation.25 | async-start | bytes 2359296 | tf_op jit(solution)/shard_map/reduce_scatter | solution.py:92
  460.1 109.5 %all-gather.25.cloned.1.call-start = ((), (), s32[]{:S(2)}) async-start(), calls=%async_computation.26 | async-start | bytes 1179648 | tf_op jit(solution)/shard_map/all_gather | solution.py:85
  528.8 54.1 %reduce-scatter.28.cloned.1.call-start = ((), (), s32[]{:S(2)}) async-start(), calls=%async_computation.27 | async-start | bytes 3145728 | tf_op jit(solution)/shard_map/reduce_scatter | solution.py:79
  573.0 23.0 %all-gather.27.cloned.1.call-start = ((), (), s32[]{:S(2)}) async-start(), calls=%async_computation.28 | async-start | bytes 1572864 | tf_op jit(solution)/shard_map/all_gather | solution.py:91
  585.6 81.3 %reduce-scatter.30.cloned.1.call-start = ((), (), s32[]{:S(2)}) async-start(), calls=%async_computation.29 | async-start | bytes 2359296 | tf_op jit(solution)/shard_map/reduce_scatter | solution.py:92
  599.3 110.2 %all-gather.29.cloned.1.call-start = ((), (), s32[]{:S(2)}) async-start(), calls=%async_computation.30 | async-start | bytes 1179648 | tf_op jit(solution)/shard_map/all_gather | solution.py:85
  669.3 53.5 %reduce-scatter.32.cloned.1.call-start = ((), (), s32[]{:S(2)}) async-start(), calls=%async_computation.31 | async-start | bytes 3145728 | tf_op jit(solution)/shard_map/reduce_scatter | solution.py:79
  (4 other events, 123.2 us)
Sparse Core Ops, SparseCore 0:
  12.6 12.0 reduce-scatter.11
  27.0 10.2 all-gather.10
  41.2 66.8 reduce-scatter.13
  110.9 39.8 all-gather.12
  154.2 9.7 reduce-scatter.15
  166.7 10.2 all-gather.14
  180.5 66.5 reduce-scatter.17
  249.8 39.9 all-gather.16
  293.3 9.7 reduce-scatter.19
  305.8 10.1 all-gather.18
  320.0 66.8 reduce-scatter.21
  389.7 39.8 all-gather.20
  433.0 9.7 reduce-scatter.23
  446.6 10.1 all-gather.22
  460.3 66.7 reduce-scatter.25
  529.6 39.9 all-gather.24
  573.1 9.7 reduce-scatter.27
  585.8 10.1 all-gather.26
  599.9 66.9 reduce-scatter.29
  669.7 39.8 all-gather.28
  713.0 9.7 reduce-scatter.31
where the time goes:
time: 735 us; the launch traced here: 734 us
  waiting for transfers between devices  653 us (89%)
  matrix products  35.7 us (5%)
  other arithmetic  28.4 us (4%)
  between operations  14.4 us (2%)
    reduce_scatter x5, waiting for transfers between devices, kernel_transposed(): lax.psum_scatter(lax.dot_general(flat, whole, (((0,), (0,)), ((), ())), p...  336 us
    all_gather x5, waiting for transfers between devices, kernel_times(): lax.all_gather(panel, 'src', axis=0, tiled=True)  204 us
    reduce_scatter x6, waiting for transfers between devices, row_reduce(): lax.psum_scatter(partial_value, 'tgt', scatter_dimension=1, tiled=True)  61.4 us
    all_gather x5, waiting for transfers between devices, kernel_transposed(): whole = lax.all_gather(panel, 'tgt', axis=1, tiled=True)  51.5 us
    dot_general x5, matrix products, kernel_transposed(): lax.dot_general(flat, whole, (((0,), (0,)), ((), ())), preferred_element_...  16.6 us
    dot_general x5, matrix products, kernel_times(): jnp.dot(flat, lax.all_gather(panel, 'src', axis=0, tiled=True), preferred...  16.5 us
  transfers between devices with their start and end apart: 21, of which 21 were waited for; matrix products, arithmetic and copies ran while one was open for 0% of the time, Pallas kernels for 0%

commit v1 on v0

v1 whole, which is shorter than its diff:
```python
import functools

import jax
import jax.numpy as jnp
import numpy as np
from jax import lax
from jax.experimental import pallas as pl
from jax.experimental.pallas import tpu as pltpu
from jax.sharding import PartitionSpec as P

CB_DEV = 2
HALF = jnp.float16
COT_SCALE = 256.0
VMEM = 56 * 1024 * 1024


def ring_order(count):
    if count == 8:
        return [0, 2, 4, 6, 7, 5, 3, 1]
    return list(range(count))


def dense_blocks(kernel_tiles, tile_cols, tile_count):
    keep = kernel_tiles.shape[1]
    live = jnp.arange(keep, dtype=jnp.int32)[None, :] < tile_count
    hits = (tile_cols[:, :, None] == jnp.arange(CB_DEV, dtype=jnp.int32)) & live[:, :, None]
    blocks = jnp.einsum(
        "rkc,rkab->racb",
        hits.astype(jnp.bfloat16),
        kernel_tiles,
        preferred_element_type=jnp.float32,
    )
    rows, cols = blocks.shape[0] * blocks.shape[1], blocks.shape[2] * blocks.shape[3]
    return blocks.astype(jnp.bfloat16).reshape(rows, cols)


def nt(x, y):
    return lax.dot_general(x, y, (((1,), (1,)), ((), ())), preferred_element_type=jnp.float32)


def nn(x, y):
    return jnp.dot(x, y, preferred_element_type=jnp.float32)


class Shape:
    def __init__(self, count, rows, cols, hists, share):
        self.count = count
        self.rows = rows
        self.cols = cols
        self.hists = hists
        self.share = share
        self.lanes = rows + 2 * share


def load_matrix(s, units, matrix, sems):
    copies = []
    for d in range(s.count):
        for t in range(2):
            copy = pltpu.make_async_copy(
                units[2 * d + t], matrix.at[d, :, pl.ds(t * s.cols, s.cols)], sems.at[d]
            )
            copy.start()
            copies.append(copy)
    return copies


def gather_targets(s, pieces, index):
    parts = []
    for t in range(2):
        lo = s.rows + t * s.share
        parts += [pieces[index(i), :, lo : lo + s.share] for i in range(s.count)]
    return jnp.concatenate(parts, axis=1)


def scatter_targets(s, out, index, values):
    for i in range(s.count):
        out[index(i), :, s.rows : s.lanes] = jnp.concatenate(
            [
                values[:, t * s.cols + i * s.share : t * s.cols + (i + 1) * s.share]
                for t in range(2)
            ],
            axis=1,
        )


def each(count, body, init):
    if count <= 8:
        for d in range(count):
            init = body(d, init)
        return init
    return lax.fori_loop(0, count, body, init)


def forward_kernel(s, table, mass, *refs):
    units, (row_two, thirds, col_one_out, col_two_out, row_one) = (
        refs[: 2 * s.count],
        refs[2 * s.count : 2 * s.count + 5],
    )
    matrix, sems = refs[2 * s.count + 5 :]
    copies = load_matrix(s, units, matrix, sems)
    zero = jnp.zeros((s.hists, 2 * s.cols), jnp.float32)
    inverse = lambda i: table[s.count + i]
    target = gather_targets(s, mass, inverse)
    for copy in copies:
        copy.wait()
    ones = jnp.ones((8, 2 * s.cols), jnp.bfloat16)

    def first(d, total):
        sums = nt(ones, matrix[d])
        row_one[d] = sums
        left = mass[d, :, : s.rows] / sums[0:1]
        return total + nn(left.astype(jnp.bfloat16), matrix[d])

    col_one = each(s.count, first, zero)
    col_one_out[...] = col_one
    panel = (target / col_one).astype(jnp.bfloat16)

    def second(d, total):
        row = nt(panel, matrix[d])
        row_two[d] = row
        left = mass[d, :, : s.rows] / row
        return total + nn(left.astype(jnp.bfloat16), matrix[d])

    col_two = each(s.count, second, zero)
    col_two_out[...] = col_two
    panel = (target / col_two).astype(jnp.bfloat16)

    def third(d, total):
        row = nt(panel, matrix[d])
        k = table[d]
        thirds[k, :, : s.rows] = row
        left = mass[d, :, : s.rows] / row
        return total + nn(left.astype(jnp.bfloat16), matrix[d])

    col_three = each(s.count, third, zero)
    scatter_targets(s, thirds, lambda i: i, col_three)


def backward_kernel(s, table, mass, cot, row_two, thirds, col_one, col_two, row_one, *refs):
    units, out, (matrix, sems) = refs[: 2 * s.count], refs[2 * s.count], refs[2 * s.count + 1 :]
    copies = load_matrix(s, units, matrix, sems)
    zero = jnp.zeros((s.hists, 2 * s.cols), jnp.float32)
    inverse = lambda i: table[s.count + i]
    target = gather_targets(s, mass, inverse)
    target_cot = gather_targets(s, cot, lambda i: i)
    col_three = gather_targets(s, thirds, lambda i: i)
    right_one = target / col_one[...]
    right_two = target / col_two[...]
    for copy in copies:
        copy.wait()
    panel = (-target_cot / col_three).astype(jnp.bfloat16)

    def third(d, total):
        k = table[d]
        grad = nt(panel, matrix[d])
        row = thirds[k, :, : s.rows]
        left = mass[d, :, : s.rows] / row
        term = grad / row
        out[d, :, : s.rows] = term
        rowgrad = -(cot[k, :, : s.rows] / row + term * left)
        return total + nn(rowgrad.astype(jnp.bfloat16), matrix[d])

    term_two = each(s.count, third, zero) / col_two[...]
    panel = (-term_two * right_two).astype(jnp.bfloat16)

    def second(d, total):
        row = row_two[d]
        term = nt(panel, matrix[d]) / row
        out[d, :, : s.rows] += term
        rowgrad = -term * (mass[d, :, : s.rows] / row)
        return total + nn(rowgrad.astype(jnp.bfloat16), matrix[d])

    term_one = each(s.count, second, zero) / col_one[...]
    panel = (-term_one * right_one).astype(jnp.bfloat16)

    def first(d, carry):
        out[d, :, : s.rows] += nt(panel, matrix[d]) / row_one[d, 0:1]
        return carry

    each(s.count, first, 0)
    scatter_targets(s, out, inverse, term_two + term_one)


def call(kernel, s, outs, table, arrays, units):
    return pl.pallas_call(
        functools.partial(kernel, s),
        out_shape=outs,
        in_specs=[pl.BlockSpec(memory_space=pltpu.SMEM)]
        + [pl.BlockSpec(memory_space=pltpu.VMEM)] * len(arrays)
        + [pl.BlockSpec(memory_space=pl.ANY)] * len(units),
        scratch_shapes=[
            pltpu.VMEM((s.count, s.rows, 2 * s.cols), jnp.bfloat16),
            pltpu.SemaphoreType.DMA((s.count,)),
        ],
        compiler_params=pltpu.CompilerParams(vmem_limit_bytes=VMEM),
    )(table, *arrays, *units)


def swap_cores(x):
    return lax.ppermute(x, "tgt", [(0, 1), (1, 0)])


def local(
    source_mass,
    target_mass,
    kernel_tiles,
    tile_cols,
    tile_count,
    source_cotangent,
    target_cotangent,
):
    count = lax.axis_size("src")
    rows, cols_here = source_mass.shape
    share = target_mass.shape[1]
    s = Shape(count, rows, CB_DEV * kernel_tiles.shape[2], cols_here // count, share)
    ring = np.array(ring_order(count), np.int32)
    place = np.argsort(ring).astype(np.int32)
    me = lax.axis_index("src")
    core = lax.axis_index("tgt")
    at = jnp.asarray(place)[me]
    order = jnp.asarray(ring)[(at + jnp.arange(count, dtype=jnp.int32)) % count]
    inverse = (jnp.asarray(place) - at) % count
    table = jnp.concatenate([order, inverse]).astype(jnp.int32)

    def shift(x, distance):
        pairs = [(int(ring[p]), int(ring[(p + distance) % count])) for p in range(count)]
        return lax.ppermute(x, "src", pairs)

    unit = dense_blocks(kernel_tiles, tile_cols, tile_count)
    held = {0: unit}
    for step in range(1, count // 2 + 1):
        if step < count - step:
            held[step] = shift(held[step - 1], -1)
            held[count - step] = shift(held[(count - step + 1) % count], 1)
        else:
            middle = rows // 2
            ahead = shift(held[step - 1][:middle], -1)
            behind = shift(held[step + 1][middle:], 1)
            held[step] = jnp.concatenate([ahead, behind])
    units = []
    for d in range(count):
        units += [held[d], swap_cores(held[d])]

    def by_histogram(source, target):
        target = target.astype(HALF).reshape(share, 2, cols_here)
        mine = lax.dynamic_index_in_dim(target, core, 1, keepdims=False)
        other = lax.dynamic_index_in_dim(target, 1 - core, 1, keepdims=False)
        both = jnp.concatenate([mine, swap_cores(other)]).T
        return jnp.concatenate(
            [
                source.astype(HALF).T.reshape(count, s.hists, rows),
                both.reshape(count, s.hists, 2 * share),
            ],
            axis=2,
        )

    message = by_histogram(source_mass, target_mass[0])
    parts = []
    for d in range(count):
        chunk = lax.dynamic_index_in_dim(message, order[(count - d) % count], 0, keepdims=False)
        parts.append(shift(chunk, -d) if d else chunk)
    mass = jnp.stack(parts).astype(jnp.float32)
    cot = lax.all_to_all(
        by_histogram(source_cotangent * COT_SCALE, target_cotangent[0] * COT_SCALE),
        "src",
        0,
        0,
        tiled=True,
    ).astype(jnp.float32)

    panel = jax.ShapeDtypeStruct((count, s.hists, rows), jnp.float32)
    wide = jax.ShapeDtypeStruct((count, s.hists, s.lanes), jnp.float32)
    column = jax.ShapeDtypeStruct((s.hists, 2 * s.cols), jnp.float32)
    sums = jax.ShapeDtypeStruct((count, 8, rows), jnp.float32)
    row_two, thirds, col_one, col_two, row_one = call(
        forward_kernel, s, (panel, wide, column, column, sums), table, (mass,), units
    )
    grads = call(
        backward_kernel,
        s,
        wide,
        table,
        (mass, cot, row_two, thirds, col_one, col_two, row_one),
        units,
    )

    def by_point(pieces):
        flat = pieces.reshape(cols_here, s.lanes).astype(jnp.float32)
        target = flat[:, rows:].T.reshape(2, share, cols_here)
        other = swap_cores(target[1].astype(HALF)).astype(jnp.float32)
        own = target[0]
        halves = [jnp.where(core == t, own, other) for t in range(2)]
        return flat[:, :rows].T, jnp.concatenate(halves, axis=1)

    row_three, col_three = by_point(lax.all_to_all(thirds.astype(HALF), "src", 0, 0, tiled=True))
    parts = []
    narrow = grads.astype(HALF)
    for d in range(count):
        parts.append(shift(narrow[d], d) if d else narrow[d])
    back = jnp.stack(parts)[(at - jnp.asarray(place)) % count]
    source_term, target_term = by_point(back)
    return (
        jnp.log(source_mass / row_three),
        jnp.log(target_mass[0] / col_three)[None],
        source_cotangent / source_mass + source_term * (1 / COT_SCALE),
        (target_cotangent[0] / target_mass[0] + target_term * (1 / COT_SCALE))[None],
    )


def solution(mesh):
    return jax.shard_map(
        local,
        mesh=mesh,
        in_specs=(
            P(("grp", "src"), "tgt"),
            P("tgt", ("grp", "src"), None),
            P(("grp", "src"), "tgt", None, None),
            P(("grp", "src"), "tgt"),
            P(("grp", "src"), "tgt"),
            P(("grp", "src"), "tgt"),
            P("tgt", ("grp", "src"), None),
        ),
        out_specs=(
            P(("grp", "src"), "tgt"),
            P("tgt", ("grp", "src"), None),
            P(("grp", "src"), "tgt"),
            P("tgt", ("grp", "src"), None),
        ),
        check_vma=False,
    )
```

time: 735 us -> 200 us (0.27)
  waiting for transfers between devices: 653 us -> 38.1 us
  starting transfers between devices: 0.88 us -> 63.1 us
  Pallas kernels: 0 us -> 38.8 us
  matrix products: 35.7 us -> 1.41 us
  local copies, waits for them, and re-layouts: 1.92 us -> 21.4 us
  other arithmetic: 28.4 us -> 19.9 us
    reduce_scatter x11 -> x0, waiting for transfers between devices: 397 us -> none  [the longest x5 336 us: kernel_transposed(): lax.psum_scatter(lax.dot_general(flat, whole, (((0,), (0,)), ((), ())), p...]
    all_gather x10 -> x0, waiting for transfers between devices: 255 us -> none  [the longest x5 204 us: kernel_times(): lax.all_gather(panel, 'src', axis=0, tiled=True)]
    ppermute x0 -> x34, starting transfers between devices: none -> 55.2 us  [the longest x22 37.5 us: shift(): return lax.ppermute(x, 'src', pairs)]
    pallas_call x0 -> x2, Pallas kernels: none -> 38.8 us  [call(): pl.pallas_call(functools.partial(kernel, s), out_shape=outs, in_specs=[pl...]
    ppermute x0 -> x34, waiting for transfers between devices: none -> 38.1 us  [the longest x22 38.1 us: shift(): return lax.ppermute(x, 'src', pairs)]
    dot_general x11 -> x1, matrix products: 35.7 us -> 1.41 us  [dense_blocks(): jnp.einsum('rkc,rkab->racb', hits.astype(jnp.bfloat16), kernel_tiles, pre...]
    convert_element_type x9 -> x8, other arithmetic: 20.4 us -> 7.22 us  [the longest x1 2.26 us: local(): mass = jnp.stack(parts).astype(jnp.float32)]
    unnamed x16 -> x62, local copies, waits for them, and re-layouts: 0.35 us -> 11 us
  transfers between devices with their start and end apart: 21 -> 36, of which waited for: 21 -> 7; matrix products, arithmetic and copies ran while one was open for 0% -> 17% of each run, Pallas kernels for 0% -> 0%
where the time goes in v1:
time: 200 us; the launch traced here: 199 us
  starting transfers between devices  63.1 us (32%)
  Pallas kernels  38.8 us (19%)
  waiting for transfers between devices  38.1 us (19%)
  local copies, waits for them, and re-layouts  21.4 us (11%)
  other arithmetic  19.9 us (10%)
  between operations  16.4 us (8%)
    pallas_call x2, Pallas kernels, call(): pl.pallas_call(functools.partial(kernel, s), out_shape=outs, in_specs=[pl...  38.8 us
    ppermute x22, waiting for transfers between devices, shift(): return lax.ppermute(x, 'src', pairs)  38.1 us
    ppermute x22, starting transfers between devices, shift(): return lax.ppermute(x, 'src', pairs)  37.5 us
    ppermute x12, starting transfers between devices, swap_cores(): return lax.ppermute(x, 'tgt', [(0, 1), (1, 0)])  17.7 us
    unnamed x62, local copies, waits for them, and re-layouts  11 us
    all_to_all x1, starting transfers between devices, local(): lax.all_to_all(thirds.astype(HALF), 'src', 0, 0, tiled=True)  4.2 us
  transfers between devices with their start and end apart: 36, of which 7 were waited for; matrix products, arithmetic and copies ran while one was open for 17% of the time, Pallas kernels for 0%

profile of v1, /device:TPU:1, one launch (start us, length us, event | category | flops | bytes accessed | tf_op | source)
XLA Modules:
  0.0 199.2 jit_solution(13871279435251663916)
XLA Ops:
  3.4 2.7 %collective-permute-start.9 = (bf16[512,512]{1,0:T(8,128)(2,1)S(1)}, bf16[512,512]{1,0:T(8,128)(2,1)}, u32[]{:S(2)}, u32[]{:S(2)}) collective-permute-start(bf16[512,512]{1,0:T(8,128)(2,1)S(1)} %bitcast.116), channel_id=1, source_target_pairs={{0,2},{4,0},{8,4},{12,8},{14,12},{10,14},{6,10},{2,6},{1,3},{5,1},... | collective-permute-start | bytes 1572872 | tf_op jit(solution)/shard_map/ppermute | solution.py:227
  16.4 2.0 %collective-permute-done.9.refs_2_ = bf16[512,512]{1,0:T(8,128)(2,1)} collective-permute-done((bf16[512,512]{1,0:T(8,128)(2,1)S(1)}, bf16[512,512]{1,0:T(8,128)(2,1)}, u32[]{:S(2)}, u32[]{:S(2)}) %collective-permute-start.9) | collective-permute-done | bytes 524320 | tf_op jit(solution)/shard_map/ppermute | solution.py:227
  41.1 2.3 %collective-permute-start.2 = (f16[64,640]{1,0:T(8,128)(2,1)}, f16[64,640]{1,0:T(8,128)(2,1)}, u32[]{:S(2)}, u32[]{:S(2)}) collective-permute-start(f16[64,640]{1,0:T(8,128)(2,1)} %get-tuple-element.27), channel_id=1, source_target_pairs={{0,6},{4,2},{8,0},{12,4},{14,8},{10,12},{6,14},{2,10},{1,7},{5,3},... | collective-permute-start | bytes 245768 | tf_op jit(solution)/shard_map/ppermute | solution.py:227
  44.6 3.7 %all-to-all-start.1 = ((f16[8,64,640]{2,1,0:T(8,128)(2,1)}), f16[8,64,640]{2,1,0:T(8,128)(2,1)S(1)}, u32[]{:S(2)}, u32[]{:S(2)}) async-start(f16[8,64,640]{2,1,0:T(8,128)(2,1)} %pad_maximum_fusion), calls=%async_computation.1 | async-start | bytes 1310720 | tf_op jit(solution)/shard_map/all_to_all | solution.py:263
  49.9 3.2 %collective-permute-start.3 = (f16[64,640]{1,0:T(8,128)(2,1)}, f16[64,640]{1,0:T(8,128)(2,1)S(1)}, u32[]{:S(2)}, u32[]{:S(2)}) collective-permute-start(f16[64,640]{1,0:T(8,128)(2,1)} %get-tuple-element.28), channel_id=1, source_target_pairs={{0,10},{4,6},{8,2},{12,0},{14,4},{10,8},{6,12},{2,14},{1,11},{5,7}... | collective-permute-start | bytes 245768 | tf_op jit(solution)/shard_map/ppermute | solution.py:227
  57.3 13.0 %collective-permute-done.13.refs_6_ = bf16[512,512]{1,0:T(8,128)(2,1)S(1)} collective-permute-done((bf16[512,512]{1,0:T(8,128)(2,1)}, bf16[512,512]{1,0:T(8,128)(2,1)S(1)}, u32[]{:S(2)}, u32[]{:S(2)}) %collective-permute-start.13) | collective-permute-done | bytes 524320 | tf_op jit(solution)/shard_map/ppermute | solution.py:227
  70.4 3.5 %collective-permute-start.10 = (bf16[512,512]{1,0:T(8,128)(2,1)}, bf16[512,512]{1,0:T(8,128)(2,1)S(1)}, u32[]{:S(2)}, u32[]{:S(2)}) collective-permute-start(bf16[512,512]{1,0:T(8,128)(2,1)} %collective-permute-done.9.refs_2_), channel_id=1, source_target_pairs={{0,1},{1,0},{2,3},{3,2},{4,5},{5,4},{6,7},{7,6},{8,9},{9,8},{10,11... | collective-permute-start | bytes 1572872 | tf_op jit(solution)/shard_map/ppermute | solution.py:200
  73.9 3.9 %collective-permute-start.23 = (bf16[512,512]{1,0:T(8,128)(2,1)}, bf16[512,512]{1,0:T(8,128)(2,1)S(1)}, u32[]{:S(2)}, u32[]{:S(2)}) collective-permute-start(bf16[512,512]{1,0:T(8,128)(2,1)} %collective-permute-done.16.refs_14_), channel_id=1, source_target_pairs={{0,1},{1,0},{2,3},{3,2},{4,5},{5,4},{6,7},{7,6},{8,9},{9,8},{10,11... | collective-permute-start | bytes 1572872 | tf_op jit(solution)/shard_map/ppermute | solution.py:200
  77.9 7.2 %collective-permute-start.15 = (bf16[256,512]{1,0:T(8,128)(2,1)S(1)}, bf16[256,512]{1,0:T(8,128)(2,1)S(1)}, u32[]{:S(2)}, u32[]{:S(2)}) collective-permute-start(bf16[256,512]{1,0:T(8,128)(2,1)S(1)} %slice.114), channel_id=1, source_target_pairs={{0,2},{4,0},{8,4},{12,8},{14,12},{10,14},{6,10},{2,6},{1,3},{5,1},... | collective-permute-start | bytes 786440 | tf_op jit(solution)/shard_map/ppermute | solution.py:227
  86.5 4.3 %collective-permute-done.15 = bf16[256,512]{1,0:T(8,128)(2,1)S(1)} collective-permute-done((bf16[256,512]{1,0:T(8,128)(2,1)S(1)}, bf16[256,512]{1,0:T(8,128)(2,1)S(1)}, u32[]{:S(2)}, u32[]{:S(2)}) %collective-permute-start.15) | collective-permute-done | bytes 262176 | tf_op jit(solution)/shard_map/ppermute | solution.py:227
  90.7 2.9 %collective-permute-start.5 = (f16[64,640]{1,0:T(8,128)(2,1)S(1)}, f16[64,640]{1,0:T(8,128)(2,1)S(1)}, u32[]{:S(2)}, u32[]{:S(2)}) collective-permute-start(f16[64,640]{1,0:T(8,128)(2,1)S(1)} %get-tuple-element.31), channel_id=1, source_target_pairs={{0,12},{4,14},{8,10},{12,6},{14,2},{10,0},{6,4},{2,8},{1,13},{5,15... | collective-permute-start | bytes 245768 | tf_op jit(solution)/shard_map/ppermute | solution.py:227
  93.7 2.2 %collective-permute-done.5 = f16[64,640]{1,0:T(8,128)(2,1)S(1)} collective-permute-done((f16[64,640]{1,0:T(8,128)(2,1)S(1)}, f16[64,640]{1,0:T(8,128)(2,1)S(1)}, u32[]{:S(2)}, u32[]{:S(2)}) %collective-permute-start.5) | collective-permute-done | bytes 81952 | tf_op jit(solution)/shard_map/ppermute | solution.py:227
  95.8 1.9 collective-permute-start.6
  100.0 4.4 %collective-permute-start.12 = (bf16[512,512]{1,0:T(8,128)(2,1)}, bf16[512,512]{1,0:T(8,128)(2,1)}, u32[]{:S(2)}, u32[]{:S(2)}) collective-permute-start(bf16[512,512]{1,0:T(8,128)(2,1)} %collective-permute-done.11.refs_4_), channel_id=1, source_target_pairs={{0,1},{1,0},{2,3},{3,2},{4,5},{5,4},{6,7},{7,6},{8,9},{9,8},{10,11... | collective-permute-start | bytes 1572872 | tf_op jit(solution)/shard_map/ppermute | solution.py:200
  109.2 2.3 %convert_element_type.62.mass = f32[8,64,640]{2,1,0:T(8,128)} convert(f16[8,64,640]{2,1,0:T(8,128)(2,1)} %bitcast_dynamic-update-slice_fusion.7) | non-fusion elementwise | flops 327680 | bytes 1966080 | tf_op jit(solution)/shard_map/convert_element_type | solution.py:262
  113.4 19.6 %shard_map.123 = (f32[8,64,512]{2,1,0:T(8,128)}, f32[8,64,640]{2,1,0:T(8,128)}, f32[64,1024]{1,0:T(8,128)}, f32[64,1024]{1,0:T(8,128)}, f32[8,8,512]{2,1,0:T(8,128)}) custom-call(s32[16]{0:T(128)} %pad_add_fusion.table, f32[8,64,640]{2,1,0:T(8,128)} %convert_element_type.62.mass, bf16[512,512]{1,0:T(8,128)(2,1)} %bitcast.118, ...), custom_call_target="tpu_custom_call" | custom-call | tf_op jit(solution)/shard_map/pallas_call | solution.py:185
  133.1 19.2 %shard_map.124 = f32[8,64,640]{2,1,0:T(8,128)} custom-call(s32[16]{0:T(128)} %pad_add_fusion.table, f32[8,64,640]{2,1,0:T(8,128)} %convert_element_type.62.mass, f32[8,64,640]{2,1,0:T(8,128)} %convert_element_type.72.cot, f32[8,64,512]{2,1,0:T(8,128)} %get-tuple-element.10.row_two, f32[8,64,640]{2,1,0:T(8,128)} %get-tuple-element.9.thirds, ...), custom_call_target="tpu_custom_call" | custom-call | tf_op jit(solution)/shard_map/pallas_call | solution.py:185
  157.2 2.2 %collective-permute-start.28 = (f16[64,640]{1,0:T(8,128)(2,1)S(1)}, f16[64,640]{1,0:T(8,128)(2,1)S(1)}, u32[]{:S(2)}, u32[]{:S(2)}) collective-permute-start(f16[64,640]{1,0:T(8,128)(2,1)S(1)} %get-tuple-element.20), channel_id=1, source_target_pairs={{0,12},{4,14},{8,10},{12,6},{14,2},{10,0},{6,4},{2,8},{1,13},{5,15... | collective-permute-start | bytes 245768 | tf_op jit(solution)/shard_map/ppermute | solution.py:227
  159.4 1.9 collective-permute-start.29
  161.8 4.2 %all-to-all-start = ((f16[8,64,640]{2,1,0:T(8,128)(2,1)}), f16[8,64,640]{2,1,0:T(8,128)(2,1)}, u32[]{:S(2)}, u32[]{:S(2)}) async-start(f16[8,64,640]{2,1,0:T(8,128)(2,1)} %convert_element_type.65), calls=%async_computation | async-start | bytes 1310720 | tf_op jit(solution)/shard_map/all_to_all | solution.py:295
  166.0 2.2 %collective-permute-start.31 = (f16[64,640]{1,0:T(8,128)(2,1)S(1)}, f16[64,640]{1,0:T(8,128)(2,1)S(1)}, u32[]{:S(2)}, u32[]{:S(2)}) collective-permute-start(f16[64,640]{1,0:T(8,128)(2,1)S(1)} %get-tuple-element.17), channel_id=1, source_target_pairs={{0,6},{4,2},{8,0},{12,4},{14,8},{10,12},{6,14},{2,10},{1,7},{5,3},... | collective-permute-start | bytes 245768 | tf_op jit(solution)/shard_map/ppermute | solution.py:227
  170.5 14.9 %collective-permute-done.31 = f16[64,640]{1,0:T(8,128)(2,1)S(1)} collective-permute-done((f16[64,640]{1,0:T(8,128)(2,1)S(1)}, f16[64,640]{1,0:T(8,128)(2,1)S(1)}, u32[]{:S(2)}, u32[]{:S(2)}) %collective-permute-start.31) | collective-permute-done | bytes 81952 | tf_op jit(solution)/shard_map/ppermute | solution.py:227
  186.7 3.4 %collective-permute-start.33 = (f16[64,512]{1,0:T(8,128)(2,1)S(1)}, f16[64,512]{1,0:T(8,128)(2,1)S(1)}, u32[]{:S(2)}, u32[]{:S(2)}) collective-permute-start(f16[64,512]{1,0:T(8,128)(2,1)S(1)} %slice_convert_fusion), channel_id=1, source_target_pairs={{0,1},{1,0},{2,3},{3,2},{4,5},{5,4},{6,7},{7,6},{8,9},{9,8},{10,11... | collective-permute-start | bytes 196616 | tf_op jit(solution)/shard_map/ppermute | solution.py:200
  194.5 3.7 %bitcast_add_fusion = (f32[512,512]{1,0:T(8,128)}, f32[512,512]{1,0:T(8,128)}) fusion(f32[512,512]{0,1:T(8,128)} %copy.38, f32[512,512]{1,0:T(8,128)} %param.14, f32[512,512]{1,0:T(8,128)S(1)} %copy-done.5, f32[512,512]{0,1:T(8,128)} %copy.36), kind=kLoop, calls=%fused_computation.11 | loop fusion | flops 1048576 | bytes 6291456 | tf_op jit(solution)/shard_map/add | solution.py:305
  (164 shorter events, 51.8 us)
Async XLA Ops:
  3.2 101.9 %collective-permute-start.8 = (bf16[512,512]{1,0:T(8,128)(2,1)S(1)}, bf16[512,512]{1,0:T(8,128)(2,1)}, u32[]{:S(2)}, u32[]{:S(2)}) collective-permute-start(bf16[512,512]{1,0:T(8,128)(2,1)S(1)} %bitcast.115), channel_id=1, source_target_pairs={{0,1},{1,0},{2,3},{3,2},{4,5},{5,4},{6,7},{7,6},{8,9},{9,8},{10,11... | collective-permute-start | bytes 1572872 | tf_op jit(solution)/shard_map/ppermute | solution.py:200
  3.4 15.1 %collective-permute-start.9 = (bf16[512,512]{1,0:T(8,128)(2,1)S(1)}, bf16[512,512]{1,0:T(8,128)(2,1)}, u32[]{:S(2)}, u32[]{:S(2)}) collective-permute-start(bf16[512,512]{1,0:T(8,128)(2,1)S(1)} %bitcast.116), channel_id=1, source_target_pairs={{0,2},{4,0},{8,4},{12,8},{14,12},{10,14},{6,10},{2,6},{1,3},{5,1},... | collective-permute-start | bytes 1572872 | tf_op jit(solution)/shard_map/ppermute | solution.py:227
  6.0 13.6 %collective-permute-start.16 = (bf16[512,512]{1,0:T(8,128)(2,1)S(1)}, bf16[512,512]{1,0:T(8,128)(2,1)}, u32[]{:S(2)}, u32[]{:S(2)}) collective-permute-start(bf16[512,512]{1,0:T(8,128)(2,1)S(1)} %bitcast.117), channel_id=1, source_target_pairs={{0,4},{4,8},{8,12},{12,14},{14,10},{10,6},{6,2},{2,0},{1,5},{5,9},... | collective-permute-start | bytes 1572872 | tf_op jit(solution)/shard_map/ppermute | solution.py:227
  9.6 28.5 %collective-permute-start = (f16[64,512]{0,1:T(8,128)(2,1)}, f16[64,512]{0,1:T(8,128)(2,1)}, u32[]{:S(2)}, u32[]{:S(2)}) collective-permute-start(f16[64,512]{0,1:T(8,128)(2,1)} %bitcast.134), channel_id=1, source_target_pairs={{0,1},{1,0},{2,3},{3,2},{4,5},{5,4},{6,7},{7,6},{8,9},{9,8},{10,11... | collective-permute-start | bytes 196616 | tf_op jit(solution)/shard_map/ppermute | solution.py:200
  10.8 30.3 %collective-permute-start.25 = (f16[64,512]{0,1:T(8,128)(2,1)}, f16[64,512]{0,1:T(8,128)(2,1)S(1)}, u32[]{:S(2)}, u32[]{:S(2)}) collective-permute-start(f16[64,512]{0,1:T(8,128)(2,1)} %bitcast.133), channel_id=1, source_target_pairs={{0,1},{1,0},{2,3},{3,2},{4,5},{5,4},{6,7},{7,6},{8,9},{9,8},{10,11... | collective-permute-start | bytes 196616 | tf_op jit(solution)/shard_map/ppermute | solution.py:200
  18.4 29.8 %collective-permute-start.11 = (bf16[512,512]{1,0:T(8,128)(2,1)}, bf16[512,512]{1,0:T(8,128)(2,1)}, u32[]{:S(2)}, u32[]{:S(2)}) collective-permute-start(bf16[512,512]{1,0:T(8,128)(2,1)} %collective-permute-done.9.refs_2_), channel_id=1, source_target_pairs={{0,2},{4,0},{8,4},{12,8},{14,12},{10,14},{6,10},{2,6},{1,3},{5,1},... | collective-permute-start | bytes 1572872 | tf_op jit(solution)/shard_map/ppermute | solution.py:227
  19.6 30.0 %collective-permute-start.17 = (bf16[512,512]{1,0:T(8,128)(2,1)}, bf16[512,512]{1,0:T(8,128)(2,1)}, u32[]{:S(2)}, u32[]{:S(2)}) collective-permute-start(bf16[512,512]{1,0:T(8,128)(2,1)} %collective-permute-done.16.refs_14_), channel_id=1, source_target_pairs={{0,4},{4,8},{8,12},{12,14},{14,10},{10,6},{6,2},{2,0},{1,5},{5,9},... | collective-permute-start | bytes 1572872 | tf_op jit(solution)/shard_map/ppermute | solution.py:227
  41.1 13.5 %collective-permute-start.2 = (f16[64,640]{1,0:T(8,128)(2,1)}, f16[64,640]{1,0:T(8,128)(2,1)}, u32[]{:S(2)}, u32[]{:S(2)}) collective-permute-start(f16[64,640]{1,0:T(8,128)(2,1)} %get-tuple-element.27), channel_id=1, source_target_pairs={{0,6},{4,2},{8,0},{12,4},{14,8},{10,12},{6,14},{2,10},{1,7},{5,3},... | collective-permute-start | bytes 245768 | tf_op jit(solution)/shard_map/ppermute | solution.py:227
  44.6 66.9 %all-to-all-start.1 = ((f16[8,64,640]{2,1,0:T(8,128)(2,1)}), f16[8,64,640]{2,1,0:T(8,128)(2,1)S(1)}, u32[]{:S(2)}, u32[]{:S(2)}) async-start(f16[8,64,640]{2,1,0:T(8,128)(2,1)} %pad_maximum_fusion), calls=%async_computation.1 | async-start | bytes 1310720 | tf_op jit(solution)/shard_map/all_to_all | solution.py:263
  48.3 22.1 %collective-permute-start.13 = (bf16[512,512]{1,0:T(8,128)(2,1)}, bf16[512,512]{1,0:T(8,128)(2,1)S(1)}, u32[]{:S(2)}, u32[]{:S(2)}) collective-permute-start(bf16[512,512]{1,0:T(8,128)(2,1)} %collective-permute-done.11.refs_4_), channel_id=1, source_target_pairs={{0,2},{4,0},{8,4},{12,8},{14,12},{10,14},{6,10},{2,6},{1,3},{5,1},... | collective-permute-start | bytes 1572872 | tf_op jit(solution)/shard_map/ppermute | solution.py:227
  49.6 28.2 %collective-permute-start.18 = (bf16[512,512]{1,0:T(8,128)(2,1)}, bf16[512,512]{1,0:T(8,128)(2,1)S(1)}, u32[]{:S(2)}, u32[]{:S(2)}) collective-permute-start(bf16[512,512]{1,0:T(8,128)(2,1)} %collective-permute-done.17.refs_12_), channel_id=1, source_target_pairs={{0,4},{4,8},{8,12},{12,14},{14,10},{10,6},{6,2},{2,0},{1,5},{5,9},... | collective-permute-start | bytes 1572872 | tf_op jit(solution)/shard_map/ppermute | solution.py:227
  49.9 24.0 %collective-permute-start.3 = (f16[64,640]{1,0:T(8,128)(2,1)}, f16[64,640]{1,0:T(8,128)(2,1)S(1)}, u32[]{:S(2)}, u32[]{:S(2)}) collective-permute-start(f16[64,640]{1,0:T(8,128)(2,1)} %get-tuple-element.28), channel_id=1, source_target_pairs={{0,10},{4,6},{8,2},{12,0},{14,4},{10,8},{6,12},{2,14},{1,11},{5,7}... | collective-permute-start | bytes 245768 | tf_op jit(solution)/shard_map/ppermute | solution.py:227
  54.6 31.1 %collective-permute-start.4 = (f16[64,640]{1,0:T(8,128)(2,1)S(1)}, f16[64,640]{1,0:T(8,128)(2,1)S(1)}, u32[]{:S(2)}, u32[]{:S(2)}) collective-permute-start(f16[64,640]{1,0:T(8,128)(2,1)S(1)} %copy-done.18), channel_id=1, source_target_pairs={{0,14},{4,10},{8,6},{12,2},{14,0},{10,4},{6,8},{2,12},{1,15},{5,11... | collective-permute-start | bytes 245768 | tf_op jit(solution)/shard_map/ppermute | solution.py:227
  70.4 34.8 %collective-permute-start.10 = (bf16[512,512]{1,0:T(8,128)(2,1)}, bf16[512,512]{1,0:T(8,128)(2,1)S(1)}, u32[]{:S(2)}, u32[]{:S(2)}) collective-permute-start(bf16[512,512]{1,0:T(8,128)(2,1)} %collective-permute-done.9.refs_2_), channel_id=1, source_target_pairs={{0,1},{1,0},{2,3},{3,2},{4,5},{5,4},{6,7},{7,6},{8,9},{9,8},{10,11... | collective-permute-start | bytes 1572872 | tf_op jit(solution)/shard_map/ppermute | solution.py:200
  73.9 32.0 %collective-permute-start.23 = (bf16[512,512]{1,0:T(8,128)(2,1)}, bf16[512,512]{1,0:T(8,128)(2,1)S(1)}, u32[]{:S(2)}, u32[]{:S(2)}) collective-permute-start(bf16[512,512]{1,0:T(8,128)(2,1)} %collective-permute-done.16.refs_14_), channel_id=1, source_target_pairs={{0,1},{1,0},{2,3},{3,2},{4,5},{5,4},{6,7},{7,6},{8,9},{9,8},{10,11... | collective-permute-start | bytes 1572872 | tf_op jit(solution)/shard_map/ppermute | solution.py:200
  77.9 12.9 %collective-permute-start.15 = (bf16[256,512]{1,0:T(8,128)(2,1)S(1)}, bf16[256,512]{1,0:T(8,128)(2,1)S(1)}, u32[]{:S(2)}, u32[]{:S(2)}) collective-permute-start(bf16[256,512]{1,0:T(8,128)(2,1)S(1)} %slice.114), channel_id=1, source_target_pairs={{0,2},{4,0},{8,4},{12,8},{14,12},{10,14},{6,10},{2,6},{1,3},{5,1},... | collective-permute-start | bytes 786440 | tf_op jit(solution)/shard_map/ppermute | solution.py:227
  85.7 12.0 %collective-permute-start.19 = (bf16[256,512]{1,0:T(8,128)(2,1)S(1)}, bf16[256,512]{1,0:T(8,128)(2,1)S(1)}, u32[]{:S(2)}, u32[]{:S(2)}) collective-permute-start(bf16[256,512]{1,0:T(8,128)(2,1)S(1)} %slice.115), channel_id=1, source_target_pairs={{0,4},{4,8},{8,12},{12,14},{14,10},{10,6},{6,2},{2,0},{1,5},{5,9},... | collective-permute-start | bytes 786440 | tf_op jit(solution)/shard_map/ppermute | solution.py:227
  100.0 12.6 %collective-permute-start.12 = (bf16[512,512]{1,0:T(8,128)(2,1)}, bf16[512,512]{1,0:T(8,128)(2,1)}, u32[]{:S(2)}, u32[]{:S(2)}) collective-permute-start(bf16[512,512]{1,0:T(8,128)(2,1)} %collective-permute-done.11.refs_4_), channel_id=1, source_target_pairs={{0,1},{1,0},{2,3},{3,2},{4,5},{5,4},{6,7},{7,6},{8,9},{9,8},{10,11... | collective-permute-start | bytes 1572872 | tf_op jit(solution)/shard_map/ppermute | solution.py:200
  153.9 12.1 %collective-permute-start.26 = (f16[64,640]{1,0:T(8,128)(2,1)S(1)}, f16[64,640]{1,0:T(8,128)(2,1)S(1)}, u32[]{:S(2)}, u32[]{:S(2)}) collective-permute-start(f16[64,640]{1,0:T(8,128)(2,1)S(1)} %get-tuple-element.22), channel_id=1, source_target_pairs={{0,4},{4,8},{8,12},{12,14},{14,10},{10,6},{6,2},{2,0},{1,5},{5,9},... | collective-permute-start | bytes 245768 | tf_op jit(solution)/shard_map/ppermute | solution.py:227
  155.5 12.8 %collective-permute-start.27 = (f16[64,640]{1,0:T(8,128)(2,1)S(1)}, f16[64,640]{1,0:T(8,128)(2,1)S(1)}, u32[]{:S(2)}, u32[]{:S(2)}) collective-permute-start(f16[64,640]{1,0:T(8,128)(2,1)S(1)} %get-tuple-element.21), channel_id=1, source_target_pairs={{0,8},{4,12},{8,14},{12,10},{14,6},{10,2},{6,0},{2,4},{1,9},{5,13}... | collective-permute-start | bytes 245768 | tf_op jit(solution)/shard_map/ppermute | solution.py:227
  157.2 13.2 %collective-permute-start.28 = (f16[64,640]{1,0:T(8,128)(2,1)S(1)}, f16[64,640]{1,0:T(8,128)(2,1)S(1)}, u32[]{:S(2)}, u32[]{:S(2)}) collective-permute-start(f16[64,640]{1,0:T(8,128)(2,1)S(1)} %get-tuple-element.20), channel_id=1, source_target_pairs={{0,12},{4,14},{8,10},{12,6},{14,2},{10,0},{6,4},{2,8},{1,13},{5,15... | collective-permute-start | bytes 245768 | tf_op jit(solution)/shard_map/ppermute | solution.py:227
  161.8 29.7 %all-to-all-start = ((f16[8,64,640]{2,1,0:T(8,128)(2,1)}), f16[8,64,640]{2,1,0:T(8,128)(2,1)}, u32[]{:S(2)}, u32[]{:S(2)}) async-start(f16[8,64,640]{2,1,0:T(8,128)(2,1)} %convert_element_type.65), calls=%async_computation | async-start | bytes 1310720 | tf_op jit(solution)/shard_map/all_to_all | solution.py:295
  166.0 19.4 %collective-permute-start.31 = (f16[64,640]{1,0:T(8,128)(2,1)S(1)}, f16[64,640]{1,0:T(8,128)(2,1)S(1)}, u32[]{:S(2)}, u32[]{:S(2)}) collective-permute-start(f16[64,640]{1,0:T(8,128)(2,1)S(1)} %get-tuple-element.17), channel_id=1, source_target_pairs={{0,6},{4,2},{8,0},{12,4},{14,8},{10,12},{6,14},{2,10},{1,7},{5,3},... | collective-permute-start | bytes 245768 | tf_op jit(solution)/shard_map/ppermute | solution.py:227
  168.3 17.1 %collective-permute-start.32 = (f16[64,640]{1,0:T(8,128)(2,1)S(1)}, f16[64,640]{1,0:T(8,128)(2,1)S(1)}, u32[]{:S(2)}, u32[]{:S(2)}) collective-permute-start(f16[64,640]{1,0:T(8,128)(2,1)S(1)} %get-tuple-element.16), channel_id=1, source_target_pairs={{0,2},{4,0},{8,4},{12,8},{14,12},{10,14},{6,10},{2,6},{1,3},{5,1},... | collective-permute-start | bytes 245768 | tf_op jit(solution)/shard_map/ppermute | solution.py:227
  (34 other events, 298.5 us)

commit v2 on v1

--- a/solution.py
+++ b/solution.py
@@ -50,31 +50,39 @@
         self.hists = hists
         self.share = share
         self.lanes = rows + 2 * share
+        self.units = []
+        for d in range(count):
+            if 2 * d == count:
+                self.units += [(d, 0, rows // 2), (d, rows // 2, rows // 2)]
+            else:
+                self.units.append((d, 0, rows))
 
 
 def load_matrix(s, units, matrix, sems):
     copies = []
-    for d in range(s.count):
+    for k, (d, start, size) in enumerate(s.units):
         for t in range(2):
             copy = pltpu.make_async_copy(
-                units[2 * d + t], matrix.at[d, :, pl.ds(t * s.cols, s.cols)], sems.at[d]
+                units[2 * k + t],
+                matrix.at[d, pl.ds(start, size), pl.ds(t * s.cols, s.cols)],
+                sems.at[d],
             )
             copy.start()
             copies.append(copy)
     return copies
 
 
-def gather_targets(s, pieces, index):
+def gather_targets(s, pieces):
     parts = []
     for t in range(2):
         lo = s.rows + t * s.share
-        parts += [pieces[index(i), :, lo : lo + s.share] for i in range(s.count)]
+        parts += [pieces[i, :, lo : lo + s.share] for i in range(s.count)]
     return jnp.concatenate(parts, axis=1)
 
 
-def scatter_targets(s, out, index, values):
+def scatter_targets(s, out, values):
     for i in range(s.count):
-        out[index(i), :, s.rows : s.lanes] = jnp.concatenate(
+        out[i, :, s.rows : s.lanes] = jnp.concatenate(
             [
                 values[:, t * s.cols + i * s.share : t * s.cols + (i + 1) * s.share]
                 for t in range(2)
@@ -92,15 +100,12 @@
 
 
 def forward_kernel(s, table, mass, *refs):
-    units, (row_two, thirds, col_one_out, col_two_out, row_one) = (
-        refs[: 2 * s.count],
-        refs[2 * s.count : 2 * s.count + 5],
-    )
-    matrix, sems = refs[2 * s.count + 5 :]
+    given = 2 * len(s.units)
+    units = refs[:given]
+    row_two, thirds, col_one_out, col_two_out, row_one, matrix, sems = refs[given:]
     copies = load_matrix(s, units, matrix, sems)
     zero = jnp.zeros((s.hists, 2 * s.cols), jnp.float32)
-    inverse = lambda i: table[s.count + i]
-    target = gather_targets(s, mass, inverse)
+    target = gather_targets(s, mass)
     for copy in copies:
         copy.wait()
     ones = jnp.ones((8, 2 * s.cols), jnp.bfloat16)
@@ -108,7 +113,7 @@
     def first(d, total):
         sums = nt(ones, matrix[d])
         row_one[d] = sums
-        left = mass[d, :, : s.rows] / sums[0:1]
+        left = mass[table[d], :, : s.rows] / sums[0:1]
         return total + nn(left.astype(jnp.bfloat16), matrix[d])
 
     col_one = each(s.count, first, zero)
@@ -118,7 +123,7 @@
     def second(d, total):
         row = nt(panel, matrix[d])
         row_two[d] = row
-        left = mass[d, :, : s.rows] / row
+        left = mass[table[d], :, : s.rows] / row
         return total + nn(left.astype(jnp.bfloat16), matrix[d])
 
     col_two = each(s.count, second, zero)
@@ -129,21 +134,22 @@
         row = nt(panel, matrix[d])
         k = table[d]
         thirds[k, :, : s.rows] = row
-        left = mass[d, :, : s.rows] / row
+        left = mass[table[d], :, : s.rows] / row
         return total + nn(left.astype(jnp.bfloat16), matrix[d])
 
     col_three = each(s.count, third, zero)
-    scatter_targets(s, thirds, lambda i: i, col_three)
+    scatter_targets(s, thirds, col_three)
 
 
 def backward_kernel(s, table, mass, cot, row_two, thirds, col_one, col_two, row_one, *refs):
-    units, out, (matrix, sems) = refs[: 2 * s.count], refs[2 * s.count], refs[2 * s.count + 1 :]
+    given = 2 * len(s.units)
+    units = refs[:given]
+    out, matrix, sems = refs[given:]
     copies = load_matrix(s, units, matrix, sems)
     zero = jnp.zeros((s.hists, 2 * s.cols), jnp.float32)
-    inverse = lambda i: table[s.count + i]
-    target = gather_targets(s, mass, inverse)
-    target_cot = gather_targets(s, cot, lambda i: i)
-    col_three = gather_targets(s, thirds, lambda i: i)
+    target = gather_targets(s, mass)
+    target_cot = gather_targets(s, cot)
+    col_three = gather_targets(s, thirds)
     right_one = target / col_one[...]
     right_two = target / col_two[...]
     for copy in copies:
@@ -154,9 +160,9 @@
         k = table[d]
         grad = nt(panel, matrix[d])
         row = thirds[k, :, : s.rows]
-        left = mass[d, :, : s.rows] / row
+        left = mass[table[d], :, : s.rows] / row
         term = grad / row
-        out[d, :, : s.rows] = term
+        out[table[d], :, : s.rows] = term
         rowgrad = -(cot[k, :, : s.rows] / row + term * left)
         return total + nn(rowgrad.astype(jnp.bfloat16), matrix[d])
 
@@ -166,19 +172,19 @@
     def second(d, total):
         row = row_two[d]
         term = nt(panel, matrix[d]) / row
-        out[d, :, : s.rows] += term
-        rowgrad = -term * (mass[d, :, : s.rows] / row)
+        out[table[d], :, : s.rows] += term
+        rowgrad = -term * (mass[table[d], :, : s.rows] / row)
         return total + nn(rowgrad.astype(jnp.bfloat16), matrix[d])
 
     term_one = each(s.count, second, zero) / col_one[...]
     panel = (-term_one * right_one).astype(jnp.bfloat16)
 
     def first(d, carry):
-        out[d, :, : s.rows] += nt(panel, matrix[d]) / row_one[d, 0:1]
+        out[table[d], :, : s.rows] += nt(panel, matrix[d]) / row_one[d, 0:1]
         return carry
 
     each(s.count, first, 0)
-    scatter_targets(s, out, inverse, term_two + term_one)
+    scatter_targets(s, out, term_two + term_one)
 
 
 def call(kernel, s, outs, table, arrays, units):
@@ -192,6 +198,11 @@
             pltpu.VMEM((s.count, s.rows, 2 * s.cols), jnp.bfloat16),
             pltpu.SemaphoreType.DMA((s.count,)),
         ],
+        cost_estimate=pl.CostEstimate(
+            flops=6 * 2 * s.count * s.rows * 2 * s.cols * 256,
+            bytes_accessed=s.count * s.rows * 2 * s.cols * 4,
+            transcendentals=0,
+        ),
         compiler_params=pltpu.CompilerParams(vmem_limit_bytes=VMEM),
     )(table, *arrays, *units)
 
@@ -218,28 +229,14 @@
     me = lax.axis_index("src")
     core = lax.axis_index("tgt")
     at = jnp.asarray(place)[me]
-    order = jnp.asarray(ring)[(at + jnp.arange(count, dtype=jnp.int32)) % count]
-    inverse = (jnp.asarray(place) - at) % count
-    table = jnp.concatenate([order, inverse]).astype(jnp.int32)
+    table = jnp.asarray(ring)[(at + jnp.arange(count, dtype=jnp.int32)) % count]
 
     def shift(x, distance):
         pairs = [(int(ring[p]), int(ring[(p + distance) % count])) for p in range(count)]
         return lax.ppermute(x, "src", pairs)
 
-    unit = dense_blocks(kernel_tiles, tile_cols, tile_count)
-    held = {0: unit}
-    for step in range(1, count // 2 + 1):
-        if step < count - step:
-            held[step] = shift(held[step - 1], -1)
-            held[count - step] = shift(held[(count - step + 1) % count], 1)
-        else:
-            middle = rows // 2
-            ahead = shift(held[step - 1][:middle], -1)
-            behind = shift(held[step + 1][middle:], 1)
-            held[step] = jnp.concatenate([ahead, behind])
-    units = []
-    for d in range(count):
-        units += [held[d], swap_cores(held[d])]
+    def exchange(x):
+        return lax.all_to_all(x, "src", 0, 0, tiled=True)
 
     def by_histogram(source, target):
         target = target.astype(HALF).reshape(share, 2, cols_here)
@@ -254,19 +251,42 @@
             axis=2,
         )
 
-    message = by_histogram(source_mass, target_mass[0])
-    parts = []
-    for d in range(count):
-        chunk = lax.dynamic_index_in_dim(message, order[(count - d) % count], 0, keepdims=False)
-        parts.append(shift(chunk, -d) if d else chunk)
-    mass = jnp.stack(parts).astype(jnp.float32)
-    cot = lax.all_to_all(
-        by_histogram(source_cotangent * COT_SCALE, target_cotangent[0] * COT_SCALE),
-        "src",
-        0,
-        0,
-        tiled=True,
-    ).astype(jnp.float32)
+    mass_message = by_histogram(source_mass, target_mass[0])
+    cot_message = by_histogram(source_cotangent * COT_SCALE, target_cotangent[0] * COT_SCALE)
+    mass = None
+
+    ahead = behind = dense_blocks(kernel_tiles, tile_cols, tile_count)
+    pieces = {(0, 0): ahead}
+    swapped = {(0, 0): swap_cores(ahead)}
+    before = []
+    rounds = count // 2
+    for step in range(1, rounds + 1):
+        ready = [swapped[k] for k in before]
+        if step == min(2, rounds):
+            ready.append(mass_message)
+        if step == rounds:
+            mass = exchange(mass_message).astype(jnp.float32)
+            ready += [mass, cot_message]
+        (ahead, behind), ready = lax.optimization_barrier(((ahead, behind), ready))
+        for k, piece in zip(before, ready):
+            swapped[k] = piece
+        if step == min(2, rounds):
+            mass_message = ready[len(before)]
+        if step == rounds:
+            mass, cot_message = ready[-2:]
+        if 2 * step == count:
+            ahead, behind = ahead[: rows // 2], behind[rows // 2 :]
+            new = {(step, 0): shift(ahead, -1), (step, rows // 2): shift(behind, 1)}
+        else:
+            ahead, behind = shift(ahead, -1), shift(behind, 1)
+            new = {(step, 0): ahead, (count - step, 0): behind}
+        before = list(new) if step > 1 else [(0, 0), *new]
+        pieces.update(new)
+        swapped.update({k: swap_cores(v) for k, v in new.items()})
+    units = []
+    for d, start, _ in s.units:
+        units += [pieces[d, start], swapped[d, start]]
+    cot = exchange(cot_message).astype(jnp.float32)
 
     panel = jax.ShapeDtypeStruct((count, s.hists, rows), jnp.float32)
     wide = jax.ShapeDtypeStruct((count, s.hists, s.lanes), jnp.float32)
@@ -292,13 +312,8 @@
         halves = [jnp.where(core == t, own, other) for t in range(2)]
         return flat[:, :rows].T, jnp.concatenate(halves, axis=1)
 
-    row_three, col_three = by_point(lax.all_to_all(thirds.astype(HALF), "src", 0, 0, tiled=True))
-    parts = []
-    narrow = grads.astype(HALF)
-    for d in range(count):
-        parts.append(shift(narrow[d], d) if d else narrow[d])
-    back = jnp.stack(parts)[(at - jnp.asarray(place)) % count]
-    source_term, target_term = by_point(back)
+    row_three, col_three = by_point(exchange(thirds.astype(HALF)))
+    source_term, target_term = by_point(exchange(grads.astype(HALF)))
     return (
         jnp.log(source_mass / row_three),
         jnp.log(target_mass[0] / col_three)[None],

time: 200 us -> 176 us (0.88)
  waiting for transfers between devices: 38.1 us -> 63.4 us
  starting transfers between devices: 63.1 us -> 41 us
  between operations: 16.4 us -> 1.07 us
  local copies, waits for them, and re-layouts: 21.4 us -> 11.5 us
    ppermute x22 -> x8, starting transfers between devices: 37.5 us -> 10.1 us  [shift(): return lax.ppermute(x, 'src', pairs)]
    ppermute x22 -> x8, waiting for transfers between devices: 38.1 us -> 51.4 us  [shift(): return lax.ppermute(x, 'src', pairs)]
    all_to_all x2 -> x4, waiting for transfers between devices: 0.01 us -> 10.7 us  [exchange(): return lax.all_to_all(x, 'src', 0, 0, tiled=True)]
    all_to_all x2 -> x4, starting transfers between devices: 7.88 us -> 17.9 us  [exchange(): return lax.all_to_all(x, 'src', 0, 0, tiled=True)]
    unnamed x62 -> x47, local copies, waits for them, and re-layouts: 11 us -> 4.69 us
    ppermute x12 -> x13, starting transfers between devices: 17.7 us -> 12.9 us  [swap_cores(): return lax.ppermute(x, 'tgt', [(0, 1), (1, 0)])]
  transfers between devices with their start and end apart: 36 -> 25, of which waited for: 7 -> 9; matrix products, arithmetic and copies ran while one was open for 17% -> 14% of each run, Pallas kernels for 0% -> 22%
where the time goes in v2:
time: 176 us; the launch traced here: 175 us
  waiting for transfers between devices  63.4 us (36%)
  starting transfers between devices  41 us (23%)
  Pallas kernels  38.6 us (22%)
  other arithmetic  18 us (10%)
  local copies, waits for them, and re-layouts  11.5 us (7%)
    ppermute x8, waiting for transfers between devices, shift(): return lax.ppermute(x, 'src', pairs)  51.4 us
    pallas_call x2, Pallas kernels, call(): pl.pallas_call(functools.partial(kernel, s), out_shape=outs, in_specs=[pl...  38.6 us
    all_to_all x4, starting transfers between devices, exchange(): return lax.all_to_all(x, 'src', 0, 0, tiled=True)  17.9 us
    ppermute x13, starting transfers between devices, swap_cores(): return lax.ppermute(x, 'tgt', [(0, 1), (1, 0)])  12.9 us
    all_to_all x4, waiting for transfers between devices, exchange(): return lax.all_to_all(x, 'src', 0, 0, tiled=True)  10.7 us
    ppermute x8, starting transfers between devices, shift(): return lax.ppermute(x, 'src', pairs)  10.1 us
    unnamed x47, local copies, waits for them, and re-layouts  4.69 us
    add x1, other arithmetic, local(): source_cotangent / source_mass + source_term * (1 / COT_SCALE)  3.69 us
  transfers between devices with their start and end apart: 25, of which 9 were waited for; matrix products, arithmetic and copies ran while one was open for 14% of the time, Pallas kernels for 22%

profile of v2, /device:TPU:1, one launch (start us, length us, event | category | flops | bytes accessed | tf_op | source)
XLA Modules:
  0.0 175.1 jit_solution(460556677626709568)
XLA Ops:
  1.7 1.4 convolution_convert_fusion
  3.2 2.1 %collective-permute-start = (bf16[512,512]{1,0:T(8,128)(2,1)S(1)}, bf16[512,512]{1,0:T(8,128)(2,1)}, u32[]{:S(2)}, u32[]{:S(2)}) collective-permute-start(bf16[512,512]{1,0:T(8,128)(2,1)S(1)} %bitcast.61), channel_id=1, source_target_pairs={{0,2},{4,0},{8,4},{12,8},{14,12},{10,14},{6,10},{2,6},{1,3},{5,1},... | collective-permute-start | bytes 1572872 | tf_op jit(solution)/shard_map/ppermute | solution.py:236
  6.7 10.5 %collective-permute-done.refs_2_ = bf16[512,512]{1,0:T(8,128)(2,1)} collective-permute-done((bf16[512,512]{1,0:T(8,128)(2,1)S(1)}, bf16[512,512]{1,0:T(8,128)(2,1)}, u32[]{:S(2)}, u32[]{:S(2)}) %collective-permute-start) | collective-permute-done | bytes 524320 | tf_op jit(solution)/shard_map/ppermute | solution.py:236
  18.4 1.4 collective-permute-start.4
  24.0 1.3 collective-permute-start.6
  25.6 12.2 %collective-permute-done.6.refs_4_ = bf16[512,512]{1,0:T(8,128)(2,1)S(1)} collective-permute-done((bf16[512,512]{1,0:T(8,128)(2,1)}, bf16[512,512]{1,0:T(8,128)(2,1)S(1)}, u32[]{:S(2)}, u32[]{:S(2)}) %collective-permute-start.6) | collective-permute-done | bytes 524320 | tf_op jit(solution)/shard_map/ppermute | solution.py:236
  40.0 3.6 %all-to-all-start = ((f16[8,64,640]{2,1,0:T(8,128)(2,1)}), f16[8,64,640]{2,1,0:T(8,128)(2,1)S(1)}, u32[]{:S(2)}, u32[]{:S(2)}) async-start(f16[8,64,640]{2,1,0:T(8,128)(2,1)} %pad_maximum_fusion), calls=%async_computation | async-start | bytes 1310720 | tf_op jit(solution)/shard_map/all_to_all | solution.py:239
  43.7 1.5 collective-permute-start.10
  45.2 22.2 %collective-permute-done.10.refs_6_ = bf16[512,512]{1,0:T(8,128)(2,1)S(1)} collective-permute-done((bf16[512,512]{1,0:T(8,128)(2,1)}, bf16[512,512]{1,0:T(8,128)(2,1)S(1)}, u32[]{:S(2)}, u32[]{:S(2)}) %collective-permute-start.10) | collective-permute-done | bytes 524320 | tf_op jit(solution)/shard_map/ppermute | solution.py:236
  75.8 3.8 %collective-permute-start.17 = (bf16[256,512]{1,0:T(8,128)(2,1)S(1)}, bf16[256,512]{1,0:T(8,128)(2,1)S(1)}, u32[]{:S(2)}, u32[]{:S(2)}) collective-permute-start(bf16[256,512]{1,0:T(8,128)(2,1)S(1)} %slice.37), channel_id=1, source_target_pairs={{0,4},{4,8},{8,12},{12,14},{14,10},{10,6},{6,2},{2,0},{1,5},{5,9},... | collective-permute-start | bytes 786440 | tf_op jit(solution)/shard_map/ppermute | solution.py:236
  79.6 5.3 %collective-permute-done.15.refs_8_ = bf16[256,512]{1,0:T(8,128)(2,1)S(1)} collective-permute-done((bf16[256,512]{1,0:T(8,128)(2,1)S(1)}, bf16[256,512]{1,0:T(8,128)(2,1)S(1)}, u32[]{:S(2)}, u32[]{:S(2)}) %collective-permute-start.15) | collective-permute-done | bytes 262176 | tf_op jit(solution)/shard_map/ppermute | solution.py:236
  90.2 3.7 %all-to-all-start.2 = ((f16[8,64,640]{2,1,0:T(8,128)(2,1)}), f16[8,64,640]{2,1,0:T(8,128)(2,1)S(1)}, u32[]{:S(2)}, u32[]{:S(2)}) async-start(f16[8,64,640]{2,1,0:T(8,128)(2,1)} %pad_maximum_fusion.1), calls=%async_computation.2 | async-start | bytes 1310720 | tf_op jit(solution)/shard_map/all_to_all | solution.py:239
  95.4 19.6 %shard_map.123 = (f32[8,64,512]{2,1,0:T(8,128)}, f32[8,64,640]{2,1,0:T(8,128)}, f32[64,1024]{1,0:T(8,128)}, f32[64,1024]{1,0:T(8,128)}, f32[8,8,512]{2,1,0:T(8,128)}) custom-call(s32[8]{0:T(128)} %gather_fusion, f32[8,64,640]{2,1,0:T(8,128)} %convert_element_type.64.mass, bf16[512,512]{1,0:T(8,128)(2,1)} %bitcast.64, ...), custom_call_target="tpu_custom_call" | custom-call | flops 12884901888 | bytes 16777216 | tf_op jit(solution)/shard_map/pallas_call | solution.py:191
  115.0 2.3 %convert_element_type.68 = f16[8,64,640]{2,1,0:T(8,128)(2,1)} convert(f32[8,64,640]{2,1,0:T(8,128)} %get-tuple-element.44.thirds) | non-fusion elementwise | flops 327680 | bytes 1966080 | tf_op jit(solution)/shard_map/convert_element_type | solution.py:315
  117.2 5.2 %all-to-all-start.1 = ((f16[8,64,640]{2,1,0:T(8,128)(2,1)}), f16[8,64,640]{2,1,0:T(8,128)(2,1)S(1)}, u32[]{:S(2)}, u32[]{:S(2)}) async-start(f16[8,64,640]{2,1,0:T(8,128)(2,1)} %convert_element_type.68), calls=%async_computation.1 | async-start | bytes 1310720 | tf_op jit(solution)/shard_map/all_to_all | solution.py:239
  123.6 18.9 %shard_map.124 = f32[8,64,640]{2,1,0:T(8,128)} custom-call(s32[8]{0:T(128)} %gather_fusion, f32[8,64,640]{2,1,0:T(8,128)} %convert_element_type.64.mass, f32[8,64,640]{2,1,0:T(8,128)} %convert_element_type.72.cot, f32[8,64,512]{2,1,0:T(8,128)} %get-tuple-element.46.row_two, f32[8,64,640]{2,1,0:T(8,128)} %get-tuple-element.44.thirds, ...), custom_call_target="tpu_custom_call" | custom-call | flops 12884901888 | bytes 16777216 | tf_op jit(solution)/shard_map/pallas_call | solution.py:191
  142.5 2.2 %convert_element_type.73 = f16[8,64,640]{2,1,0:T(8,128)(2,1)} convert(f32[8,64,640]{2,1,0:T(8,128)} %shard_map.124) | non-fusion elementwise | flops 327680 | bytes 1966080 | tf_op jit(solution)/shard_map/convert_element_type | solution.py:316
  144.8 5.4 %all-to-all-start.3 = ((f16[8,64,640]{2,1,0:T(8,128)(2,1)}), f16[8,64,640]{2,1,0:T(8,128)(2,1)S(1)}, u32[]{:S(2)}, u32[]{:S(2)}) async-start(f16[8,64,640]{2,1,0:T(8,128)(2,1)} %convert_element_type.73), calls=%async_computation.3 | async-start | bytes 1310720 | tf_op jit(solution)/shard_map/all_to_all | solution.py:239
  152.5 1.3 copy.36
  153.9 1.6 fusion.5
  155.4 10.7 %all-to-all-done.3 = f16[8,64,640]{2,1,0:T(8,128)(2,1)S(1)} async-done(((f16[8,64,640]{2,1,0:T(8,128)(2,1)}), f16[8,64,640]{2,1,0:T(8,128)(2,1)S(1)}, u32[]{:S(2)}, u32[]{:S(2)}) %all-to-all-start.3) | async-done | bytes 655392 | tf_op jit(solution)/shard_map/all_to_all | solution.py:239
  166.4 1.3 copy.38
  167.9 2.5 %collective-permute-start.20 = (f16[64,512]{1,0:T(8,128)(2,1)S(1)}, f16[64,512]{1,0:T(8,128)(2,1)S(1)}, u32[]{:S(2)}, u32[]{:S(2)}) collective-permute-start(f16[64,512]{1,0:T(8,128)(2,1)S(1)} %slice_convert_fusion), channel_id=1, source_target_pairs={{0,1},{1,0},{2,3},{3,2},{4,5},{5,4},{6,7},{7,6},{8,9},{9,8},{10,11... | collective-permute-start | bytes 196616 | tf_op jit(solution)/shard_map/ppermute | solution.py:211
  170.4 3.7 %bitcast_add_fusion = (f32[512,512]{1,0:T(8,128)}, f32[512,512]{1,0:T(8,128)}) fusion(f32[512,512]{0,1:T(8,128)} %copy.38, f32[512,512]{1,0:T(8,128)} %param.14, f32[512,512]{1,0:T(8,128)S(1)} %copy-done.3, f32[512,512]{0,1:T(8,128)} %copy.36), kind=kLoop, calls=%fused_computation.2 | loop fusion | flops 1048576 | bytes 6291456 | tf_op jit(solution)/shard_map/add | solution.py:320
  (116 shorter events, 30.2 us)
Async XLA Ops:
  3.2 13.9 %collective-permute-start = (bf16[512,512]{1,0:T(8,128)(2,1)S(1)}, bf16[512,512]{1,0:T(8,128)(2,1)}, u32[]{:S(2)}, u32[]{:S(2)}) collective-permute-start(bf16[512,512]{1,0:T(8,128)(2,1)S(1)} %bitcast.61), channel_id=1, source_target_pairs={{0,2},{4,0},{8,4},{12,8},{14,12},{10,14},{6,10},{2,6},{1,3},{5,1},... | collective-permute-start | bytes 1572872 | tf_op jit(solution)/shard_map/ppermute | solution.py:236
  5.4 13.0 %collective-permute-start.1 = (bf16[512,512]{1,0:T(8,128)(2,1)S(1)}, bf16[512,512]{1,0:T(8,128)(2,1)}, u32[]{:S(2)}, u32[]{:S(2)}) collective-permute-start(bf16[512,512]{1,0:T(8,128)(2,1)S(1)} %bitcast.62), channel_id=1, source_target_pairs={{0,4},{4,8},{8,12},{12,14},{14,10},{10,6},{6,2},{2,0},{1,5},{5,9},... | collective-permute-start | bytes 1572872 | tf_op jit(solution)/shard_map/ppermute | solution.py:236
  5.5 18.6 %collective-permute-start.2 = (bf16[512,512]{1,0:T(8,128)(2,1)S(1)}, bf16[512,512]{1,0:T(8,128)(2,1)}, u32[]{:S(2)}, u32[]{:S(2)}) collective-permute-start(bf16[512,512]{1,0:T(8,128)(2,1)S(1)} %bitcast.63), channel_id=1, source_target_pairs={{0,1},{1,0},{2,3},{3,2},{4,5},{5,4},{6,7},{7,6},{8,9},{9,8},{10,11... | collective-permute-start | bytes 1572872 | tf_op jit(solution)/shard_map/ppermute | solution.py:211
  17.2 6.9 %collective-permute-start.3 = (bf16[512,512]{1,0:T(8,128)(2,1)}, bf16[512,512]{1,0:T(8,128)(2,1)}, u32[]{:S(2)}, u32[]{:S(2)}) collective-permute-start(bf16[512,512]{1,0:T(8,128)(2,1)} %collective-permute-done.refs_2_), channel_id=1, source_target_pairs={{0,1},{1,0},{2,3},{3,2},{4,5},{5,4},{6,7},{7,6},{8,9},{9,8},{10,11... | collective-permute-start | bytes 1572872 | tf_op jit(solution)/shard_map/ppermute | solution.py:211
  18.4 5.6 %collective-permute-start.4 = (bf16[512,512]{1,0:T(8,128)(2,1)}, bf16[512,512]{1,0:T(8,128)(2,1)}, u32[]{:S(2)}, u32[]{:S(2)}) collective-permute-start(bf16[512,512]{1,0:T(8,128)(2,1)} %collective-permute-done.1.refs_16_), channel_id=1, source_target_pairs={{0,1},{1,0},{2,3},{3,2},{4,5},{5,4},{6,7},{7,6},{8,9},{9,8},{10,11... | collective-permute-start | bytes 1572872 | tf_op jit(solution)/shard_map/ppermute | solution.py:211
  24.0 13.7 %collective-permute-start.6 = (bf16[512,512]{1,0:T(8,128)(2,1)}, bf16[512,512]{1,0:T(8,128)(2,1)S(1)}, u32[]{:S(2)}, u32[]{:S(2)}) collective-permute-start(bf16[512,512]{1,0:T(8,128)(2,1)} %collective-permute-done.refs_2_), channel_id=1, source_target_pairs={{0,2},{4,0},{8,4},{12,8},{14,12},{10,14},{6,10},{2,6},{1,3},{5,1},... | collective-permute-start | bytes 1572872 | tf_op jit(solution)/shard_map/ppermute | solution.py:236
  25.4 13.4 %collective-permute-start.7 = (bf16[512,512]{1,0:T(8,128)(2,1)}, bf16[512,512]{1,0:T(8,128)(2,1)}, u32[]{:S(2)}, u32[]{:S(2)}) collective-permute-start(bf16[512,512]{1,0:T(8,128)(2,1)} %collective-permute-done.1.refs_16_), channel_id=1, source_target_pairs={{0,4},{4,8},{8,12},{12,14},{14,10},{10,6},{6,2},{2,0},{1,5},{5,9},... | collective-permute-start | bytes 1572872 | tf_op jit(solution)/shard_map/ppermute | solution.py:236
  37.8 5.8 %collective-permute-start.8 = (bf16[512,512]{1,0:T(8,128)(2,1)S(1)}, bf16[512,512]{1,0:T(8,128)(2,1)}, u32[]{:S(2)}, u32[]{:S(2)}) collective-permute-start(bf16[512,512]{1,0:T(8,128)(2,1)S(1)} %collective-permute-done.6.refs_4_), channel_id=1, source_target_pairs={{0,1},{1,0},{2,3},{3,2},{4,5},{5,4},{6,7},{7,6},{8,9},{9,8},{10,11... | collective-permute-start | bytes 1572872 | tf_op jit(solution)/shard_map/ppermute | solution.py:211
  38.8 4.9 %collective-permute-start.9 = (bf16[512,512]{1,0:T(8,128)(2,1)}, bf16[512,512]{1,0:T(8,128)(2,1)}, u32[]{:S(2)}, u32[]{:S(2)}) collective-permute-start(bf16[512,512]{1,0:T(8,128)(2,1)} %collective-permute-done.7.refs_14_), channel_id=1, source_target_pairs={{0,1},{1,0},{2,3},{3,2},{4,5},{5,4},{6,7},{7,6},{8,9},{9,8},{10,11... | collective-permute-start | bytes 1572872 | tf_op jit(solution)/shard_map/ppermute | solution.py:211
  40.0 32.5 %all-to-all-start = ((f16[8,64,640]{2,1,0:T(8,128)(2,1)}), f16[8,64,640]{2,1,0:T(8,128)(2,1)S(1)}, u32[]{:S(2)}, u32[]{:S(2)}) async-start(f16[8,64,640]{2,1,0:T(8,128)(2,1)} %pad_maximum_fusion), calls=%async_computation | async-start | bytes 1310720 | tf_op jit(solution)/shard_map/all_to_all | solution.py:239
  43.7 23.8 %collective-permute-start.10 = (bf16[512,512]{1,0:T(8,128)(2,1)}, bf16[512,512]{1,0:T(8,128)(2,1)S(1)}, u32[]{:S(2)}, u32[]{:S(2)}) collective-permute-start(bf16[512,512]{1,0:T(8,128)(2,1)} %copy-done.15), channel_id=1, source_target_pairs={{0,2},{4,0},{8,4},{12,8},{14,12},{10,14},{6,10},{2,6},{1,3},{5,1},... | collective-permute-start | bytes 1572872 | tf_op jit(solution)/shard_map/ppermute | solution.py:236
  45.2 23.5 %collective-permute-start.11 = (bf16[512,512]{1,0:T(8,128)(2,1)}, bf16[512,512]{1,0:T(8,128)(2,1)}, u32[]{:S(2)}, u32[]{:S(2)}) collective-permute-start(bf16[512,512]{1,0:T(8,128)(2,1)} %collective-permute-done.7.refs_14_), channel_id=1, source_target_pairs={{0,4},{4,8},{8,12},{12,14},{14,10},{10,6},{6,2},{2,0},{1,5},{5,9},... | collective-permute-start | bytes 1572872 | tf_op jit(solution)/shard_map/ppermute | solution.py:236
  67.5 6.3 %collective-permute-start.12 = (bf16[512,512]{1,0:T(8,128)(2,1)S(1)}, bf16[512,512]{1,0:T(8,128)(2,1)}, u32[]{:S(2)}, u32[]{:S(2)}) collective-permute-start(bf16[512,512]{1,0:T(8,128)(2,1)S(1)} %collective-permute-done.10.refs_6_), channel_id=1, source_target_pairs={{0,1},{1,0},{2,3},{3,2},{4,5},{5,4},{6,7},{7,6},{8,9},{9,8},{10,11... | collective-permute-start | bytes 1572872 | tf_op jit(solution)/shard_map/ppermute | solution.py:211
  68.7 5.0 %collective-permute-start.13 = (bf16[512,512]{1,0:T(8,128)(2,1)}, bf16[512,512]{1,0:T(8,128)(2,1)}, u32[]{:S(2)}, u32[]{:S(2)}) collective-permute-start(bf16[512,512]{1,0:T(8,128)(2,1)} %collective-permute-done.11.refs_12_), channel_id=1, source_target_pairs={{0,1},{1,0},{2,3},{3,2},{4,5},{5,4},{6,7},{7,6},{8,9},{9,8},{10,11... | collective-permute-start | bytes 1572872 | tf_op jit(solution)/shard_map/ppermute | solution.py:211
  69.6 1.8 %collective-permute-start.14 = (f16[64,512]{0,1:T(8,128)(2,1)}, f16[64,512]{0,1:T(8,128)(2,1)S(1)}, u32[]{:S(2)}, u32[]{:S(2)}) collective-permute-start(f16[64,512]{0,1:T(8,128)(2,1)} %bitcast.15), channel_id=1, source_target_pairs={{0,1},{1,0},{2,3},{3,2},{4,5},{5,4},{6,7},{7,6},{8,9},{9,8},{10,11... | collective-permute-start | bytes 196616 | tf_op jit(solution)/shard_map/ppermute | solution.py:211
  73.8 11.1 %collective-permute-start.15 = (bf16[256,512]{1,0:T(8,128)(2,1)S(1)}, bf16[256,512]{1,0:T(8,128)(2,1)S(1)}, u32[]{:S(2)}, u32[]{:S(2)}) collective-permute-start(bf16[256,512]{1,0:T(8,128)(2,1)S(1)} %slice.36), channel_id=1, source_target_pairs={{0,2},{4,0},{8,4},{12,8},{14,12},{10,14},{6,10},{2,6},{1,3},{5,1},... | collective-permute-start | bytes 786440 | tf_op jit(solution)/shard_map/ppermute | solution.py:236
  75.8 11.0 %collective-permute-start.17 = (bf16[256,512]{1,0:T(8,128)(2,1)S(1)}, bf16[256,512]{1,0:T(8,128)(2,1)S(1)}, u32[]{:S(2)}, u32[]{:S(2)}) collective-permute-start(bf16[256,512]{1,0:T(8,128)(2,1)S(1)} %slice.37), channel_id=1, source_target_pairs={{0,4},{4,8},{8,12},{12,14},{14,10},{10,6},{6,2},{2,0},{1,5},{5,9},... | collective-permute-start | bytes 786440 | tf_op jit(solution)/shard_map/ppermute | solution.py:236
  84.9 9.0 %collective-permute-start.16 = (bf16[256,512]{1,0:T(8,128)(2,1)S(1)}, bf16[256,512]{1,0:T(8,128)(2,1)S(1)}, u32[]{:S(2)}, u32[]{:S(2)}) collective-permute-start(bf16[256,512]{1,0:T(8,128)(2,1)S(1)} %collective-permute-done.15.refs_8_), channel_id=1, source_target_pairs={{0,1},{1,0},{2,3},{3,2},{4,5},{5,4},{6,7},{7,6},{8,9},{9,8},{10,11... | collective-permute-start | bytes 786440 | tf_op jit(solution)/shard_map/ppermute | solution.py:211
  86.8 7.1 %collective-permute-start.18 = (bf16[256,512]{1,0:T(8,128)(2,1)S(1)}, bf16[256,512]{1,0:T(8,128)(2,1)S(1)}, u32[]{:S(2)}, u32[]{:S(2)}) collective-permute-start(bf16[256,512]{1,0:T(8,128)(2,1)S(1)} %collective-permute-done.17.refs_10_), channel_id=1, source_target_pairs={{0,1},{1,0},{2,3},{3,2},{4,5},{5,4},{6,7},{7,6},{8,9},{9,8},{10,11... | collective-permute-start | bytes 786440 | tf_op jit(solution)/shard_map/ppermute | solution.py:211
  90.2 27.0 %all-to-all-start.2 = ((f16[8,64,640]{2,1,0:T(8,128)(2,1)}), f16[8,64,640]{2,1,0:T(8,128)(2,1)S(1)}, u32[]{:S(2)}, u32[]{:S(2)}) async-start(f16[8,64,640]{2,1,0:T(8,128)(2,1)} %pad_maximum_fusion.1), calls=%async_computation.2 | async-start | bytes 1310720 | tf_op jit(solution)/shard_map/all_to_all | solution.py:239
  117.2 27.6 %all-to-all-start.1 = ((f16[8,64,640]{2,1,0:T(8,128)(2,1)}), f16[8,64,640]{2,1,0:T(8,128)(2,1)S(1)}, u32[]{:S(2)}, u32[]{:S(2)}) async-start(f16[8,64,640]{2,1,0:T(8,128)(2,1)} %convert_element_type.68), calls=%async_computation.1 | async-start | bytes 1310720 | tf_op jit(solution)/shard_map/all_to_all | solution.py:239
  144.8 21.3 %all-to-all-start.3 = ((f16[8,64,640]{2,1,0:T(8,128)(2,1)}), f16[8,64,640]{2,1,0:T(8,128)(2,1)S(1)}, u32[]{:S(2)}, u32[]{:S(2)}) async-start(f16[8,64,640]{2,1,0:T(8,128)(2,1)} %convert_element_type.73), calls=%async_computation.3 | async-start | bytes 1310720 | tf_op jit(solution)/shard_map/all_to_all | solution.py:239
  151.2 2.6 %collective-permute-start.19 = (f16[64,512]{1,0:T(8,128)(2,1)}, f16[64,512]{1,0:T(8,128)(2,1)}, u32[]{:S(2)}, u32[]{:S(2)}) collective-permute-start(f16[64,512]{1,0:T(8,128)(2,1)} %slice_convert_fusion.1), channel_id=1, source_target_pairs={{0,1},{1,0},{2,3},{3,2},{4,5},{5,4},{6,7},{7,6},{8,9},{9,8},{10,11... | collective-permute-start | bytes 196616 | tf_op jit(solution)/shard_map/ppermute | solution.py:211
  167.9 6.1 %collective-permute-start.20 = (f16[64,512]{1,0:T(8,128)(2,1)S(1)}, f16[64,512]{1,0:T(8,128)(2,1)S(1)}, u32[]{:S(2)}, u32[]{:S(2)}) collective-permute-start(f16[64,512]{1,0:T(8,128)(2,1)S(1)} %slice_convert_fusion), channel_id=1, source_target_pairs={{0,1},{1,0},{2,3},{3,2},{4,5},{5,4},{6,7},{7,6},{8,9},{9,8},{10,11... | collective-permute-start | bytes 196616 | tf_op jit(solution)/shard_map/ppermute | solution.py:211
  (22 other events, 184.4 us)

commit v3 on v2

--- a/solution.py
+++ b/solution.py
@@ -11,7 +11,7 @@
 CB_DEV = 2
 HALF = jnp.float16
 COT_SCALE = 256.0
-VMEM = 56 * 1024 * 1024
+VMEM_REST = 16 * 1024 * 1024
 
 
 def ring_order(count):
@@ -59,7 +59,7 @@
 
 
 def load_matrix(s, units, matrix, sems):
-    copies = []
+    copies = {}
     for k, (d, start, size) in enumerate(s.units):
         for t in range(2):
             copy = pltpu.make_async_copy(
@@ -68,16 +68,32 @@
                 sems.at[d],
             )
             copy.start()
-            copies.append(copy)
+            copies.setdefault(d, []).append(copy)
     return copies
 
 
-def gather_targets(s, pieces):
-    parts = []
-    for t in range(2):
-        lo = s.rows + t * s.share
-        parts += [pieces[i, :, lo : lo + s.share] for i in range(s.count)]
-    return jnp.concatenate(parts, axis=1)
+def arrived(s, copies, d):
+    if s.count > 8:
+        if d is not None:
+            return
+        waited = range(s.count)
+    else:
+        waited = () if d is None else (d,)
+    for k in waited:
+        for copy in copies[k]:
+            copy.wait()
+
+
+def gather_targets(s, pieces, core, part):
+    lo = part * s.share
+    return jnp.concatenate(
+        [
+            pieces[2 * i + side, :, lo : lo + s.share]
+            for side in (core, 1 - core)
+            for i in range(s.count)
+        ],
+        axis=1,
+    )
 
 
 def scatter_targets(s, out, values):
@@ -99,21 +115,21 @@
     return lax.fori_loop(0, count, body, init)
 
 
-def forward_kernel(s, table, mass, *refs):
+def forward_kernel(s, table, mass, points, *refs):
     given = 2 * len(s.units)
     units = refs[:given]
-    row_two, thirds, col_one_out, col_two_out, row_one, matrix, sems = refs[given:]
+    row_two, thirds, col_one_out, col_two_out, col_three_out, row_one, matrix, sems = refs[given:]
     copies = load_matrix(s, units, matrix, sems)
     zero = jnp.zeros((s.hists, 2 * s.cols), jnp.float32)
-    target = gather_targets(s, mass)
-    for copy in copies:
-        copy.wait()
+    target = gather_targets(s, points, table[s.count], 0)
+    arrived(s, copies, None)
     ones = jnp.ones((8, 2 * s.cols), jnp.bfloat16)
 
     def first(d, total):
+        arrived(s, copies, d)
         sums = nt(ones, matrix[d])
         row_one[d] = sums
-        left = mass[table[d], :, : s.rows] / sums[0:1]
+        left = mass[table[d]] / sums[0:1]
         return total + nn(left.astype(jnp.bfloat16), matrix[d])
 
     col_one = each(s.count, first, zero)
@@ -123,7 +139,7 @@
     def second(d, total):
         row = nt(panel, matrix[d])
         row_two[d] = row
-        left = mass[table[d], :, : s.rows] / row
+        left = mass[table[d]] / row
         return total + nn(left.astype(jnp.bfloat16), matrix[d])
 
     col_two = each(s.count, second, zero)
@@ -134,36 +150,38 @@
         row = nt(panel, matrix[d])
         k = table[d]
         thirds[k, :, : s.rows] = row
-        left = mass[table[d], :, : s.rows] / row
+        left = mass[table[d]] / row
         return total + nn(left.astype(jnp.bfloat16), matrix[d])
 
     col_three = each(s.count, third, zero)
+    col_three_out[...] = col_three
     scatter_targets(s, thirds, col_three)
 
 
-def backward_kernel(s, table, mass, cot, row_two, thirds, col_one, col_two, row_one, *refs):
+def backward_kernel(
+    s, table, mass, points, cot, row_two, thirds, col_one, col_two, col_three, row_one, *refs
+):
     given = 2 * len(s.units)
     units = refs[:given]
     out, matrix, sems = refs[given:]
     copies = load_matrix(s, units, matrix, sems)
     zero = jnp.zeros((s.hists, 2 * s.cols), jnp.float32)
-    target = gather_targets(s, mass)
-    target_cot = gather_targets(s, cot)
-    col_three = gather_targets(s, thirds)
+    target = gather_targets(s, points, table[s.count], 0)
+    target_cot = gather_targets(s, points, table[s.count], 1)
     right_one = target / col_one[...]
     right_two = target / col_two[...]
-    for copy in copies:
-        copy.wait()
-    panel = (-target_cot / col_three).astype(jnp.bfloat16)
+    arrived(s, copies, None)
+    panel = (-target_cot / col_three[...]).astype(jnp.bfloat16)
 
     def third(d, total):
+        arrived(s, copies, d)
         k = table[d]
         grad = nt(panel, matrix[d])
         row = thirds[k, :, : s.rows]
-        left = mass[table[d], :, : s.rows] / row
+        left = mass[table[d]] / row
         term = grad / row
         out[table[d], :, : s.rows] = term
-        rowgrad = -(cot[k, :, : s.rows] / row + term * left)
+        rowgrad = -(cot[k] / row + term * left)
         return total + nn(rowgrad.astype(jnp.bfloat16), matrix[d])
 
     term_two = each(s.count, third, zero) / col_two[...]
@@ -173,7 +191,7 @@
         row = row_two[d]
         term = nt(panel, matrix[d]) / row
         out[table[d], :, : s.rows] += term
-        rowgrad = -term * (mass[table[d], :, : s.rows] / row)
+        rowgrad = -term * (mass[table[d]] / row)
         return total + nn(rowgrad.astype(jnp.bfloat16), matrix[d])
 
     term_one = each(s.count, second, zero) / col_one[...]
@@ -203,7 +221,9 @@
             bytes_accessed=s.count * s.rows * 2 * s.cols * 4,
             transcendentals=0,
         ),
-        compiler_params=pltpu.CompilerParams(vmem_limit_bytes=VMEM),
+        compiler_params=pltpu.CompilerParams(
+            vmem_limit_bytes=VMEM_REST + s.count * s.rows * 2 * s.cols * 2
+        ),
     )(table, *arrays, *units)
 
 
@@ -230,6 +250,7 @@
     core = lax.axis_index("tgt")
     at = jnp.asarray(place)[me]
     table = jnp.asarray(ring)[(at + jnp.arange(count, dtype=jnp.int32)) % count]
+    table = jnp.concatenate([table, core[None]]).astype(jnp.int32)
 
     def shift(x, distance):
         pairs = [(int(ring[p]), int(ring[(p + distance) % count])) for p in range(count)]
@@ -238,51 +259,48 @@
     def exchange(x):
         return lax.all_to_all(x, "src", 0, 0, tiled=True)
 
-    def by_histogram(source, target):
-        target = target.astype(HALF).reshape(share, 2, cols_here)
-        mine = lax.dynamic_index_in_dim(target, core, 1, keepdims=False)
-        other = lax.dynamic_index_in_dim(target, 1 - core, 1, keepdims=False)
-        both = jnp.concatenate([mine, swap_cores(other)]).T
-        return jnp.concatenate(
-            [
-                source.astype(HALF).T.reshape(count, s.hists, rows),
-                both.reshape(count, s.hists, 2 * share),
-            ],
-            axis=2,
-        )
-
-    mass_message = by_histogram(source_mass, target_mass[0])
-    cot_message = by_histogram(source_cotangent * COT_SCALE, target_cotangent[0] * COT_SCALE)
-    mass = None
-
-    ahead = behind = dense_blocks(kernel_tiles, tile_cols, tile_count)
-    pieces = {(0, 0): ahead}
-    swapped = {(0, 0): swap_cores(ahead)}
-    before = []
-    rounds = count // 2
-    for step in range(1, rounds + 1):
-        ready = [swapped[k] for k in before]
-        if step == min(2, rounds):
-            ready.append(mass_message)
-        if step == rounds:
+    def by_histogram(source):
+        return source.astype(HALF).T.reshape(count, s.hists, rows)
+
+    unit = dense_blocks(kernel_tiles, tile_cols, tile_count)
+    mass_message = by_histogram(source_mass)
+    cot_message = by_histogram(source_cotangent * COT_SCALE)
+    both = jnp.stack([target_mass[0], target_cotangent[0] * COT_SCALE]).astype(HALF)
+    both = both.reshape(2, share, 2, count, s.hists).transpose(3, 2, 4, 0, 1)
+    points_message = both.reshape(2 * count, s.hists, 2 * share)
+
+    pieces = {(0, 0): unit}
+    swapped = {(0, 0): swap_cores(unit)}
+    ahead = behind = unit
+    before = {}
+    last = count // 2
+    for step in range(1, last + 1):
+        due = before.get(step - 2, [])
+        extra = [swapped[key] for key in due]
+        if step == 2:
+            extra += [mass_message, points_message, table]
+        if step == last:
             mass = exchange(mass_message).astype(jnp.float32)
-            ready += [mass, cot_message]
-        (ahead, behind), ready = lax.optimization_barrier(((ahead, behind), ready))
-        for k, piece in zip(before, ready):
-            swapped[k] = piece
-        if step == min(2, rounds):
-            mass_message = ready[len(before)]
-        if step == rounds:
-            mass, cot_message = ready[-2:]
+            points = lax.all_to_all(points_message, ("src", "tgt"), 0, 0, tiled=True)
+            extra += [mass, points.astype(jnp.float32), cot_message]
+        ahead, behind, extra = lax.optimization_barrier((ahead, behind, extra))
+        swapped.update(zip(due, extra))
+        if step == 2:
+            mass_message, points_message, table = extra[-3:]
+        if step == last:
+            mass, points, cot_message = extra[-3:]
         if 2 * step == count:
-            ahead, behind = ahead[: rows // 2], behind[rows // 2 :]
-            new = {(step, 0): shift(ahead, -1), (step, rows // 2): shift(behind, 1)}
+            middle = rows // 2
+            new = {
+                (step, 0): shift(ahead[:middle], -1),
+                (step, middle): shift(behind[middle:], 1),
+            }
         else:
             ahead, behind = shift(ahead, -1), shift(behind, 1)
             new = {(step, 0): ahead, (count - step, 0): behind}
-        before = list(new) if step > 1 else [(0, 0), *new]
         pieces.update(new)
-        swapped.update({k: swap_cores(v) for k, v in new.items()})
+        swapped.update({key: swap_cores(piece) for key, piece in new.items()})
+        before[step] = list(new) + ([(0, 0)] if step == 1 else [])
     units = []
     for d, start, _ in s.units:
         units += [pieces[d, start], swapped[d, start]]
@@ -292,15 +310,20 @@
     wide = jax.ShapeDtypeStruct((count, s.hists, s.lanes), jnp.float32)
     column = jax.ShapeDtypeStruct((s.hists, 2 * s.cols), jnp.float32)
     sums = jax.ShapeDtypeStruct((count, 8, rows), jnp.float32)
-    row_two, thirds, col_one, col_two, row_one = call(
-        forward_kernel, s, (panel, wide, column, column, sums), table, (mass,), units
+    row_two, thirds, col_one, col_two, col_three, row_one = call(
+        forward_kernel,
+        s,
+        (panel, wide, column, column, column, sums),
+        table,
+        (mass, points),
+        units,
     )
     grads = call(
         backward_kernel,
         s,
         wide,
         table,
-        (mass, cot, row_two, thirds, col_one, col_two, row_one),
+        (mass, points, cot, row_two, thirds, col_one, col_two, col_three, row_one),
         units,
     )
 
@@ -313,10 +336,15 @@
         return flat[:, :rows].T, jnp.concatenate(halves, axis=1)
 
     row_three, col_three = by_point(exchange(thirds.astype(HALF)))
-    source_term, target_term = by_point(exchange(grads.astype(HALF)))
+    source_potential = jnp.log(source_mass / row_three)
+    target_potential = jnp.log(target_mass[0] / col_three)
+    back, source_potential, target_potential = lax.optimization_barrier(
+        (exchange(grads.astype(HALF)), source_potential, target_potential)
+    )
+    source_term, target_term = by_point(back)
     return (
-        jnp.log(source_mass / row_three),
-        jnp.log(target_mass[0] / col_three)[None],
+        source_potential,
+        target_potential[None],
         source_cotangent / source_mass + source_term * (1 / COT_SCALE),
         (target_cotangent[0] / target_mass[0] + target_term * (1 / COT_SCALE))[None],
     )

time: 176 us -> 169 us (0.960)
  waiting for transfers between devices: 63.4 us -> 32.7 us
  local copies, waits for them, and re-layouts: 11.5 us -> 36.4 us
  Pallas kernels: 38.6 us -> 28.5 us
  starting transfers between devices: 41 us -> 48.4 us
    ppermute x8, waiting for transfers between devices: 51.4 us -> 16.5 us  [shift(): return lax.ppermute(x, 'src', pairs)]
    unnamed x47 -> x93, local copies, waits for them, and re-layouts: 4.69 us -> 26 us
    pallas_call x2, Pallas kernels: 38.6 us -> 28.5 us  [call(): pl.pallas_call(functools.partial(kernel, s), out_shape=outs, in_specs=[pl...]
    all_to_all x0 -> x1, starting transfers between devices: none -> 6.76 us  [local(): points = lax.all_to_all(points_message, ('src', 'tgt'), 0, 0, tiled=True)]
    all_to_all x0 -> x1, waiting for transfers between devices: none -> 6.6 us  [local(): points = lax.all_to_all(points_message, ('src', 'tgt'), 0, 0, tiled=True)]
    transpose x2 -> x3, other arithmetic: 0.23 us -> 4.8 us  [the longest x1 2.55 us: local(): both = both.reshape(2, share, 2, count, s.hists).transpose(3, 2, 4, 0, 1)]
    dynamic_slice x5 -> x0, local copies, waits for them, and re-layouts: 2.71 us -> none  [the longest x2 1.64 us: by_histogram(): other = lax.dynamic_index_in_dim(target, 1 - core, 1, keepdims=False)]
    ppermute x13 -> x11, starting transfers between devices: 12.9 us -> 10.4 us  [swap_cores(): return lax.ppermute(x, 'tgt', [(0, 1), (1, 0)])]
  transfers between devices with their start and end apart: 25 -> 24, of which waited for: 9 -> 8; matrix products, arithmetic and copies ran while one was open for 14% -> 18% of each run, Pallas kernels for 22% -> 17%
where the time goes in v3:
time: 169 us; the launch traced here: 167 us
  starting transfers between devices  48.4 us (29%)
  local copies, waits for them, and re-layouts  36.4 us (22%)
  waiting for transfers between devices  32.7 us (19%)
  Pallas kernels  28.5 us (17%)
  other arithmetic  18.7 us (11%)
    pallas_call x2, Pallas kernels, call(): pl.pallas_call(functools.partial(kernel, s), out_shape=outs, in_specs=[pl...  28.5 us
    unnamed x93, local copies, waits for them, and re-layouts  26 us
    all_to_all x4, starting transfers between devices, exchange(): return lax.all_to_all(x, 'src', 0, 0, tiled=True)  19 us
    ppermute x8, waiting for transfers between devices, shift(): return lax.ppermute(x, 'src', pairs)  16.5 us
    ppermute x8, starting transfers between devices, shift(): return lax.ppermute(x, 'src', pairs)  12.2 us
    ppermute x11, starting transfers between devices, swap_cores(): return lax.ppermute(x, 'tgt', [(0, 1), (1, 0)])  10.4 us
    all_to_all x4, waiting for transfers between devices, exchange(): return lax.all_to_all(x, 'src', 0, 0, tiled=True)  9.58 us
    all_to_all x1, starting transfers between devices, local(): points = lax.all_to_all(points_message, ('src', 'tgt'), 0, 0, tiled=True)  6.76 us
  transfers between devices with their start and end apart: 24, of which 8 were waited for; matrix products, arithmetic and copies ran while one was open for 18% of the time, Pallas kernels for 17%

profile of v3, /device:TPU:1, one launch (start us, length us, event | category | flops | bytes accessed | tf_op | source)
XLA Modules:
  0.0 167.3 jit_solution(14605770743887023747)
XLA Ops:
  3.3 2.1 %collective-permute-start = (bf16[512,512]{1,0:T(8,128)(2,1)S(1)}, bf16[512,512]{1,0:T(8,128)(2,1)S(1)}, u32[]{:S(2)}, u32[]{:S(2)}) collective-permute-start(bf16[512,512]{1,0:T(8,128)(2,1)S(1)} %bitcast.43), channel_id=1, source_target_pairs={{0,2},{4,0},{8,4},{12,8},{14,12},{10,14},{6,10},{2,6},{1,3},{5,1},... | collective-permute-start | bytes 1572872 | tf_op jit(solution)/shard_map/ppermute | solution.py:257
  8.7 2.6 %maximum_bitcast_fusion = f16[8,2,64,2,64]{4,3,2,1,0:T(2,128)(2,1)} fusion(f16[1,64,2,8,64]{1,0,4,2,3:T(2,128)(2,1)S(1)} %copy.25, f16[1,64,2,8,64]{1,0,4,2,3:T(2,128)(2,1)S(1)} %copy.24), kind=kLoop, calls=%fused_computation.9 | loop fusion | flops 131072 | bytes 524288 | tf_op jit(solution)/shard_map/transpose | solution.py:269
  11.2 2.1 %reshape.144 = f16[16,64,128]{2,1,0:T(8,128)(2,1)} reshape(f16[8,2,64,2,64]{4,3,2,1,0:T(2,128)(2,1)} %maximum_bitcast_fusion) | data formatting | bytes 524288 | tf_op jit(solution)/shard_map/reshape | solution.py:270
  15.3 1.8 %collective-permute-done.refs_2_ = bf16[512,512]{1,0:T(8,128)(2,1)S(1)} collective-permute-done((bf16[512,512]{1,0:T(8,128)(2,1)S(1)}, bf16[512,512]{1,0:T(8,128)(2,1)S(1)}, u32[]{:S(2)}, u32[]{:S(2)}) %collective-permute-start) | collective-permute-done | bytes 524320 | tf_op jit(solution)/shard_map/ppermute | solution.py:257
  17.9 6.8 %all-to-all-start.1 = ((f16[16,64,128]{2,1,0:T(8,128)(2,1)}), f16[16,64,128]{2,1,0:T(8,128)(2,1)S(1)}, u32[]{:S(2)}, u32[]{:S(2)}) async-start(f16[16,64,128]{2,1,0:T(8,128)(2,1)} %reshape.144), calls=%async_computation.1 | async-start | bytes 524288 | tf_op jit(solution)/shard_map/all_to_all | solution.py:284
  27.2 6.6 %all-to-all-done.1 = f16[16,64,128]{2,1,0:T(8,128)(2,1)S(1)} async-done(((f16[16,64,128]{2,1,0:T(8,128)(2,1)}), f16[16,64,128]{2,1,0:T(8,128)(2,1)S(1)}, u32[]{:S(2)}, u32[]{:S(2)}) %all-to-all-start.1) | async-done | bytes 262176 | tf_op jit(solution)/shard_map/all_to_all | solution.py:284
  33.8 4.1 %all-to-all-start = ((f16[8,64,512]{2,1,0:T(8,128)(2,1)}), f16[8,64,512]{2,1,0:T(8,128)(2,1)}, u32[]{:S(2)}, u32[]{:S(2)}) async-start(f16[8,64,512]{2,1,0:T(8,128)(2,1)} %bitcast.48), calls=%async_computation | async-start | bytes 1048576 | tf_op jit(solution)/shard_map/all_to_all | solution.py:260
  38.0 4.5 %collective-permute-done.2.refs_4_ = bf16[512,512]{1,0:T(8,128)(2,1)} collective-permute-done((bf16[512,512]{1,0:T(8,128)(2,1)S(1)}, bf16[512,512]{1,0:T(8,128)(2,1)}, u32[]{:S(2)}, u32[]{:S(2)}) %collective-permute-start.2) | collective-permute-done | bytes 524320 | tf_op jit(solution)/shard_map/ppermute | solution.py:257
  45.3 2.0 %collective-permute-start.9 = (bf16[512,512]{1,0:T(8,128)(2,1)}, bf16[512,512]{1,0:T(8,128)(2,1)}, u32[]{:S(2)}, u32[]{:S(2)}) collective-permute-start(bf16[512,512]{1,0:T(8,128)(2,1)} %collective-permute-done.2.refs_4_), channel_id=1, source_target_pairs={{0,1},{1,0},{2,3},{3,2},{4,5},{5,4},{6,7},{7,6},{8,9},{9,8},{10,11... | collective-permute-start | bytes 1572872 | tf_op jit(solution)/shard_map/ppermute | solution.py:231
  47.3 2.1 %fusion.1 = f16[512,512]{0,1:T(8,128)(2,1)} fusion(f32[512,512]{1,0:T(8,128)} %param.14), kind=kLoop, calls=%fused_computation.8 | loop fusion | flops 524288 | bytes 1572864 | tf_op jit(solution)/shard_map/transpose | solution.py:263
  49.5 2.2 %copy.26 = f16[512,512]{1,0:T(8,128)(2,1)} copy(f16[512,512]{0,1:T(8,128)(2,1)} %fusion.1) | data formatting | bytes 1048576 | tf_op jit(solution)/shard_map/transpose | solution.py:263
  52.7 3.5 %all-to-all-done = f16[8,64,512]{2,1,0:T(8,128)(2,1)} async-done(((f16[8,64,512]{2,1,0:T(8,128)(2,1)}), f16[8,64,512]{2,1,0:T(8,128)(2,1)}, u32[]{:S(2)}, u32[]{:S(2)}) %all-to-all-start) | async-done | bytes 524320 | tf_op jit(solution)/shard_map/all_to_all | solution.py:260
  57.3 4.7 %collective-permute-done.7.refs_6_ = bf16[512,512]{1,0:T(8,128)(2,1)S(1)} collective-permute-done((bf16[512,512]{1,0:T(8,128)(2,1)}, bf16[512,512]{1,0:T(8,128)(2,1)S(1)}, u32[]{:S(2)}, u32[]{:S(2)}) %collective-permute-start.7) | collective-permute-done | bytes 524320 | tf_op jit(solution)/shard_map/ppermute | solution.py:257
  62.1 2.0 %collective-permute-start.12 = (bf16[256,512]{1,0:T(8,128)(2,1)S(1)}, bf16[256,512]{1,0:T(8,128)(2,1)S(1)}, u32[]{:S(2)}, u32[]{:S(2)}) collective-permute-start(bf16[256,512]{1,0:T(8,128)(2,1)S(1)} %slice.36), channel_id=1, source_target_pairs={{0,2},{4,0},{8,4},{12,8},{14,12},{10,14},{6,10},{2,6},{1,3},{5,1},... | collective-permute-start | bytes 786440 | tf_op jit(solution)/shard_map/ppermute | solution.py:257
  64.1 3.6 %collective-permute-start.14 = (bf16[256,512]{1,0:T(8,128)(2,1)S(1)}, bf16[256,512]{1,0:T(8,128)(2,1)}, u32[]{:S(2)}, u32[]{:S(2)}) collective-permute-start(bf16[256,512]{1,0:T(8,128)(2,1)S(1)} %slice.37), channel_id=1, source_target_pairs={{0,4},{4,8},{8,12},{12,14},{14,10},{10,6},{6,2},{2,0},{1,5},{5,9},... | collective-permute-start | bytes 786440 | tf_op jit(solution)/shard_map/ppermute | solution.py:257
  68.9 4.7 %collective-permute-done.12.refs_8_ = bf16[256,512]{1,0:T(8,128)(2,1)S(1)} collective-permute-done((bf16[256,512]{1,0:T(8,128)(2,1)S(1)}, bf16[256,512]{1,0:T(8,128)(2,1)S(1)}, u32[]{:S(2)}, u32[]{:S(2)}) %collective-permute-start.12) | collective-permute-done | bytes 262176 | tf_op jit(solution)/shard_map/ppermute | solution.py:257
  76.2 4.3 %all-to-all-start.2 = ((f16[8,64,512]{2,1,0:T(8,128)(2,1)}), f16[8,64,512]{2,1,0:T(8,128)(2,1)}, u32[]{:S(2)}, u32[]{:S(2)}) async-start(f16[8,64,512]{2,1,0:T(8,128)(2,1)} %bitcast.49), calls=%async_computation.2 | async-start | bytes 1048576 | tf_op jit(solution)/shard_map/all_to_all | solution.py:260
  88.9 15.1 %shard_map.123 = (f32[8,64,512]{2,1,0:T(8,128)S(1)}, f32[8,64,640]{2,1,0:T(8,128)S(1)}, f32[64,1024]{1,0:T(8,128)S(1)}, f32[64,1024]{1,0:T(8,128)S(1)}, f32[64,1...) custom-call(s32[9]{0:T(128)S(1)} %pad_add_fusion.table, f32[8,64,512]{2,1,0:T(8,128)S(1)} %convert_element_type.53.mass, ...), custom_call_target="tpu_custom_call" | custom-call | flops 12884901888 | bytes 16777216 | tf_op jit(solution)/shard_map/pallas_call | solution.py:209
  108.0 5.1 %all-to-all-start.4 = ((f16[8,64,640]{2,1,0:T(8,128)(2,1)}), f16[8,64,640]{2,1,0:T(8,128)(2,1)}, u32[]{:S(2)}, u32[]{:S(2)}) async-start(f16[8,64,640]{2,1,0:T(8,128)(2,1)} %convert_element_type.58), calls=%async_computation.4 | async-start | bytes 1310720 | tf_op jit(solution)/shard_map/all_to_all | solution.py:260
  123.8 13.4 %shard_map.124 = f32[8,64,640]{2,1,0:T(8,128)S(1)} custom-call(s32[9]{0:T(128)S(1)} %pad_add_fusion.table, f32[8,64,512]{2,1,0:T(8,128)S(1)} %convert_element_type.53.mass, f32[16,64,128]{2,1,0:T(8,128)S(1)} %convert_element_type.54.points, f32[8,64,512]{2,1,0:T(8,128)S(1)} %convert_element_type.56.cot, f32[8,64,512]{2,1,0:T(8,128)S(1)} %copy-done.26, ...), custom_call_target="tpu_custom_call" | custom-call | flops 12884901888 | bytes 16777216 | tf_op jit(solution)/shard_map/pallas_call | solution.py:209
  138.1 5.4 %all-to-all-start.3 = ((f16[8,64,640]{2,1,0:T(8,128)(2,1)}), f16[8,64,640]{2,1,0:T(8,128)(2,1)S(1)}, u32[]{:S(2)}, u32[]{:S(2)}) async-start(f16[8,64,640]{2,1,0:T(8,128)(2,1)} %convert_element_type.57), calls=%async_computation.3 | async-start | bytes 1310720 | tf_op jit(solution)/shard_map/all_to_all | solution.py:260
  153.4 6.1 %all-to-all-done.3 = f16[8,64,640]{2,1,0:T(8,128)(2,1)S(1)} async-done(((f16[8,64,640]{2,1,0:T(8,128)(2,1)}), f16[8,64,640]{2,1,0:T(8,128)(2,1)S(1)}, u32[]{:S(2)}, u32[]{:S(2)}) %all-to-all-start.3) | async-done | bytes 655392 | tf_op jit(solution)/shard_map/all_to_all | solution.py:260
  161.2 2.4 %collective-permute-start.18 = (f16[64,512]{1,0:T(8,128)(2,1)S(1)}, f16[64,512]{1,0:T(8,128)(2,1)S(1)}, u32[]{:S(2)}, u32[]{:S(2)}) collective-permute-start(f16[64,512]{1,0:T(8,128)(2,1)S(1)} %slice_convert_fusion), channel_id=1, source_target_pairs={{0,1},{1,0},{2,3},{3,2},{4,5},{5,4},{6,7},{7,6},{8,9},{9,8},{10,11... | collective-permute-start | bytes 196616 | tf_op jit(solution)/shard_map/ppermute | solution.py:231
  163.7 2.9 %bitcast_add_fusion = f32[512,512]{1,0:T(8,128)} fusion(f32[512,512]{0,1:T(8,128)} %copy.34, f32[512,512]{1,0:T(8,128)} %param.14, f32[512,512]{1,0:T(8,128)S(1)} %copy-done.35), kind=kLoop, calls=%fused_computation.2 | loop fusion | flops 786432 | bytes 4194304 | tf_op jit(solution)/shard_map/add | solution.py:348
  (159 shorter events, 55.9 us)
Async XLA Ops:
  3.3 13.8 %collective-permute-start = (bf16[512,512]{1,0:T(8,128)(2,1)S(1)}, bf16[512,512]{1,0:T(8,128)(2,1)S(1)}, u32[]{:S(2)}, u32[]{:S(2)}) collective-permute-start(bf16[512,512]{1,0:T(8,128)(2,1)S(1)} %bitcast.43), channel_id=1, source_target_pairs={{0,2},{4,0},{8,4},{12,8},{14,12},{10,14},{6,10},{2,6},{1,3},{5,1},... | collective-permute-start | bytes 1572872 | tf_op jit(solution)/shard_map/ppermute | solution.py:257
  5.4 12.5 %collective-permute-start.1 = (bf16[512,512]{1,0:T(8,128)(2,1)S(1)}, bf16[512,512]{1,0:T(8,128)(2,1)S(1)}, u32[]{:S(2)}, u32[]{:S(2)}) collective-permute-start(bf16[512,512]{1,0:T(8,128)(2,1)S(1)} %bitcast.44), channel_id=1, source_target_pairs={{0,4},{4,8},{8,12},{12,14},{14,10},{10,6},{6,2},{2,0},{1,5},{5,9},... | collective-permute-start | bytes 1572872 | tf_op jit(solution)/shard_map/ppermute | solution.py:257
  17.9 16.0 %all-to-all-start.1 = ((f16[16,64,128]{2,1,0:T(8,128)(2,1)}), f16[16,64,128]{2,1,0:T(8,128)(2,1)S(1)}, u32[]{:S(2)}, u32[]{:S(2)}) async-start(f16[16,64,128]{2,1,0:T(8,128)(2,1)} %reshape.144), calls=%async_computation.1 | async-start | bytes 524288 | tf_op jit(solution)/shard_map/all_to_all | solution.py:284
  24.6 13.4 %collective-permute-start.6 = (bf16[512,512]{1,0:T(8,128)(2,1)S(1)}, bf16[512,512]{1,0:T(8,128)(2,1)S(1)}, u32[]{:S(2)}, u32[]{:S(2)}) collective-permute-start(bf16[512,512]{1,0:T(8,128)(2,1)S(1)} %bitcast.45), channel_id=1, source_target_pairs={{0,1},{1,0},{2,3},{3,2},{4,5},{5,4},{6,7},{7,6},{8,9},{9,8},{10,11... | collective-permute-start | bytes 1572872 | tf_op jit(solution)/shard_map/ppermute | solution.py:231
  24.8 17.7 %collective-permute-start.2 = (bf16[512,512]{1,0:T(8,128)(2,1)S(1)}, bf16[512,512]{1,0:T(8,128)(2,1)}, u32[]{:S(2)}, u32[]{:S(2)}) collective-permute-start(bf16[512,512]{1,0:T(8,128)(2,1)S(1)} %collective-permute-done.refs_2_), channel_id=1, source_target_pairs={{0,2},{4,0},{8,4},{12,8},{14,12},{10,14},{6,10},{2,6},{1,3},{5,1},... | collective-permute-start | bytes 1572872 | tf_op jit(solution)/shard_map/ppermute | solution.py:257
  26.4 16.1 %collective-permute-start.3 = (bf16[512,512]{1,0:T(8,128)(2,1)S(1)}, bf16[512,512]{1,0:T(8,128)(2,1)}, u32[]{:S(2)}, u32[]{:S(2)}) collective-permute-start(bf16[512,512]{1,0:T(8,128)(2,1)S(1)} %collective-permute-done.1.refs_16_), channel_id=1, source_target_pairs={{0,4},{4,8},{8,12},{12,14},{14,10},{10,6},{6,2},{2,0},{1,5},{5,9},... | collective-permute-start | bytes 1572872 | tf_op jit(solution)/shard_map/ppermute | solution.py:257
  26.5 16.1 %collective-permute-start.4 = (bf16[512,512]{1,0:T(8,128)(2,1)S(1)}, bf16[512,512]{1,0:T(8,128)(2,1)S(1)}, u32[]{:S(2)}, u32[]{:S(2)}) collective-permute-start(bf16[512,512]{1,0:T(8,128)(2,1)S(1)} %collective-permute-done.refs_2_), channel_id=1, source_target_pairs={{0,1},{1,0},{2,3},{3,2},{4,5},{5,4},{6,7},{7,6},{8,9},{9,8},{10,11... | collective-permute-start | bytes 1572872 | tf_op jit(solution)/shard_map/ppermute | solution.py:231
  27.2 15.3 %collective-permute-start.5 = (bf16[512,512]{1,0:T(8,128)(2,1)S(1)}, bf16[512,512]{1,0:T(8,128)(2,1)}, u32[]{:S(2)}, u32[]{:S(2)}) collective-permute-start(bf16[512,512]{1,0:T(8,128)(2,1)S(1)} %collective-permute-done.1.refs_16_), channel_id=1, source_target_pairs={{0,1},{1,0},{2,3},{3,2},{4,5},{5,4},{6,7},{7,6},{8,9},{9,8},{10,11... | collective-permute-start | bytes 1572872 | tf_op jit(solution)/shard_map/ppermute | solution.py:231
  33.8 22.3 %all-to-all-start = ((f16[8,64,512]{2,1,0:T(8,128)(2,1)}), f16[8,64,512]{2,1,0:T(8,128)(2,1)}, u32[]{:S(2)}, u32[]{:S(2)}) async-start(f16[8,64,512]{2,1,0:T(8,128)(2,1)} %bitcast.48), calls=%async_computation | async-start | bytes 1048576 | tf_op jit(solution)/shard_map/all_to_all | solution.py:260
  42.6 19.5 %collective-permute-start.7 = (bf16[512,512]{1,0:T(8,128)(2,1)}, bf16[512,512]{1,0:T(8,128)(2,1)S(1)}, u32[]{:S(2)}, u32[]{:S(2)}) collective-permute-start(bf16[512,512]{1,0:T(8,128)(2,1)} %collective-permute-done.2.refs_4_), channel_id=1, source_target_pairs={{0,2},{4,0},{8,4},{12,8},{14,12},{10,14},{6,10},{2,6},{1,3},{5,1},... | collective-permute-start | bytes 1572872 | tf_op jit(solution)/shard_map/ppermute | solution.py:257
  44.1 18.0 %collective-permute-start.8 = (bf16[512,512]{1,0:T(8,128)(2,1)}, bf16[512,512]{1,0:T(8,128)(2,1)S(1)}, u32[]{:S(2)}, u32[]{:S(2)}) collective-permute-start(bf16[512,512]{1,0:T(8,128)(2,1)} %collective-permute-done.3.refs_14_), channel_id=1, source_target_pairs={{0,4},{4,8},{8,12},{12,14},{14,10},{10,6},{6,2},{2,0},{1,5},{5,9},... | collective-permute-start | bytes 1572872 | tf_op jit(solution)/shard_map/ppermute | solution.py:257
  45.3 16.8 %collective-permute-start.9 = (bf16[512,512]{1,0:T(8,128)(2,1)}, bf16[512,512]{1,0:T(8,128)(2,1)}, u32[]{:S(2)}, u32[]{:S(2)}) collective-permute-start(bf16[512,512]{1,0:T(8,128)(2,1)} %collective-permute-done.2.refs_4_), channel_id=1, source_target_pairs={{0,1},{1,0},{2,3},{3,2},{4,5},{5,4},{6,7},{7,6},{8,9},{9,8},{10,11... | collective-permute-start | bytes 1572872 | tf_op jit(solution)/shard_map/ppermute | solution.py:231
  47.3 14.8 %collective-permute-start.10 = (bf16[512,512]{1,0:T(8,128)(2,1)}, bf16[512,512]{1,0:T(8,128)(2,1)}, u32[]{:S(2)}, u32[]{:S(2)}) collective-permute-start(bf16[512,512]{1,0:T(8,128)(2,1)} %collective-permute-done.3.refs_14_), channel_id=1, source_target_pairs={{0,1},{1,0},{2,3},{3,2},{4,5},{5,4},{6,7},{7,6},{8,9},{9,8},{10,11... | collective-permute-start | bytes 1572872 | tf_op jit(solution)/shard_map/ppermute | solution.py:231
  62.1 11.5 %collective-permute-start.12 = (bf16[256,512]{1,0:T(8,128)(2,1)S(1)}, bf16[256,512]{1,0:T(8,128)(2,1)S(1)}, u32[]{:S(2)}, u32[]{:S(2)}) collective-permute-start(bf16[256,512]{1,0:T(8,128)(2,1)S(1)} %slice.36), channel_id=1, source_target_pairs={{0,2},{4,0},{8,4},{12,8},{14,12},{10,14},{6,10},{2,6},{1,3},{5,1},... | collective-permute-start | bytes 786440 | tf_op jit(solution)/shard_map/ppermute | solution.py:257
  64.1 10.8 %collective-permute-start.14 = (bf16[256,512]{1,0:T(8,128)(2,1)S(1)}, bf16[256,512]{1,0:T(8,128)(2,1)}, u32[]{:S(2)}, u32[]{:S(2)}) collective-permute-start(bf16[256,512]{1,0:T(8,128)(2,1)S(1)} %slice.37), channel_id=1, source_target_pairs={{0,4},{4,8},{8,12},{12,14},{14,10},{10,6},{6,2},{2,0},{1,5},{5,9},... | collective-permute-start | bytes 786440 | tf_op jit(solution)/shard_map/ppermute | solution.py:257
  67.7 12.8 %collective-permute-start.11 = (bf16[512,512]{1,0:T(8,128)(2,1)S(1)}, bf16[512,512]{1,0:T(8,128)(2,1)}, u32[]{:S(2)}, u32[]{:S(2)}) collective-permute-start(bf16[512,512]{1,0:T(8,128)(2,1)S(1)} %collective-permute-done.7.refs_6_), channel_id=1, source_target_pairs={{0,1},{1,0},{2,3},{3,2},{4,5},{5,4},{6,7},{7,6},{8,9},{9,8},{10,11... | collective-permute-start | bytes 1572872 | tf_op jit(solution)/shard_map/ppermute | solution.py:231
  68.9 11.7 %collective-permute-start.16 = (bf16[512,512]{1,0:T(8,128)(2,1)S(1)}, bf16[512,512]{1,0:T(8,128)(2,1)}, u32[]{:S(2)}, u32[]{:S(2)}) collective-permute-start(bf16[512,512]{1,0:T(8,128)(2,1)S(1)} %collective-permute-done.8.refs_12_), channel_id=1, source_target_pairs={{0,1},{1,0},{2,3},{3,2},{4,5},{5,4},{6,7},{7,6},{8,9},{9,8},{10,11... | collective-permute-start | bytes 1572872 | tf_op jit(solution)/shard_map/ppermute | solution.py:231
  73.6 7.0 %collective-permute-start.13 = (bf16[256,512]{1,0:T(8,128)(2,1)S(1)}, bf16[256,512]{1,0:T(8,128)(2,1)}, u32[]{:S(2)}, u32[]{:S(2)}) collective-permute-start(bf16[256,512]{1,0:T(8,128)(2,1)S(1)} %collective-permute-done.12.refs_8_), channel_id=1, source_target_pairs={{0,1},{1,0},{2,3},{3,2},{4,5},{5,4},{6,7},{7,6},{8,9},{9,8},{10,11... | collective-permute-start | bytes 786440 | tf_op jit(solution)/shard_map/ppermute | solution.py:231
  74.9 5.6 %collective-permute-start.15 = (bf16[256,512]{1,0:T(8,128)(2,1)}, bf16[256,512]{1,0:T(8,128)(2,1)}, u32[]{:S(2)}, u32[]{:S(2)}) collective-permute-start(bf16[256,512]{1,0:T(8,128)(2,1)} %collective-permute-done.14.refs_10_), channel_id=1, source_target_pairs={{0,1},{1,0},{2,3},{3,2},{4,5},{5,4},{6,7},{7,6},{8,9},{9,8},{10,11... | collective-permute-start | bytes 786440 | tf_op jit(solution)/shard_map/ppermute | solution.py:231
  76.2 31.8 %all-to-all-start.2 = ((f16[8,64,512]{2,1,0:T(8,128)(2,1)}), f16[8,64,512]{2,1,0:T(8,128)(2,1)}, u32[]{:S(2)}, u32[]{:S(2)}) async-start(f16[8,64,512]{2,1,0:T(8,128)(2,1)} %bitcast.49), calls=%async_computation.2 | async-start | bytes 1048576 | tf_op jit(solution)/shard_map/all_to_all | solution.py:260
  108.0 30.1 %all-to-all-start.4 = ((f16[8,64,640]{2,1,0:T(8,128)(2,1)}), f16[8,64,640]{2,1,0:T(8,128)(2,1)}, u32[]{:S(2)}, u32[]{:S(2)}) async-start(f16[8,64,640]{2,1,0:T(8,128)(2,1)} %convert_element_type.58), calls=%async_computation.4 | async-start | bytes 1310720 | tf_op jit(solution)/shard_map/all_to_all | solution.py:260
  138.1 21.3 %all-to-all-start.3 = ((f16[8,64,640]{2,1,0:T(8,128)(2,1)}), f16[8,64,640]{2,1,0:T(8,128)(2,1)S(1)}, u32[]{:S(2)}, u32[]{:S(2)}) async-start(f16[8,64,640]{2,1,0:T(8,128)(2,1)} %convert_element_type.57), calls=%async_computation.3 | async-start | bytes 1310720 | tf_op jit(solution)/shard_map/all_to_all | solution.py:260
  150.1 2.5 %collective-permute-start.17 = (f16[64,512]{1,0:T(8,128)(2,1)S(1)}, f16[64,512]{1,0:T(8,128)(2,1)S(1)}, u32[]{:S(2)}, u32[]{:S(2)}) collective-permute-start(f16[64,512]{1,0:T(8,128)(2,1)S(1)} %slice_convert_fusion.1), channel_id=1, source_target_pairs={{0,1},{1,0},{2,3},{3,2},{4,5},{5,4},{6,7},{7,6},{8,9},{9,8},{10,11... | collective-permute-start | bytes 196616 | tf_op jit(solution)/shard_map/ppermute | solution.py:231
  161.2 5.3 %collective-permute-start.18 = (f16[64,512]{1,0:T(8,128)(2,1)S(1)}, f16[64,512]{1,0:T(8,128)(2,1)S(1)}, u32[]{:S(2)}, u32[]{:S(2)}) collective-permute-start(f16[64,512]{1,0:T(8,128)(2,1)S(1)} %slice_convert_fusion), channel_id=1, source_target_pairs={{0,1},{1,0},{2,3},{3,2},{4,5},{5,4},{6,7},{7,6},{8,9},{9,8},{10,11... | collective-permute-start | bytes 196616 | tf_op jit(solution)/shard_map/ppermute | solution.py:231
  (44 other events, 220.1 us)

commit v4 on v3

--- a/solution.py
+++ b/solution.py
@@ -11,7 +11,8 @@
 CB_DEV = 2
 HALF = jnp.float16
 COT_SCALE = 256.0
-VMEM_REST = 16 * 1024 * 1024
+VMEM = 56 * 1024 * 1024
+STREAMS = 2
 
 
 def ring_order(count):
@@ -50,12 +51,15 @@
         self.hists = hists
         self.share = share
         self.lanes = rows + 2 * share
+        streams = STREAMS if count <= 8 else 1
+        self.streams = [(k * rows // streams, rows // streams) for k in range(streams)]
         self.units = []
         for d in range(count):
-            if 2 * d == count:
-                self.units += [(d, 0, rows // 2), (d, rows // 2, rows // 2)]
-            else:
-                self.units.append((d, 0, rows))
+            for start, size in self.streams:
+                if 2 * d == count and streams == 1:
+                    self.units += [(d, 0, rows // 2), (d, rows // 2, rows // 2)]
+                else:
+                    self.units.append((d, start, size))
 
 
 def load_matrix(s, units, matrix, sems):
@@ -222,7 +226,7 @@
             transcendentals=0,
         ),
         compiler_params=pltpu.CompilerParams(
-            vmem_limit_bytes=VMEM_REST + s.count * s.rows * 2 * s.cols * 2
+            vmem_limit_bytes=VMEM
         ),
     )(table, *arrays, *units)
 
@@ -269,38 +273,57 @@
     both = both.reshape(2, share, 2, count, s.hists).transpose(3, 2, 4, 0, 1)
     points_message = both.reshape(2 * count, s.hists, 2 * share)
 
-    pieces = {(0, 0): unit}
-    swapped = {(0, 0): swap_cores(unit)}
-    ahead = behind = unit
-    before = {}
+    streams = s.streams
+    pieces, swapped, heads, before = {}, {}, {}, {}
+    for k, (start, size) in enumerate(streams):
+        piece = unit[start : start + size]
+        pieces[0, start] = piece
+        heads[k] = {-1: piece, 1: piece}
+        swapped[0, start] = swap_cores(piece)
+        before[0, k] = [(0, start)]
     last = count // 2
     for step in range(1, last + 1):
-        due = before.get(step - 2, [])
-        extra = [swapped[key] for key in due]
-        if step == 2:
-            extra += [mass_message, points_message, table]
-        if step == last:
-            mass = exchange(mass_message).astype(jnp.float32)
-            points = lax.all_to_all(points_message, ("src", "tgt"), 0, 0, tiled=True)
-            extra += [mass, points.astype(jnp.float32), cot_message]
-        ahead, behind, extra = lax.optimization_barrier((ahead, behind, extra))
-        swapped.update(zip(due, extra))
-        if step == 2:
-            mass_message, points_message, table = extra[-3:]
-        if step == last:
-            mass, points, cot_message = extra[-3:]
-        if 2 * step == count:
-            middle = rows // 2
-            new = {
-                (step, 0): shift(ahead[:middle], -1),
-                (step, middle): shift(behind[middle:], 1),
-            }
-        else:
-            ahead, behind = shift(ahead, -1), shift(behind, 1)
-            new = {(step, 0): ahead, (count - step, 0): behind}
-        pieces.update(new)
-        swapped.update({key: swap_cores(piece) for key, piece in new.items()})
-        before[step] = list(new) + ([(0, 0)] if step == 1 else [])
+        for k, (start, size) in enumerate(streams):
+            if 2 * step < count:
+                ways = {-1: (0, size), 1: (0, size)}
+            elif len(streams) > 1:
+                ways = {(-1, 1)[k % 2]: (0, size)}
+            else:
+                ways = {-1: (0, size // 2), 1: (size // 2, size // 2)}
+            due = before.get((step - 2, k), [])
+            extra = [swapped[key] for key in due]
+            names = []
+            if k == 0 and step == 2:
+                mass = exchange(mass_message).astype(jnp.float32)
+                names = ["mass", "table"]
+                extra += [mass, table]
+            if k == 0 and step == last - 1:
+                points = lax.all_to_all(points_message, ("src", "tgt"), 0, 0, tiled=True)
+                points = points.astype(jnp.float32)
+                names = ["points"]
+                extra += [points]
+            if k == 0 and step == last:
+                names = ["cot_message"]
+                extra += [cot_message]
+            now = [heads[k][way] for way in ways]
+            now, extra = lax.optimization_barrier((now, extra))
+            swapped.update(zip(due, extra))
+            for name, value in zip(names, extra[len(due) :]):
+                if name == "mass":
+                    mass = value
+                elif name == "table":
+                    table = value
+                elif name == "points":
+                    points = value
+                else:
+                    cot_message = value
+            new = {}
+            for (way, (lo, some)), piece in zip(ways.items(), now):
+                piece = heads[k][way] = shift(piece[lo : lo + some], way)
+                new[(-way * step) % count, start + lo] = piece
+            pieces.update(new)
+            swapped.update({key: swap_cores(piece) for key, piece in new.items()})
+            before[step, k] = list(new)
     units = []
     for d, start, _ in s.units:
         units += [pieces[d, start], swapped[d, start]]

time: 169 us -> 162 us (0.959)
  local copies, waits for them, and re-layouts: 36.4 us -> 14.4 us
  starting transfers between devices: 48.4 us -> 59.8 us
  Pallas kernels: 28.5 us -> 34.9 us
  waiting for transfers between devices: 32.7 us -> 30.7 us
    unnamed x93 -> x56, local copies, waits for them, and re-layouts: 26 us -> 5.76 us
    ppermute x8 -> x14, waiting for transfers between devices: 16.5 us -> 24.1 us  [shift(): return lax.ppermute(x, 'src', pairs)]
    pallas_call x2, Pallas kernels: 28.5 us -> 34.9 us  [call(): pl.pallas_call(functools.partial(kernel, s), out_shape=outs, in_specs=[pl...]
    all_to_all x1, waiting for transfers between devices: 6.6 us -> 1.23 us  [local(): points = lax.all_to_all(points_message, ('src', 'tgt'), 0, 0, tiled=True)]
    all_to_all x4, waiting for transfers between devices: 9.58 us -> 5.34 us  [exchange(): return lax.all_to_all(x, 'src', 0, 0, tiled=True)]
    ppermute x11 -> x18, starting transfers between devices: 10.4 us -> 14.6 us  [swap_cores(): return lax.ppermute(x, 'tgt', [(0, 1), (1, 0)])]
    ppermute x8 -> x14, starting transfers between devices: 12.2 us -> 16.3 us  [shift(): return lax.ppermute(x, 'src', pairs)]
    all_to_all x4, starting transfers between devices: 19 us -> 21 us  [exchange(): return lax.all_to_all(x, 'src', 0, 0, tiled=True)]
  transfers between devices with their start and end apart: 24 -> 37, of which waited for: 8 -> 8; matrix products, arithmetic and copies ran while one was open for 18% -> 18% of each run, Pallas kernels for 17% -> 22%
where the time goes in v4:
time: 162 us; the launch traced here: 161 us
  starting transfers between devices  59.8 us (37%)
  Pallas kernels  34.9 us (22%)
  waiting for transfers between devices  30.7 us (19%)
  other arithmetic  19.2 us (12%)
  local copies, waits for them, and re-layouts  14.4 us (9%)
    pallas_call x2, Pallas kernels, call(): pl.pallas_call(functools.partial(kernel, s), out_shape=outs, in_specs=[pl...  34.9 us
    ppermute x14, waiting for transfers between devices, shift(): return lax.ppermute(x, 'src', pairs)  24.1 us
    all_to_all x4, starting transfers between devices, exchange(): return lax.all_to_all(x, 'src', 0, 0, tiled=True)  21 us
    ppermute x14, starting transfers between devices, shift(): return lax.ppermute(x, 'src', pairs)  16.3 us
    ppermute x18, starting transfers between devices, swap_cores(): return lax.ppermute(x, 'tgt', [(0, 1), (1, 0)])  14.6 us
    all_to_all x1, starting transfers between devices, local(): points = lax.all_to_all(points_message, ('src', 'tgt'), 0, 0, tiled=True)  7.92 us
    unnamed x56, local copies, waits for them, and re-layouts  5.76 us
    all_to_all x4, waiting for transfers between devices, exchange(): return lax.all_to_all(x, 'src', 0, 0, tiled=True)  5.34 us
  transfers between devices with their start and end apart: 37, of which 8 were waited for; matrix products, arithmetic and copies ran while one was open for 18% of the time, Pallas kernels for 22%

profile of v4, /device:TPU:1, one launch (start us, length us, event | category | flops | bytes accessed | tf_op | source)
XLA Modules:
  0.0 160.8 jit_solution(6771581393090211669)
XLA Ops:
  3.2 6.4 %all-to-all-start = ((f16[8,64,512]{2,1,0:T(8,128)(2,1)}), f16[8,64,512]{2,1,0:T(8,128)(2,1)S(1)}, u32[]{:S(2)}, u32[]{:S(2)}) async-start(f16[8,64,512]{2,1,0:T(8,128)(2,1)} %bitcast.5), calls=%async_computation | async-start | bytes 1048576 | tf_op jit(solution)/shard_map/all_to_all | solution.py:264
  15.5 8.7 %collective-permute-done.10.refs_6_ = bf16[256,512]{1,0:T(8,128)(2,1)} collective-permute-done((bf16[256,512]{1,0:T(8,128)(2,1)S(1)}, bf16[256,512]{1,0:T(8,128)(2,1)}, u32[]{:S(2)}, u32[]{:S(2)}) %collective-permute-start.10) | collective-permute-done | bytes 262176 | tf_op jit(solution)/shard_map/ppermute | solution.py:261
  24.2 5.0 %collective-permute-start.11 = (bf16[256,512]{1,0:T(8,128)(2,1)S(1)}, bf16[256,512]{1,0:T(8,128)(2,1)}, u32[]{:S(2)}, u32[]{:S(2)}) collective-permute-start(bf16[256,512]{1,0:T(8,128)(2,1)S(1)} %bitcast.56), channel_id=1, source_target_pairs={{0,4},{4,8},{8,12},{12,14},{14,10},{10,6},{6,2},{2,0},{1,5},{5,9},... | collective-permute-start | bytes 786440 | tf_op jit(solution)/shard_map/ppermute | solution.py:261
  31.1 1.8 %maximum_bitcast_fusion = f16[8,2,64,2,64]{4,3,2,1,0:T(2,128)(2,1)S(1)} fusion(f16[1,64,2,8,64]{1,0,4,2,3:T(2,128)(2,1)S(1)} %copy.25, f16[1,64,2,8,64]{1,0,4,2,3:T(2,128)(2,1)S(1)} %copy.24), kind=kLoop, calls=%fused_computation.10 | loop fusion | flops 131072 | bytes 524288 | tf_op jit(solution)/shard_map/transpose | solution.py:273
  34.5 1.5 collective-permute-start.13
  36.0 7.9 %all-to-all-start.1 = ((f16[16,64,128]{2,1,0:T(8,128)(2,1)}), f16[16,64,128]{2,1,0:T(8,128)(2,1)S(1)}, u32[]{:S(2)}, u32[]{:S(2)}) async-start(f16[16,64,128]{2,1,0:T(8,128)(2,1)} %reshape.143), calls=%async_computation.1 | async-start | bytes 524288 | tf_op jit(solution)/shard_map/all_to_all | solution.py:301
  54.8 2.4 %collective-permute-done.3.refs_8_ = bf16[256,512]{1,0:T(8,128)(2,1)} collective-permute-done((bf16[256,512]{1,0:T(8,128)(2,1)}, bf16[256,512]{1,0:T(8,128)(2,1)}, u32[]{:S(2)}, u32[]{:S(2)}) %collective-permute-start.3) | collective-permute-done | bytes 262176 | tf_op jit(solution)/shard_map/ppermute | solution.py:261
  59.5 4.0 %collective-permute-done.17.refs_22_ = bf16[256,512]{1,0:T(8,128)(2,1)S(1)} collective-permute-done((bf16[256,512]{1,0:T(8,128)(2,1)S(1)}, bf16[256,512]{1,0:T(8,128)(2,1)S(1)}, u32[]{:S(2)}, u32[]{:S(2)}) %collective-permute-start.17) | collective-permute-done | bytes 262176 | tf_op jit(solution)/shard_map/ppermute | solution.py:261
  67.9 2.1 %collective-permute-start.27 = (bf16[256,512]{1,0:T(8,128)(2,1)}, bf16[256,512]{1,0:T(8,128)(2,1)S(1)}, u32[]{:S(2)}, u32[]{:S(2)}) collective-permute-start(bf16[256,512]{1,0:T(8,128)(2,1)} %collective-permute-done.4.refs_24_), channel_id=1, source_target_pairs={{0,4},{4,8},{8,12},{12,14},{14,10},{10,6},{6,2},{2,0},{1,5},{5,9},... | collective-permute-start | bytes 786440 | tf_op jit(solution)/shard_map/ppermute | solution.py:261
  71.3 3.3 %collective-permute-done.25.refs_18_ = bf16[256,512]{1,0:T(8,128)(2,1)S(1)} collective-permute-done((bf16[256,512]{1,0:T(8,128)(2,1)S(1)}, bf16[256,512]{1,0:T(8,128)(2,1)S(1)}, u32[]{:S(2)}, u32[]{:S(2)}) %collective-permute-start.25) | collective-permute-done | bytes 262176 | tf_op jit(solution)/shard_map/ppermute | solution.py:261
  75.8 4.4 %collective-permute-done.27.refs_20_ = bf16[256,512]{1,0:T(8,128)(2,1)S(1)} collective-permute-done((bf16[256,512]{1,0:T(8,128)(2,1)}, bf16[256,512]{1,0:T(8,128)(2,1)S(1)}, u32[]{:S(2)}, u32[]{:S(2)}) %collective-permute-start.27) | collective-permute-done | bytes 262176 | tf_op jit(solution)/shard_map/ppermute | solution.py:261
  81.0 3.7 %all-to-all-start.2 = ((f16[8,64,512]{2,1,0:T(8,128)(2,1)}), f16[8,64,512]{2,1,0:T(8,128)(2,1)S(1)}, u32[]{:S(2)}, u32[]{:S(2)}) async-start(f16[8,64,512]{2,1,0:T(8,128)(2,1)} %bitcast.11), calls=%async_computation.2 | async-start | bytes 1048576 | tf_op jit(solution)/shard_map/all_to_all | solution.py:264
  85.6 17.7 %shard_map.123 = (f32[8,64,512]{2,1,0:T(8,128)}, f32[8,64,640]{2,1,0:T(8,128)}, f32[64,1024]{1,0:T(8,128)}, f32[64,1024]{1,0:T(8,128)}, f32[64,1024]{1,0:T(8,128)}, /*index=5*/f32[8,8,512]{2,1,0:T(8,128)}) custom-call(s32[9]{0:T(128)} %pad_add_fusion.table, f32[8,64,512]{2,1,0:T(8,128)} %convert_element_type.53.mass, ...), custom_call_target="tpu_custom_call" | custom-call | flops 12884901888 | bytes 16777216 | tf_op jit(solution)/shard_map/pallas_call | solution.py:213
  103.4 2.3 %convert_element_type.58 = f16[8,64,640]{2,1,0:T(8,128)(2,1)} convert(f32[8,64,640]{2,1,0:T(8,128)} %get-tuple-element.70.thirds) | non-fusion elementwise | flops 327680 | bytes 1966080 | tf_op jit(solution)/shard_map/convert_element_type | solution.py:361
  105.6 5.5 %all-to-all-start.4 = ((f16[8,64,640]{2,1,0:T(8,128)(2,1)}), f16[8,64,640]{2,1,0:T(8,128)(2,1)S(1)}, u32[]{:S(2)}, u32[]{:S(2)}) async-start(f16[8,64,640]{2,1,0:T(8,128)(2,1)} %convert_element_type.58), calls=%async_computation.4 | async-start | bytes 1310720 | tf_op jit(solution)/shard_map/all_to_all | solution.py:264
  112.2 17.1 %shard_map.124 = f32[8,64,640]{2,1,0:T(8,128)} custom-call(s32[9]{0:T(128)} %pad_add_fusion.table, f32[8,64,512]{2,1,0:T(8,128)} %convert_element_type.53.mass, f32[16,64,128]{2,1,0:T(8,128)} %convert_element_type.54.points, f32[8,64,512]{2,1,0:T(8,128)} %convert_element_type.56.cot, f32[8,64,512]{2,1,0:T(8,128)} %get-tuple-element.69.row_two, ...), custom_call_target="tpu_custom_call" | custom-call | flops 12884901888 | bytes 16777216 | tf_op jit(solution)/shard_map/pallas_call | solution.py:213
  129.3 2.2 %convert_element_type.57 = f16[8,64,640]{2,1,0:T(8,128)(2,1)} convert(f32[8,64,640]{2,1,0:T(8,128)} %shard_map.124) | non-fusion elementwise | flops 327680 | bytes 1966080 | tf_op jit(solution)/shard_map/convert_element_type | solution.py:365
  131.6 5.4 %all-to-all-start.3 = ((f16[8,64,640]{2,1,0:T(8,128)(2,1)}), f16[8,64,640]{2,1,0:T(8,128)(2,1)S(1)}, u32[]{:S(2)}, u32[]{:S(2)}) async-start(f16[8,64,640]{2,1,0:T(8,128)(2,1)} %convert_element_type.57), calls=%async_computation.3 | async-start | bytes 1310720 | tf_op jit(solution)/shard_map/all_to_all | solution.py:264
  139.0 1.6 %copy.32 = f32[512,512]{0,1:T(8,128)S(1)} copy(f32[512,512]{1,0:T(8,128)} %slice.58) | data formatting | bytes 2097152
  140.6 1.8 %copy.33 = f32[512,128]{0,1:T(8,128)} copy(f32[512,128]{1,0:T(8,128)} %slice.59) | data formatting | bytes 524288
  143.4 1.9 %collective-permute-start.30 = (f16[64,512]{1,0:T(8,128)(2,1)S(1)}, f16[64,512]{1,0:T(8,128)(2,1)S(1)}, u32[]{:S(2)}, u32[]{:S(2)}) collective-permute-start(f16[64,512]{1,0:T(8,128)(2,1)S(1)} %slice_convert_fusion.1), channel_id=1, source_target_pairs={{0,1},{1,0},{2,3},{3,2},{4,5},{5,4},{6,7},{7,6},{8,9},{9,8},{10,11... | collective-permute-start | bytes 196616 | tf_op jit(solution)/shard_map/ppermute | solution.py:235
  147.3 5.3 %all-to-all-done.3 = f16[8,64,640]{2,1,0:T(8,128)(2,1)S(1)} async-done(((f16[8,64,640]{2,1,0:T(8,128)(2,1)}), f16[8,64,640]{2,1,0:T(8,128)(2,1)S(1)}, u32[]{:S(2)}, u32[]{:S(2)}) %all-to-all-start.3) | async-done | bytes 655392 | tf_op jit(solution)/shard_map/all_to_all | solution.py:264
  154.5 2.7 %collective-permute-start.31 = (f16[64,512]{1,0:T(8,128)(2,1)S(1)}, f16[64,512]{1,0:T(8,128)(2,1)S(1)}, u32[]{:S(2)}, u32[]{:S(2)}) collective-permute-start(f16[64,512]{1,0:T(8,128)(2,1)S(1)} %slice_convert_fusion), channel_id=1, source_target_pairs={{0,1},{1,0},{2,3},{3,2},{4,5},{5,4},{6,7},{7,6},{8,9},{9,8},{10,11... | collective-permute-start | bytes 196616 | tf_op jit(solution)/shard_map/ppermute | solution.py:235
  157.2 2.9 %bitcast_add_fusion = f32[512,512]{1,0:T(8,128)} fusion(f32[512,512]{0,1:T(8,128)} %copy.34, f32[512,512]{1,0:T(8,128)} %param.14, f32[512,512]{1,0:T(8,128)S(1)} %copy-done.2), kind=kLoop, calls=%fused_computation.3 | loop fusion | flops 786432 | bytes 4194304 | tf_op jit(solution)/shard_map/add | solution.py:371
  (147 shorter events, 42.0 us)
Async XLA Ops:
  3.2 32.8 %all-to-all-start = ((f16[8,64,512]{2,1,0:T(8,128)(2,1)}), f16[8,64,512]{2,1,0:T(8,128)(2,1)S(1)}, u32[]{:S(2)}, u32[]{:S(2)}) async-start(f16[8,64,512]{2,1,0:T(8,128)(2,1)} %bitcast.5), calls=%async_computation | async-start | bytes 1048576 | tf_op jit(solution)/shard_map/all_to_all | solution.py:264
  10.8 13.4 %collective-permute-start.10 = (bf16[256,512]{1,0:T(8,128)(2,1)S(1)}, bf16[256,512]{1,0:T(8,128)(2,1)}, u32[]{:S(2)}, u32[]{:S(2)}) collective-permute-start(bf16[256,512]{1,0:T(8,128)(2,1)S(1)} %bitcast.54), channel_id=1, source_target_pairs={{0,2},{4,0},{8,4},{12,8},{14,12},{10,14},{6,10},{2,6},{1,3},{5,1},... | collective-permute-start | bytes 786440 | tf_op jit(solution)/shard_map/ppermute | solution.py:261
  12.3 22.1 %collective-permute-start.12 = (bf16[256,512]{1,0:T(8,128)(2,1)S(1)}, bf16[256,512]{1,0:T(8,128)(2,1)}, u32[]{:S(2)}, u32[]{:S(2)}) collective-permute-start(bf16[256,512]{1,0:T(8,128)(2,1)S(1)} %bitcast.55), channel_id=1, source_target_pairs={{0,1},{1,0},{2,3},{3,2},{4,5},{5,4},{6,7},{7,6},{8,9},{9,8},{10,11... | collective-permute-start | bytes 786440 | tf_op jit(solution)/shard_map/ppermute | solution.py:235
  13.9 30.6 %collective-permute-start.2 = (bf16[256,512]{1,0:T(8,128)(2,1)S(1)}, bf16[256,512]{1,0:T(8,128)(2,1)}, u32[]{:S(2)}, u32[]{:S(2)}) collective-permute-start(bf16[256,512]{1,0:T(8,128)(2,1)S(1)} %bitcast.59), channel_id=1, source_target_pairs={{0,1},{1,0},{2,3},{3,2},{4,5},{5,4},{6,7},{7,6},{8,9},{9,8},{10,11... | collective-permute-start | bytes 786440 | tf_op jit(solution)/shard_map/ppermute | solution.py:235
  14.0 30.0 %collective-permute-start = (bf16[256,512]{1,0:T(8,128)(2,1)S(1)}, bf16[256,512]{1,0:T(8,128)(2,1)}, u32[]{:S(2)}, u32[]{:S(2)}) collective-permute-start(bf16[256,512]{1,0:T(8,128)(2,1)S(1)} %bitcast.60), channel_id=1, source_target_pairs={{0,2},{4,0},{8,4},{12,8},{14,12},{10,14},{6,10},{2,6},{1,3},{5,1},... | collective-permute-start | bytes 786440 | tf_op jit(solution)/shard_map/ppermute | solution.py:261
  15.2 28.9 %collective-permute-start.1 = (bf16[256,512]{1,0:T(8,128)(2,1)S(1)}, bf16[256,512]{1,0:T(8,128)(2,1)}, u32[]{:S(2)}, u32[]{:S(2)}) collective-permute-start(bf16[256,512]{1,0:T(8,128)(2,1)S(1)} %bitcast.61), channel_id=1, source_target_pairs={{0,4},{4,8},{8,12},{12,14},{14,10},{10,6},{6,2},{2,0},{1,5},{5,9},... | collective-permute-start | bytes 786440 | tf_op jit(solution)/shard_map/ppermute | solution.py:261
  24.2 10.2 %collective-permute-start.11 = (bf16[256,512]{1,0:T(8,128)(2,1)S(1)}, bf16[256,512]{1,0:T(8,128)(2,1)}, u32[]{:S(2)}, u32[]{:S(2)}) collective-permute-start(bf16[256,512]{1,0:T(8,128)(2,1)S(1)} %bitcast.56), channel_id=1, source_target_pairs={{0,4},{4,8},{8,12},{12,14},{14,10},{10,6},{6,2},{2,0},{1,5},{5,9},... | collective-permute-start | bytes 786440 | tf_op jit(solution)/shard_map/ppermute | solution.py:261
  34.5 13.2 %collective-permute-start.13 = (bf16[256,512]{1,0:T(8,128)(2,1)}, bf16[256,512]{1,0:T(8,128)(2,1)S(1)}, u32[]{:S(2)}, u32[]{:S(2)}) collective-permute-start(bf16[256,512]{1,0:T(8,128)(2,1)} %collective-permute-done.10.refs_6_), channel_id=1, source_target_pairs={{0,2},{4,0},{8,4},{12,8},{14,12},{10,14},{6,10},{2,6},{1,3},{5,1},... | collective-permute-start | bytes 786440 | tf_op jit(solution)/shard_map/ppermute | solution.py:261
  36.0 12.1 %collective-permute-start.14 = (bf16[256,512]{1,0:T(8,128)(2,1)}, bf16[256,512]{1,0:T(8,128)(2,1)S(1)}, u32[]{:S(2)}, u32[]{:S(2)}) collective-permute-start(bf16[256,512]{1,0:T(8,128)(2,1)} %collective-permute-done.11.refs_30_), channel_id=1, source_target_pairs={{0,4},{4,8},{8,12},{12,14},{14,10},{10,6},{6,2},{2,0},{1,5},{5,9},... | collective-permute-start | bytes 786440 | tf_op jit(solution)/shard_map/ppermute | solution.py:261
  36.0 17.4 %all-to-all-start.1 = ((f16[16,64,128]{2,1,0:T(8,128)(2,1)}), f16[16,64,128]{2,1,0:T(8,128)(2,1)S(1)}, u32[]{:S(2)}, u32[]{:S(2)}) async-start(f16[16,64,128]{2,1,0:T(8,128)(2,1)} %reshape.143), calls=%async_computation.1 | async-start | bytes 524288 | tf_op jit(solution)/shard_map/all_to_all | solution.py:301
  48.1 9.1 %collective-permute-start.3 = (bf16[256,512]{1,0:T(8,128)(2,1)}, bf16[256,512]{1,0:T(8,128)(2,1)}, u32[]{:S(2)}, u32[]{:S(2)}) collective-permute-start(bf16[256,512]{1,0:T(8,128)(2,1)} %collective-permute-done.refs_4_), channel_id=1, source_target_pairs={{0,2},{4,0},{8,4},{12,8},{14,12},{10,14},{6,10},{2,6},{1,3},{5,1},... | collective-permute-start | bytes 786440 | tf_op jit(solution)/shard_map/ppermute | solution.py:261
  49.6 13.9 %collective-permute-start.17 = (bf16[256,512]{1,0:T(8,128)(2,1)S(1)}, bf16[256,512]{1,0:T(8,128)(2,1)S(1)}, u32[]{:S(2)}, u32[]{:S(2)}) collective-permute-start(bf16[256,512]{1,0:T(8,128)(2,1)S(1)} %collective-permute-done.14.refs_26_), channel_id=1, source_target_pairs={{0,4},{4,8},{8,12},{12,14},{14,10},{10,6},{6,2},{2,0},{1,5},{5,9},... | collective-permute-start | bytes 786440 | tf_op jit(solution)/shard_map/ppermute | solution.py:261
  51.0 13.6 %collective-permute-start.18 = (bf16[256,512]{1,0:T(8,128)(2,1)S(1)}, bf16[256,512]{1,0:T(8,128)(2,1)}, u32[]{:S(2)}, u32[]{:S(2)}) collective-permute-start(bf16[256,512]{1,0:T(8,128)(2,1)S(1)} %collective-permute-done.13.refs_10_), channel_id=1, source_target_pairs={{0,1},{1,0},{2,3},{3,2},{4,5},{5,4},{6,7},{7,6},{8,9},{9,8},{10,11... | collective-permute-start | bytes 786440 | tf_op jit(solution)/shard_map/ppermute | solution.py:235
  54.3 12.4 %collective-permute-start.21 = (bf16[256,512]{1,0:T(8,128)(2,1)S(1)}, bf16[256,512]{1,0:T(8,128)(2,1)}, u32[]{:S(2)}, u32[]{:S(2)}) collective-permute-start(bf16[256,512]{1,0:T(8,128)(2,1)S(1)} %collective-permute-done.13.refs_10_), channel_id=1, source_target_pairs={{0,2},{4,0},{8,4},{12,8},{14,12},{10,14},{6,10},{2,6},{1,3},{5,1},... | collective-permute-start | bytes 786440 | tf_op jit(solution)/shard_map/ppermute | solution.py:261
  57.2 9.3 %collective-permute-start.19 = (bf16[256,512]{1,0:T(8,128)(2,1)S(1)}, bf16[256,512]{1,0:T(8,128)(2,1)}, u32[]{:S(2)}, u32[]{:S(2)}) collective-permute-start(bf16[256,512]{1,0:T(8,128)(2,1)S(1)} %collective-permute-done.14.refs_26_), channel_id=1, source_target_pairs={{0,1},{1,0},{2,3},{3,2},{4,5},{5,4},{6,7},{7,6},{8,9},{9,8},{10,11... | collective-permute-start | bytes 786440 | tf_op jit(solution)/shard_map/ppermute | solution.py:235
  58.2 9.8 %collective-permute-start.7 = (bf16[256,512]{1,0:T(8,128)(2,1)}, bf16[256,512]{1,0:T(8,128)(2,1)}, u32[]{:S(2)}, u32[]{:S(2)}) collective-permute-start(bf16[256,512]{1,0:T(8,128)(2,1)} %collective-permute-done.3.refs_8_), channel_id=1, source_target_pairs={{0,2},{4,0},{8,4},{12,8},{14,12},{10,14},{6,10},{2,6},{1,3},{5,1},... | collective-permute-start | bytes 786440 | tf_op jit(solution)/shard_map/ppermute | solution.py:261
  67.9 12.2 %collective-permute-start.27 = (bf16[256,512]{1,0:T(8,128)(2,1)}, bf16[256,512]{1,0:T(8,128)(2,1)S(1)}, u32[]{:S(2)}, u32[]{:S(2)}) collective-permute-start(bf16[256,512]{1,0:T(8,128)(2,1)} %collective-permute-done.4.refs_24_), channel_id=1, source_target_pairs={{0,4},{4,8},{8,12},{12,14},{14,10},{10,6},{6,2},{2,0},{1,5},{5,9},... | collective-permute-start | bytes 786440 | tf_op jit(solution)/shard_map/ppermute | solution.py:261
  70.0 10.9 %collective-permute-start.23 = (bf16[256,512]{1,0:T(8,128)(2,1)}, bf16[256,512]{1,0:T(8,128)(2,1)S(1)}, u32[]{:S(2)}, u32[]{:S(2)}) collective-permute-start(bf16[256,512]{1,0:T(8,128)(2,1)} %collective-permute-done.7.refs_12_), channel_id=1, source_target_pairs={{0,2},{4,0},{8,4},{12,8},{14,12},{10,14},{6,10},{2,6},{1,3},{5,1},... | collective-permute-start | bytes 786440 | tf_op jit(solution)/shard_map/ppermute | solution.py:261
  70.0 14.7 %collective-permute-start.29 = (bf16[256,512]{1,0:T(8,128)(2,1)S(1)}, bf16[256,512]{1,0:T(8,128)(2,1)S(1)}, u32[]{:S(2)}, u32[]{:S(2)}) collective-permute-start(bf16[256,512]{1,0:T(8,128)(2,1)S(1)} %copy-done.15), channel_id=1, source_target_pairs={{0,1},{1,0},{2,3},{3,2},{4,5},{5,4},{6,7},{7,6},{8,9},{9,8},{10,11... | collective-permute-start | bytes 786440 | tf_op jit(solution)/shard_map/ppermute | solution.py:235
  74.6 10.2 %collective-permute-start.26 = (bf16[256,512]{1,0:T(8,128)(2,1)S(1)}, bf16[256,512]{1,0:T(8,128)(2,1)S(1)}, u32[]{:S(2)}, u32[]{:S(2)}) collective-permute-start(bf16[256,512]{1,0:T(8,128)(2,1)S(1)} %collective-permute-done.25.refs_18_), channel_id=1, source_target_pairs={{0,1},{1,0},{2,3},{3,2},{4,5},{5,4},{6,7},{7,6},{8,9},{9,8},{10,11... | collective-permute-start | bytes 786440 | tf_op jit(solution)/shard_map/ppermute | solution.py:235
  75.7 9.1 %collective-permute-start.20 = (bf16[256,512]{1,0:T(8,128)(2,1)}, bf16[256,512]{1,0:T(8,128)(2,1)}, u32[]{:S(2)}, u32[]{:S(2)}) collective-permute-start(bf16[256,512]{1,0:T(8,128)(2,1)} %collective-permute-done.7.refs_12_), channel_id=1, source_target_pairs={{0,1},{1,0},{2,3},{3,2},{4,5},{5,4},{6,7},{7,6},{8,9},{9,8},{10,11... | collective-permute-start | bytes 786440 | tf_op jit(solution)/shard_map/ppermute | solution.py:235
  81.0 24.6 %all-to-all-start.2 = ((f16[8,64,512]{2,1,0:T(8,128)(2,1)}), f16[8,64,512]{2,1,0:T(8,128)(2,1)S(1)}, u32[]{:S(2)}, u32[]{:S(2)}) async-start(f16[8,64,512]{2,1,0:T(8,128)(2,1)} %bitcast.11), calls=%async_computation.2 | async-start | bytes 1048576 | tf_op jit(solution)/shard_map/all_to_all | solution.py:264
  105.6 25.9 %all-to-all-start.4 = ((f16[8,64,640]{2,1,0:T(8,128)(2,1)}), f16[8,64,640]{2,1,0:T(8,128)(2,1)S(1)}, u32[]{:S(2)}, u32[]{:S(2)}) async-start(f16[8,64,640]{2,1,0:T(8,128)(2,1)} %convert_element_type.58), calls=%async_computation.4 | async-start | bytes 1310720 | tf_op jit(solution)/shard_map/all_to_all | solution.py:264
  131.6 21.1 %all-to-all-start.3 = ((f16[8,64,640]{2,1,0:T(8,128)(2,1)}), f16[8,64,640]{2,1,0:T(8,128)(2,1)S(1)}, u32[]{:S(2)}, u32[]{:S(2)}) async-start(f16[8,64,640]{2,1,0:T(8,128)(2,1)} %convert_element_type.57), calls=%async_computation.3 | async-start | bytes 1310720 | tf_op jit(solution)/shard_map/all_to_all | solution.py:264
  (38 other events, 324.7 us)

commit v5 on v4

--- a/solution.py
+++ b/solution.py
@@ -13,6 +13,7 @@
 COT_SCALE = 256.0
 VMEM = 56 * 1024 * 1024
 STREAMS = 2
+GATHERED = 2
 
 
 def ring_order(count):
@@ -60,17 +61,26 @@
                     self.units += [(d, 0, rows // 2), (d, rows // 2, rows // 2)]
                 else:
                     self.units.append((d, start, size))
-
-
-def load_matrix(s, units, matrix, sems):
+        self.given = sum(1 if self.whole(d) else 2 for d, _, _ in self.units)
+
+    def whole(self, d):
+        return min(d, self.count - d) <= GATHERED
+
+
+def load_matrix(s, table, units, matrix, sems):
     copies = {}
-    for k, (d, start, size) in enumerate(s.units):
-        for t in range(2):
-            copy = pltpu.make_async_copy(
-                units[2 * k + t],
-                matrix.at[d, pl.ds(start, size), pl.ds(t * s.cols, s.cols)],
-                sems.at[d],
-            )
+    units = iter(units)
+    for d, start, size in s.units:
+        rows = pl.ds(start, size)
+        if s.whole(d):
+            pairs = [(next(units), matrix.at[d, rows])]
+        else:
+            pairs = []
+            for side in (table[s.count], 1 - table[s.count]):
+                columns = pl.ds(pl.multiple_of(side * s.cols, s.cols), s.cols)
+                pairs.append((next(units), matrix.at[d, rows, columns]))
+        for source, target in pairs:
+            copy = pltpu.make_async_copy(source, target, sems.at[d])
             copy.start()
             copies.setdefault(d, []).append(copy)
     return copies
@@ -88,12 +98,12 @@
             copy.wait()
 
 
-def gather_targets(s, pieces, core, part):
+def gather_targets(s, pieces, part):
     lo = part * s.share
     return jnp.concatenate(
         [
             pieces[2 * i + side, :, lo : lo + s.share]
-            for side in (core, 1 - core)
+            for side in range(2)
             for i in range(s.count)
         ],
         axis=1,
@@ -120,12 +130,12 @@
 
 
 def forward_kernel(s, table, mass, points, *refs):
-    given = 2 * len(s.units)
+    given = s.given
     units = refs[:given]
     row_two, thirds, col_one_out, col_two_out, col_three_out, row_one, matrix, sems = refs[given:]
-    copies = load_matrix(s, units, matrix, sems)
+    copies = load_matrix(s, table, units, matrix, sems)
     zero = jnp.zeros((s.hists, 2 * s.cols), jnp.float32)
-    target = gather_targets(s, points, table[s.count], 0)
+    target = gather_targets(s, points, 0)
     arrived(s, copies, None)
     ones = jnp.ones((8, 2 * s.cols), jnp.bfloat16)
 
@@ -165,13 +175,13 @@
 def backward_kernel(
     s, table, mass, points, cot, row_two, thirds, col_one, col_two, col_three, row_one, *refs
 ):
-    given = 2 * len(s.units)
+    given = s.given
     units = refs[:given]
     out, matrix, sems = refs[given:]
-    copies = load_matrix(s, units, matrix, sems)
+    copies = load_matrix(s, table, units, matrix, sems)
     zero = jnp.zeros((s.hists, 2 * s.cols), jnp.float32)
-    target = gather_targets(s, points, table[s.count], 0)
-    target_cot = gather_targets(s, points, table[s.count], 1)
+    target = gather_targets(s, points, 0)
+    target_cot = gather_targets(s, points, 1)
     right_one = target / col_one[...]
     right_two = target / col_two[...]
     arrived(s, copies, None)
@@ -231,6 +241,10 @@
     )(table, *arrays, *units)
 
 
+def both_sets(x):
+    return lax.all_gather(x, "tgt", axis=1, tiled=True)
+
+
 def swap_cores(x):
     return lax.ppermute(x, "tgt", [(0, 1), (1, 0)])
 
@@ -279,8 +293,7 @@
         piece = unit[start : start + size]
         pieces[0, start] = piece
         heads[k] = {-1: piece, 1: piece}
-        swapped[0, start] = swap_cores(piece)
-        before[0, k] = [(0, start)]
+        swapped[0, start] = both_sets(piece)
     last = count // 2
     for step in range(1, last + 1):
         for k, (start, size) in enumerate(streams):
@@ -293,18 +306,15 @@
             due = before.get((step - 2, k), [])
             extra = [swapped[key] for key in due]
             names = []
-            if k == 0 and step == 2:
+            if k == 0 and step == last - 1:
                 mass = exchange(mass_message).astype(jnp.float32)
                 names = ["mass", "table"]
                 extra += [mass, table]
-            if k == 0 and step == last - 1:
+            if k == 0 and step == last:
                 points = lax.all_to_all(points_message, ("src", "tgt"), 0, 0, tiled=True)
                 points = points.astype(jnp.float32)
-                names = ["points"]
-                extra += [points]
-            if k == 0 and step == last:
-                names = ["cot_message"]
-                extra += [cot_message]
+                names = ["points", "cot_message"]
+                extra += [points, cot_message]
             now = [heads[k][way] for way in ways]
             now, extra = lax.optimization_barrier((now, extra))
             swapped.update(zip(due, extra))
@@ -322,11 +332,12 @@
                 piece = heads[k][way] = shift(piece[lo : lo + some], way)
                 new[(-way * step) % count, start + lo] = piece
             pieces.update(new)
-            swapped.update({key: swap_cores(piece) for key, piece in new.items()})
-            before[step, k] = list(new)
+            for key, piece in new.items():
+                swapped[key] = both_sets(piece) if s.whole(key[0]) else swap_cores(piece)
+            before[step, k] = [key for key in new if not s.whole(key[0])]
     units = []
     for d, start, _ in s.units:
-        units += [pieces[d, start], swapped[d, start]]
+        units += [swapped[d, start]] if s.whole(d) else [pieces[d, start], swapped[d, start]]
     cot = exchange(cot_message).astype(jnp.float32)
 
     panel = jax.ShapeDtypeStruct((count, s.hists, rows), jnp.float32)
@@ -353,8 +364,9 @@
     def by_point(pieces):
         flat = pieces.reshape(cols_here, s.lanes).astype(jnp.float32)
         target = flat[:, rows:].T.reshape(2, share, cols_here)
-        other = swap_cores(target[1].astype(HALF)).astype(jnp.float32)
-        own = target[0]
+        own = lax.dynamic_index_in_dim(target, core, 0, keepdims=False)
+        other = lax.dynamic_index_in_dim(target, 1 - core, 0, keepdims=False)
+        other = swap_cores(other.astype(HALF)).astype(jnp.float32)
         halves = [jnp.where(core == t, own, other) for t in range(2)]
         return flat[:, :rows].T, jnp.concatenate(halves, axis=1)
 

time: 162 us -> 171 us (1.056)
  blocking collectives: 0 us -> 34.1 us
  waiting for transfers between devices: 30.7 us -> 11 us
  starting transfers between devices: 59.8 us -> 47.9 us
  other arithmetic: 19.2 us -> 22.9 us
  local copies, waits for them, and re-layouts: 14.4 us -> 17.3 us
    all_gather x0 -> x10, blocking collectives: none -> 34.1 us  [both_sets(): return lax.all_gather(x, 'tgt', axis=1, tiled=True)]
    ppermute x14, waiting for transfers between devices: 24.1 us -> 4.29 us  [shift(): return lax.ppermute(x, 'src', pairs)]
    ppermute x18 -> x8, starting transfers between devices: 14.6 us -> 8.58 us  [swap_cores(): return lax.ppermute(x, 'tgt', [(0, 1), (1, 0)])]
    ppermute x14, starting transfers between devices: 16.3 us -> 11.5 us  [shift(): return lax.ppermute(x, 'src', pairs)]
    transpose x1, other arithmetic: 1.76 us -> 3.86 us  [local(): both = both.reshape(2, share, 2, count, s.hists).transpose(3, 2, 4, 0, 1)]
    unnamed x56 -> x32, local copies, waits for them, and re-layouts: 5.76 us -> 5.7 us
  transfers between devices with their start and end apart: 37 -> 27, of which waited for: 8 -> 3; matrix products, arithmetic and copies ran while one was open for 18% -> 20% of each run, Pallas kernels for 22% -> 20%
where the time goes in v5:
time: 171 us; the launch traced here: 170 us
  starting transfers between devices  47.9 us (28%)
  Pallas kernels  34.7 us (20%)
  blocking collectives  34.1 us (20%)
  other arithmetic  22.9 us (13%)
  local copies, waits for them, and re-layouts  17.3 us (10%)
  waiting for transfers between devices  11 us (6%)
    pallas_call x2, Pallas kernels, call(): pl.pallas_call(functools.partial(kernel, s), out_shape=outs, in_specs=[pl...  34.7 us
    all_gather x10, blocking collectives, both_sets(): return lax.all_gather(x, 'tgt', axis=1, tiled=True)  34.1 us
    all_to_all x4, starting transfers between devices, exchange(): return lax.all_to_all(x, 'src', 0, 0, tiled=True)  20.8 us
    ppermute x14, starting transfers between devices, shift(): return lax.ppermute(x, 'src', pairs)  11.5 us
    ppermute x8, starting transfers between devices, swap_cores(): return lax.ppermute(x, 'tgt', [(0, 1), (1, 0)])  8.58 us
    all_to_all x1, starting transfers between devices, local(): points = lax.all_to_all(points_message, ('src', 'tgt'), 0, 0, tiled=True)  6.95 us
    all_to_all x4, waiting for transfers between devices, exchange(): return lax.all_to_all(x, 'src', 0, 0, tiled=True)  6.67 us
    unnamed x32, local copies, waits for them, and re-layouts  5.7 us
  transfers between devices with their start and end apart: 27, of which 3 were waited for; matrix products, arithmetic and copies ran while one was open for 20% of the time, Pallas kernels for 20%

profile of v5, /device:TPU:1, one launch (start us, length us, event | category | flops | bytes accessed | tf_op | source)
XLA Modules:
  0.0 170.2 jit_solution(935255031917969989)
XLA Ops:
  7.0 5.7 %all-to-all-start = ((f16[8,64,512]{2,1,0:T(8,128)(2,1)}), f16[8,64,512]{2,1,0:T(8,128)(2,1)S(1)}, u32[]{:S(2)}, u32[]{:S(2)}) async-start(f16[8,64,512]{2,1,0:T(8,128)(2,1)} %bitcast.5), calls=%async_computation | async-start | bytes 1048576 | tf_op jit(solution)/shard_map/all_to_all | solution.py:278
  18.1 3.9 %maximum_bitcast_fusion = f16[8,2,64,2,64]{4,3,2,1,0:T(2,128)(2,1)} fusion(f16[1,64,2,8,64]{1,0,4,2,3:T(2,128)(2,1)} %copy.25, f16[1,64,2,8,64]{1,0,4,2,3:T(2,128)(2,1)} %copy.24), kind=kLoop, calls=%fused_computation.10 | loop fusion | flops 131072 | bytes 524288 | tf_op jit(solution)/shard_map/transpose | solution.py:287
  29.6 4.0 %all_gather.30.refs_0_ = bf16[256,1024]{1,0:T(8,128)(2,1)} all-gather(bf16[256,512]{1,0:T(8,128)(2,1)S(1)} %bitcast.63), channel_id=1, replica_groups=mesh['grp'=2,'src'=8,'tgt'=2] {'tgt'}, dimensions={1}, use_global_device_ids=true | all-gather | bytes 786432 | tf_op jit(solution)/shard_map/all_gather | solution.py:245
  33.6 4.1 %all_gather.31.refs_1_ = bf16[256,1024]{1,0:T(8,128)(2,1)} all-gather(bf16[256,512]{1,0:T(8,128)(2,1)} %bitcast.36), channel_id=1, replica_groups=mesh['grp'=2,'src'=8,'tgt'=2] {'tgt'}, dimensions={1}, use_global_device_ids=true | all-gather | bytes 786432 | tf_op jit(solution)/shard_map/all_gather | solution.py:245
  41.0 7.0 %all-to-all-start.1 = ((f16[16,64,128]{2,1,0:T(8,128)(2,1)}), f16[16,64,128]{2,1,0:T(8,128)(2,1)S(1)}, u32[]{:S(2)}, u32[]{:S(2)}) async-start(f16[16,64,128]{2,1,0:T(8,128)(2,1)} %reshape.141), calls=%async_computation.1 | async-start | bytes 524288 | tf_op jit(solution)/shard_map/all_to_all | solution.py:314
  48.0 3.8 %all_gather.32.refs_2_ = bf16[256,1024]{1,0:T(8,128)(2,1)} all-gather(bf16[256,512]{1,0:T(8,128)(2,1)} %collective-permute-done), channel_id=1, replica_groups=mesh['grp'=2,'src'=8,'tgt'=2] {'tgt'}, dimensions={1}, use_global_device_ids=true | all-gather | bytes 786432 | tf_op jit(solution)/shard_map/all_gather | solution.py:245
  51.8 4.1 %all_gather.33.refs_3_ = bf16[256,1024]{1,0:T(8,128)(2,1)} all-gather(bf16[256,512]{1,0:T(8,128)(2,1)} %collective-permute-done.5), channel_id=1, replica_groups=mesh['grp'=2,'src'=8,'tgt'=2] {'tgt'}, dimensions={1}, use_global_device_ids=true | all-gather | bytes 786432 | tf_op jit(solution)/shard_map/all_gather | solution.py:245
  59.8 4.9 %all_gather.38.refs_20_ = bf16[256,1024]{1,0:T(8,128)(2,1)} all-gather(bf16[256,512]{1,0:T(8,128)(2,1)} %collective-permute-done.1), channel_id=1, replica_groups=mesh['grp'=2,'src'=8,'tgt'=2] {'tgt'}, dimensions={1}, use_global_device_ids=true | all-gather | bytes 786432 | tf_op jit(solution)/shard_map/all_gather | solution.py:245
  64.7 3.8 %all_gather.39.refs_21_ = bf16[256,1024]{1,0:T(8,128)(2,1)} all-gather(bf16[256,512]{1,0:T(8,128)(2,1)} %collective-permute-done.6), channel_id=1, replica_groups=mesh['grp'=2,'src'=8,'tgt'=2] {'tgt'}, dimensions={1}, use_global_device_ids=true | all-gather | bytes 786432 | tf_op jit(solution)/shard_map/all_gather | solution.py:245
  71.6 2.4 %all_gather.34.refs_4_ = bf16[256,1024]{1,0:T(8,128)(2,1)} all-gather(bf16[256,512]{1,0:T(8,128)(2,1)S(1)} %collective-permute-done.2), channel_id=1, replica_groups=mesh['grp'=2,'src'=8,'tgt'=2] {'tgt'}, dimensions={1}, use_global_device_ids=true | all-gather | bytes 786432 | tf_op jit(solution)/shard_map/all_gather | solution.py:245
  74.0 2.3 %all_gather.35.refs_5_ = bf16[256,1024]{1,0:T(8,128)(2,1)} all-gather(bf16[256,512]{1,0:T(8,128)(2,1)S(1)} %collective-permute-done.7), channel_id=1, replica_groups=mesh['grp'=2,'src'=8,'tgt'=2] {'tgt'}, dimensions={1}, use_global_device_ids=true | all-gather | bytes 786432 | tf_op jit(solution)/shard_map/all_gather | solution.py:245
  79.3 3.6 %collective-permute-done.17.refs_14_ = bf16[256,512]{1,0:T(8,128)(2,1)} collective-permute-done((bf16[256,512]{1,0:T(8,128)(2,1)S(1)}, bf16[256,512]{1,0:T(8,128)(2,1)}, u32[]{:S(2)}, u32[]{:S(2)}) %collective-permute-start.17) | collective-permute-done | bytes 262176 | tf_op jit(solution)/shard_map/ppermute | solution.py:275
  84.1 2.4 %all_gather.36.refs_18_ = bf16[256,1024]{1,0:T(8,128)(2,1)} all-gather(bf16[256,512]{1,0:T(8,128)(2,1)S(1)} %collective-permute-done.3), channel_id=1, replica_groups=mesh['grp'=2,'src'=8,'tgt'=2] {'tgt'}, dimensions={1}, use_global_device_ids=true | all-gather | bytes 786432 | tf_op jit(solution)/shard_map/all_gather | solution.py:245
  86.6 2.3 %all_gather.37.refs_19_ = bf16[256,1024]{1,0:T(8,128)(2,1)} all-gather(bf16[256,512]{1,0:T(8,128)(2,1)S(1)} %collective-permute-done.9), channel_id=1, replica_groups=mesh['grp'=2,'src'=8,'tgt'=2] {'tgt'}, dimensions={1}, use_global_device_ids=true | all-gather | bytes 786432 | tf_op jit(solution)/shard_map/all_gather | solution.py:245
  88.9 4.3 %all-to-all-start.2 = ((f16[8,64,512]{2,1,0:T(8,128)(2,1)}), f16[8,64,512]{2,1,0:T(8,128)(2,1)S(1)}, u32[]{:S(2)}, u32[]{:S(2)}) async-start(f16[8,64,512]{2,1,0:T(8,128)(2,1)} %bitcast.11), calls=%async_computation.2 | async-start | bytes 1048576 | tf_op jit(solution)/shard_map/all_to_all | solution.py:278
  94.0 17.7 %shard_map.123 = (f32[8,64,512]{2,1,0:T(8,128)}, f32[8,64,640]{2,1,0:T(8,128)}, f32[64,1024]{1,0:T(8,128)}, f32[64,1024]{1,0:T(8,128)}, f32[64,1024]{1,0:T(8,128)}, /*index=5*/f32[8,8,512]{2,1,0:T(8,128)}) custom-call(s32[9]{0:T(128)} %pad_add_fusion.table, f32[8,64,512]{2,1,0:T(8,128)} %convert_element_type.63.mass, ...), custom_call_target="tpu_custom_call" | custom-call | flops 12884901888 | bytes 16777216 | tf_op jit(solution)/shard_map/pallas_call | solution.py:223
  114.0 5.4 %all-to-all-start.4 = ((f16[8,64,640]{2,1,0:T(8,128)(2,1)}), f16[8,64,640]{2,1,0:T(8,128)(2,1)S(1)}, u32[]{:S(2)}, u32[]{:S(2)}) async-start(f16[8,64,640]{2,1,0:T(8,128)(2,1)} %convert_element_type.68), calls=%async_computation.4 | async-start | bytes 1310720 | tf_op jit(solution)/shard_map/all_to_all | solution.py:278
  120.6 17.0 %shard_map.124 = f32[8,64,640]{2,1,0:T(8,128)} custom-call(s32[9]{0:T(128)} %pad_add_fusion.table, f32[8,64,512]{2,1,0:T(8,128)} %convert_element_type.63.mass, f32[16,64,128]{2,1,0:T(8,128)} %convert_element_type.64.points, f32[8,64,512]{2,1,0:T(8,128)} %convert_element_type.66.cot, f32[8,64,512]{2,1,0:T(8,128)} %get-tuple-element.47.row_two, ...), custom_call_target="tpu_custom_call" | custom-call | flops 12884901888 | bytes 16777216 | tf_op jit(solution)/shard_map/pallas_call | solution.py:223
  139.8 5.4 %all-to-all-start.3 = ((f16[8,64,640]{2,1,0:T(8,128)(2,1)}), f16[8,64,640]{2,1,0:T(8,128)(2,1)}, u32[]{:S(2)}, u32[]{:S(2)}) async-start(f16[8,64,640]{2,1,0:T(8,128)(2,1)} %convert_element_type.67), calls=%async_computation.3 | async-start | bytes 1310720 | tf_op jit(solution)/shard_map/all_to_all | solution.py:278
  146.5 2.5 %copy.32 = f32[512,512]{0,1:T(8,128)} copy(f32[512,512]{1,0:T(8,128)} %slice.36) | data formatting | bytes 2097152
  151.1 2.5 %fusion.1 = f32[512,512]{1,0:T(8,128)} fusion(f32[512,512]{1,0:T(8,128)S(1)} %copy-done.2, f32[512,512]{0,1:T(8,128)} %copy.32), kind=kLoop, calls=%fused_computation.5 | loop fusion | flops 262144 | bytes 3145728 | tf_op jit(solution)/shard_map/log | solution.py:374
  154.4 6.7 %all-to-all-done.3 = f16[8,64,640]{2,1,0:T(8,128)(2,1)} async-done(((f16[8,64,640]{2,1,0:T(8,128)(2,1)}), f16[8,64,640]{2,1,0:T(8,128)(2,1)}, u32[]{:S(2)}, u32[]{:S(2)}) %all-to-all-start.3) | async-done | bytes 655392 | tf_op jit(solution)/shard_map/all_to_all | solution.py:278
  163.9 2.7 %collective-permute-start.21 = (f16[64,512]{1,0:T(8,128)(2,1)S(1)}, f16[64,512]{1,0:T(8,128)(2,1)S(1)}, u32[]{:S(2)}, u32[]{:S(2)}) collective-permute-start(f16[64,512]{1,0:T(8,128)(2,1)S(1)} %fusion.9), channel_id=1, source_target_pairs={{0,1},{1,0},{2,3},{3,2},{4,5},{5,4},{6,7},{7,6},{8,9},{9,8},{10,11... | collective-permute-start | bytes 196616 | tf_op jit(solution)/shard_map/ppermute | solution.py:249
  166.6 2.9 %bitcast_add_fusion = f32[512,512]{1,0:T(8,128)} fusion(f32[512,512]{0,1:T(8,128)} %copy.33, f32[512,512]{1,0:T(8,128)} %param.14, f32[512,512]{1,0:T(8,128)S(1)} %copy-done.2), kind=kLoop, calls=%fused_computation.3 | loop fusion | flops 786432 | bytes 4194304 | tf_op jit(solution)/shard_map/add | solution.py:383
  (115 shorter events, 48.0 us)
Async XLA Ops:
  3.5 34.2 %collective-permute-start = (bf16[256,512]{1,0:T(8,128)(2,1)S(1)}, bf16[256,512]{1,0:T(8,128)(2,1)}, u32[]{:S(2)}, u32[]{:S(2)}) collective-permute-start(bf16[256,512]{1,0:T(8,128)(2,1)S(1)} %bitcast.61), channel_id=1, source_target_pairs={{0,2},{4,0},{8,4},{12,8},{14,12},{10,14},{6,10},{2,6},{1,3},{5,1},... | collective-permute-start | bytes 786440 | tf_op jit(solution)/shard_map/ppermute | solution.py:275
  5.6 32.1 %collective-permute-start.1 = (bf16[256,512]{1,0:T(8,128)(2,1)S(1)}, bf16[256,512]{1,0:T(8,128)(2,1)}, u32[]{:S(2)}, u32[]{:S(2)}) collective-permute-start(bf16[256,512]{1,0:T(8,128)(2,1)S(1)} %bitcast.62), channel_id=1, source_target_pairs={{0,4},{4,8},{8,12},{12,14},{14,10},{10,6},{6,2},{2,0},{1,5},{5,9},... | collective-permute-start | bytes 786440 | tf_op jit(solution)/shard_map/ppermute | solution.py:275
  7.0 34.0 %all-to-all-start = ((f16[8,64,512]{2,1,0:T(8,128)(2,1)}), f16[8,64,512]{2,1,0:T(8,128)(2,1)S(1)}, u32[]{:S(2)}, u32[]{:S(2)}) async-start(f16[8,64,512]{2,1,0:T(8,128)(2,1)} %bitcast.5), calls=%async_computation | async-start | bytes 1048576 | tf_op jit(solution)/shard_map/all_to_all | solution.py:278
  13.4 26.1 %collective-permute-start.5 = (bf16[256,512]{1,0:T(8,128)(2,1)}, bf16[256,512]{1,0:T(8,128)(2,1)}, u32[]{:S(2)}, u32[]{:S(2)}) collective-permute-start(bf16[256,512]{1,0:T(8,128)(2,1)} %bitcast.36), channel_id=1, source_target_pairs={{0,2},{4,0},{8,4},{12,8},{14,12},{10,14},{6,10},{2,6},{1,3},{5,1},... | collective-permute-start | bytes 786440 | tf_op jit(solution)/shard_map/ppermute | solution.py:275
  14.8 24.7 %collective-permute-start.6 = (bf16[256,512]{1,0:T(8,128)(2,1)}, bf16[256,512]{1,0:T(8,128)(2,1)}, u32[]{:S(2)}, u32[]{:S(2)}) collective-permute-start(bf16[256,512]{1,0:T(8,128)(2,1)} %bitcast.36), channel_id=1, source_target_pairs={{0,4},{4,8},{8,12},{12,14},{14,10},{10,6},{6,2},{2,0},{1,5},{5,9},... | collective-permute-start | bytes 786440 | tf_op jit(solution)/shard_map/ppermute | solution.py:275
  37.7 20.8 %collective-permute-start.2 = (bf16[256,512]{1,0:T(8,128)(2,1)}, bf16[256,512]{1,0:T(8,128)(2,1)S(1)}, u32[]{:S(2)}, u32[]{:S(2)}) collective-permute-start(bf16[256,512]{1,0:T(8,128)(2,1)} %collective-permute-done), channel_id=1, source_target_pairs={{0,2},{4,0},{8,4},{12,8},{14,12},{10,14},{6,10},{2,6},{1,3},{5,1},... | collective-permute-start | bytes 786440 | tf_op jit(solution)/shard_map/ppermute | solution.py:275
  39.5 19.0 %collective-permute-start.3 = (bf16[256,512]{1,0:T(8,128)(2,1)}, bf16[256,512]{1,0:T(8,128)(2,1)S(1)}, u32[]{:S(2)}, u32[]{:S(2)}) collective-permute-start(bf16[256,512]{1,0:T(8,128)(2,1)} %collective-permute-done.1), channel_id=1, source_target_pairs={{0,4},{4,8},{8,12},{12,14},{14,10},{10,6},{6,2},{2,0},{1,5},{5,9},... | collective-permute-start | bytes 786440 | tf_op jit(solution)/shard_map/ppermute | solution.py:275
  39.5 16.3 %collective-permute-start.7 = (bf16[256,512]{1,0:T(8,128)(2,1)}, bf16[256,512]{1,0:T(8,128)(2,1)S(1)}, u32[]{:S(2)}, u32[]{:S(2)}) collective-permute-start(bf16[256,512]{1,0:T(8,128)(2,1)} %collective-permute-done.5), channel_id=1, source_target_pairs={{0,2},{4,0},{8,4},{12,8},{14,12},{10,14},{6,10},{2,6},{1,3},{5,1},... | collective-permute-start | bytes 786440 | tf_op jit(solution)/shard_map/ppermute | solution.py:275
  40.9 14.9 %collective-permute-start.9 = (bf16[256,512]{1,0:T(8,128)(2,1)}, bf16[256,512]{1,0:T(8,128)(2,1)S(1)}, u32[]{:S(2)}, u32[]{:S(2)}) collective-permute-start(bf16[256,512]{1,0:T(8,128)(2,1)} %collective-permute-done.6), channel_id=1, source_target_pairs={{0,4},{4,8},{8,12},{12,14},{14,10},{10,6},{6,2},{2,0},{1,5},{5,9},... | collective-permute-start | bytes 786440 | tf_op jit(solution)/shard_map/ppermute | solution.py:275
  41.0 27.6 %all-to-all-start.1 = ((f16[16,64,128]{2,1,0:T(8,128)(2,1)}), f16[16,64,128]{2,1,0:T(8,128)(2,1)S(1)}, u32[]{:S(2)}, u32[]{:S(2)}) async-start(f16[16,64,128]{2,1,0:T(8,128)(2,1)} %reshape.141), calls=%async_computation.1 | async-start | bytes 524288 | tf_op jit(solution)/shard_map/all_to_all | solution.py:314
  55.9 13.6 %collective-permute-start.10 = (bf16[256,512]{1,0:T(8,128)(2,1)S(1)}, bf16[256,512]{1,0:T(8,128)(2,1)}, u32[]{:S(2)}, u32[]{:S(2)}) collective-permute-start(bf16[256,512]{1,0:T(8,128)(2,1)S(1)} %collective-permute-done.7), channel_id=1, source_target_pairs={{0,2},{4,0},{8,4},{12,8},{14,12},{10,14},{6,10},{2,6},{1,3},{5,1},... | collective-permute-start | bytes 786440 | tf_op jit(solution)/shard_map/ppermute | solution.py:275
  57.3 12.2 %collective-permute-start.14 = (bf16[256,512]{1,0:T(8,128)(2,1)S(1)}, bf16[256,512]{1,0:T(8,128)(2,1)}, u32[]{:S(2)}, u32[]{:S(2)}) collective-permute-start(bf16[256,512]{1,0:T(8,128)(2,1)S(1)} %collective-permute-done.9), channel_id=1, source_target_pairs={{0,4},{4,8},{8,12},{12,14},{14,10},{10,6},{6,2},{2,0},{1,5},{5,9},... | collective-permute-start | bytes 786440 | tf_op jit(solution)/shard_map/ppermute | solution.py:275
  58.5 13.1 %collective-permute-start.4 = (bf16[256,512]{1,0:T(8,128)(2,1)S(1)}, bf16[256,512]{1,0:T(8,128)(2,1)S(1)}, u32[]{:S(2)}, u32[]{:S(2)}) collective-permute-start(bf16[256,512]{1,0:T(8,128)(2,1)S(1)} %collective-permute-done.2), channel_id=1, source_target_pairs={{0,2},{4,0},{8,4},{12,8},{14,12},{10,14},{6,10},{2,6},{1,3},{5,1},... | collective-permute-start | bytes 786440 | tf_op jit(solution)/shard_map/ppermute | solution.py:275
  69.5 9.7 %collective-permute-start.11 = (bf16[256,512]{1,0:T(8,128)(2,1)}, bf16[256,512]{1,0:T(8,128)(2,1)S(1)}, u32[]{:S(2)}, u32[]{:S(2)}) collective-permute-start(bf16[256,512]{1,0:T(8,128)(2,1)} %collective-permute-done.10.refs_8_), channel_id=1, source_target_pairs={{0,1},{1,0},{2,3},{3,2},{4,5},{5,4},{6,7},{7,6},{8,9},{9,8},{10,11... | collective-permute-start | bytes 786440 | tf_op jit(solution)/shard_map/ppermute | solution.py:249
  70.0 12.9 %collective-permute-start.17 = (bf16[256,512]{1,0:T(8,128)(2,1)S(1)}, bf16[256,512]{1,0:T(8,128)(2,1)}, u32[]{:S(2)}, u32[]{:S(2)}) collective-permute-start(bf16[256,512]{1,0:T(8,128)(2,1)S(1)} %collective-permute-done.3), channel_id=1, source_target_pairs={{0,4},{4,8},{8,12},{12,14},{14,10},{10,6},{6,2},{2,0},{1,5},{5,9},... | collective-permute-start | bytes 786440 | tf_op jit(solution)/shard_map/ppermute | solution.py:275
  71.6 12.5 %collective-permute-start.12 = (bf16[256,512]{1,0:T(8,128)(2,1)S(1)}, bf16[256,512]{1,0:T(8,128)(2,1)}, u32[]{:S(2)}, u32[]{:S(2)}) collective-permute-start(bf16[256,512]{1,0:T(8,128)(2,1)S(1)} %collective-permute-done.4.refs_6_), channel_id=1, source_target_pairs={{0,2},{4,0},{8,4},{12,8},{14,12},{10,14},{6,10},{2,6},{1,3},{5,1},... | collective-permute-start | bytes 786440 | tf_op jit(solution)/shard_map/ppermute | solution.py:275
  76.3 16.8 %collective-permute-start.19 = (bf16[256,512]{1,0:T(8,128)(2,1)}, bf16[256,512]{1,0:T(8,128)(2,1)S(1)}, u32[]{:S(2)}, u32[]{:S(2)}) collective-permute-start(bf16[256,512]{1,0:T(8,128)(2,1)} %collective-permute-done.14.refs_16_), channel_id=1, source_target_pairs={{0,1},{1,0},{2,3},{3,2},{4,5},{5,4},{6,7},{7,6},{8,9},{9,8},{10,11... | collective-permute-start | bytes 786440 | tf_op jit(solution)/shard_map/ppermute | solution.py:249
  77.3 15.8 %collective-permute-start.16 = (bf16[256,512]{1,0:T(8,128)(2,1)S(1)}, bf16[256,512]{1,0:T(8,128)(2,1)S(1)}, u32[]{:S(2)}, u32[]{:S(2)}) collective-permute-start(bf16[256,512]{1,0:T(8,128)(2,1)S(1)} %collective-permute-done.15.refs_12_), channel_id=1, source_target_pairs={{0,1},{1,0},{2,3},{3,2},{4,5},{5,4},{6,7},{7,6},{8,9},{9,8},{10,11... | collective-permute-start | bytes 786440 | tf_op jit(solution)/shard_map/ppermute | solution.py:249
  79.2 14.0 %collective-permute-start.8 = (bf16[256,512]{1,0:T(8,128)(2,1)S(1)}, bf16[256,512]{1,0:T(8,128)(2,1)}, u32[]{:S(2)}, u32[]{:S(2)}) collective-permute-start(bf16[256,512]{1,0:T(8,128)(2,1)S(1)} %collective-permute-done.4.refs_6_), channel_id=1, source_target_pairs={{0,1},{1,0},{2,3},{3,2},{4,5},{5,4},{6,7},{7,6},{8,9},{9,8},{10,11... | collective-permute-start | bytes 786440 | tf_op jit(solution)/shard_map/ppermute | solution.py:249
  82.9 10.3 %collective-permute-start.18 = (bf16[256,512]{1,0:T(8,128)(2,1)}, bf16[256,512]{1,0:T(8,128)(2,1)}, u32[]{:S(2)}, u32[]{:S(2)}) collective-permute-start(bf16[256,512]{1,0:T(8,128)(2,1)} %collective-permute-done.17.refs_14_), channel_id=1, source_target_pairs={{0,1},{1,0},{2,3},{3,2},{4,5},{5,4},{6,7},{7,6},{8,9},{9,8},{10,11... | collective-permute-start | bytes 786440 | tf_op jit(solution)/shard_map/ppermute | solution.py:249
  84.1 9.1 %collective-permute-start.13 = (bf16[256,512]{1,0:T(8,128)(2,1)}, bf16[256,512]{1,0:T(8,128)(2,1)}, u32[]{:S(2)}, u32[]{:S(2)}) collective-permute-start(bf16[256,512]{1,0:T(8,128)(2,1)} %collective-permute-done.12.refs_10_), channel_id=1, source_target_pairs={{0,1},{1,0},{2,3},{3,2},{4,5},{5,4},{6,7},{7,6},{8,9},{9,8},{10,11... | collective-permute-start | bytes 786440 | tf_op jit(solution)/shard_map/ppermute | solution.py:249
  88.9 25.1 %all-to-all-start.2 = ((f16[8,64,512]{2,1,0:T(8,128)(2,1)}), f16[8,64,512]{2,1,0:T(8,128)(2,1)S(1)}, u32[]{:S(2)}, u32[]{:S(2)}) async-start(f16[8,64,512]{2,1,0:T(8,128)(2,1)} %bitcast.11), calls=%async_computation.2 | async-start | bytes 1048576 | tf_op jit(solution)/shard_map/all_to_all | solution.py:278
  114.0 25.9 %all-to-all-start.4 = ((f16[8,64,640]{2,1,0:T(8,128)(2,1)}), f16[8,64,640]{2,1,0:T(8,128)(2,1)S(1)}, u32[]{:S(2)}, u32[]{:S(2)}) async-start(f16[8,64,640]{2,1,0:T(8,128)(2,1)} %convert_element_type.68), calls=%async_computation.4 | async-start | bytes 1310720 | tf_op jit(solution)/shard_map/all_to_all | solution.py:278
  139.8 21.2 %all-to-all-start.3 = ((f16[8,64,640]{2,1,0:T(8,128)(2,1)}), f16[8,64,640]{2,1,0:T(8,128)(2,1)}, u32[]{:S(2)}, u32[]{:S(2)}) async-start(f16[8,64,640]{2,1,0:T(8,128)(2,1)} %convert_element_type.67), calls=%async_computation.3 | async-start | bytes 1310720 | tf_op jit(solution)/shard_map/all_to_all | solution.py:278
  (17 other events, 95.4 us)

commit v6 on v4

--- a/solution.py
+++ b/solution.py
@@ -11,7 +11,7 @@
 CB_DEV = 2
 HALF = jnp.float16
 COT_SCALE = 256.0
-VMEM = 56 * 1024 * 1024
+VMEM_REST = 16 * 1024 * 1024
 STREAMS = 2
 
 
@@ -88,12 +88,11 @@
             copy.wait()
 
 
-def gather_targets(s, pieces, core, part):
-    lo = part * s.share
+def gather_targets(s, pieces):
     return jnp.concatenate(
         [
-            pieces[2 * i + side, :, lo : lo + s.share]
-            for side in (core, 1 - core)
+            pieces[i, :, s.rows + t * s.share : s.rows + (t + 1) * s.share]
+            for t in range(2)
             for i in range(s.count)
         ],
         axis=1,
@@ -119,13 +118,14 @@
     return lax.fori_loop(0, count, body, init)
 
 
-def forward_kernel(s, table, mass, points, *refs):
-    given = 2 * len(s.units)
-    units = refs[:given]
-    row_two, thirds, col_one_out, col_two_out, col_three_out, row_one, matrix, sems = refs[given:]
+def forward_kernel(s, table, mass, *refs):
+    units = refs[: 2 * len(s.units)]
+    thirds, state_out, refs = refs[len(units)], refs[len(units) + 1 : len(units) + 6], refs[len(units) + 6 :]
+    matrix, sems, state, state_sems = refs[0], refs[1], refs[2:7], refs[7]
+    row_two, row_one, col_one, col_two, col_three = state
     copies = load_matrix(s, units, matrix, sems)
     zero = jnp.zeros((s.hists, 2 * s.cols), jnp.float32)
-    target = gather_targets(s, points, table[s.count], 0)
+    target = gather_targets(s, mass)
     arrived(s, copies, None)
     ones = jnp.ones((8, 2 * s.cols), jnp.bfloat16)
 
@@ -133,73 +133,88 @@
         arrived(s, copies, d)
         sums = nt(ones, matrix[d])
         row_one[d] = sums
-        left = mass[table[d]] / sums[0:1]
+        left = mass[table[d], :, : s.rows] / sums[0:1]
         return total + nn(left.astype(jnp.bfloat16), matrix[d])
 
-    col_one = each(s.count, first, zero)
-    col_one_out[...] = col_one
-    panel = (target / col_one).astype(jnp.bfloat16)
+    total = each(s.count, first, zero)
+    col_one[...] = total
+    panel = (target / total).astype(jnp.bfloat16)
 
     def second(d, total):
         row = nt(panel, matrix[d])
         row_two[d] = row
-        left = mass[table[d]] / row
+        left = mass[table[d], :, : s.rows] / row
         return total + nn(left.astype(jnp.bfloat16), matrix[d])
 
-    col_two = each(s.count, second, zero)
-    col_two_out[...] = col_two
-    panel = (target / col_two).astype(jnp.bfloat16)
+    total = each(s.count, second, zero)
+    col_two[...] = total
+    leaving = [
+        pltpu.make_async_copy(state[k], state_out[k], state_sems.at[k]) for k in range(len(state))
+    ]
+    for copy in leaving[:-1]:
+        copy.start()
+    panel = (target / total).astype(jnp.bfloat16)
 
     def third(d, total):
         row = nt(panel, matrix[d])
-        k = table[d]
-        thirds[k, :, : s.rows] = row
-        left = mass[table[d]] / row
+        thirds[table[d], :, : s.rows] = row
+        left = mass[table[d], :, : s.rows] / row
         return total + nn(left.astype(jnp.bfloat16), matrix[d])
 
-    col_three = each(s.count, third, zero)
-    col_three_out[...] = col_three
-    scatter_targets(s, thirds, col_three)
-
-
-def backward_kernel(
-    s, table, mass, points, cot, row_two, thirds, col_one, col_two, col_three, row_one, *refs
-):
-    given = 2 * len(s.units)
-    units = refs[:given]
-    out, matrix, sems = refs[given:]
+    total = each(s.count, third, zero)
+    col_three[...] = total
+    leaving[-1].start()
+    scatter_targets(s, thirds, total)
+    for copy in leaving:
+        copy.wait()
+
+
+def backward_kernel(s, table, mass, cot, thirds, *refs):
+    state_in, refs = refs[:5], refs[5:]
+    units, refs = refs[: 2 * len(s.units)], refs[2 * len(s.units) :]
+    out, matrix, sems, state, state_sems = refs[0], refs[1], refs[2], refs[3:8], refs[8]
+    row_two, row_one, col_one, col_two, col_three = state
+    arriving = [
+        pltpu.make_async_copy(state_in[k], state[k], state_sems.at[k]) for k in range(len(state))
+    ]
+    arriving[-1].start()
     copies = load_matrix(s, units, matrix, sems)
+    for copy in arriving[:-1]:
+        copy.start()
     zero = jnp.zeros((s.hists, 2 * s.cols), jnp.float32)
-    target = gather_targets(s, points, table[s.count], 0)
-    target_cot = gather_targets(s, points, table[s.count], 1)
-    right_one = target / col_one[...]
-    right_two = target / col_two[...]
+    target = gather_targets(s, mass)
+    target_cot = gather_targets(s, cot)
+    arriving[-1].wait()
+    panel = (-target_cot / col_three[...]).astype(jnp.bfloat16)
     arrived(s, copies, None)
-    panel = (-target_cot / col_three[...]).astype(jnp.bfloat16)
 
     def third(d, total):
         arrived(s, copies, d)
         k = table[d]
         grad = nt(panel, matrix[d])
         row = thirds[k, :, : s.rows]
-        left = mass[table[d]] / row
+        left = mass[k, :, : s.rows] / row
         term = grad / row
-        out[table[d], :, : s.rows] = term
-        rowgrad = -(cot[k] / row + term * left)
+        out[k, :, : s.rows] = term
+        rowgrad = -(cot[k, :, : s.rows] / row + term * left)
         return total + nn(rowgrad.astype(jnp.bfloat16), matrix[d])
 
-    term_two = each(s.count, third, zero) / col_two[...]
-    panel = (-term_two * right_two).astype(jnp.bfloat16)
+    total = each(s.count, third, zero)
+    for copy in arriving[:-1]:
+        copy.wait()
+    term_two = total / col_two[...]
+    panel = (-term_two * (target / col_two[...])).astype(jnp.bfloat16)
 
     def second(d, total):
+        k = table[d]
         row = row_two[d]
         term = nt(panel, matrix[d]) / row
-        out[table[d], :, : s.rows] += term
-        rowgrad = -term * (mass[table[d]] / row)
+        out[k, :, : s.rows] += term
+        rowgrad = -term * (mass[k, :, : s.rows] / row)
         return total + nn(rowgrad.astype(jnp.bfloat16), matrix[d])
 
     term_one = each(s.count, second, zero) / col_one[...]
-    panel = (-term_one * right_one).astype(jnp.bfloat16)
+    panel = (-term_one * (target / col_one[...])).astype(jnp.bfloat16)
 
     def first(d, carry):
         out[table[d], :, : s.rows] += nt(panel, matrix[d]) / row_one[d, 0:1]
@@ -209,16 +224,25 @@
     scatter_targets(s, out, term_two + term_one)
 
 
-def call(kernel, s, outs, table, arrays, units):
+def call(kernel, s, outs, states, table, arrays, units):
+    out_shape, out_specs = list(outs), [pl.BlockSpec(memory_space=pltpu.VMEM)] * len(outs)
+    forward = len(arrays) == 1
+    if forward:
+        out_shape += states
+        out_specs += [pl.BlockSpec(memory_space=pltpu.HBM)] * len(states)
+    taken = len(units) + (0 if forward else len(states))
     return pl.pallas_call(
         functools.partial(kernel, s),
-        out_shape=outs,
+        out_shape=out_shape,
         in_specs=[pl.BlockSpec(memory_space=pltpu.SMEM)]
-        + [pl.BlockSpec(memory_space=pltpu.VMEM)] * len(arrays)
-        + [pl.BlockSpec(memory_space=pl.ANY)] * len(units),
+        + [pl.BlockSpec(memory_space=pltpu.VMEM)] * (len(arrays) - (taken - len(units)))
+        + [pl.BlockSpec(memory_space=pltpu.HBM)] * taken,
+        out_specs=out_specs,
         scratch_shapes=[
             pltpu.VMEM((s.count, s.rows, 2 * s.cols), jnp.bfloat16),
             pltpu.SemaphoreType.DMA((s.count,)),
+            *[pltpu.VMEM(state.shape, state.dtype) for state in states],
+            pltpu.SemaphoreType.DMA((len(states),)),
         ],
         cost_estimate=pl.CostEstimate(
             flops=6 * 2 * s.count * s.rows * 2 * s.cols * 256,
@@ -226,7 +250,7 @@
             transcendentals=0,
         ),
         compiler_params=pltpu.CompilerParams(
-            vmem_limit_bytes=VMEM
+            vmem_limit_bytes=VMEM_REST + s.count * s.rows * 2 * s.cols * 2
         ),
     )(table, *arrays, *units)
 
@@ -254,7 +278,6 @@
     core = lax.axis_index("tgt")
     at = jnp.asarray(place)[me]
     table = jnp.asarray(ring)[(at + jnp.arange(count, dtype=jnp.int32)) % count]
-    table = jnp.concatenate([table, core[None]]).astype(jnp.int32)
 
     def shift(x, distance):
         pairs = [(int(ring[p]), int(ring[(p + distance) % count])) for p in range(count)]
@@ -263,15 +286,20 @@
     def exchange(x):
         return lax.all_to_all(x, "src", 0, 0, tiled=True)
 
-    def by_histogram(source):
-        return source.astype(HALF).T.reshape(count, s.hists, rows)
+    def by_histogram(source, target):
+        target = target.astype(HALF).reshape(share, 2, cols_here)
+        mine = lax.dynamic_index_in_dim(target, core, 1, keepdims=False)
+        other = lax.dynamic_index_in_dim(target, 1 - core, 1, keepdims=False)
+        both = jnp.concatenate([mine, swap_cores(other)]).T
+        return jnp.concatenate(
+            [
+                source.astype(HALF).T.reshape(count, s.hists, rows),
+                both.reshape(count, s.hists, 2 * share),
+            ],
+            axis=2,
+        )
 
     unit = dense_blocks(kernel_tiles, tile_cols, tile_count)
-    mass_message = by_histogram(source_mass)
-    cot_message = by_histogram(source_cotangent * COT_SCALE)
-    both = jnp.stack([target_mass[0], target_cotangent[0] * COT_SCALE]).astype(HALF)
-    both = both.reshape(2, share, 2, count, s.hists).transpose(3, 2, 4, 0, 1)
-    points_message = both.reshape(2 * count, s.hists, 2 * share)
 
     streams = s.streams
     pieces, swapped, heads, before = {}, {}, {}, {}
@@ -291,32 +319,15 @@
             else:
                 ways = {-1: (0, size // 2), 1: (size // 2, size // 2)}
             due = before.get((step - 2, k), [])
-            extra = [swapped[key] for key in due]
-            names = []
-            if k == 0 and step == 2:
+            now, ready = [heads[k][way] for way in ways], [swapped[key] for key in due]
+            if k == 0 and step == max(last - 1, 2):
                 mass = exchange(mass_message).astype(jnp.float32)
-                names = ["mass", "table"]
-                extra += [mass, table]
-            if k == 0 and step == last - 1:
-                points = lax.all_to_all(points_message, ("src", "tgt"), 0, 0, tiled=True)
-                points = points.astype(jnp.float32)
-                names = ["points"]
-                extra += [points]
-            if k == 0 and step == last:
-                names = ["cot_message"]
-                extra += [cot_message]
-            now = [heads[k][way] for way in ways]
-            now, extra = lax.optimization_barrier((now, extra))
-            swapped.update(zip(due, extra))
-            for name, value in zip(names, extra[len(due) :]):
-                if name == "mass":
-                    mass = value
-                elif name == "table":
-                    table = value
-                elif name == "points":
-                    points = value
-                else:
-                    cot_message = value
+                now, ready, mass, table = lax.optimization_barrier((now, ready, mass, table))
+            elif k == 0 and step == last:
+                now, ready, cot_message = lax.optimization_barrier((now, ready, cot_message))
+            else:
+                now, ready = lax.optimization_barrier((now, ready))
+            swapped.update(zip(due, ready))
             new = {}
             for (way, (lo, some)), piece in zip(ways.items(), now):
                 piece = heads[k][way] = shift(piece[lo : lo + some], way)
@@ -324,30 +335,33 @@
             pieces.update(new)
             swapped.update({key: swap_cores(piece) for key, piece in new.items()})
             before[step, k] = list(new)
+            if k == 0 and step == 1:
+                head, mass_here, points_here = lax.optimization_barrier(
+                    (heads[0][-1], source_mass, target_mass)
+                )
+                heads[0][-1] = pieces[1 % count, start] = head
+                mass_message = by_histogram(mass_here, points_here[0])
+            if k == 0 and step == max(last - 2, 1):
+                cot_message = by_histogram(
+                    source_cotangent * COT_SCALE, target_cotangent[0] * COT_SCALE
+                )
     units = []
     for d, start, _ in s.units:
         units += [pieces[d, start], swapped[d, start]]
     cot = exchange(cot_message).astype(jnp.float32)
 
-    panel = jax.ShapeDtypeStruct((count, s.hists, rows), jnp.float32)
     wide = jax.ShapeDtypeStruct((count, s.hists, s.lanes), jnp.float32)
     column = jax.ShapeDtypeStruct((s.hists, 2 * s.cols), jnp.float32)
-    sums = jax.ShapeDtypeStruct((count, 8, rows), jnp.float32)
-    row_two, thirds, col_one, col_two, col_three, row_one = call(
-        forward_kernel,
-        s,
-        (panel, wide, column, column, column, sums),
-        table,
-        (mass, points),
-        units,
-    )
-    grads = call(
-        backward_kernel,
-        s,
-        wide,
-        table,
-        (mass, points, cot, row_two, thirds, col_one, col_two, col_three, row_one),
-        units,
+    states = [
+        jax.ShapeDtypeStruct((count, s.hists, rows), jnp.float32),
+        jax.ShapeDtypeStruct((count, 8, rows), jnp.float32),
+        column,
+        column,
+        column,
+    ]
+    thirds, *state = call(forward_kernel, s, [wide], states, table, (mass,), units)
+    (grads,) = call(
+        backward_kernel, s, [wide], states, table, (mass, cot, thirds, *state), units
     )
 
     def by_point(pieces):
@@ -361,15 +375,23 @@
     row_three, col_three = by_point(exchange(thirds.astype(HALF)))
     source_potential = jnp.log(source_mass / row_three)
     target_potential = jnp.log(target_mass[0] / col_three)
-    back, source_potential, target_potential = lax.optimization_barrier(
-        (exchange(grads.astype(HALF)), source_potential, target_potential)
+    source_known = source_cotangent / source_mass
+    target_known = target_cotangent[0] / target_mass[0]
+    back, source_potential, target_potential, source_known, target_known = lax.optimization_barrier(
+        (
+            exchange(grads.astype(HALF)),
+            source_potential,
+            target_potential,
+            source_known,
+            target_known,
+        )
     )
     source_term, target_term = by_point(back)
     return (
         source_potential,
         target_potential[None],
-        source_cotangent / source_mass + source_term * (1 / COT_SCALE),
-        (target_cotangent[0] / target_mass[0] + target_term * (1 / COT_SCALE))[None],
+        source_known + source_term * (1 / COT_SCALE),
+        (target_known + target_term * (1 / COT_SCALE))[None],
     )
 
 

time: 162 us -> 198 us (1.22)
  local copies, waits for them, and re-layouts: 14.4 us -> 49.1 us
  Pallas kernels: 34.9 us -> 29.4 us
  waiting for transfers between devices: 30.7 us -> 33.6 us
  starting transfers between devices: 59.8 us -> 62.4 us
    unnamed x56 -> x138, local copies, waits for them, and re-layouts: 5.76 us -> 37.8 us
    all_to_all x1 -> x0, starting transfers between devices: 7.92 us -> none  [local(): points = lax.all_to_all(points_message, ('src', 'tgt'), 0, 0, tiled=True)]
    ppermute x18 -> x20, starting transfers between devices: 14.6 us -> 20 us  [swap_cores(): return lax.ppermute(x, 'tgt', [(0, 1), (1, 0)])]
    pallas_call x2, Pallas kernels: 34.9 us -> 29.4 us  [call(): pl.pallas_call(functools.partial(kernel, s), out_shape=out_shape, in_spec...]
    ppermute x14, starting transfers between devices: 16.3 us -> 21.6 us  [shift(): return lax.ppermute(x, 'src', pairs)]
    dynamic_slice x0 -> x5, local copies, waits for them, and re-layouts: none -> 4.88 us  [the longest x2 2.52 us: by_histogram(): other = lax.dynamic_index_in_dim(target, 1 - core, 1, keepdims=False)]
    concatenate x2 -> x4, other arithmetic: 0.66 us -> 5.2 us  [the longest x2 3.05 us: by_histogram(): jnp.concatenate([source.astype(HALF).T.reshape(count, s.hists, rows), bot...]
    div x0 -> x2, other arithmetic: none -> 3.75 us  [the longest x1 2.93 us: local(): source_known = source_cotangent / source_mass]
  transfers between devices with their start and end apart: 37 -> 38, of which waited for: 8 -> 9; matrix products, arithmetic and copies ran while one was open for 18% -> 13% of each run, Pallas kernels for 22% -> 15%
where the time goes in v6:
time: 198 us; the launch traced here: 196 us
  starting transfers between devices  62.4 us (32%)
  local copies, waits for them, and re-layouts  49.1 us (25%)
  waiting for transfers between devices  33.6 us (17%)
  Pallas kernels  29.4 us (15%)
  other arithmetic  19.1 us (10%)
    unnamed x138, local copies, waits for them, and re-layouts  37.8 us
    pallas_call x2, Pallas kernels, call(): pl.pallas_call(functools.partial(kernel, s), out_shape=out_shape, in_spec...  29.4 us
    ppermute x14, waiting for transfers between devices, shift(): return lax.ppermute(x, 'src', pairs)  27.3 us
    ppermute x14, starting transfers between devices, shift(): return lax.ppermute(x, 'src', pairs)  21.6 us
    all_to_all x4, starting transfers between devices, exchange(): return lax.all_to_all(x, 'src', 0, 0, tiled=True)  20.8 us
    ppermute x20, starting transfers between devices, swap_cores(): return lax.ppermute(x, 'tgt', [(0, 1), (1, 0)])  20 us
    all_to_all x4, waiting for transfers between devices, exchange(): return lax.all_to_all(x, 'src', 0, 0, tiled=True)  5.71 us
  transfers between devices with their start and end apart: 38, of which 9 were waited for; matrix products, arithmetic and copies ran while one was open for 13% of the time, Pallas kernels for 15%

profile of v6, /device:TPU:1, one launch (start us, length us, event | category | flops | bytes accessed | tf_op | source)
XLA Modules:
  0.0 196.3 jit_solution(10129957956117295483)
XLA Ops:
  3.5 2.1 %collective-permute-start = (bf16[256,512]{1,0:T(8,128)(2,1)S(1)}, bf16[256,512]{1,0:T(8,128)(2,1)S(1)}, u32[]{:S(2)}, u32[]{:S(2)}) collective-permute-start(bf16[256,512]{1,0:T(8,128)(2,1)S(1)} %bitcast.55), channel_id=1, source_target_pairs={{0,2},{4,0},{8,4},{12,8},{14,12},{10,14},{6,10},{2,6},{1,3},{5,1},... | collective-permute-start | bytes 786440 | tf_op jit(solution)/shard_map/ppermute | solution.py:284
  5.8 6.0 %collective-permute-done.refs_4_.refs_9_ = bf16[256,512]{1,0:T(8,128)(2,1)S(1)} collective-permute-done((bf16[256,512]{1,0:T(8,128)(2,1)S(1)}, bf16[256,512]{1,0:T(8,128)(2,1)S(1)}, u32[]{:S(2)}, u32[]{:S(2)}) %collective-permute-start) | collective-permute-done | bytes 262176 | tf_op jit(solution)/shard_map/ppermute | solution.py:284
  18.6 5.8 %all-to-all-start = ((f16[8,64,640]{2,1,0:T(8,128)(2,1)}), f16[8,64,640]{2,1,0:T(8,128)(2,1)}, u32[]{:S(2)}, u32[]{:S(2)}) async-start(f16[8,64,640]{2,1,0:T(8,128)(2,1)} %pad_maximum_fusion), calls=%async_computation | async-start | bytes 1310720 | tf_op jit(solution)/shard_map/all_to_all | solution.py:287
  29.3 11.7 %collective-permute-done.12.refs_6_.refs_11_ = bf16[256,512]{1,0:T(8,128)(2,1)S(1)} collective-permute-done((bf16[256,512]{1,0:T(8,128)(2,1)S(1)}, bf16[256,512]{1,0:T(8,128)(2,1)S(1)}, u32[]{:S(2)}, u32[]{:S(2)}) %collective-permute-start.12) | collective-permute-done | bytes 262176 | tf_op jit(solution)/shard_map/ppermute | solution.py:284
  41.7 2.1 %collective-permute-start.15 = (bf16[256,512]{1,0:T(8,128)(2,1)S(1)}, bf16[256,512]{1,0:T(8,128)(2,1)S(1)}, u32[]{:S(2)}, u32[]{:S(2)}) collective-permute-start(bf16[256,512]{1,0:T(8,128)(2,1)S(1)} %collective-permute-done.12.refs_6_.refs_11_), channel_id=1, source_target_pairs={{0,2},{4,0},{8,4},{12,8},{14,12},{10,14},{6,10},{2,6},{1,3},{5,1},... | collective-permute-start | bytes 786440 | tf_op jit(solution)/shard_map/ppermute | solution.py:284
  43.9 4.1 %collective-permute-start.16 = (bf16[256,512]{1,0:T(8,128)(2,1)S(1)}, bf16[256,512]{1,0:T(8,128)(2,1)S(1)}, u32[]{:S(2)}, u32[]{:S(2)}) collective-permute-start(bf16[256,512]{1,0:T(8,128)(2,1)S(1)} %collective-permute-done.13.refs_30_.refs_35_), channel_id=1, source_target_pairs={{0,4},{4,8},{8,12},{12,14},{14,10},{10,6},{6,2},{2,0},{1,5},{5,9},... | collective-permute-start | bytes 786440 | tf_op jit(solution)/shard_map/ppermute | solution.py:284
  47.9 1.8 collective-permute-start.17
  50.5 2.2 %collective-permute-start.3 = (bf16[256,512]{1,0:T(8,128)(2,1)S(1)}, bf16[256,512]{1,0:T(8,128)(2,1)}, u32[]{:S(2)}, u32[]{:S(2)}) collective-permute-start(bf16[256,512]{1,0:T(8,128)(2,1)S(1)} %collective-permute-done.refs_4_.refs_9_), channel_id=1, source_target_pairs={{0,2},{4,0},{8,4},{12,8},{14,12},{10,14},{6,10},{2,6},{1,3},{5,1},... | collective-permute-start | bytes 786440 | tf_op jit(solution)/shard_map/ppermute | solution.py:284
  54.2 2.8 %collective-permute-start.5 = (bf16[256,512]{1,0:T(8,128)(2,1)S(1)}, bf16[256,512]{1,0:T(8,128)(2,1)}, u32[]{:S(2)}, u32[]{:S(2)}) collective-permute-start(bf16[256,512]{1,0:T(8,128)(2,1)S(1)} %collective-permute-done.refs_4_.refs_9_), channel_id=1, source_target_pairs={{0,1},{1,0},{2,3},{3,2},{4,5},{5,4},{6,7},{7,6},{8,9},{9,8},{10,11... | collective-permute-start | bytes 786440 | tf_op jit(solution)/shard_map/ppermute | solution.py:259
  67.0 1.8 collective-permute-start.23
  70.1 2.2 %collective-permute-start.8 = (bf16[256,512]{1,0:T(8,128)(2,1)}, bf16[256,512]{1,0:T(8,128)(2,1)}, u32[]{:S(2)}, u32[]{:S(2)}) collective-permute-start(bf16[256,512]{1,0:T(8,128)(2,1)} %collective-permute-done.3.refs_8_.refs_13_), channel_id=1, source_target_pairs={{0,2},{4,0},{8,4},{12,8},{14,12},{10,14},{6,10},{2,6},{1,3},{5,1},... | collective-permute-start | bytes 786440 | tf_op jit(solution)/shard_map/ppermute | solution.py:284
  73.2 2.2 %copy.28 = f16[512,512]{1,0:T(8,128)(2,1)} copy(f16[512,512]{0,1:T(8,128)(2,1)} %fusion.2) | data formatting | bytes 1048576 | tf_op jit(solution)/shard_map/transpose | solution.py:296
  77.4 2.0 %pad_maximum_fusion.1 = f16[8,64,640]{2,1,0:T(8,128)(2,1)} fusion(f16[8,64,128]{2,1,0:T(8,128)(2,1)S(1)} %bitcast.74, f16[8,64,512]{2,1,0:T(8,128)(2,1)} %bitcast.66), kind=kLoop, calls=%fused_computation.8 | loop fusion | flops 327680 | bytes 1310720 | tf_op jit(solution)/shard_map/concatenate | solution.py:294
  83.5 3.7 %collective-permute-done.27.refs_18_.refs_23_ = bf16[256,512]{1,0:T(8,128)(2,1)S(1)} collective-permute-done((bf16[256,512]{1,0:T(8,128)(2,1)}, bf16[256,512]{1,0:T(8,128)(2,1)S(1)}, u32[]{:S(2)}, u32[]{:S(2)}) %collective-permute-start.27) | collective-permute-done | bytes 262176 | tf_op jit(solution)/shard_map/ppermute | solution.py:284
  87.3 1.8 collective-permute-start.28
  89.2 3.7 %collective-permute-done.29.refs_20_.refs_25_ = bf16[256,512]{1,0:T(8,128)(2,1)} collective-permute-done((bf16[256,512]{1,0:T(8,128)(2,1)}, bf16[256,512]{1,0:T(8,128)(2,1)}, u32[]{:S(2)}, u32[]{:S(2)}) %collective-permute-start.29) | collective-permute-done | bytes 262176 | tf_op jit(solution)/shard_map/ppermute | solution.py:284
  94.1 4.4 %all-to-all-start.1 = ((f16[8,64,640]{2,1,0:T(8,128)(2,1)}), f16[8,64,640]{2,1,0:T(8,128)(2,1)}, u32[]{:S(2)}, u32[]{:S(2)}) async-start(f16[8,64,640]{2,1,0:T(8,128)(2,1)} %pad_maximum_fusion.1), calls=%async_computation.1 | async-start | bytes 1310720 | tf_op jit(solution)/shard_map/all_to_all | solution.py:287
  113.8 15.7 %shard_map.123 = (f32[8,64,640]{2,1,0:T(8,128)S(1)}, f32[8,64,512]{2,1,0:T(8,128)S(1)}, f32[8,8,512]{2,1,0:T(8,128)S(1)}, f32[64,1024]{1,0:T(8,128)S(1)}, f32[64...) custom-call(s32[8]{0:T(128)S(1)} %gather_fusion, f32[8,64,640]{2,1,0:T(8,128)S(1)} %convert_element_type.64.mass, ...), custom_call_target="tpu_custom_call" | custom-call | flops 12884901888 | bytes 16777216 | tf_op jit(solution)/shard_map/pallas_call | solution.py:234
  133.5 5.2 %all-to-all-start.3 = ((f16[8,64,640]{2,1,0:T(8,128)(2,1)}), f16[8,64,640]{2,1,0:T(8,128)(2,1)}, u32[]{:S(2)}, u32[]{:S(2)}) async-start(f16[8,64,640]{2,1,0:T(8,128)(2,1)} %convert_element_type.70), calls=%async_computation.3 | async-start | bytes 1310720 | tf_op jit(solution)/shard_map/all_to_all | solution.py:287
  152.9 13.8 %shard_map.124 = f32[8,64,640]{2,1,0:T(8,128)S(1)} custom-call(s32[8]{0:T(128)S(1)} %gather_fusion, f32[8,64,640]{2,1,0:T(8,128)S(1)} %convert_element_type.64.mass, f32[8,64,640]{2,1,0:T(8,128)S(1)} %convert_element_type.68.cot, f32[8,64,640]{2,1,0:T(8,128)S(1)} %get-tuple-element.75.thirds, f32[8,64,512]{2,1,0:T(8,128)S(1)} %copy-done.50, ...), custom_call_target="tpu_custom_call" | custom-call | flops 12884901888 | bytes 16777216 | tf_op jit(solution)/shard_map/pallas_call | solution.py:234
  167.6 5.4 %all-to-all-start.2 = ((f16[8,64,640]{2,1,0:T(8,128)(2,1)}), f16[8,64,640]{2,1,0:T(8,128)(2,1)S(1)}, u32[]{:S(2)}, u32[]{:S(2)}) async-start(f16[8,64,640]{2,1,0:T(8,128)(2,1)} %convert_element_type.69), calls=%async_computation.2 | async-start | bytes 1310720 | tf_op jit(solution)/shard_map/all_to_all | solution.py:287
  179.2 2.9 %fusion.13 = (f32[512,512]{1,0:T(8,128)S(1)}, f32[512,512]{1,0:T(8,128)}) fusion(f32[512,512]{1,0:T(8,128)S(1)} %copy-done.59, f32[512,512]{1,0:T(8,128)} %param.9, f32[512,512]{0,1:T(8,128)} %copy.36), kind=kLoop, calls=%fused_computation.46 | loop fusion | flops 524288 | bytes 5242880 | tf_op jit(solution)/shard_map/div | solution.py:378
  183.0 5.7 %all-to-all-done.2 = f16[8,64,640]{2,1,0:T(8,128)(2,1)S(1)} async-done(((f16[8,64,640]{2,1,0:T(8,128)(2,1)}), f16[8,64,640]{2,1,0:T(8,128)(2,1)S(1)}, u32[]{:S(2)}, u32[]{:S(2)}) %all-to-all-start.2) | async-done | bytes 655392 | tf_op jit(solution)/shard_map/all_to_all | solution.py:287
  191.7 2.7 %collective-permute-start.33 = (f16[64,512]{1,0:T(8,128)(2,1)S(1)}, f16[64,512]{1,0:T(8,128)(2,1)S(1)}, u32[]{:S(2)}, u32[]{:S(2)}) collective-permute-start(f16[64,512]{1,0:T(8,128)(2,1)S(1)} %slice_convert_fusion), channel_id=1, source_target_pairs={{0,1},{1,0},{2,3},{3,2},{4,5},{5,4},{6,7},{7,6},{8,9},{9,8},{10,11... | collective-permute-start | bytes 196616 | tf_op jit(solution)/shard_map/ppermute | solution.py:259
  (234 shorter events, 83.4 us)
Async XLA Ops:
  18.6 47.0 %all-to-all-start = ((f16[8,64,640]{2,1,0:T(8,128)(2,1)}), f16[8,64,640]{2,1,0:T(8,128)(2,1)}, u32[]{:S(2)}, u32[]{:S(2)}) async-start(f16[8,64,640]{2,1,0:T(8,128)(2,1)} %pad_maximum_fusion), calls=%async_computation | async-start | bytes 1310720 | tf_op jit(solution)/shard_map/all_to_all | solution.py:287
  24.5 16.4 %collective-permute-start.12 = (bf16[256,512]{1,0:T(8,128)(2,1)S(1)}, bf16[256,512]{1,0:T(8,128)(2,1)S(1)}, u32[]{:S(2)}, u32[]{:S(2)}) collective-permute-start(bf16[256,512]{1,0:T(8,128)(2,1)S(1)} %bitcast.60), channel_id=1, source_target_pairs={{0,2},{4,0},{8,4},{12,8},{14,12},{10,14},{6,10},{2,6},{1,3},{5,1},... | collective-permute-start | bytes 786440 | tf_op jit(solution)/shard_map/ppermute | solution.py:284
  26.0 14.9 %collective-permute-start.13 = (bf16[256,512]{1,0:T(8,128)(2,1)S(1)}, bf16[256,512]{1,0:T(8,128)(2,1)S(1)}, u32[]{:S(2)}, u32[]{:S(2)}) collective-permute-start(bf16[256,512]{1,0:T(8,128)(2,1)S(1)} %bitcast.61), channel_id=1, source_target_pairs={{0,4},{4,8},{8,12},{12,14},{14,10},{10,6},{6,2},{2,0},{1,5},{5,9},... | collective-permute-start | bytes 786440 | tf_op jit(solution)/shard_map/ppermute | solution.py:284
  26.1 14.8 %collective-permute-start.14 = (bf16[256,512]{1,0:T(8,128)(2,1)S(1)}, bf16[256,512]{1,0:T(8,128)(2,1)S(1)}, u32[]{:S(2)}, u32[]{:S(2)}) collective-permute-start(bf16[256,512]{1,0:T(8,128)(2,1)S(1)} %bitcast.62), channel_id=1, source_target_pairs={{0,1},{1,0},{2,3},{3,2},{4,5},{5,4},{6,7},{7,6},{8,9},{9,8},{10,11... | collective-permute-start | bytes 786440 | tf_op jit(solution)/shard_map/ppermute | solution.py:259
  27.3 22.4 %collective-permute-start.1 = (bf16[256,512]{1,0:T(8,128)(2,1)S(1)}, bf16[256,512]{1,0:T(8,128)(2,1)S(1)}, u32[]{:S(2)}, u32[]{:S(2)}) collective-permute-start(bf16[256,512]{1,0:T(8,128)(2,1)S(1)} %bitcast.56), channel_id=1, source_target_pairs={{0,4},{4,8},{8,12},{12,14},{14,10},{10,6},{6,2},{2,0},{1,5},{5,9},... | collective-permute-start | bytes 786440 | tf_op jit(solution)/shard_map/ppermute | solution.py:284
  29.0 20.8 %collective-permute-start.2 = (bf16[256,512]{1,0:T(8,128)(2,1)S(1)}, bf16[256,512]{1,0:T(8,128)(2,1)S(1)}, u32[]{:S(2)}, u32[]{:S(2)}) collective-permute-start(bf16[256,512]{1,0:T(8,128)(2,1)S(1)} %bitcast.57), channel_id=1, source_target_pairs={{0,1},{1,0},{2,3},{3,2},{4,5},{5,4},{6,7},{7,6},{8,9},{9,8},{10,11... | collective-permute-start | bytes 786440 | tf_op jit(solution)/shard_map/ppermute | solution.py:259
  41.7 11.3 %collective-permute-start.15 = (bf16[256,512]{1,0:T(8,128)(2,1)S(1)}, bf16[256,512]{1,0:T(8,128)(2,1)S(1)}, u32[]{:S(2)}, u32[]{:S(2)}) collective-permute-start(bf16[256,512]{1,0:T(8,128)(2,1)S(1)} %collective-permute-done.12.refs_6_.refs_11_), channel_id=1, source_target_pairs={{0,2},{4,0},{8,4},{12,8},{14,12},{10,14},{6,10},{2,6},{1,3},{5,1},... | collective-permute-start | bytes 786440 | tf_op jit(solution)/shard_map/ppermute | solution.py:284
  43.9 10.3 %collective-permute-start.16 = (bf16[256,512]{1,0:T(8,128)(2,1)S(1)}, bf16[256,512]{1,0:T(8,128)(2,1)S(1)}, u32[]{:S(2)}, u32[]{:S(2)}) collective-permute-start(bf16[256,512]{1,0:T(8,128)(2,1)S(1)} %collective-permute-done.13.refs_30_.refs_35_), channel_id=1, source_target_pairs={{0,4},{4,8},{8,12},{12,14},{14,10},{10,6},{6,2},{2,0},{1,5},{5,9},... | collective-permute-start | bytes 786440 | tf_op jit(solution)/shard_map/ppermute | solution.py:284
  53.0 10.8 %collective-permute-start.4 = (bf16[256,512]{1,0:T(8,128)(2,1)S(1)}, bf16[256,512]{1,0:T(8,128)(2,1)}, u32[]{:S(2)}, u32[]{:S(2)}) collective-permute-start(bf16[256,512]{1,0:T(8,128)(2,1)S(1)} %collective-permute-done.1.refs_28_.refs_33_), channel_id=1, source_target_pairs={{0,4},{4,8},{8,12},{12,14},{14,10},{10,6},{6,2},{2,0},{1,5},{5,9},... | collective-permute-start | bytes 786440 | tf_op jit(solution)/shard_map/ppermute | solution.py:284
  54.2 12.7 %collective-permute-start.5 = (bf16[256,512]{1,0:T(8,128)(2,1)S(1)}, bf16[256,512]{1,0:T(8,128)(2,1)}, u32[]{:S(2)}, u32[]{:S(2)}) collective-permute-start(bf16[256,512]{1,0:T(8,128)(2,1)S(1)} %collective-permute-done.refs_4_.refs_9_), channel_id=1, source_target_pairs={{0,1},{1,0},{2,3},{3,2},{4,5},{5,4},{6,7},{7,6},{8,9},{9,8},{10,11... | collective-permute-start | bytes 786440 | tf_op jit(solution)/shard_map/ppermute | solution.py:259
  57.7 11.1 %collective-permute-start.6 = (bf16[256,512]{1,0:T(8,128)(2,1)S(1)}, bf16[256,512]{1,0:T(8,128)(2,1)}, u32[]{:S(2)}, u32[]{:S(2)}) collective-permute-start(bf16[256,512]{1,0:T(8,128)(2,1)S(1)} %collective-permute-done.1.refs_28_.refs_33_), channel_id=1, source_target_pairs={{0,1},{1,0},{2,3},{3,2},{4,5},{5,4},{6,7},{7,6},{8,9},{9,8},{10,11... | collective-permute-start | bytes 786440 | tf_op jit(solution)/shard_map/ppermute | solution.py:259
  57.7 11.8 %collective-permute-start.19 = (bf16[256,512]{1,0:T(8,128)(2,1)S(1)}, bf16[256,512]{1,0:T(8,128)(2,1)}, u32[]{:S(2)}, u32[]{:S(2)}) collective-permute-start(bf16[256,512]{1,0:T(8,128)(2,1)S(1)} %collective-permute-done.16.refs_26_.refs_31_), channel_id=1, source_target_pairs={{0,4},{4,8},{8,12},{12,14},{14,10},{10,6},{6,2},{2,0},{1,5},{5,9},... | collective-permute-start | bytes 786440 | tf_op jit(solution)/shard_map/ppermute | solution.py:284
  60.0 10.1 %collective-permute-start.20 = (bf16[256,512]{1,0:T(8,128)(2,1)S(1)}, bf16[256,512]{1,0:T(8,128)(2,1)}, u32[]{:S(2)}, u32[]{:S(2)}) collective-permute-start(bf16[256,512]{1,0:T(8,128)(2,1)S(1)} %collective-permute-done.15.refs_10_.refs_15_), channel_id=1, source_target_pairs={{0,1},{1,0},{2,3},{3,2},{4,5},{5,4},{6,7},{7,6},{8,9},{9,8},{10,11... | collective-permute-start | bytes 786440 | tf_op jit(solution)/shard_map/ppermute | solution.py:259
  67.0 12.4 %collective-permute-start.23 = (bf16[256,512]{1,0:T(8,128)(2,1)S(1)}, bf16[256,512]{1,0:T(8,128)(2,1)S(1)}, u32[]{:S(2)}, u32[]{:S(2)}) collective-permute-start(bf16[256,512]{1,0:T(8,128)(2,1)S(1)} %collective-permute-done.15.refs_10_.refs_15_), channel_id=1, source_target_pairs={{0,2},{4,0},{8,4},{12,8},{14,12},{10,14},{6,10},{2,6},{1,3},{5,1},... | collective-permute-start | bytes 786440 | tf_op jit(solution)/shard_map/ppermute | solution.py:284
  68.8 11.0 %collective-permute-start.9 = (bf16[256,512]{1,0:T(8,128)(2,1)}, bf16[256,512]{1,0:T(8,128)(2,1)S(1)}, u32[]{:S(2)}, u32[]{:S(2)}) collective-permute-start(bf16[256,512]{1,0:T(8,128)(2,1)} %collective-permute-done.3.refs_8_.refs_13_), channel_id=1, source_target_pairs={{0,1},{1,0},{2,3},{3,2},{4,5},{5,4},{6,7},{7,6},{8,9},{9,8},{10,11... | collective-permute-start | bytes 786440 | tf_op jit(solution)/shard_map/ppermute | solution.py:259
  69.5 10.4 %collective-permute-start.10 = (bf16[256,512]{1,0:T(8,128)(2,1)}, bf16[256,512]{1,0:T(8,128)(2,1)S(1)}, u32[]{:S(2)}, u32[]{:S(2)}) collective-permute-start(bf16[256,512]{1,0:T(8,128)(2,1)} %collective-permute-done.4.refs_24_.refs_29_), channel_id=1, source_target_pairs={{0,1},{1,0},{2,3},{3,2},{4,5},{5,4},{6,7},{7,6},{8,9},{9,8},{10,11... | collective-permute-start | bytes 786440 | tf_op jit(solution)/shard_map/ppermute | solution.py:259
  70.1 10.5 %collective-permute-start.8 = (bf16[256,512]{1,0:T(8,128)(2,1)}, bf16[256,512]{1,0:T(8,128)(2,1)}, u32[]{:S(2)}, u32[]{:S(2)}) collective-permute-start(bf16[256,512]{1,0:T(8,128)(2,1)} %collective-permute-done.3.refs_8_.refs_13_), channel_id=1, source_target_pairs={{0,2},{4,0},{8,4},{12,8},{14,12},{10,14},{6,10},{2,6},{1,3},{5,1},... | collective-permute-start | bytes 786440 | tf_op jit(solution)/shard_map/ppermute | solution.py:284
  79.8 13.0 %collective-permute-start.29 = (bf16[256,512]{1,0:T(8,128)(2,1)}, bf16[256,512]{1,0:T(8,128)(2,1)}, u32[]{:S(2)}, u32[]{:S(2)}) collective-permute-start(bf16[256,512]{1,0:T(8,128)(2,1)} %collective-permute-done.4.refs_24_.refs_29_), channel_id=1, source_target_pairs={{0,4},{4,8},{8,12},{12,14},{14,10},{10,6},{6,2},{2,0},{1,5},{5,9},... | collective-permute-start | bytes 786440 | tf_op jit(solution)/shard_map/ppermute | solution.py:284
  80.7 13.4 %collective-permute-start.25 = (bf16[256,512]{1,0:T(8,128)(2,1)}, bf16[256,512]{1,0:T(8,128)(2,1)}, u32[]{:S(2)}, u32[]{:S(2)}) collective-permute-start(bf16[256,512]{1,0:T(8,128)(2,1)} %collective-permute-done.8.refs_12_.refs_17_), channel_id=1, source_target_pairs={{0,2},{4,0},{8,4},{12,8},{14,12},{10,14},{6,10},{2,6},{1,3},{5,1},... | collective-permute-start | bytes 786440 | tf_op jit(solution)/shard_map/ppermute | solution.py:284
  82.1 16.4 %collective-permute-start.31 = (bf16[256,512]{1,0:T(8,128)(2,1)}, bf16[256,512]{1,0:T(8,128)(2,1)}, u32[]{:S(2)}, u32[]{:S(2)}) collective-permute-start(bf16[256,512]{1,0:T(8,128)(2,1)} %collective-permute-done.19.refs_22_.refs_27_), channel_id=1, source_target_pairs={{0,1},{1,0},{2,3},{3,2},{4,5},{5,4},{6,7},{7,6},{8,9},{9,8},{10,11... | collective-permute-start | bytes 786440 | tf_op jit(solution)/shard_map/ppermute | solution.py:259
  87.3 11.2 %collective-permute-start.28 = (bf16[256,512]{1,0:T(8,128)(2,1)S(1)}, bf16[256,512]{1,0:T(8,128)(2,1)}, u32[]{:S(2)}, u32[]{:S(2)}) collective-permute-start(bf16[256,512]{1,0:T(8,128)(2,1)S(1)} %collective-permute-done.27.refs_18_.refs_23_), channel_id=1, source_target_pairs={{0,1},{1,0},{2,3},{3,2},{4,5},{5,4},{6,7},{7,6},{8,9},{9,8},{10,11... | collective-permute-start | bytes 786440 | tf_op jit(solution)/shard_map/ppermute | solution.py:259
  94.1 39.4 %all-to-all-start.1 = ((f16[8,64,640]{2,1,0:T(8,128)(2,1)}), f16[8,64,640]{2,1,0:T(8,128)(2,1)}, u32[]{:S(2)}, u32[]{:S(2)}) async-start(f16[8,64,640]{2,1,0:T(8,128)(2,1)} %pad_maximum_fusion.1), calls=%async_computation.1 | async-start | bytes 1310720 | tf_op jit(solution)/shard_map/all_to_all | solution.py:287
  133.5 34.1 %all-to-all-start.3 = ((f16[8,64,640]{2,1,0:T(8,128)(2,1)}), f16[8,64,640]{2,1,0:T(8,128)(2,1)}, u32[]{:S(2)}, u32[]{:S(2)}) async-start(f16[8,64,640]{2,1,0:T(8,128)(2,1)} %convert_element_type.70), calls=%async_computation.3 | async-start | bytes 1310720 | tf_op jit(solution)/shard_map/all_to_all | solution.py:287
  167.6 21.1 %all-to-all-start.2 = ((f16[8,64,640]{2,1,0:T(8,128)(2,1)}), f16[8,64,640]{2,1,0:T(8,128)(2,1)S(1)}, u32[]{:S(2)}, u32[]{:S(2)}) async-start(f16[8,64,640]{2,1,0:T(8,128)(2,1)} %convert_element_type.69), calls=%async_computation.2 | async-start | bytes 1310720 | tf_op jit(solution)/shard_map/all_to_all | solution.py:287
  (80 other events, 539.0 us)

commit v7 on v6

v7 whole, which is shorter than its diff:
```python
import copy
import functools

import jax
import jax.numpy as jnp
import numpy as np
from jax import lax
from jax.experimental import pallas as pl
from jax.experimental.pallas import tpu as pltpu
from jax.sharding import PartitionSpec as P

CB_DEV = 2
HALF = jnp.float16
COT_SCALE = 256.0
VMEM = 56 * 1024 * 1024


def ring_order(count):
    if count == 8:
        return [0, 2, 4, 6, 7, 5, 3, 1]
    return list(range(count))


def dense_blocks(kernel_tiles, tile_cols, tile_count):
    keep = kernel_tiles.shape[1]
    live = jnp.arange(keep, dtype=jnp.int32)[None, :] < tile_count
    hits = (tile_cols[:, :, None] == jnp.arange(CB_DEV, dtype=jnp.int32)) & live[:, :, None]
    blocks = jnp.einsum(
        "rkc,rkab->racb",
        hits.astype(jnp.bfloat16),
        kernel_tiles,
        preferred_element_type=jnp.float32,
    )
    rows, cols = blocks.shape[0] * blocks.shape[1], blocks.shape[2] * blocks.shape[3]
    return blocks.astype(jnp.bfloat16).reshape(rows, cols)


def nt(x, y):
    return lax.dot_general(x, y, (((1,), (1,)), ((), ())), preferred_element_type=jnp.float32)


def nn(x, y):
    return jnp.dot(x, y, preferred_element_type=jnp.float32)


class Shape:
    def only(self, units):
        kept = copy.copy(self)
        kept.units = units
        return kept

    def __init__(self, count, rows, cols, hists, share):
        self.count = count
        self.rows = rows
        self.cols = cols
        self.hists = hists
        self.share = share
        self.lanes = rows + 2 * share
        self.opposite = count // 2
        self.units = []
        for d in range(count):
            if d == self.opposite:
                self.units += [(d, 0, rows // 2), (d, rows // 2, rows // 2)]
            else:
                self.units.append((d, 0, rows))


def load_matrix(s, units, matrix, sems):
    copies = {}
    units = iter(units)
    for d, start, size in s.units:
        for t in range(2):
            copy = pltpu.make_async_copy(
                next(units),
                matrix.at[d, pl.ds(start, size), pl.ds(t * s.cols, s.cols)],
                sems.at[d],
            )
            copy.start()
            copies.setdefault(d, []).append(copy)

    def arrived(d):
        for piece in copies.pop(d, []):
            piece.wait()

    if s.count > 8:
        for d in range(s.count):
            arrived(d)
        return lambda d: None
    return arrived


def load(sources, targets, sems):
    copies = [
        pltpu.make_async_copy(source, target, sems.at[k])
        for k, (source, target) in enumerate(zip(sources, targets))
    ]
    for copy in copies:
        copy.start()
    return copies


def gather_targets(s, pieces):
    return jnp.concatenate(
        [
            pieces[i, :, s.rows + t * s.share : s.rows + (t + 1) * s.share]
            for t in range(2)
            for i in range(s.count)
        ],
        axis=1,
    )


def scatter_targets(s, out, values):
    for i in range(s.count):
        out[i, :, s.rows : s.lanes] = jnp.concatenate(
            [
                values[:, t * s.cols + i * s.share : t * s.cols + (i + 1) * s.share]
                for t in range(2)
            ],
            axis=1,
        )


def each(count, body, init):
    if count <= 8:
        for d in range(count):
            init = body(d, init)
        return init
    return lax.fori_loop(0, count, body, init)


def first_step(s, table, mass, matrix, row_one, d):
    sums = nt(jnp.ones((8, 2 * s.cols), jnp.bfloat16), matrix[d])
    row_one[d] = sums
    left = mass[table[d], :, : s.rows] / sums[0:1]
    return nn(left.astype(jnp.bfloat16), matrix[d])


def first_kernel(s, table, mass_in, *refs):
    units, (row_one, col_one, mass, matrix, sems, more_sems) = refs[:-6], refs[-6:]
    arriving = load([mass_in], [mass], more_sems)
    own = [unit for unit in s.units if unit[0] != s.opposite]
    arrived = load_matrix(s.only(own), units, matrix, sems)
    arriving[0].wait()

    def step(k, total):
        d = k + (k >= s.opposite)
        arrived(d)
        return total + first_step(s, table, mass, matrix, row_one, d)

    zero = jnp.zeros((s.hists, 2 * s.cols), jnp.float32)
    col_one[...] = each(s.count - 1, step, zero)


def forward_kernel(s, table, mass_in, row_one_in, col_one_in, *refs):
    units, refs = refs[: 2 * len(s.units)], refs[2 * len(s.units) :]
    thirds, leaving, (mass, matrix, sems, more_sems), state = refs[0], refs[1:6], refs[6:10], refs[10:]
    row_two, row_one, col_one, col_two, col_three = state
    arriving = load(
        [mass_in, row_one_in, col_one_in], [mass, row_one, col_one], more_sems
    )
    arrived = load_matrix(s, units, matrix, sems)
    for copy in arriving:
        copy.wait()
    target = gather_targets(s, mass)
    arrived(s.opposite)
    total = col_one[...] + first_step(s, table, mass, matrix, row_one, s.opposite)
    col_one[...] = total
    panel = (target / total).astype(jnp.bfloat16)
    zero = jnp.zeros((s.hists, 2 * s.cols), jnp.float32)

    def second(d, total):
        arrived(d)
        row = nt(panel, matrix[d])
        row_two[d] = row
        left = mass[table[d], :, : s.rows] / row
        return total + nn(left.astype(jnp.bfloat16), matrix[d])

    total = each(s.count, second, zero)
    col_two[...] = total
    started = load(state[:4], leaving[:4], more_sems)
    panel = (target / total).astype(jnp.bfloat16)

    def third(d, total):
        row = nt(panel, matrix[d])
        thirds[table[d], :, : s.rows] = row
        left = mass[table[d], :, : s.rows] / row
        return total + nn(left.astype(jnp.bfloat16), matrix[d])

    total = each(s.count, third, zero)
    col_three[...] = total
    last = pltpu.make_async_copy(col_three, leaving[4], more_sems.at[4])
    last.start()
    scatter_targets(s, thirds, total)
    for copy in [*started, last]:
        copy.wait()


def backward_kernel(s, table, mass_in, cot_in, thirds_in, *refs):
    state_in, units, refs = refs[:5], refs[5 : 5 + 2 * len(s.units)], refs[5 + 2 * len(s.units) :]
    out, (mass, matrix, sems, more_sems), state, (cot, thirds) = (
        refs[0],
        refs[1:5],
        refs[5:10],
        refs[10:],
    )
    row_two, row_one, col_one, col_two, col_three = state
    sources = [state_in[4], cot_in, thirds_in, mass_in]
    early = load(sources, [col_three, cot, thirds, mass], more_sems)
    arrived = load_matrix(s, units, matrix, sems)
    late = [
        pltpu.make_async_copy(state_in[k], state[k], more_sems.at[4 + k]) for k in range(4)
    ]
    for copy in late:
        copy.start()
    for copy in early:
        copy.wait()
    target = gather_targets(s, mass)
    target_cot = gather_targets(s, cot)
    panel = (-target_cot / col_three[...]).astype(jnp.bfloat16)
    zero = jnp.zeros((s.hists, 2 * s.cols), jnp.float32)

    def third(d, total):
        arrived(d)
        k = table[d]
        grad = nt(panel, matrix[d])
        row = thirds[k, :, : s.rows]
        left = mass[k, :, : s.rows] / row
        term = grad / row
        out[k, :, : s.rows] = term
        rowgrad = -(cot[k, :, : s.rows] / row + term * left)
        return total + nn(rowgrad.astype(jnp.bfloat16), matrix[d])

    total = each(s.count, third, zero)
    for copy in late:
        copy.wait()
    term_two = total / col_two[...]
    panel = (-term_two * (target / col_two[...])).astype(jnp.bfloat16)

    def second(d, total):
        k = table[d]
        row = row_two[d]
        term = nt(panel, matrix[d]) / row
        out[k, :, : s.rows] += term
        rowgrad = -term * (mass[k, :, : s.rows] / row)
        return total + nn(rowgrad.astype(jnp.bfloat16), matrix[d])

    term_one = each(s.count, second, zero) / col_one[...]
    panel = (-term_one * (target / col_one[...])).astype(jnp.bfloat16)

    def first(d, carry):
        out[table[d], :, : s.rows] += nt(panel, matrix[d]) / row_one[d, 0:1]
        return carry

    each(s.count, first, 0)
    scatter_targets(s, out, term_two + term_one)


def call(kernel, s, products, vmem_outs, hbm_outs, table, arrays, scratch):
    return pl.pallas_call(
        functools.partial(kernel, s),
        out_shape=[*vmem_outs, *hbm_outs],
        in_specs=[pl.BlockSpec(memory_space=pltpu.SMEM)]
        + [pl.BlockSpec(memory_space=pl.ANY)] * len(arrays),
        out_specs=[pl.BlockSpec(memory_space=pltpu.VMEM)] * len(vmem_outs)
        + [pl.BlockSpec(memory_space=pl.ANY)] * len(hbm_outs),
        scratch_shapes=[
            pltpu.VMEM((s.count, s.hists, s.lanes), jnp.float32),
            pltpu.VMEM((s.count, s.rows, 2 * s.cols), jnp.bfloat16),
            pltpu.SemaphoreType.DMA((s.count,)),
            pltpu.SemaphoreType.DMA((8,)),
            *[pltpu.VMEM(state.shape, state.dtype) for state in scratch],
        ],
        cost_estimate=pl.CostEstimate(
            flops=products * 2 * s.count * s.rows * 2 * s.cols * 256,
            bytes_accessed=s.count * s.rows * 2 * s.cols * 4,
            transcendentals=0,
        ),
        compiler_params=pltpu.CompilerParams(vmem_limit_bytes=VMEM),
    )(table, *arrays)


def swap_cores(x):
    return lax.ppermute(x, "tgt", [(0, 1), (1, 0)])


def local(
    source_mass,
    target_mass,
    kernel_tiles,
    tile_cols,
    tile_count,
    source_cotangent,
    target_cotangent,
):
    count = lax.axis_size("src")
    rows, cols_here = source_mass.shape
    share = target_mass.shape[1]
    s = Shape(count, rows, CB_DEV * kernel_tiles.shape[2], cols_here // count, share)
    ring = np.array(ring_order(count), np.int32)
    place = np.argsort(ring).astype(np.int32)
    me = lax.axis_index("src")
    core = lax.axis_index("tgt")
    at = jnp.asarray(place)[me]
    table = jnp.asarray(ring)[(at + jnp.arange(count, dtype=jnp.int32)) % count]

    def shift(x, distance):
        pairs = [(int(ring[p]), int(ring[(p + distance) % count])) for p in range(count)]
        return lax.ppermute(x, "src", pairs)

    def exchange(x):
        return lax.all_to_all(x, "src", 0, 0, tiled=True)

    def by_histogram(source, target):
        target = target.astype(HALF).reshape(share, 2, cols_here)
        mine = lax.dynamic_index_in_dim(target, core, 1, keepdims=False)
        other = lax.dynamic_index_in_dim(target, 1 - core, 1, keepdims=False)
        both = jnp.concatenate([mine, swap_cores(other)]).T
        return jnp.concatenate(
            [
                source.astype(HALF).T.reshape(count, s.hists, rows),
                both.reshape(count, s.hists, 2 * share),
            ],
            axis=2,
        )

    unit = dense_blocks(kernel_tiles, tile_cols, tile_count)

    pieces, before = {(0, 0): unit}, {0: [(0, 0)]}
    swapped = {(0, 0): swap_cores(unit)}
    ahead = behind = unit
    last = count // 2
    swapped[0, 0], mass_here, points_here = lax.optimization_barrier(
        (swapped[0, 0], source_mass, target_mass)
    )
    mass_message = by_histogram(mass_here, points_here[0])
    for step in range(1, last + 1):
        due = before.get(step - 2, [])
        ready = [swapped[key] for key in due]
        if step == 2:
            mass = exchange(mass_message).astype(jnp.float32)
            ahead, behind, ready, mass, table = lax.optimization_barrier(
                (ahead, behind, ready, mass, table)
            )
        elif step == last:
            ahead, behind, ready, cot_message = lax.optimization_barrier(
                (ahead, behind, ready, cot_message)
            )
        else:
            ahead, behind, ready = lax.optimization_barrier((ahead, behind, ready))
        swapped.update(zip(due, ready))
        if 2 * step == count:
            middle = rows // 2
            new = {
                (step, 0): shift(ahead[:middle], -1),
                (step, middle): shift(behind[middle:], 1),
            }
        else:
            ahead, behind = shift(ahead, -1), shift(behind, 1)
            new = {(step, 0): ahead, (count - step, 0): behind}
        pieces.update(new)
        swapped.update({key: swap_cores(piece) for key, piece in new.items()})
        before[step] = list(new)
        if step == max(last - 2, 1):
            head, cot_here, points_here = lax.optimization_barrier(
                (ahead, source_cotangent, target_cotangent)
            )
            ahead = pieces[step, 0] = head
            cot_message = by_histogram(cot_here * COT_SCALE, points_here[0] * COT_SCALE)
    units = []
    near = []
    for d, start, _ in s.units:
        units += [pieces[d, start], swapped[d, start]]
        near += [] if d == s.opposite else units[-2:]

    wide = jax.ShapeDtypeStruct((count, s.hists, s.lanes), jnp.float32)
    panel = jax.ShapeDtypeStruct((count, s.hists, rows), jnp.float32)
    sums = jax.ShapeDtypeStruct((count, 8, rows), jnp.float32)
    column = jax.ShapeDtypeStruct((s.hists, 2 * s.cols), jnp.float32)
    states = [panel, sums, column, column, column]
    row_one, col_one = call(first_kernel, s, 2, [sums, column], [], table, [mass, *near], [])
    cot = exchange(cot_message).astype(jnp.float32)
    thirds, *state = call(
        forward_kernel, s, 5, [wide], states, table, [mass, row_one, col_one, *units], states
    )
    (grads,) = call(
        backward_kernel,
        s,
        5,
        [wide],
        [],
        table,
        [mass, cot, thirds, *state, *units],
        [*states, wide, wide],
    )

    def by_point(pieces):
        flat = pieces.reshape(cols_here, s.lanes).astype(jnp.float32)
        target = flat[:, rows:].T.reshape(2, share, cols_here)
        other = swap_cores(target[1].astype(HALF)).astype(jnp.float32)
        own = target[0]
        halves = [jnp.where(core == t, own, other) for t in range(2)]
        return flat[:, :rows].T, jnp.concatenate(halves, axis=1)

    row_three, col_three = by_point(exchange(thirds.astype(HALF)))
    source_potential = jnp.log(source_mass / row_three)
    target_potential = jnp.log(target_mass[0] / col_three)
    source_known = source_cotangent / source_mass
    target_known = target_cotangent[0] / target_mass[0]
    back, source_potential, target_potential, source_known, target_known = lax.optimization_barrier(
        (
            exchange(grads.astype(HALF)),
            source_potential,
            target_potential,
            source_known,
            target_known,
        )
    )
    source_term, target_term = by_point(back)
    return (
        source_potential,
        target_potential[None],
        source_known + source_term * (1 / COT_SCALE),
        (target_known + target_term * (1 / COT_SCALE))[None],
    )


def solution(mesh):
    return jax.shard_map(
        local,
        mesh=mesh,
        in_specs=(
            P(("grp", "src"), "tgt"),
            P("tgt", ("grp", "src"), None),
            P(("grp", "src"), "tgt", None, None),
            P(("grp", "src"), "tgt"),
            P(("grp", "src"), "tgt"),
            P(("grp", "src"), "tgt"),
            P("tgt", ("grp", "src"), None),
        ),
        out_specs=(
            P(("grp", "src"), "tgt"),
            P("tgt", ("grp", "src"), None),
            P(("grp", "src"), "tgt"),
            P("tgt", ("grp", "src"), None),
        ),
        check_vma=False,
    )
```

time: 198 us -> 171 us (0.86)
  local copies, waits for them, and re-layouts: 49.1 us -> 12.6 us
  starting transfers between devices: 62.4 us -> 41 us
  waiting for transfers between devices: 33.6 us -> 53.4 us
  Pallas kernels: 29.4 us -> 44.1 us
  other arithmetic: 19.1 us -> 17 us
    unnamed x138 -> x35, local copies, waits for them, and re-layouts: 37.8 us -> 5.23 us
    all_to_all x4, waiting for transfers between devices: 5.71 us -> 21.2 us  [exchange(): return lax.all_to_all(x, 'src', 0, 0, tiled=True)]
    pallas_call x2 -> x3, Pallas kernels: 29.4 us -> 44.1 us  [call(): pl.pallas_call(functools.partial(kernel, s), out_shape=[*vmem_outs, *hbm_...]
    ppermute x14 -> x8, starting transfers between devices: 21.6 us -> 9.15 us  [shift(): return lax.ppermute(x, 'src', pairs)]
    ppermute x20 -> x13, starting transfers between devices: 20 us -> 12.5 us  [swap_cores(): return lax.ppermute(x, 'tgt', [(0, 1), (1, 0)])]
    ppermute x14 -> x8, waiting for transfers between devices: 27.3 us -> 29.7 us  [shift(): return lax.ppermute(x, 'src', pairs)]
    dynamic_slice x2, local copies, waits for them, and re-layouts: 2.52 us -> 0.38 us  [by_histogram(): other = lax.dynamic_index_in_dim(target, 1 - core, 1, keepdims=False)]
  transfers between devices with their start and end apart: 38 -> 25, of which waited for: 9 -> 10; matrix products, arithmetic and copies ran while one was open for 13% -> 13% of each run, Pallas kernels for 15% -> 26%
where the time goes in v7:
time: 171 us; the launch traced here: 170 us
  waiting for transfers between devices  53.4 us (31%)
  Pallas kernels  44.1 us (26%)
  starting transfers between devices  41 us (24%)
  other arithmetic  17 us (10%)
  local copies, waits for them, and re-layouts  12.6 us (7%)
    pallas_call x3, Pallas kernels, call(): pl.pallas_call(functools.partial(kernel, s), out_shape=[*vmem_outs, *hbm_...  44.1 us
    ppermute x8, waiting for transfers between devices, shift(): return lax.ppermute(x, 'src', pairs)  29.7 us
    all_to_all x4, waiting for transfers between devices, exchange(): return lax.all_to_all(x, 'src', 0, 0, tiled=True)  21.2 us
    all_to_all x4, starting transfers between devices, exchange(): return lax.all_to_all(x, 'src', 0, 0, tiled=True)  19.3 us
    ppermute x13, starting transfers between devices, swap_cores(): return lax.ppermute(x, 'tgt', [(0, 1), (1, 0)])  12.5 us
    ppermute x8, starting transfers between devices, shift(): return lax.ppermute(x, 'src', pairs)  9.15 us
    unnamed x35, local copies, waits for them, and re-layouts  5.23 us
  transfers between devices with their start and end apart: 25, of which 10 were waited for; matrix products, arithmetic and copies ran while one was open for 13% of the time, Pallas kernels for 26%

profile of v7, /device:TPU:1, one launch (start us, length us, event | category | flops | bytes accessed | tf_op | source)
XLA Modules:
  0.0 170.5 jit_solution(13334388386868126307)
XLA Ops:
  3.4 2.0 %collective-permute-done.2.refs_1_.refs_6_ = bf16[512,512]{1,0:T(8,128)(2,1)} collective-permute-done((bf16[512,512]{1,0:T(8,128)(2,1)S(1)}, bf16[512,512]{1,0:T(8,128)(2,1)}, u32[]{:S(2)}, u32[]{:S(2)}) %collective-permute-start.2) | collective-permute-done | bytes 524320 | tf_op jit(solution)/shard_map/ppermute | solution.py:284
  8.6 6.7 %all-to-all-start = ((f16[8,64,640]{2,1,0:T(8,128)(2,1)}), f16[8,64,640]{2,1,0:T(8,128)(2,1)S(1)}, u32[]{:S(2)}, u32[]{:S(2)}) async-start(f16[8,64,640]{2,1,0:T(8,128)(2,1)} %pad_maximum_fusion), calls=%async_computation | async-start | bytes 1310720 | tf_op jit(solution)/shard_map/all_to_all | solution.py:312
  19.3 12.5 %all-to-all-done = f16[8,64,640]{2,1,0:T(8,128)(2,1)S(1)} async-done(((f16[8,64,640]{2,1,0:T(8,128)(2,1)}), f16[8,64,640]{2,1,0:T(8,128)(2,1)S(1)}, u32[]{:S(2)}, u32[]{:S(2)}) %all-to-all-start) | async-done | bytes 655392 | tf_op jit(solution)/shard_map/all_to_all | solution.py:312
  33.0 5.9 %collective-permute-done.refs_2_.refs_7_ = bf16[512,512]{1,0:T(8,128)(2,1)} collective-permute-done((bf16[512,512]{1,0:T(8,128)(2,1)S(1)}, bf16[512,512]{1,0:T(8,128)(2,1)}, u32[]{:S(2)}, u32[]{:S(2)}) %collective-permute-start) | collective-permute-done | bytes 524320 | tf_op jit(solution)/shard_map/ppermute | solution.py:309
  40.3 1.7 collective-permute-start.6
  42.0 3.3 %collective-permute-start.5 = (bf16[512,512]{1,0:T(8,128)(2,1)}, bf16[512,512]{1,0:T(8,128)(2,1)}, u32[]{:S(2)}, u32[]{:S(2)}) collective-permute-start(bf16[512,512]{1,0:T(8,128)(2,1)} %collective-permute-done.1.refs_12_.refs_16_.refs_21_), channel_id=1, source_target_pairs={{0,4},{4,8},{8,12},{12,14},{14,10},{10,6},{6,2},{2,0},{1,5},{5,9},... | collective-permute-start | bytes 1572872 | tf_op jit(solution)/shard_map/ppermute | solution.py:309
  45.3 9.5 %collective-permute-done.4.refs_4_.refs_9_ = bf16[512,512]{1,0:T(8,128)(2,1)} collective-permute-done((bf16[512,512]{1,0:T(8,128)(2,1)}, bf16[512,512]{1,0:T(8,128)(2,1)}, u32[]{:S(2)}, u32[]{:S(2)}) %collective-permute-start.4) | collective-permute-done | bytes 524320 | tf_op jit(solution)/shard_map/ppermute | solution.py:309
  54.7 4.1 %collective-permute-done.5.refs_10_.refs_14_.refs_19_ = bf16[512,512]{1,0:T(8,128)(2,1)} collective-permute-done((bf16[512,512]{1,0:T(8,128)(2,1)}, bf16[512,512]{1,0:T(8,128)(2,1)}, u32[]{:S(2)}, u32[]{:S(2)}) %collective-permute-start.5) | collective-permute-done | bytes 524320 | tf_op jit(solution)/shard_map/ppermute | solution.py:309
  60.4 1.7 collective-permute-start.10
  63.2 8.3 %collective-permute-done.8.refs_6_.refs_11_ = bf16[512,512]{1,0:T(8,128)(2,1)S(1)} collective-permute-done((bf16[512,512]{1,0:T(8,128)(2,1)}, bf16[512,512]{1,0:T(8,128)(2,1)S(1)}, u32[]{:S(2)}, u32[]{:S(2)}) %collective-permute-start.8) | collective-permute-done | bytes 524320 | tf_op jit(solution)/shard_map/ppermute | solution.py:309
  71.5 1.9 %collective-permute-start.13 = (bf16[512,512]{1,0:T(8,128)(2,1)S(1)}, bf16[512,512]{1,0:T(8,128)(2,1)}, u32[]{:S(2)}, u32[]{:S(2)}) collective-permute-start(bf16[512,512]{1,0:T(8,128)(2,1)S(1)} %collective-permute-done.8.refs_6_.refs_11_), channel_id=1, source_target_pairs={{0,1},{1,0},{2,3},{3,2},{4,5},{5,4},{6,7},{7,6},{8,9},{9,8},{10,11... | collective-permute-start | bytes 1572872 | tf_op jit(solution)/shard_map/ppermute | solution.py:284
  79.2 3.7 %all-to-all-start.1 = ((f16[8,64,640]{2,1,0:T(8,128)(2,1)}), f16[8,64,640]{2,1,0:T(8,128)(2,1)S(1)}, u32[]{:S(2)}, u32[]{:S(2)}) async-start(f16[8,64,640]{2,1,0:T(8,128)(2,1)} %pad_maximum_fusion.1), calls=%async_computation.1 | async-start | bytes 1310720 | tf_op jit(solution)/shard_map/all_to_all | solution.py:312
  82.9 1.8 %collective-permute-done.15.refs_8_.refs_13_ = bf16[256,512]{1,0:T(8,128)(2,1)} collective-permute-done((bf16[256,512]{1,0:T(8,128)(2,1)S(1)}, bf16[256,512]{1,0:T(8,128)(2,1)}, u32[]{:S(2)}, u32[]{:S(2)}) %collective-permute-start.15) | collective-permute-done | bytes 262176 | tf_op jit(solution)/shard_map/ppermute | solution.py:309
  85.7 2.0 %collective-permute-start.18 = (bf16[256,512]{1,0:T(8,128)(2,1)}, bf16[256,512]{1,0:T(8,128)(2,1)S(1)}, u32[]{:S(2)}, u32[]{:S(2)}) collective-permute-start(bf16[256,512]{1,0:T(8,128)(2,1)} %collective-permute-done.17.refs_10_.refs_15_), channel_id=1, source_target_pairs={{0,1},{1,0},{2,3},{3,2},{4,5},{5,4},{6,7},{7,6},{8,9},{9,8},{10,11... | collective-permute-start | bytes 786440 | tf_op jit(solution)/shard_map/ppermute | solution.py:284
  87.6 9.1 %shard_map.123 = (f32[8,8,512]{2,1,0:T(8,128)}, f32[64,1024]{1,0:T(8,128)}) custom-call(s32[8]{0:T(128)} %gather_fusion, f32[8,64,640]{2,1,0:T(8,128)} %convert_element_type.64.mass_in, bf16[512,512]{1,0:T(8,128)(2,1)} %bitcast.64, bf16[512,512]{1,0:T(8,128)(2,1)} %collective-permute-done.2.refs_1_.refs_6_, ...), custom_call_target="tpu_custom_call" | custom-call | flops 4294967296 | bytes 16777216 | tf_op jit(solution)/shard_map/pallas_call | solution.py:260
  97.5 16.7 %shard_map.124 = (f32[8,64,640]{2,1,0:T(8,128)}, f32[8,64,512]{2,1,0:T(8,128)}, f32[8,8,512]{2,1,0:T(8,128)}, f32[64,1024]{1,0:T(8,128)}, f32[64,1024]{1,0:T(8,128)}, /*index=5*/f32[64,1024]{1,0:T(8,128)}) custom-call(s32[8]{0:T(128)} %gather_fusion, f32[8,64,640]{2,1,0:T(8,128)} %convert_element_type.64.mass_in, f32[8,8,512]{2,1,0:T(8,128)} %get-tuple-element.59.row_one_in, ...), custom_call_target="tpu_custom_call" | custom-call | flops 10737418240 | bytes 16777216 | tf_op jit(solution)/shard_map/pallas_call | solution.py:260
  114.3 2.2 %convert_element_type.70 = f16[8,64,640]{2,1,0:T(8,128)(2,1)} convert(f32[8,64,640]{2,1,0:T(8,128)} %get-tuple-element.63.thirds_in) | non-fusion elementwise | flops 327680 | bytes 1966080 | tf_op jit(solution)/shard_map/convert_element_type | solution.py:405
  116.5 3.8 %all-to-all-start.3 = ((f16[8,64,640]{2,1,0:T(8,128)(2,1)}), f16[8,64,640]{2,1,0:T(8,128)(2,1)S(1)}, u32[]{:S(2)}, u32[]{:S(2)}) async-start(f16[8,64,640]{2,1,0:T(8,128)(2,1)} %convert_element_type.70), calls=%async_computation.3 | async-start | bytes 1310720 | tf_op jit(solution)/shard_map/all_to_all | solution.py:312
  121.5 18.3 %shard_map.125 = f32[8,64,640]{2,1,0:T(8,128)} custom-call(s32[8]{0:T(128)} %gather_fusion, f32[8,64,640]{2,1,0:T(8,128)} %convert_element_type.64.mass_in, f32[8,64,640]{2,1,0:T(8,128)} %convert_element_type.68.cot_in, f32[8,64,640]{2,1,0:T(8,128)} %get-tuple-element.63.thirds_in, f32[8,64,512]{2,1,0:T(8,128)} %get-tuple-element.64.refs_0_, ...), custom_call_target="tpu_custom_call" | custom-call | flops 10737418240 | bytes 16777216 | tf_op jit(solution)/shard_map/pallas_call | solution.py:260
  139.8 2.3 %convert_element_type.69 = f16[8,64,640]{2,1,0:T(8,128)(2,1)} convert(f32[8,64,640]{2,1,0:T(8,128)} %shard_map.125) | non-fusion elementwise | flops 327680 | bytes 1966080 | tf_op jit(solution)/shard_map/convert_element_type | solution.py:412
  142.0 5.1 %all-to-all-start.2 = ((f16[8,64,640]{2,1,0:T(8,128)(2,1)}), f16[8,64,640]{2,1,0:T(8,128)(2,1)S(1)}, u32[]{:S(2)}, u32[]{:S(2)}) async-start(f16[8,64,640]{2,1,0:T(8,128)(2,1)} %convert_element_type.69), calls=%async_computation.2 | async-start | bytes 1310720 | tf_op jit(solution)/shard_map/all_to_all | solution.py:312
  151.3 2.9 %fusion.12 = (f32[512,512]{1,0:T(8,128)S(1)}, f32[512,512]{1,0:T(8,128)}) fusion(f32[512,512]{1,0:T(8,128)S(1)} %copy-done.2, f32[512,512]{1,0:T(8,128)} %param.9, f32[512,512]{0,1:T(8,128)} %copy.36), kind=kLoop, calls=%fused_computation.45 | loop fusion | flops 524288 | bytes 5242880 | tf_op jit(solution)/shard_map/div | solution.py:408
  155.1 8.6 %all-to-all-done.2 = f16[8,64,640]{2,1,0:T(8,128)(2,1)S(1)} async-done(((f16[8,64,640]{2,1,0:T(8,128)(2,1)}), f16[8,64,640]{2,1,0:T(8,128)(2,1)S(1)}, u32[]{:S(2)}, u32[]{:S(2)}) %all-to-all-start.2) | async-done | bytes 655392 | tf_op jit(solution)/shard_map/all_to_all | solution.py:312
  166.7 1.8 %collective-permute-start.20 = (f16[64,512]{1,0:T(8,128)(2,1)S(1)}, f16[64,512]{1,0:T(8,128)(2,1)S(1)}, u32[]{:S(2)}, u32[]{:S(2)}) collective-permute-start(f16[64,512]{1,0:T(8,128)(2,1)S(1)} %slice_convert_fusion), channel_id=1, source_target_pairs={{0,1},{1,0},{2,3},{3,2},{4,5},{5,4},{6,7},{7,6},{8,9},{9,8},{10,11... | collective-permute-start | bytes 196616 | tf_op jit(solution)/shard_map/ppermute | solution.py:284
  (108 shorter events, 33.7 us)
Async XLA Ops:
  3.2 2.1 %collective-permute-start.2 = (bf16[512,512]{1,0:T(8,128)(2,1)S(1)}, bf16[512,512]{1,0:T(8,128)(2,1)}, u32[]{:S(2)}, u32[]{:S(2)}) collective-permute-start(bf16[512,512]{1,0:T(8,128)(2,1)S(1)} %bitcast.61), channel_id=1, source_target_pairs={{0,1},{1,0},{2,3},{3,2},{4,5},{5,4},{6,7},{7,6},{8,9},{9,8},{10,11... | collective-permute-start | bytes 1572872 | tf_op jit(solution)/shard_map/ppermute | solution.py:284
  8.6 23.2 %all-to-all-start = ((f16[8,64,640]{2,1,0:T(8,128)(2,1)}), f16[8,64,640]{2,1,0:T(8,128)(2,1)S(1)}, u32[]{:S(2)}, u32[]{:S(2)}) async-start(f16[8,64,640]{2,1,0:T(8,128)(2,1)} %pad_maximum_fusion), calls=%async_computation | async-start | bytes 1310720 | tf_op jit(solution)/shard_map/all_to_all | solution.py:312
  15.3 23.7 %collective-permute-start = (bf16[512,512]{1,0:T(8,128)(2,1)S(1)}, bf16[512,512]{1,0:T(8,128)(2,1)}, u32[]{:S(2)}, u32[]{:S(2)}) collective-permute-start(bf16[512,512]{1,0:T(8,128)(2,1)S(1)} %bitcast.62), channel_id=1, source_target_pairs={{0,2},{4,0},{8,4},{12,8},{14,12},{10,14},{6,10},{2,6},{1,3},{5,1},... | collective-permute-start | bytes 1572872 | tf_op jit(solution)/shard_map/ppermute | solution.py:309
  16.8 22.2 %collective-permute-start.1 = (bf16[512,512]{1,0:T(8,128)(2,1)S(1)}, bf16[512,512]{1,0:T(8,128)(2,1)}, u32[]{:S(2)}, u32[]{:S(2)}) collective-permute-start(bf16[512,512]{1,0:T(8,128)(2,1)S(1)} %bitcast.63), channel_id=1, source_target_pairs={{0,4},{4,8},{8,12},{12,14},{14,10},{10,6},{6,2},{2,0},{1,5},{5,9},... | collective-permute-start | bytes 1572872 | tf_op jit(solution)/shard_map/ppermute | solution.py:309
  39.0 15.7 %collective-permute-start.4 = (bf16[512,512]{1,0:T(8,128)(2,1)}, bf16[512,512]{1,0:T(8,128)(2,1)}, u32[]{:S(2)}, u32[]{:S(2)}) collective-permute-start(bf16[512,512]{1,0:T(8,128)(2,1)} %collective-permute-done.refs_2_.refs_7_), channel_id=1, source_target_pairs={{0,2},{4,0},{8,4},{12,8},{14,12},{10,14},{6,10},{2,6},{1,3},{5,1},... | collective-permute-start | bytes 1572872 | tf_op jit(solution)/shard_map/ppermute | solution.py:309
  40.3 14.4 %collective-permute-start.6 = (bf16[512,512]{1,0:T(8,128)(2,1)}, bf16[512,512]{1,0:T(8,128)(2,1)S(1)}, u32[]{:S(2)}, u32[]{:S(2)}) collective-permute-start(bf16[512,512]{1,0:T(8,128)(2,1)} %collective-permute-done.refs_2_.refs_7_), channel_id=1, source_target_pairs={{0,1},{1,0},{2,3},{3,2},{4,5},{5,4},{6,7},{7,6},{8,9},{9,8},{10,11... | collective-permute-start | bytes 1572872 | tf_op jit(solution)/shard_map/ppermute | solution.py:284
  42.0 12.7 %collective-permute-start.7 = (bf16[512,512]{1,0:T(8,128)(2,1)}, bf16[512,512]{1,0:T(8,128)(2,1)S(1)}, u32[]{:S(2)}, u32[]{:S(2)}) collective-permute-start(bf16[512,512]{1,0:T(8,128)(2,1)} %collective-permute-done.1.refs_12_.refs_16_.refs_21_), channel_id=1, source_target_pairs={{0,1},{1,0},{2,3},{3,2},{4,5},{5,4},{6,7},{7,6},{8,9},{9,8},{10,11... | collective-permute-start | bytes 1572872 | tf_op jit(solution)/shard_map/ppermute | solution.py:284
  42.0 16.8 %collective-permute-start.5 = (bf16[512,512]{1,0:T(8,128)(2,1)}, bf16[512,512]{1,0:T(8,128)(2,1)}, u32[]{:S(2)}, u32[]{:S(2)}) collective-permute-start(bf16[512,512]{1,0:T(8,128)(2,1)} %collective-permute-done.1.refs_12_.refs_16_.refs_21_), channel_id=1, source_target_pairs={{0,4},{4,8},{8,12},{12,14},{14,10},{10,6},{6,2},{2,0},{1,5},{5,9},... | collective-permute-start | bytes 1572872 | tf_op jit(solution)/shard_map/ppermute | solution.py:309
  58.8 12.7 %collective-permute-start.8 = (bf16[512,512]{1,0:T(8,128)(2,1)}, bf16[512,512]{1,0:T(8,128)(2,1)S(1)}, u32[]{:S(2)}, u32[]{:S(2)}) collective-permute-start(bf16[512,512]{1,0:T(8,128)(2,1)} %collective-permute-done.4.refs_4_.refs_9_), channel_id=1, source_target_pairs={{0,2},{4,0},{8,4},{12,8},{14,12},{10,14},{6,10},{2,6},{1,3},{5,1},... | collective-permute-start | bytes 1572872 | tf_op jit(solution)/shard_map/ppermute | solution.py:309
  59.9 13.4 %collective-permute-start.9 = (bf16[512,512]{1,0:T(8,128)(2,1)}, bf16[512,512]{1,0:T(8,128)(2,1)}, u32[]{:S(2)}, u32[]{:S(2)}) collective-permute-start(bf16[512,512]{1,0:T(8,128)(2,1)} %collective-permute-done.5.refs_10_.refs_14_.refs_19_), channel_id=1, source_target_pairs={{0,4},{4,8},{8,12},{12,14},{14,10},{10,6},{6,2},{2,0},{1,5},{5,9},... | collective-permute-start | bytes 1572872 | tf_op jit(solution)/shard_map/ppermute | solution.py:309
  60.4 16.2 %collective-permute-start.10 = (bf16[512,512]{1,0:T(8,128)(2,1)}, bf16[512,512]{1,0:T(8,128)(2,1)}, u32[]{:S(2)}, u32[]{:S(2)}) collective-permute-start(bf16[512,512]{1,0:T(8,128)(2,1)} %collective-permute-done.4.refs_4_.refs_9_), channel_id=1, source_target_pairs={{0,1},{1,0},{2,3},{3,2},{4,5},{5,4},{6,7},{7,6},{8,9},{9,8},{10,11... | collective-permute-start | bytes 1572872 | tf_op jit(solution)/shard_map/ppermute | solution.py:284
  62.1 14.5 %collective-permute-start.11 = (bf16[512,512]{1,0:T(8,128)(2,1)}, bf16[512,512]{1,0:T(8,128)(2,1)}, u32[]{:S(2)}, u32[]{:S(2)}) collective-permute-start(bf16[512,512]{1,0:T(8,128)(2,1)} %collective-permute-done.5.refs_10_.refs_14_.refs_19_), channel_id=1, source_target_pairs={{0,1},{1,0},{2,3},{3,2},{4,5},{5,4},{6,7},{7,6},{8,9},{9,8},{10,11... | collective-permute-start | bytes 1572872 | tf_op jit(solution)/shard_map/ppermute | solution.py:284
  62.7 12.7 %collective-permute-start.12 = (f16[64,512]{0,1:T(8,128)(2,1)S(1)}, f16[64,512]{0,1:T(8,128)(2,1)S(1)}, u32[]{:S(2)}, u32[]{:S(2)}) collective-permute-start(f16[64,512]{0,1:T(8,128)(2,1)S(1)} %bitcast.69), channel_id=1, source_target_pairs={{0,1},{1,0},{2,3},{3,2},{4,5},{5,4},{6,7},{7,6},{8,9},{9,8},{10,11... | collective-permute-start | bytes 196616 | tf_op jit(solution)/shard_map/ppermute | solution.py:284
  71.5 16.2 %collective-permute-start.13 = (bf16[512,512]{1,0:T(8,128)(2,1)S(1)}, bf16[512,512]{1,0:T(8,128)(2,1)}, u32[]{:S(2)}, u32[]{:S(2)}) collective-permute-start(bf16[512,512]{1,0:T(8,128)(2,1)S(1)} %collective-permute-done.8.refs_6_.refs_11_), channel_id=1, source_target_pairs={{0,1},{1,0},{2,3},{3,2},{4,5},{5,4},{6,7},{7,6},{8,9},{9,8},{10,11... | collective-permute-start | bytes 1572872 | tf_op jit(solution)/shard_map/ppermute | solution.py:284
  73.4 14.3 %collective-permute-start.14 = (bf16[512,512]{1,0:T(8,128)(2,1)}, bf16[512,512]{1,0:T(8,128)(2,1)}, u32[]{:S(2)}, u32[]{:S(2)}) collective-permute-start(bf16[512,512]{1,0:T(8,128)(2,1)} %collective-permute-done.9.refs_8_.refs_12_.refs_17_), channel_id=1, source_target_pairs={{0,1},{1,0},{2,3},{3,2},{4,5},{5,4},{6,7},{7,6},{8,9},{9,8},{10,11... | collective-permute-start | bytes 1572872 | tf_op jit(solution)/shard_map/ppermute | solution.py:284
  76.6 8.1 %collective-permute-start.15 = (bf16[256,512]{1,0:T(8,128)(2,1)S(1)}, bf16[256,512]{1,0:T(8,128)(2,1)}, u32[]{:S(2)}, u32[]{:S(2)}) collective-permute-start(bf16[256,512]{1,0:T(8,128)(2,1)S(1)} %slice.36), channel_id=1, source_target_pairs={{0,2},{4,0},{8,4},{12,8},{14,12},{10,14},{6,10},{2,6},{1,3},{5,1},... | collective-permute-start | bytes 786440 | tf_op jit(solution)/shard_map/ppermute | solution.py:309
  78.0 7.7 %collective-permute-start.17 = (bf16[256,512]{1,0:T(8,128)(2,1)S(1)}, bf16[256,512]{1,0:T(8,128)(2,1)}, u32[]{:S(2)}, u32[]{:S(2)}) collective-permute-start(bf16[256,512]{1,0:T(8,128)(2,1)S(1)} %slice.37), channel_id=1, source_target_pairs={{0,4},{4,8},{8,12},{12,14},{14,10},{10,6},{6,2},{2,0},{1,5},{5,9},... | collective-permute-start | bytes 786440 | tf_op jit(solution)/shard_map/ppermute | solution.py:309
  79.2 37.3 %all-to-all-start.1 = ((f16[8,64,640]{2,1,0:T(8,128)(2,1)}), f16[8,64,640]{2,1,0:T(8,128)(2,1)S(1)}, u32[]{:S(2)}, u32[]{:S(2)}) async-start(f16[8,64,640]{2,1,0:T(8,128)(2,1)} %pad_maximum_fusion.1), calls=%async_computation.1 | async-start | bytes 1310720 | tf_op jit(solution)/shard_map/all_to_all | solution.py:312
  84.7 12.0 %collective-permute-start.16 = (bf16[256,512]{1,0:T(8,128)(2,1)}, bf16[256,512]{1,0:T(8,128)(2,1)S(1)}, u32[]{:S(2)}, u32[]{:S(2)}) collective-permute-start(bf16[256,512]{1,0:T(8,128)(2,1)} %collective-permute-done.15.refs_8_.refs_13_), channel_id=1, source_target_pairs={{0,1},{1,0},{2,3},{3,2},{4,5},{5,4},{6,7},{7,6},{8,9},{9,8},{10,11... | collective-permute-start | bytes 786440 | tf_op jit(solution)/shard_map/ppermute | solution.py:284
  85.7 11.1 %collective-permute-start.18 = (bf16[256,512]{1,0:T(8,128)(2,1)}, bf16[256,512]{1,0:T(8,128)(2,1)S(1)}, u32[]{:S(2)}, u32[]{:S(2)}) collective-permute-start(bf16[256,512]{1,0:T(8,128)(2,1)} %collective-permute-done.17.refs_10_.refs_15_), channel_id=1, source_target_pairs={{0,1},{1,0},{2,3},{3,2},{4,5},{5,4},{6,7},{7,6},{8,9},{9,8},{10,11... | collective-permute-start | bytes 786440 | tf_op jit(solution)/shard_map/ppermute | solution.py:284
  116.5 25.5 %all-to-all-start.3 = ((f16[8,64,640]{2,1,0:T(8,128)(2,1)}), f16[8,64,640]{2,1,0:T(8,128)(2,1)S(1)}, u32[]{:S(2)}, u32[]{:S(2)}) async-start(f16[8,64,640]{2,1,0:T(8,128)(2,1)} %convert_element_type.70), calls=%async_computation.3 | async-start | bytes 1310720 | tf_op jit(solution)/shard_map/all_to_all | solution.py:312
  142.0 21.7 %all-to-all-start.2 = ((f16[8,64,640]{2,1,0:T(8,128)(2,1)}), f16[8,64,640]{2,1,0:T(8,128)(2,1)S(1)}, u32[]{:S(2)}, u32[]{:S(2)}) async-start(f16[8,64,640]{2,1,0:T(8,128)(2,1)} %convert_element_type.69), calls=%async_computation.2 | async-start | bytes 1310720 | tf_op jit(solution)/shard_map/all_to_all | solution.py:312
  150.6 3.6 %collective-permute-start.19 = (f16[64,512]{1,0:T(8,128)(2,1)S(1)}, f16[64,512]{1,0:T(8,128)(2,1)S(1)}, u32[]{:S(2)}, u32[]{:S(2)}) collective-permute-start(f16[64,512]{1,0:T(8,128)(2,1)S(1)} %slice_convert_fusion.1), channel_id=1, source_target_pairs={{0,1},{1,0},{2,3},{3,2},{4,5},{5,4},{6,7},{7,6},{8,9},{9,8},{10,11... | collective-permute-start | bytes 196616 | tf_op jit(solution)/shard_map/ppermute | solution.py:284
  166.7 3.0 %collective-permute-start.20 = (f16[64,512]{1,0:T(8,128)(2,1)S(1)}, f16[64,512]{1,0:T(8,128)(2,1)S(1)}, u32[]{:S(2)}, u32[]{:S(2)}) collective-permute-start(f16[64,512]{1,0:T(8,128)(2,1)S(1)} %slice_convert_fusion), channel_id=1, source_target_pairs={{0,1},{1,0},{2,3},{3,2},{4,5},{5,4},{6,7},{7,6},{8,9},{9,8},{10,11... | collective-permute-start | bytes 196616 | tf_op jit(solution)/shard_map/ppermute | solution.py:284
  (16 other events, 167.1 us)

commit v8 on v7

--- a/solution.py
+++ b/solution.py
@@ -1,4 +1,3 @@
-import copy
 import functools
 
 import jax
@@ -13,6 +12,7 @@
 HALF = jnp.float16
 COT_SCALE = 256.0
 VMEM = 56 * 1024 * 1024
+AHEAD = 3
 
 
 def ring_order(count):
@@ -44,11 +44,6 @@
 
 
 class Shape:
-    def only(self, units):
-        kept = copy.copy(self)
-        kept.units = units
-        return kept
-
     def __init__(self, count, rows, cols, hists, share):
         self.count = count
         self.rows = rows
@@ -65,28 +60,40 @@
                 self.units.append((d, 0, rows))
 
 
-def load_matrix(s, units, matrix, sems):
-    copies = {}
-    units = iter(units)
-    for d, start, size in s.units:
-        for t in range(2):
-            copy = pltpu.make_async_copy(
-                next(units),
-                matrix.at[d, pl.ds(start, size), pl.ds(t * s.cols, s.cols)],
-                sems.at[d],
-            )
-            copy.start()
-            copies.setdefault(d, []).append(copy)
-
-    def arrived(d):
-        for piece in copies.pop(d, []):
+class Arrivals:
+    def __init__(self, s, table, units, matrix, sems, paired):
+        self.count, self.copies = s.count, {d: [] for d in range(s.count)}
+        units = iter(units)
+        for d, start, size in s.units:
+            for t in range(2):
+                target = matrix.at[d, pl.ds(start, size), pl.ds(t * s.cols, s.cols)]
+                self.copies[d].append(pltpu.make_async_copy(next(units), target, sems.at[d]))
+        for d in range(s.count):
+            k = table[d]
+            for source, target in paired:
+                self.copies[d].append(
+                    pltpu.make_async_copy(source.at[k], target.at[k], sems.at[d])
+                )
+        self.ahead = AHEAD if s.count <= 8 else s.count
+        for d in range(min(self.ahead, s.count)):
+            self.start(d)
+        if s.count > 8:
+            for d in range(s.count):
+                self.wait(d)
+
+    def start(self, d):
+        for piece in self.copies[d]:
+            piece.start()
+
+    def wait(self, d):
+        for piece in self.copies[d]:
             piece.wait()
 
-    if s.count > 8:
-        for d in range(s.count):
-            arrived(d)
-        return lambda d: None
-    return arrived
+    def __call__(self, d):
+        if self.count <= 8:
+            self.wait(d)
+            if d + self.ahead < self.count:
+                self.start(d + self.ahead)
 
 
 def load(sources, targets, sems):
@@ -129,48 +136,27 @@
     return lax.fori_loop(0, count, body, init)
 
 
-def first_step(s, table, mass, matrix, row_one, d):
-    sums = nt(jnp.ones((8, 2 * s.cols), jnp.bfloat16), matrix[d])
-    row_one[d] = sums
-    left = mass[table[d], :, : s.rows] / sums[0:1]
-    return nn(left.astype(jnp.bfloat16), matrix[d])
-
-
-def first_kernel(s, table, mass_in, *refs):
-    units, (row_one, col_one, mass, matrix, sems, more_sems) = refs[:-6], refs[-6:]
-    arriving = load([mass_in], [mass], more_sems)
-    own = [unit for unit in s.units if unit[0] != s.opposite]
-    arrived = load_matrix(s.only(own), units, matrix, sems)
-    arriving[0].wait()
-
-    def step(k, total):
-        d = k + (k >= s.opposite)
-        arrived(d)
-        return total + first_step(s, table, mass, matrix, row_one, d)
-
-    zero = jnp.zeros((s.hists, 2 * s.cols), jnp.float32)
-    col_one[...] = each(s.count - 1, step, zero)
-
-
-def forward_kernel(s, table, mass_in, row_one_in, col_one_in, *refs):
+def forward_kernel(s, table, mass_in, *refs):
     units, refs = refs[: 2 * len(s.units)], refs[2 * len(s.units) :]
     thirds, leaving, (mass, matrix, sems, more_sems), state = refs[0], refs[1:6], refs[6:10], refs[10:]
     row_two, row_one, col_one, col_two, col_three = state
-    arriving = load(
-        [mass_in, row_one_in, col_one_in], [mass, row_one, col_one], more_sems
-    )
-    arrived = load_matrix(s, units, matrix, sems)
-    for copy in arriving:
-        copy.wait()
+    arrived = Arrivals(s, table, units, matrix, sems, [(mass_in, mass)])
+    ones = jnp.ones((8, 2 * s.cols), jnp.bfloat16)
+    zero = jnp.zeros((s.hists, 2 * s.cols), jnp.float32)
+
+    def first(d, total):
+        arrived(d)
+        sums = nt(ones, matrix[d])
+        row_one[d] = sums
+        left = mass[table[d], :, : s.rows] / sums[0:1]
+        return total + nn(left.astype(jnp.bfloat16), matrix[d])
+
+    total = each(s.count, first, zero)
+    col_one[...] = total
     target = gather_targets(s, mass)
-    arrived(s.opposite)
-    total = col_one[...] + first_step(s, table, mass, matrix, row_one, s.opposite)
-    col_one[...] = total
     panel = (target / total).astype(jnp.bfloat16)
-    zero = jnp.zeros((s.hists, 2 * s.cols), jnp.float32)
 
     def second(d, total):
-        arrived(d)
         row = nt(panel, matrix[d])
         row_two[d] = row
         left = mass[table[d], :, : s.rows] / row
@@ -205,23 +191,23 @@
         refs[10:],
     )
     row_two, row_one, col_one, col_two, col_three = state
-    sources = [state_in[4], cot_in, thirds_in, mass_in]
-    early = load(sources, [col_three, cot, thirds, mass], more_sems)
-    arrived = load_matrix(s, units, matrix, sems)
+    early = load([state_in[4], cot_in], [col_three, cot], more_sems)
+    paired = [(mass_in, mass), (thirds_in, thirds)]
+    arrived = Arrivals(s, table, units, matrix, sems, paired)
     late = [
-        pltpu.make_async_copy(state_in[k], state[k], more_sems.at[4 + k]) for k in range(4)
+        pltpu.make_async_copy(state_in[k], state[k], more_sems.at[2 + k]) for k in range(4)
     ]
-    for copy in late:
-        copy.start()
     for copy in early:
         copy.wait()
-    target = gather_targets(s, mass)
     target_cot = gather_targets(s, cot)
     panel = (-target_cot / col_three[...]).astype(jnp.bfloat16)
     zero = jnp.zeros((s.hists, 2 * s.cols), jnp.float32)
 
     def third(d, total):
         arrived(d)
+        if s.count <= 8 and d == s.count - AHEAD:
+            for copy in late:
+                copy.start()
         k = table[d]
         grad = nt(panel, matrix[d])
         row = thirds[k, :, : s.rows]
@@ -233,7 +219,10 @@
 
     total = each(s.count, third, zero)
     for copy in late:
+        if s.count > 8:
+            copy.start()
         copy.wait()
+    target = gather_targets(s, mass)
     term_two = total / col_two[...]
     panel = (-term_two * (target / col_two[...])).astype(jnp.bfloat16)
 
@@ -330,21 +319,19 @@
     swapped = {(0, 0): swap_cores(unit)}
     ahead = behind = unit
     last = count // 2
-    swapped[0, 0], mass_here, points_here = lax.optimization_barrier(
-        (swapped[0, 0], source_mass, target_mass)
-    )
-    mass_message = by_histogram(mass_here, points_here[0])
+    mass_message = by_histogram(source_mass, target_mass[0])
+    cot_message = by_histogram(source_cotangent * COT_SCALE, target_cotangent[0] * COT_SCALE)
     for step in range(1, last + 1):
         due = before.get(step - 2, [])
         ready = [swapped[key] for key in due]
         if step == 2:
-            mass = exchange(mass_message).astype(jnp.float32)
-            ahead, behind, ready, mass, table = lax.optimization_barrier(
-                (ahead, behind, ready, mass, table)
+            ahead, behind, ready, mass_message, table = lax.optimization_barrier(
+                (ahead, behind, ready, mass_message, table)
             )
         elif step == last:
-            ahead, behind, ready, cot_message = lax.optimization_barrier(
-                (ahead, behind, ready, cot_message)
+            mass = exchange(mass_message).astype(jnp.float32)
+            ahead, behind, ready, mass, cot_message = lax.optimization_barrier(
+                (ahead, behind, ready, mass, cot_message)
             )
         else:
             ahead, behind, ready = lax.optimization_barrier((ahead, behind, ready))
@@ -361,27 +348,18 @@
         pieces.update(new)
         swapped.update({key: swap_cores(piece) for key, piece in new.items()})
         before[step] = list(new)
-        if step == max(last - 2, 1):
-            head, cot_here, points_here = lax.optimization_barrier(
-                (ahead, source_cotangent, target_cotangent)
-            )
-            ahead = pieces[step, 0] = head
-            cot_message = by_histogram(cot_here * COT_SCALE, points_here[0] * COT_SCALE)
     units = []
-    near = []
     for d, start, _ in s.units:
         units += [pieces[d, start], swapped[d, start]]
-        near += [] if d == s.opposite else units[-2:]
 
     wide = jax.ShapeDtypeStruct((count, s.hists, s.lanes), jnp.float32)
     panel = jax.ShapeDtypeStruct((count, s.hists, rows), jnp.float32)
     sums = jax.ShapeDtypeStruct((count, 8, rows), jnp.float32)
     column = jax.ShapeDtypeStruct((s.hists, 2 * s.cols), jnp.float32)
     states = [panel, sums, column, column, column]
-    row_one, col_one = call(first_kernel, s, 2, [sums, column], [], table, [mass, *near], [])
     cot = exchange(cot_message).astype(jnp.float32)
     thirds, *state = call(
-        forward_kernel, s, 5, [wide], states, table, [mass, row_one, col_one, *units], states
+        forward_kernel, s, 7, [wide], states, table, [mass, *units], states
     )
     (grads,) = call(
         backward_kernel,

time: 171 us -> 161 us (0.942)
  waiting for transfers between devices: 53.4 us -> 38 us
  Pallas kernels: 44.1 us -> 34.4 us
  local copies, waits for them, and re-layouts: 12.6 us -> 19.6 us
  starting transfers between devices: 41 us -> 45.2 us
  other arithmetic: 17 us -> 20.3 us
    all_to_all x4, waiting for transfers between devices: 21.2 us -> 6.31 us  [exchange(): return lax.all_to_all(x, 'src', 0, 0, tiled=True)]
    pallas_call x3 -> x2, Pallas kernels: 44.1 us -> 34.4 us  [call(): pl.pallas_call(functools.partial(kernel, s), out_shape=[*vmem_outs, *hbm_...]
    ppermute x13, starting transfers between devices: 12.5 us -> 15.6 us  [swap_cores(): return lax.ppermute(x, 'tgt', [(0, 1), (1, 0)])]
    ppermute x13, waiting for transfers between devices: 2.45 us -> 0.21 us  [swap_cores(): return lax.ppermute(x, 'tgt', [(0, 1), (1, 0)])]
    dynamic_slice x4 -> x3, local copies, waits for them, and re-layouts: 1.09 us -> 3.03 us  [by_histogram(): mine = lax.dynamic_index_in_dim(target, core, 1, keepdims=False)]
    concatenate x2, other arithmetic: 0.28 us -> 2.21 us  [by_histogram(): both = jnp.concatenate([mine, swap_cores(other)]).T]
    unnamed x35 -> x33, local copies, waits for them, and re-layouts: 5.23 us -> 7.12 us
    ppermute x8, waiting for transfers between devices: 29.7 us -> 31.5 us  [shift(): return lax.ppermute(x, 'src', pairs)]
  transfers between devices with their start and end apart: 25 -> 25, of which waited for: 10 -> 8; matrix products, arithmetic and copies ran while one was open for 13% -> 21% of each run, Pallas kernels for 26% -> 22%
where the time goes in v8:
time: 161 us; the launch traced here: 160 us
  starting transfers between devices  45.2 us (28%)
  waiting for transfers between devices  38 us (24%)
  Pallas kernels  34.4 us (21%)
  other arithmetic  20.3 us (13%)
  local copies, waits for them, and re-layouts  19.6 us (12%)
    pallas_call x2, Pallas kernels, call(): pl.pallas_call(functools.partial(kernel, s), out_shape=[*vmem_outs, *hbm_...  34.4 us
    ppermute x8, waiting for transfers between devices, shift(): return lax.ppermute(x, 'src', pairs)  31.5 us
    all_to_all x4, starting transfers between devices, exchange(): return lax.all_to_all(x, 'src', 0, 0, tiled=True)  19 us
    ppermute x13, starting transfers between devices, swap_cores(): return lax.ppermute(x, 'tgt', [(0, 1), (1, 0)])  15.6 us
    ppermute x8, starting transfers between devices, shift(): return lax.ppermute(x, 'src', pairs)  10.7 us
    unnamed x33, local copies, waits for them, and re-layouts  7.12 us
    all_to_all x4, waiting for transfers between devices, exchange(): return lax.all_to_all(x, 'src', 0, 0, tiled=True)  6.31 us
  transfers between devices with their start and end apart: 25, of which 8 were waited for; matrix products, arithmetic and copies ran while one was open for 21% of the time, Pallas kernels for 22%

profile of v8, /device:TPU:1, one launch (start us, length us, event | category | flops | bytes accessed | tf_op | source)
XLA Modules:
  0.0 159.9 jit_solution(11625169660076881323)
XLA Ops:
  4.1 2.7 %collective-permute-start = (bf16[512,512]{1,0:T(8,128)(2,1)}, bf16[512,512]{1,0:T(8,128)(2,1)}, u32[]{:S(2)}, u32[]{:S(2)}) collective-permute-start(bf16[512,512]{1,0:T(8,128)(2,1)} %bitcast.35.refs_0_.refs_5_), channel_id=1, source_target_pairs={{0,2},{4,0},{8,4},{12,8},{14,12},{10,14},{6,10},{2,6},{1,3},{5,1},... | collective-permute-start | bytes 1572872 | tf_op jit(solution)/shard_map/ppermute | solution.py:298
  9.6 2.5 %fusion.12 = (f32[512,512]{1,0:T(8,128)}, f16[512,512]{0,1:T(8,128)(2,1)S(1)}, f16[512,512]{0,1:T(8,128)(2,1)S(1)}) fusion(f32[512,512]{1,0:T(8,128)} %param.14, f32[512,512]{1,0:T(8,128)S(1)} %copy-done.2), kind=kLoop, calls=%fused_computation.45 | loop fusion | flops 1048576 | bytes 4194304 | tf_op jit(solution)/shard_map/div | solution.py:386
  20.3 4.6 %all-to-all-start = ((f16[8,64,640]{2,1,0:T(8,128)(2,1)}), f16[8,64,640]{2,1,0:T(8,128)(2,1)S(1)}, u32[]{:S(2)}, u32[]{:S(2)}) async-start(f16[8,64,640]{2,1,0:T(8,128)(2,1)} %pad_maximum_fusion), calls=%async_computation | async-start | bytes 1310720 | tf_op jit(solution)/shard_map/all_to_all | solution.py:301
  26.5 1.9 %collective-permute-start.6 = (bf16[512,512]{1,0:T(8,128)(2,1)}, bf16[512,512]{1,0:T(8,128)(2,1)}, u32[]{:S(2)}, u32[]{:S(2)}) collective-permute-start(bf16[512,512]{1,0:T(8,128)(2,1)} %collective-permute-done.refs_2_.refs_7_), channel_id=1, source_target_pairs={{0,1},{1,0},{2,3},{3,2},{4,5},{5,4},{6,7},{7,6},{8,9},{9,8},{10,11... | collective-permute-start | bytes 1572872 | tf_op jit(solution)/shard_map/ppermute | solution.py:273
  28.4 19.5 %collective-permute-done.4.refs_4_.refs_9_ = bf16[512,512]{1,0:T(8,128)(2,1)} collective-permute-done((bf16[512,512]{1,0:T(8,128)(2,1)}, bf16[512,512]{1,0:T(8,128)(2,1)}, u32[]{:S(2)}, u32[]{:S(2)}) %collective-permute-start.4) | collective-permute-done | bytes 524320 | tf_op jit(solution)/shard_map/ppermute | solution.py:298
  47.9 2.0 %collective-permute-start.8 = (bf16[512,512]{1,0:T(8,128)(2,1)}, bf16[512,512]{1,0:T(8,128)(2,1)}, u32[]{:S(2)}, u32[]{:S(2)}) collective-permute-start(bf16[512,512]{1,0:T(8,128)(2,1)} %collective-permute-done.4.refs_4_.refs_9_), channel_id=1, source_target_pairs={{0,2},{4,0},{8,4},{12,8},{14,12},{10,14},{6,10},{2,6},{1,3},{5,1},... | collective-permute-start | bytes 1572872 | tf_op jit(solution)/shard_map/ppermute | solution.py:298
  49.9 2.8 %collective-permute-start.9 = (bf16[512,512]{1,0:T(8,128)(2,1)}, bf16[512,512]{1,0:T(8,128)(2,1)}, u32[]{:S(2)}, u32[]{:S(2)}) collective-permute-start(bf16[512,512]{1,0:T(8,128)(2,1)} %collective-permute-done.5.refs_14_.refs_19_), channel_id=1, source_target_pairs={{0,4},{4,8},{8,12},{12,14},{14,10},{10,6},{6,2},{2,0},{1,5},{5,9},... | collective-permute-start | bytes 1572872 | tf_op jit(solution)/shard_map/ppermute | solution.py:298
  52.8 2.5 %collective-permute-start.10 = (bf16[512,512]{1,0:T(8,128)(2,1)}, bf16[512,512]{1,0:T(8,128)(2,1)}, u32[]{:S(2)}, u32[]{:S(2)}) collective-permute-start(bf16[512,512]{1,0:T(8,128)(2,1)} %collective-permute-done.4.refs_4_.refs_9_), channel_id=1, source_target_pairs={{0,1},{1,0},{2,3},{3,2},{4,5},{5,4},{6,7},{7,6},{8,9},{9,8},{10,11... | collective-permute-start | bytes 1572872 | tf_op jit(solution)/shard_map/ppermute | solution.py:273
  60.2 2.8 %collective-permute-done.8.refs_6_.refs_11_ = bf16[512,512]{1,0:T(8,128)(2,1)} collective-permute-done((bf16[512,512]{1,0:T(8,128)(2,1)}, bf16[512,512]{1,0:T(8,128)(2,1)}, u32[]{:S(2)}, u32[]{:S(2)}) %collective-permute-start.8) | collective-permute-done | bytes 524320 | tf_op jit(solution)/shard_map/ppermute | solution.py:298
  63.0 2.9 %collective-permute-start.13 = (bf16[512,512]{1,0:T(8,128)(2,1)}, bf16[512,512]{1,0:T(8,128)(2,1)S(1)}, u32[]{:S(2)}, u32[]{:S(2)}) collective-permute-start(bf16[512,512]{1,0:T(8,128)(2,1)} %collective-permute-done.8.refs_6_.refs_11_), channel_id=1, source_target_pairs={{0,1},{1,0},{2,3},{3,2},{4,5},{5,4},{6,7},{7,6},{8,9},{9,8},{10,11... | collective-permute-start | bytes 1572872 | tf_op jit(solution)/shard_map/ppermute | solution.py:273
  65.9 1.9 %collective-permute-start.18 = (bf16[512,512]{1,0:T(8,128)(2,1)}, bf16[512,512]{1,0:T(8,128)(2,1)}, u32[]{:S(2)}, u32[]{:S(2)}) collective-permute-start(bf16[512,512]{1,0:T(8,128)(2,1)} %collective-permute-done.9.refs_12_.refs_17_), channel_id=1, source_target_pairs={{0,1},{1,0},{2,3},{3,2},{4,5},{5,4},{6,7},{7,6},{8,9},{9,8},{10,11... | collective-permute-start | bytes 1572872 | tf_op jit(solution)/shard_map/ppermute | solution.py:273
  72.5 5.4 %collective-permute-done.14.refs_8_.refs_13_ = bf16[256,512]{1,0:T(8,128)(2,1)S(1)} collective-permute-done((bf16[256,512]{1,0:T(8,128)(2,1)S(1)}, bf16[256,512]{1,0:T(8,128)(2,1)S(1)}, u32[]{:S(2)}, u32[]{:S(2)}) %collective-permute-start.14) | collective-permute-done | bytes 262176 | tf_op jit(solution)/shard_map/ppermute | solution.py:298
  81.2 3.7 %all-to-all-start.1 = ((f16[8,64,640]{2,1,0:T(8,128)(2,1)}), f16[8,64,640]{2,1,0:T(8,128)(2,1)S(1)}, u32[]{:S(2)}, u32[]{:S(2)}) async-start(f16[8,64,640]{2,1,0:T(8,128)(2,1)} %pad_maximum_fusion.1), calls=%async_computation.1 | async-start | bytes 1310720 | tf_op jit(solution)/shard_map/all_to_all | solution.py:301
  85.8 17.7 %shard_map.123 = (f32[8,64,640]{2,1,0:T(8,128)}, f32[8,64,512]{2,1,0:T(8,128)}, f32[8,8,512]{2,1,0:T(8,128)}, f32[64,1024]{1,0:T(8,128)}, f32[64,1024]{1,0:T(8,128)}, /*index=5*/f32[64,1024]{1,0:T(8,128)}) custom-call(s32[8]{0:T(128)} %gather_fusion, f32[8,64,640]{2,1,0:T(8,128)} %convert_element_type.64.mass_in, bf16[512,512]{1,0:T(8,128)(2,1)} %bitcast.35.refs_0_.refs_5_, ...), custom_call_target="tpu_custom_call" | custom-call | flops 15032385536 | bytes 16777216 | tf_op jit(solution)/shard_map/pallas_call | solution.py:249
  103.5 2.3 %convert_element_type.70 = f16[8,64,640]{2,1,0:T(8,128)(2,1)} convert(f32[8,64,640]{2,1,0:T(8,128)} %get-tuple-element.49.thirds_in) | non-fusion elementwise | flops 327680 | bytes 1966080 | tf_op jit(solution)/shard_map/convert_element_type | solution.py:383
  105.7 5.2 %all-to-all-start.3 = ((f16[8,64,640]{2,1,0:T(8,128)(2,1)}), f16[8,64,640]{2,1,0:T(8,128)(2,1)S(1)}, u32[]{:S(2)}, u32[]{:S(2)}) async-start(f16[8,64,640]{2,1,0:T(8,128)(2,1)} %convert_element_type.70), calls=%async_computation.3 | async-start | bytes 1310720 | tf_op jit(solution)/shard_map/all_to_all | solution.py:301
  112.1 16.7 %shard_map.124 = f32[8,64,640]{2,1,0:T(8,128)} custom-call(s32[8]{0:T(128)} %gather_fusion, f32[8,64,640]{2,1,0:T(8,128)} %convert_element_type.64.mass_in, f32[8,64,640]{2,1,0:T(8,128)} %convert_element_type.68.cot_in, f32[8,64,640]{2,1,0:T(8,128)} %get-tuple-element.49.thirds_in, f32[8,64,512]{2,1,0:T(8,128)} %get-tuple-element.50.refs_0_, ...), custom_call_target="tpu_custom_call" | custom-call | flops 10737418240 | bytes 16777216 | tf_op jit(solution)/shard_map/pallas_call | solution.py:249
  128.8 2.2 %convert_element_type.69 = f16[8,64,640]{2,1,0:T(8,128)(2,1)} convert(f32[8,64,640]{2,1,0:T(8,128)} %shard_map.124) | non-fusion elementwise | flops 327680 | bytes 1966080 | tf_op jit(solution)/shard_map/convert_element_type | solution.py:390
  131.1 5.4 %all-to-all-start.2 = ((f16[8,64,640]{2,1,0:T(8,128)(2,1)}), f16[8,64,640]{2,1,0:T(8,128)(2,1)S(1)}, u32[]{:S(2)}, u32[]{:S(2)}) async-start(f16[8,64,640]{2,1,0:T(8,128)(2,1)} %convert_element_type.69), calls=%async_computation.2 | async-start | bytes 1310720 | tf_op jit(solution)/shard_map/all_to_all | solution.py:301
  138.5 1.6 copy.36
  140.1 1.8 %copy.37 = f32[512,128]{0,1:T(8,128)} copy(f32[512,128]{1,0:T(8,128)} %slice.49) | data formatting | bytes 524288
  146.1 6.3 %all-to-all-done.2 = f16[8,64,640]{2,1,0:T(8,128)(2,1)S(1)} async-done(((f16[8,64,640]{2,1,0:T(8,128)(2,1)}), f16[8,64,640]{2,1,0:T(8,128)(2,1)S(1)}, u32[]{:S(2)}, u32[]{:S(2)}) %all-to-all-start.2) | async-done | bytes 655392 | tf_op jit(solution)/shard_map/all_to_all | solution.py:301
  153.7 1.6 %copy.38 = f32[512,512]{0,1:T(8,128)S(1)} copy(f32[512,512]{1,0:T(8,128)} %slice.52) | data formatting | bytes 2097152
  155.5 2.4 %collective-permute-start.20 = (f16[64,512]{1,0:T(8,128)(2,1)S(1)}, f16[64,512]{1,0:T(8,128)(2,1)S(1)}, u32[]{:S(2)}, u32[]{:S(2)}) collective-permute-start(f16[64,512]{1,0:T(8,128)(2,1)S(1)} %slice_convert_fusion), channel_id=1, source_target_pairs={{0,1},{1,0},{2,3},{3,2},{4,5},{5,4},{6,7},{7,6},{8,9},{9,8},{10,11... | collective-permute-start | bytes 196616 | tf_op jit(solution)/shard_map/ppermute | solution.py:273
  (103 shorter events, 40.4 us)
Async XLA Ops:
  4.0 16.3 %collective-permute-start.2 = (bf16[512,512]{1,0:T(8,128)(2,1)}, bf16[512,512]{1,0:T(8,128)(2,1)}, u32[]{:S(2)}, u32[]{:S(2)}) collective-permute-start(bf16[512,512]{1,0:T(8,128)(2,1)} %bitcast.35.refs_0_.refs_5_), channel_id=1, source_target_pairs={{0,1},{1,0},{2,3},{3,2},{4,5},{5,4},{6,7},{7,6},{8,9},{9,8},{10,11... | collective-permute-start | bytes 1572872 | tf_op jit(solution)/shard_map/ppermute | solution.py:273
  4.1 15.4 %collective-permute-start = (bf16[512,512]{1,0:T(8,128)(2,1)}, bf16[512,512]{1,0:T(8,128)(2,1)}, u32[]{:S(2)}, u32[]{:S(2)}) collective-permute-start(bf16[512,512]{1,0:T(8,128)(2,1)} %bitcast.35.refs_0_.refs_5_), channel_id=1, source_target_pairs={{0,2},{4,0},{8,4},{12,8},{14,12},{10,14},{6,10},{2,6},{1,3},{5,1},... | collective-permute-start | bytes 1572872 | tf_op jit(solution)/shard_map/ppermute | solution.py:298
  6.8 13.6 %collective-permute-start.1 = (bf16[512,512]{1,0:T(8,128)(2,1)}, bf16[512,512]{1,0:T(8,128)(2,1)}, u32[]{:S(2)}, u32[]{:S(2)}) collective-permute-start(bf16[512,512]{1,0:T(8,128)(2,1)} %bitcast.35.refs_0_.refs_5_), channel_id=1, source_target_pairs={{0,4},{4,8},{8,12},{12,14},{14,10},{10,6},{6,2},{2,0},{1,5},{5,9},... | collective-permute-start | bytes 1572872 | tf_op jit(solution)/shard_map/ppermute | solution.py:298
  9.3 6.5 %collective-permute-start.3 = (f16[64,512]{0,1:T(8,128)(2,1)}, f16[64,512]{0,1:T(8,128)(2,1)}, u32[]{:S(2)}, u32[]{:S(2)}) collective-permute-start(f16[64,512]{0,1:T(8,128)(2,1)} %bitcast.7), channel_id=1, source_target_pairs={{0,1},{1,0},{2,3},{3,2},{4,5},{5,4},{6,7},{7,6},{8,9},{9,8},{10,11... | collective-permute-start | bytes 196616 | tf_op jit(solution)/shard_map/ppermute | solution.py:273
  20.3 47.4 %all-to-all-start = ((f16[8,64,640]{2,1,0:T(8,128)(2,1)}), f16[8,64,640]{2,1,0:T(8,128)(2,1)S(1)}, u32[]{:S(2)}, u32[]{:S(2)}) async-start(f16[8,64,640]{2,1,0:T(8,128)(2,1)} %pad_maximum_fusion), calls=%async_computation | async-start | bytes 1310720 | tf_op jit(solution)/shard_map/all_to_all | solution.py:301
  25.0 22.9 %collective-permute-start.4 = (bf16[512,512]{1,0:T(8,128)(2,1)}, bf16[512,512]{1,0:T(8,128)(2,1)}, u32[]{:S(2)}, u32[]{:S(2)}) collective-permute-start(bf16[512,512]{1,0:T(8,128)(2,1)} %collective-permute-done.refs_2_.refs_7_), channel_id=1, source_target_pairs={{0,2},{4,0},{8,4},{12,8},{14,12},{10,14},{6,10},{2,6},{1,3},{5,1},... | collective-permute-start | bytes 1572872 | tf_op jit(solution)/shard_map/ppermute | solution.py:298
  26.4 21.5 %collective-permute-start.5 = (bf16[512,512]{1,0:T(8,128)(2,1)}, bf16[512,512]{1,0:T(8,128)(2,1)}, u32[]{:S(2)}, u32[]{:S(2)}) collective-permute-start(bf16[512,512]{1,0:T(8,128)(2,1)} %collective-permute-done.1.refs_16_.refs_21_), channel_id=1, source_target_pairs={{0,4},{4,8},{8,12},{12,14},{14,10},{10,6},{6,2},{2,0},{1,5},{5,9},... | collective-permute-start | bytes 1572872 | tf_op jit(solution)/shard_map/ppermute | solution.py:298
  26.5 21.4 %collective-permute-start.6 = (bf16[512,512]{1,0:T(8,128)(2,1)}, bf16[512,512]{1,0:T(8,128)(2,1)}, u32[]{:S(2)}, u32[]{:S(2)}) collective-permute-start(bf16[512,512]{1,0:T(8,128)(2,1)} %collective-permute-done.refs_2_.refs_7_), channel_id=1, source_target_pairs={{0,1},{1,0},{2,3},{3,2},{4,5},{5,4},{6,7},{7,6},{8,9},{9,8},{10,11... | collective-permute-start | bytes 1572872 | tf_op jit(solution)/shard_map/ppermute | solution.py:273
  28.4 19.5 %collective-permute-start.7 = (bf16[512,512]{1,0:T(8,128)(2,1)}, bf16[512,512]{1,0:T(8,128)(2,1)}, u32[]{:S(2)}, u32[]{:S(2)}) collective-permute-start(bf16[512,512]{1,0:T(8,128)(2,1)} %collective-permute-done.1.refs_16_.refs_21_), channel_id=1, source_target_pairs={{0,1},{1,0},{2,3},{3,2},{4,5},{5,4},{6,7},{7,6},{8,9},{9,8},{10,11... | collective-permute-start | bytes 1572872 | tf_op jit(solution)/shard_map/ppermute | solution.py:273
  47.9 15.1 %collective-permute-start.8 = (bf16[512,512]{1,0:T(8,128)(2,1)}, bf16[512,512]{1,0:T(8,128)(2,1)}, u32[]{:S(2)}, u32[]{:S(2)}) collective-permute-start(bf16[512,512]{1,0:T(8,128)(2,1)} %collective-permute-done.4.refs_4_.refs_9_), channel_id=1, source_target_pairs={{0,2},{4,0},{8,4},{12,8},{14,12},{10,14},{6,10},{2,6},{1,3},{5,1},... | collective-permute-start | bytes 1572872 | tf_op jit(solution)/shard_map/ppermute | solution.py:298
  49.9 16.0 %collective-permute-start.9 = (bf16[512,512]{1,0:T(8,128)(2,1)}, bf16[512,512]{1,0:T(8,128)(2,1)}, u32[]{:S(2)}, u32[]{:S(2)}) collective-permute-start(bf16[512,512]{1,0:T(8,128)(2,1)} %collective-permute-done.5.refs_14_.refs_19_), channel_id=1, source_target_pairs={{0,4},{4,8},{8,12},{12,14},{14,10},{10,6},{6,2},{2,0},{1,5},{5,9},... | collective-permute-start | bytes 1572872 | tf_op jit(solution)/shard_map/ppermute | solution.py:298
  52.8 16.2 %collective-permute-start.10 = (bf16[512,512]{1,0:T(8,128)(2,1)}, bf16[512,512]{1,0:T(8,128)(2,1)}, u32[]{:S(2)}, u32[]{:S(2)}) collective-permute-start(bf16[512,512]{1,0:T(8,128)(2,1)} %collective-permute-done.4.refs_4_.refs_9_), channel_id=1, source_target_pairs={{0,1},{1,0},{2,3},{3,2},{4,5},{5,4},{6,7},{7,6},{8,9},{9,8},{10,11... | collective-permute-start | bytes 1572872 | tf_op jit(solution)/shard_map/ppermute | solution.py:273
  55.3 13.7 %collective-permute-start.11 = (bf16[512,512]{1,0:T(8,128)(2,1)}, bf16[512,512]{1,0:T(8,128)(2,1)}, u32[]{:S(2)}, u32[]{:S(2)}) collective-permute-start(bf16[512,512]{1,0:T(8,128)(2,1)} %collective-permute-done.5.refs_14_.refs_19_), channel_id=1, source_target_pairs={{0,1},{1,0},{2,3},{3,2},{4,5},{5,4},{6,7},{7,6},{8,9},{9,8},{10,11... | collective-permute-start | bytes 1572872 | tf_op jit(solution)/shard_map/ppermute | solution.py:273
  63.0 22.0 %collective-permute-start.13 = (bf16[512,512]{1,0:T(8,128)(2,1)}, bf16[512,512]{1,0:T(8,128)(2,1)S(1)}, u32[]{:S(2)}, u32[]{:S(2)}) collective-permute-start(bf16[512,512]{1,0:T(8,128)(2,1)} %collective-permute-done.8.refs_6_.refs_11_), channel_id=1, source_target_pairs={{0,1},{1,0},{2,3},{3,2},{4,5},{5,4},{6,7},{7,6},{8,9},{9,8},{10,11... | collective-permute-start | bytes 1572872 | tf_op jit(solution)/shard_map/ppermute | solution.py:273
  65.9 19.1 %collective-permute-start.18 = (bf16[512,512]{1,0:T(8,128)(2,1)}, bf16[512,512]{1,0:T(8,128)(2,1)}, u32[]{:S(2)}, u32[]{:S(2)}) collective-permute-start(bf16[512,512]{1,0:T(8,128)(2,1)} %collective-permute-done.9.refs_12_.refs_17_), channel_id=1, source_target_pairs={{0,1},{1,0},{2,3},{3,2},{4,5},{5,4},{6,7},{7,6},{8,9},{9,8},{10,11... | collective-permute-start | bytes 1572872 | tf_op jit(solution)/shard_map/ppermute | solution.py:273
  69.9 8.0 %collective-permute-start.14 = (bf16[256,512]{1,0:T(8,128)(2,1)S(1)}, bf16[256,512]{1,0:T(8,128)(2,1)S(1)}, u32[]{:S(2)}, u32[]{:S(2)}) collective-permute-start(bf16[256,512]{1,0:T(8,128)(2,1)S(1)} %slice.36), channel_id=1, source_target_pairs={{0,2},{4,0},{8,4},{12,8},{14,12},{10,14},{6,10},{2,6},{1,3},{5,1},... | collective-permute-start | bytes 786440 | tf_op jit(solution)/shard_map/ppermute | solution.py:298
  72.4 7.7 %collective-permute-start.16 = (bf16[256,512]{1,0:T(8,128)(2,1)S(1)}, bf16[256,512]{1,0:T(8,128)(2,1)S(1)}, u32[]{:S(2)}, u32[]{:S(2)}) collective-permute-start(bf16[256,512]{1,0:T(8,128)(2,1)S(1)} %slice.37), channel_id=1, source_target_pairs={{0,4},{4,8},{8,12},{12,14},{14,10},{10,6},{6,2},{2,0},{1,5},{5,9},... | collective-permute-start | bytes 786440 | tf_op jit(solution)/shard_map/ppermute | solution.py:298
  77.9 7.0 %collective-permute-start.15 = (bf16[256,512]{1,0:T(8,128)(2,1)S(1)}, bf16[256,512]{1,0:T(8,128)(2,1)}, u32[]{:S(2)}, u32[]{:S(2)}) collective-permute-start(bf16[256,512]{1,0:T(8,128)(2,1)S(1)} %collective-permute-done.14.refs_8_.refs_13_), channel_id=1, source_target_pairs={{0,1},{1,0},{2,3},{3,2},{4,5},{5,4},{6,7},{7,6},{8,9},{9,8},{10,11... | collective-permute-start | bytes 786440 | tf_op jit(solution)/shard_map/ppermute | solution.py:273
  80.1 4.9 %collective-permute-start.17 = (bf16[256,512]{1,0:T(8,128)(2,1)S(1)}, bf16[256,512]{1,0:T(8,128)(2,1)}, u32[]{:S(2)}, u32[]{:S(2)}) collective-permute-start(bf16[256,512]{1,0:T(8,128)(2,1)S(1)} %collective-permute-done.16.refs_10_.refs_15_), channel_id=1, source_target_pairs={{0,1},{1,0},{2,3},{3,2},{4,5},{5,4},{6,7},{7,6},{8,9},{9,8},{10,11... | collective-permute-start | bytes 786440 | tf_op jit(solution)/shard_map/ppermute | solution.py:273
  81.2 24.5 %all-to-all-start.1 = ((f16[8,64,640]{2,1,0:T(8,128)(2,1)}), f16[8,64,640]{2,1,0:T(8,128)(2,1)S(1)}, u32[]{:S(2)}, u32[]{:S(2)}) async-start(f16[8,64,640]{2,1,0:T(8,128)(2,1)} %pad_maximum_fusion.1), calls=%async_computation.1 | async-start | bytes 1310720 | tf_op jit(solution)/shard_map/all_to_all | solution.py:301
  105.7 25.4 %all-to-all-start.3 = ((f16[8,64,640]{2,1,0:T(8,128)(2,1)}), f16[8,64,640]{2,1,0:T(8,128)(2,1)S(1)}, u32[]{:S(2)}, u32[]{:S(2)}) async-start(f16[8,64,640]{2,1,0:T(8,128)(2,1)} %convert_element_type.70), calls=%async_computation.3 | async-start | bytes 1310720 | tf_op jit(solution)/shard_map/all_to_all | solution.py:301
  131.1 21.3 %all-to-all-start.2 = ((f16[8,64,640]{2,1,0:T(8,128)(2,1)}), f16[8,64,640]{2,1,0:T(8,128)(2,1)S(1)}, u32[]{:S(2)}, u32[]{:S(2)}) async-start(f16[8,64,640]{2,1,0:T(8,128)(2,1)} %convert_element_type.69), calls=%async_computation.2 | async-start | bytes 1310720 | tf_op jit(solution)/shard_map/all_to_all | solution.py:301
  142.8 2.5 %collective-permute-start.19 = (f16[64,512]{1,0:T(8,128)(2,1)S(1)}, f16[64,512]{1,0:T(8,128)(2,1)S(1)}, u32[]{:S(2)}, u32[]{:S(2)}) collective-permute-start(f16[64,512]{1,0:T(8,128)(2,1)S(1)} %slice_convert_fusion.1), channel_id=1, source_target_pairs={{0,1},{1,0},{2,3},{3,2},{4,5},{5,4},{6,7},{7,6},{8,9},{9,8},{10,11... | collective-permute-start | bytes 196616 | tf_op jit(solution)/shard_map/ppermute | solution.py:273
  155.5 3.6 %collective-permute-start.20 = (f16[64,512]{1,0:T(8,128)(2,1)S(1)}, f16[64,512]{1,0:T(8,128)(2,1)S(1)}, u32[]{:S(2)}, u32[]{:S(2)}) collective-permute-start(f16[64,512]{1,0:T(8,128)(2,1)S(1)} %slice_convert_fusion), channel_id=1, source_target_pairs={{0,1},{1,0},{2,3},{3,2},{4,5},{5,4},{6,7},{7,6},{8,9},{9,8},{10,11... | collective-permute-start | bytes 196616 | tf_op jit(solution)/shard_map/ppermute | solution.py:273
  (15 other events, 118.8 us)

commit v9 on v8

--- a/solution.py
+++ b/solution.py
@@ -52,22 +52,20 @@
         self.share = share
         self.lanes = rows + 2 * share
         self.opposite = count // 2
-        self.units = []
-        for d in range(count):
-            if d == self.opposite:
-                self.units += [(d, 0, rows // 2), (d, rows // 2, rows // 2)]
-            else:
-                self.units.append((d, 0, rows))
 
 
 class Arrivals:
     def __init__(self, s, table, units, matrix, sems, paired):
-        self.count, self.copies = s.count, {d: [] for d in range(s.count)}
-        units = iter(units)
-        for d, start, size in s.units:
-            for t in range(2):
-                target = matrix.at[d, pl.ds(start, size), pl.ds(t * s.cols, s.cols)]
-                self.copies[d].append(pltpu.make_async_copy(next(units), target, sems.at[d]))
+        self.count = s.count
+        self.copies = {
+            d: [pltpu.make_async_copy(units[d], matrix.at[d], sems.at[d])]
+            for d in range(s.count - 1)
+        }
+        half, d = s.rows // 2, s.count - 1
+        self.copies[d] = []
+        for unit, side in zip(units[d:], (table[s.count], 1 - table[s.count])):
+            target = matrix.at[d, pl.ds(pl.multiple_of(side * half, half), half)]
+            self.copies[d].append(pltpu.make_async_copy(unit, target, sems.at[d]))
         for d in range(s.count):
             k = table[d]
             for source, target in paired:
@@ -128,52 +126,55 @@
         )
 
 
-def each(count, body, init):
-    if count <= 8:
-        for d in range(count):
-            init = body(d, init)
-        return init
-    return lax.fori_loop(0, count, body, init)
+def chain(count, product, use, total):
+    if count > 8:
+        return lax.fori_loop(0, count, lambda d, t: use(d, product(d), t), total)
+    ready = product(0)
+    for d in range(count):
+        later = product(d + 1) if d + 1 < count else None
+        total = use(d, ready, total)
+        ready = later
+    return total
 
 
 def forward_kernel(s, table, mass_in, *refs):
-    units, refs = refs[: 2 * len(s.units)], refs[2 * len(s.units) :]
+    units, refs = refs[: s.count + 1], refs[s.count + 1 :]
     thirds, leaving, (mass, matrix, sems, more_sems), state = refs[0], refs[1:6], refs[6:10], refs[10:]
     row_two, row_one, col_one, col_two, col_three = state
     arrived = Arrivals(s, table, units, matrix, sems, [(mass_in, mass)])
     ones = jnp.ones((8, 2 * s.cols), jnp.bfloat16)
     zero = jnp.zeros((s.hists, 2 * s.cols), jnp.float32)
 
-    def first(d, total):
+    def sums(d):
         arrived(d)
-        sums = nt(ones, matrix[d])
-        row_one[d] = sums
-        left = mass[table[d], :, : s.rows] / sums[0:1]
+        return nt(ones, matrix[d])
+
+    def first(d, row, total):
+        row_one[d] = row
+        left = mass[table[d], :, : s.rows] / row[0:1]
         return total + nn(left.astype(jnp.bfloat16), matrix[d])
 
-    total = each(s.count, first, zero)
+    total = chain(s.count, sums, first, zero)
     col_one[...] = total
     target = gather_targets(s, mass)
     panel = (target / total).astype(jnp.bfloat16)
 
-    def second(d, total):
-        row = nt(panel, matrix[d])
+    def second(d, row, total):
         row_two[d] = row
         left = mass[table[d], :, : s.rows] / row
         return total + nn(left.astype(jnp.bfloat16), matrix[d])
 
-    total = each(s.count, second, zero)
+    total = chain(s.count, lambda d: nt(panel, matrix[d]), second, zero)
     col_two[...] = total
     started = load(state[:4], leaving[:4], more_sems)
-    panel = (target / total).astype(jnp.bfloat16)
-
-    def third(d, total):
-        row = nt(panel, matrix[d])
+    last_panel = (target / total).astype(jnp.bfloat16)
+
+    def third(d, row, total):
         thirds[table[d], :, : s.rows] = row
         left = mass[table[d], :, : s.rows] / row
         return total + nn(left.astype(jnp.bfloat16), matrix[d])
 
-    total = each(s.count, third, zero)
+    total = chain(s.count, lambda d: nt(last_panel, matrix[d]), third, zero)
     col_three[...] = total
     last = pltpu.make_async_copy(col_three, leaving[4], more_sems.at[4])
     last.start()
@@ -183,7 +184,7 @@
 
 
 def backward_kernel(s, table, mass_in, cot_in, thirds_in, *refs):
-    state_in, units, refs = refs[:5], refs[5 : 5 + 2 * len(s.units)], refs[5 + 2 * len(s.units) :]
+    state_in, units, refs = refs[:5], refs[5 : 6 + s.count], refs[6 + s.count :]
     out, (mass, matrix, sems, more_sems), state, (cot, thirds) = (
         refs[0],
         refs[1:5],
@@ -203,13 +204,15 @@
     panel = (-target_cot / col_three[...]).astype(jnp.bfloat16)
     zero = jnp.zeros((s.hists, 2 * s.cols), jnp.float32)
 
-    def third(d, total):
+    def first_product(d):
         arrived(d)
         if s.count <= 8 and d == s.count - AHEAD:
             for copy in late:
                 copy.start()
+        return nt(panel, matrix[d])
+
+    def third(d, grad, total):
         k = table[d]
-        grad = nt(panel, matrix[d])
         row = thirds[k, :, : s.rows]
         left = mass[k, :, : s.rows] / row
         term = grad / row
@@ -217,31 +220,32 @@
         rowgrad = -(cot[k, :, : s.rows] / row + term * left)
         return total + nn(rowgrad.astype(jnp.bfloat16), matrix[d])
 
-    total = each(s.count, third, zero)
+    total = chain(s.count, first_product, third, zero)
     for copy in late:
         if s.count > 8:
             copy.start()
         copy.wait()
     target = gather_targets(s, mass)
     term_two = total / col_two[...]
-    panel = (-term_two * (target / col_two[...])).astype(jnp.bfloat16)
-
-    def second(d, total):
+    panel_two = (-term_two * (target / col_two[...])).astype(jnp.bfloat16)
+
+    def second(d, grad, total):
         k = table[d]
         row = row_two[d]
-        term = nt(panel, matrix[d]) / row
+        term = grad / row
         out[k, :, : s.rows] += term
         rowgrad = -term * (mass[k, :, : s.rows] / row)
         return total + nn(rowgrad.astype(jnp.bfloat16), matrix[d])
 
-    term_one = each(s.count, second, zero) / col_one[...]
-    panel = (-term_one * (target / col_one[...])).astype(jnp.bfloat16)
-
-    def first(d, carry):
-        out[table[d], :, : s.rows] += nt(panel, matrix[d]) / row_one[d, 0:1]
+    total = chain(s.count, lambda d: nt(panel_two, matrix[d]), second, zero)
+    term_one = total / col_one[...]
+    panel_one = (-term_one * (target / col_one[...])).astype(jnp.bfloat16)
+
+    def first(d, grad, carry):
+        out[table[d], :, : s.rows] += grad / row_one[d, 0:1]
         return carry
 
-    each(s.count, first, 0)
+    chain(s.count, lambda d: nt(panel_one, matrix[d]), first, 0)
     scatter_targets(s, out, term_two + term_one)
 
 
@@ -291,20 +295,32 @@
     me = lax.axis_index("src")
     core = lax.axis_index("tgt")
     at = jnp.asarray(place)[me]
-    table = jnp.asarray(ring)[(at + jnp.arange(count, dtype=jnp.int32)) % count]
-
-    def shift(x, distance):
-        pairs = [(int(ring[p]), int(ring[(p + distance) % count])) for p in range(count)]
-        return lax.ppermute(x, "src", pairs)
+    last = count // 2
+    away = 2 * core - 1
+    steps = [0] + [sign * k for k in range(1, last) for sign in (1, -1)] + [last]
+    slots = (at + away * jnp.asarray(steps, jnp.int32)) % count
+    table = jnp.concatenate([jnp.asarray(ring)[slots], core[None]]).astype(jnp.int32)
+
+    def onward(x):
+        pairs = []
+        for p in range(count):
+            pairs.append((int(ring[p]) * 2, int(ring[(p + 1) % count]) * 2))
+            pairs.append((int(ring[p]) * 2 + 1, int(ring[(p - 1) % count]) * 2 + 1))
+        return lax.ppermute(x, ("src", "tgt"), pairs)
 
     def exchange(x):
         return lax.all_to_all(x, "src", 0, 0, tiled=True)
+
+    def in_order(mine, other, axis):
+        return jnp.concatenate(
+            [jnp.where(core == 0, mine, other), jnp.where(core == 0, other, mine)], axis=axis
+        )
 
     def by_histogram(source, target):
         target = target.astype(HALF).reshape(share, 2, cols_here)
         mine = lax.dynamic_index_in_dim(target, core, 1, keepdims=False)
         other = lax.dynamic_index_in_dim(target, 1 - core, 1, keepdims=False)
-        both = jnp.concatenate([mine, swap_cores(other)]).T
+        both = in_order(mine, swap_cores(other), 0).T
         return jnp.concatenate(
             [
                 source.astype(HALF).T.reshape(count, s.hists, rows),
@@ -313,51 +329,33 @@
             axis=2,
         )
 
-    unit = dense_blocks(kernel_tiles, tile_cols, tile_count)
-
-    pieces, before = {(0, 0): unit}, {0: [(0, 0)]}
-    swapped = {(0, 0): swap_cores(unit)}
-    ahead = behind = unit
-    last = count // 2
+    mine = dense_blocks(kernel_tiles, tile_cols, tile_count)
+    unit = in_order(mine, swap_cores(mine), 1)
     mass_message = by_histogram(source_mass, target_mass[0])
     cot_message = by_histogram(source_cotangent * COT_SCALE, target_cotangent[0] * COT_SCALE)
+    units = [unit]
     for step in range(1, last + 1):
-        due = before.get(step - 2, [])
-        ready = [swapped[key] for key in due]
         if step == 2:
-            ahead, behind, ready, mass_message, table = lax.optimization_barrier(
-                (ahead, behind, ready, mass_message, table)
-            )
+            unit, table = lax.optimization_barrier((unit, table))
+            units[-1], mass_message = lax.optimization_barrier((units[-1], mass_message))
         elif step == last:
             mass = exchange(mass_message).astype(jnp.float32)
-            ahead, behind, ready, mass, cot_message = lax.optimization_barrier(
-                (ahead, behind, ready, mass, cot_message)
+            unit, units[-3], mass, cot_message = lax.optimization_barrier(
+                (unit, units[-3], mass, cot_message)
             )
-        else:
-            ahead, behind, ready = lax.optimization_barrier((ahead, behind, ready))
-        swapped.update(zip(due, ready))
-        if 2 * step == count:
-            middle = rows // 2
-            new = {
-                (step, 0): shift(ahead[:middle], -1),
-                (step, middle): shift(behind[middle:], 1),
-            }
-        else:
-            ahead, behind = shift(ahead, -1), shift(behind, 1)
-            new = {(step, 0): ahead, (count - step, 0): behind}
-        pieces.update(new)
-        swapped.update({key: swap_cores(piece) for key, piece in new.items()})
-        before[step] = list(new)
-    units = []
-    for d, start, _ in s.units:
-        units += [pieces[d, start], swapped[d, start]]
+        elif step > 2:
+            unit, units[-3] = lax.optimization_barrier((unit, units[-3]))
+        if step == last:
+            unit = lax.dynamic_slice_in_dim(unit, core * (rows // 2), rows // 2, 0)
+        unit = onward(unit)
+        units += [unit, swap_cores(unit)]
+    cot = exchange(cot_message).astype(jnp.float32)
 
     wide = jax.ShapeDtypeStruct((count, s.hists, s.lanes), jnp.float32)
     panel = jax.ShapeDtypeStruct((count, s.hists, rows), jnp.float32)
     sums = jax.ShapeDtypeStruct((count, 8, rows), jnp.float32)
     column = jax.ShapeDtypeStruct((s.hists, 2 * s.cols), jnp.float32)
     states = [panel, sums, column, column, column]
-    cot = exchange(cot_message).astype(jnp.float32)
     thirds, *state = call(
         forward_kernel, s, 7, [wide], states, table, [mass, *units], states
     )
@@ -375,10 +373,10 @@
     def by_point(pieces):
         flat = pieces.reshape(cols_here, s.lanes).astype(jnp.float32)
         target = flat[:, rows:].T.reshape(2, share, cols_here)
-        other = swap_cores(target[1].astype(HALF)).astype(jnp.float32)
-        own = target[0]
-        halves = [jnp.where(core == t, own, other) for t in range(2)]
-        return flat[:, :rows].T, jnp.concatenate(halves, axis=1)
+        own = lax.dynamic_index_in_dim(target, core, 0, keepdims=False)
+        other = lax.dynamic_index_in_dim(target, 1 - core, 0, keepdims=False)
+        other = swap_cores(other.astype(HALF)).astype(jnp.float32)
+        return flat[:, :rows].T, in_order(own, other, 1)
 
     row_three, col_three = by_point(exchange(thirds.astype(HALF)))
     source_potential = jnp.log(source_mass / row_three)

time: 161 us -> 152 us (0.944)
  starting transfers between devices: 45.2 us -> 35.5 us
  waiting for transfers between devices: 38 us -> 47.6 us
  local copies, waits for them, and re-layouts: 19.6 us -> 13.4 us
  Pallas kernels: 34.4 us -> 31.8 us
    ppermute x8 -> x4, waiting for transfers between devices: 31.5 us -> 39.5 us  [onward(): return lax.ppermute(x, ('src', 'tgt'), pairs)]
    ppermute x13 -> x9, starting transfers between devices: 15.6 us -> 8.46 us  [swap_cores(): return lax.ppermute(x, 'tgt', [(0, 1), (1, 0)])]
    ppermute x8 -> x4, starting transfers between devices: 10.7 us -> 7.02 us  [onward(): return lax.ppermute(x, ('src', 'tgt'), pairs)]
    slice x6 -> x2, local copies, waits for them, and re-layouts: 4.93 us -> 2.24 us  [by_point(): return (flat[:, :rows].T, in_order(own, other, 1))]
    pallas_call x2, Pallas kernels: 34.4 us -> 31.8 us  [call(): pl.pallas_call(functools.partial(kernel, s), out_shape=[*vmem_outs, *hbm_...]
    transpose x0 -> x6, local copies, waits for them, and re-layouts: none -> 2.28 us  [the longest x4 1.94 us: by_point(): target = flat[:, rows:].T.reshape(2, share, cols_here)]
    unnamed x33 -> x35, local copies, waits for them, and re-layouts: 7.12 us -> 5.18 us
    dynamic_slice x3 -> x2, local copies, waits for them, and re-layouts: 3.03 us -> 1.35 us  [by_histogram(): mine = lax.dynamic_index_in_dim(target, core, 1, keepdims=False)]
  transfers between devices with their start and end apart: 25 -> 17, of which waited for: 8 -> 5; matrix products, arithmetic and copies ran while one was open for 21% -> 18% of each run, Pallas kernels for 22% -> 21%
where the time goes in v9:
time: 152 us; the launch traced here: 151 us
  waiting for transfers between devices  47.6 us (31%)
  starting transfers between devices  35.5 us (23%)
  Pallas kernels  31.8 us (21%)
  other arithmetic  20.4 us (13%)
  local copies, waits for them, and re-layouts  13.4 us (9%)
    ppermute x4, waiting for transfers between devices, onward(): return lax.ppermute(x, ('src', 'tgt'), pairs)  39.5 us
    pallas_call x2, Pallas kernels, call(): pl.pallas_call(functools.partial(kernel, s), out_shape=[*vmem_outs, *hbm_...  31.8 us
    all_to_all x4, starting transfers between devices, exchange(): return lax.all_to_all(x, 'src', 0, 0, tiled=True)  20 us
    ppermute x9, starting transfers between devices, swap_cores(): return lax.ppermute(x, 'tgt', [(0, 1), (1, 0)])  8.46 us
    ppermute x4, starting transfers between devices, onward(): return lax.ppermute(x, ('src', 'tgt'), pairs)  7.02 us
    all_to_all x4, waiting for transfers between devices, exchange(): return lax.all_to_all(x, 'src', 0, 0, tiled=True)  6.21 us
    unnamed x35, local copies, waits for them, and re-layouts  5.18 us
  transfers between devices with their start and end apart: 17, of which 5 were waited for; matrix products, arithmetic and copies ran while one was open for 18% of the time, Pallas kernels for 21%

profile of v9, /device:TPU:1, one launch (start us, length us, event | category | flops | bytes accessed | tf_op | source)
XLA Modules:
  0.0 151.1 jit_solution(16460333290047875391)
XLA Ops:
  3.3 1.9 %collective-permute-done = bf16[512,512]{1,0:T(8,128)(2,1)S(1)} collective-permute-done((bf16[512,512]{1,0:T(8,128)(2,1)S(1)}, bf16[512,512]{1,0:T(8,128)(2,1)S(1)}, u32[]{:S(2)}, u32[]{:S(2)}) %collective-permute-start) | collective-permute-done | bytes 524320 | tf_op jit(solution)/shard_map/ppermute | solution.py:277
  5.4 2.4 %collective-permute-start.1 = (bf16[512,1024]{1,0:T(8,128)(2,1)S(1)}, bf16[512,1024]{1,0:T(8,128)(2,1)}, u32[]{:S(2)}, u32[]{:S(2)}) collective-permute-start(bf16[512,1024]{1,0:T(8,128)(2,1)S(1)} %pad_maximum_fusion.refs_0_.refs_5_), channel_id=1, source_target_pairs={{0,4},{1,3},{4,8},{5,1},{8,12},{9,5},{12,14},{13,9},{14,10},{15,13... | collective-permute-start | bytes 3145736 | tf_op jit(solution)/shard_map/ppermute | solution.py:309
  10.6 9.9 %collective-permute-done.1.refs_1_.refs_6_ = bf16[512,1024]{1,0:T(8,128)(2,1)} collective-permute-done((bf16[512,1024]{1,0:T(8,128)(2,1)S(1)}, bf16[512,1024]{1,0:T(8,128)(2,1)}, u32[]{:S(2)}, u32[]{:S(2)}) %collective-permute-start.1) | collective-permute-done | bytes 1048608 | tf_op jit(solution)/shard_map/ppermute | solution.py:309
  20.5 1.4 collective-permute-start.2
  21.9 1.6 %collective-permute-start.3 = (bf16[512,1024]{1,0:T(8,128)(2,1)}, bf16[512,1024]{1,0:T(8,128)(2,1)}, u32[]{:S(2)}, u32[]{:S(2)}) collective-permute-start(bf16[512,1024]{1,0:T(8,128)(2,1)} %collective-permute-done.1.refs_1_.refs_6_), channel_id=1, source_target_pairs={{0,1},{1,0},{2,3},{3,2},{4,5},{5,4},{6,7},{7,6},{8,9},{9,8},{10,11... | collective-permute-start | bytes 3145736 | tf_op jit(solution)/shard_map/ppermute | solution.py:277
  26.2 2.5 %fusion.13 = (f32[512,512]{1,0:T(8,128)}, f16[512,512]{0,1:T(8,128)(2,1)S(1)}, f16[512,512]{0,1:T(8,128)(2,1)S(1)}) fusion(f32[512,512]{1,0:T(8,128)} %param.15, f32[512,512]{1,0:T(8,128)S(1)} %copy-done.2), kind=kLoop, calls=%fused_computation.61 | loop fusion | flops 1048576 | bytes 4194304 | tf_op jit(solution)/shard_map/div | solution.py:384
  31.3 4.5 %all-to-all-start = ((f16[8,64,640]{2,1,0:T(8,128)(2,1)}), f16[8,64,640]{2,1,0:T(8,128)(2,1)S(1)}, u32[]{:S(2)}, u32[]{:S(2)}) async-start(f16[8,64,640]{2,1,0:T(8,128)(2,1)} %pad_maximum_fusion.1), calls=%async_computation | async-start | bytes 1310720 | tf_op jit(solution)/shard_map/all_to_all | solution.py:312
  35.9 1.5 collective-permute-start.5
  40.3 20.0 %collective-permute-done.5.refs_5_.refs_10_ = bf16[512,1024]{1,0:T(8,128)(2,1)S(1)} collective-permute-done((bf16[512,1024]{1,0:T(8,128)(2,1)}, bf16[512,1024]{1,0:T(8,128)(2,1)S(1)}, u32[]{:S(2)}, u32[]{:S(2)}) %collective-permute-start.5) | collective-permute-done | bytes 1048608 | tf_op jit(solution)/shard_map/ppermute | solution.py:309
  61.7 1.7 %collective-permute-start.9 = (bf16[256,1024]{1,0:T(8,128)(2,1)S(1)}, bf16[256,1024]{1,0:T(8,128)(2,1)S(1)}, u32[]{:S(2)}, u32[]{:S(2)}) collective-permute-start(bf16[256,1024]{1,0:T(8,128)(2,1)S(1)} %constant_dynamic-slice_fusion), channel_id=1, source_target_pairs={{0,4},{1,3},{4,8},{5,1},{8,12},{9,5},{12,14},{13,9},{14,10},{15,13... | collective-permute-start | bytes 1572872 | tf_op jit(solution)/shard_map/ppermute | solution.py:309
  63.4 9.6 %collective-permute-done.9.refs_7_.refs_12_ = bf16[256,1024]{1,0:T(8,128)(2,1)S(1)} collective-permute-done((bf16[256,1024]{1,0:T(8,128)(2,1)S(1)}, bf16[256,1024]{1,0:T(8,128)(2,1)S(1)}, u32[]{:S(2)}, u32[]{:S(2)}) %collective-permute-start.9) | collective-permute-done | bytes 524320 | tf_op jit(solution)/shard_map/ppermute | solution.py:309
  73.8 4.6 %all-to-all-start.1 = ((f16[8,64,640]{2,1,0:T(8,128)(2,1)}), f16[8,64,640]{2,1,0:T(8,128)(2,1)S(1)}, u32[]{:S(2)}, u32[]{:S(2)}) async-start(f16[8,64,640]{2,1,0:T(8,128)(2,1)} %pad_maximum_fusion.2), calls=%async_computation.1 | async-start | bytes 1310720 | tf_op jit(solution)/shard_map/all_to_all | solution.py:312
  79.3 16.0 %shard_map.132 = (f32[8,64,640]{2,1,0:T(8,128)}, f32[8,64,512]{2,1,0:T(8,128)}, f32[8,8,512]{2,1,0:T(8,128)}, f32[64,1024]{1,0:T(8,128)}, f32[64,1024]{1,0:T(8,128)}, /*index=5*/f32[64,1024]{1,0:T(8,128)}) custom-call(s32[9]{0:T(128)} %pad_add_fusion.table, f32[8,64,640]{2,1,0:T(8,128)} %convert_element_type.74.mass_in, bf16[512,1024]{1,0:T(8,128)(2,1)} %copy-done.8, ...), custom_call_target="tpu_custom_call" | custom-call | flops 15032385536 | bytes 16777216 | tf_op jit(solution)/shard_map/pallas_call | solution.py:253
  95.3 2.3 %convert_element_type.80 = f16[8,64,640]{2,1,0:T(8,128)(2,1)} convert(f32[8,64,640]{2,1,0:T(8,128)} %get-tuple-element.35.thirds_in) | non-fusion elementwise | flops 327680 | bytes 1966080 | tf_op jit(solution)/shard_map/convert_element_type | solution.py:381
  97.5 5.4 %all-to-all-start.3 = ((f16[8,64,640]{2,1,0:T(8,128)(2,1)}), f16[8,64,640]{2,1,0:T(8,128)(2,1)S(1)}, u32[]{:S(2)}, u32[]{:S(2)}) async-start(f16[8,64,640]{2,1,0:T(8,128)(2,1)} %convert_element_type.80), calls=%async_computation.3 | async-start | bytes 1310720 | tf_op jit(solution)/shard_map/all_to_all | solution.py:312
  104.2 15.8 %shard_map.133 = f32[8,64,640]{2,1,0:T(8,128)} custom-call(s32[9]{0:T(128)} %pad_add_fusion.table, f32[8,64,640]{2,1,0:T(8,128)} %convert_element_type.74.mass_in, f32[8,64,640]{2,1,0:T(8,128)} %convert_element_type.78.cot_in, f32[8,64,640]{2,1,0:T(8,128)} %get-tuple-element.35.thirds_in, f32[8,64,512]{2,1,0:T(8,128)} %get-tuple-element.36.refs_0_, ...), custom_call_target="tpu_custom_call" | custom-call | flops 10737418240 | bytes 16777216 | tf_op jit(solution)/shard_map/pallas_call | solution.py:253
  119.9 2.2 %convert_element_type.79 = f16[8,64,640]{2,1,0:T(8,128)(2,1)} convert(f32[8,64,640]{2,1,0:T(8,128)} %shard_map.133) | non-fusion elementwise | flops 327680 | bytes 1966080 | tf_op jit(solution)/shard_map/convert_element_type | solution.py:388
  122.2 5.4 %all-to-all-start.2 = ((f16[8,64,640]{2,1,0:T(8,128)(2,1)}), f16[8,64,640]{2,1,0:T(8,128)(2,1)S(1)}, u32[]{:S(2)}, u32[]{:S(2)}) async-start(f16[8,64,640]{2,1,0:T(8,128)(2,1)} %convert_element_type.79), calls=%async_computation.2 | async-start | bytes 1310720 | tf_op jit(solution)/shard_map/all_to_all | solution.py:312
  128.9 1.6 %copy.45 = f32[512,512]{0,1:T(8,128)S(1)} copy(f32[512,512]{1,0:T(8,128)} %slice.18) | data formatting | bytes 2097152
  132.3 1.5 collective-permute-start.11
  133.8 2.5 %fusion = f32[512,512]{1,0:T(8,128)} fusion(f32[512,512]{1,0:T(8,128)} %param.10, f32[512,512]{0,1:T(8,128)S(1)} %copy.45), kind=kLoop, calls=%fused_computation.5 | loop fusion | flops 262144 | bytes 3145728 | tf_op jit(solution)/shard_map/log | solution.py:382
  137.1 6.2 %all-to-all-done.2 = f16[8,64,640]{2,1,0:T(8,128)(2,1)S(1)} async-done(((f16[8,64,640]{2,1,0:T(8,128)(2,1)}), f16[8,64,640]{2,1,0:T(8,128)(2,1)S(1)}, u32[]{:S(2)}, u32[]{:S(2)}) %all-to-all-start.2) | async-done | bytes 655392 | tf_op jit(solution)/shard_map/all_to_all | solution.py:312
  144.6 1.6 %copy.46 = f32[512,512]{0,1:T(8,128)S(1)} copy(f32[512,512]{1,0:T(8,128)} %slice.20) | data formatting | bytes 2097152
  146.4 2.7 %collective-permute-start.12 = (f16[64,512]{1,0:T(8,128)(2,1)S(1)}, f16[64,512]{1,0:T(8,128)(2,1)S(1)}, u32[]{:S(2)}, u32[]{:S(2)}) collective-permute-start(f16[64,512]{1,0:T(8,128)(2,1)S(1)} %fusion.7), channel_id=1, source_target_pairs={{0,1},{1,0},{2,3},{3,2},{4,5},{5,4},{6,7},{7,6},{8,9},{9,8},{10,11... | collective-permute-start | bytes 196616 | tf_op jit(solution)/shard_map/ppermute | solution.py:277
  (93 shorter events, 25.3 us)
Async XLA Ops:
  3.2 2.0 %collective-permute-start = (bf16[512,512]{1,0:T(8,128)(2,1)S(1)}, bf16[512,512]{1,0:T(8,128)(2,1)S(1)}, u32[]{:S(2)}, u32[]{:S(2)}) collective-permute-start(bf16[512,512]{1,0:T(8,128)(2,1)S(1)} %bitcast.78), channel_id=1, source_target_pairs={{0,1},{1,0},{2,3},{3,2},{4,5},{5,4},{6,7},{7,6},{8,9},{9,8},{10,11... | collective-permute-start | bytes 1572872 | tf_op jit(solution)/shard_map/ppermute | solution.py:277
  5.4 20.2 %copy-start.8 = (bf16[512,1024]{1,0:T(8,128)(2,1)}, bf16[512,1024]{1,0:T(8,128)(2,1)S(1)}, u32[]{:S(2)}) copy-start(bf16[512,1024]{1,0:T(8,128)(2,1)S(1)} %pad_maximum_fusion.refs_0_.refs_5_) | copy-start | bytes 3145732
  5.4 19.1 %copy-start.6 = (f32[1,64,1024]{2,1,0:T(8,128)S(1)}, f32[1,64,1024]{2,1,0:T(8,128)}, u32[]{:S(2)}) copy-start(f32[1,64,1024]{2,1,0:T(8,128)} %param.11) | copy-start | bytes 786436
  5.4 15.1 %collective-permute-start.1 = (bf16[512,1024]{1,0:T(8,128)(2,1)S(1)}, bf16[512,1024]{1,0:T(8,128)(2,1)}, u32[]{:S(2)}, u32[]{:S(2)}) collective-permute-start(bf16[512,1024]{1,0:T(8,128)(2,1)S(1)} %pad_maximum_fusion.refs_0_.refs_5_), channel_id=1, source_target_pairs={{0,4},{1,3},{4,8},{5,1},{8,12},{9,5},{12,14},{13,9},{14,10},{15,13... | collective-permute-start | bytes 3145736 | tf_op jit(solution)/shard_map/ppermute | solution.py:309
  9.3 16.9 %copy-start.2 = (f32[512,512]{1,0:T(8,128)S(1)}, f32[512,512]{1,0:T(8,128)}, u32[]{:S(2)}) copy-start(f32[512,512]{1,0:T(8,128)} %param.10) | copy-start | bytes 3145732
  20.5 15.4 %collective-permute-start.2 = (bf16[512,1024]{1,0:T(8,128)(2,1)}, bf16[512,1024]{1,0:T(8,128)(2,1)}, u32[]{:S(2)}, u32[]{:S(2)}) collective-permute-start(bf16[512,1024]{1,0:T(8,128)(2,1)} %collective-permute-done.1.refs_1_.refs_6_), channel_id=1, source_target_pairs={{0,4},{1,3},{4,8},{5,1},{8,12},{9,5},{12,14},{13,9},{14,10},{15,13... | collective-permute-start | bytes 3145736 | tf_op jit(solution)/shard_map/ppermute | solution.py:309
  21.9 9.4 %collective-permute-start.3 = (bf16[512,1024]{1,0:T(8,128)(2,1)}, bf16[512,1024]{1,0:T(8,128)(2,1)}, u32[]{:S(2)}, u32[]{:S(2)}) collective-permute-start(bf16[512,1024]{1,0:T(8,128)(2,1)} %collective-permute-done.1.refs_1_.refs_6_), channel_id=1, source_target_pairs={{0,1},{1,0},{2,3},{3,2},{4,5},{5,4},{6,7},{7,6},{8,9},{9,8},{10,11... | collective-permute-start | bytes 3145736 | tf_op jit(solution)/shard_map/ppermute | solution.py:277
  24.4 4.7 %collective-permute-start.7 = (f16[64,512]{1,0:T(8,128)(2,1)}, f16[64,512]{1,0:T(8,128)(2,1)}, u32[]{:S(2)}, u32[]{:S(2)}) collective-permute-start(f16[64,512]{1,0:T(8,128)(2,1)} %bitcast.76), channel_id=1, source_target_pairs={{0,1},{1,0},{2,3},{3,2},{4,5},{5,4},{6,7},{7,6},{8,9},{9,8},{10,11... | collective-permute-start | bytes 196616 | tf_op jit(solution)/shard_map/ppermute | solution.py:277
  25.6 3.6 %collective-permute-start.4 = (f16[64,512]{1,0:T(8,128)(2,1)S(1)}, f16[64,512]{1,0:T(8,128)(2,1)S(1)}, u32[]{:S(2)}, u32[]{:S(2)}) collective-permute-start(f16[64,512]{1,0:T(8,128)(2,1)S(1)} %bitcast.90), channel_id=1, source_target_pairs={{0,1},{1,0},{2,3},{3,2},{4,5},{5,4},{6,7},{7,6},{8,9},{9,8},{10,11... | collective-permute-start | bytes 196616 | tf_op jit(solution)/shard_map/ppermute | solution.py:277
  31.3 29.0 %all-to-all-start = ((f16[8,64,640]{2,1,0:T(8,128)(2,1)}), f16[8,64,640]{2,1,0:T(8,128)(2,1)S(1)}, u32[]{:S(2)}, u32[]{:S(2)}) async-start(f16[8,64,640]{2,1,0:T(8,128)(2,1)} %pad_maximum_fusion.1), calls=%async_computation | async-start | bytes 1310720 | tf_op jit(solution)/shard_map/all_to_all | solution.py:312
  35.9 24.4 %collective-permute-start.5 = (bf16[512,1024]{1,0:T(8,128)(2,1)}, bf16[512,1024]{1,0:T(8,128)(2,1)S(1)}, u32[]{:S(2)}, u32[]{:S(2)}) collective-permute-start(bf16[512,1024]{1,0:T(8,128)(2,1)} %collective-permute-done.2.refs_3_.refs_8_), channel_id=1, source_target_pairs={{0,4},{1,3},{4,8},{5,1},{8,12},{9,5},{12,14},{13,9},{14,10},{15,13... | collective-permute-start | bytes 3145736 | tf_op jit(solution)/shard_map/ppermute | solution.py:309
  37.3 24.2 %collective-permute-start.6 = (bf16[512,1024]{1,0:T(8,128)(2,1)}, bf16[512,1024]{1,0:T(8,128)(2,1)}, u32[]{:S(2)}, u32[]{:S(2)}) collective-permute-start(bf16[512,1024]{1,0:T(8,128)(2,1)} %collective-permute-done.2.refs_3_.refs_8_), channel_id=1, source_target_pairs={{0,1},{1,0},{2,3},{3,2},{4,5},{5,4},{6,7},{7,6},{8,9},{9,8},{10,11... | collective-permute-start | bytes 3145736 | tf_op jit(solution)/shard_map/ppermute | solution.py:277
  60.3 18.1 %collective-permute-start.8 = (bf16[512,1024]{1,0:T(8,128)(2,1)S(1)}, bf16[512,1024]{1,0:T(8,128)(2,1)}, u32[]{:S(2)}, u32[]{:S(2)}) collective-permute-start(bf16[512,1024]{1,0:T(8,128)(2,1)S(1)} %collective-permute-done.5.refs_5_.refs_10_), channel_id=1, source_target_pairs={{0,1},{1,0},{2,3},{3,2},{4,5},{5,4},{6,7},{7,6},{8,9},{9,8},{10,11... | collective-permute-start | bytes 3145736 | tf_op jit(solution)/shard_map/ppermute | solution.py:277
  61.7 11.3 %collective-permute-start.9 = (bf16[256,1024]{1,0:T(8,128)(2,1)S(1)}, bf16[256,1024]{1,0:T(8,128)(2,1)S(1)}, u32[]{:S(2)}, u32[]{:S(2)}) collective-permute-start(bf16[256,1024]{1,0:T(8,128)(2,1)S(1)} %constant_dynamic-slice_fusion), channel_id=1, source_target_pairs={{0,4},{1,3},{4,8},{5,1},{8,12},{9,5},{12,14},{13,9},{14,10},{15,13... | collective-permute-start | bytes 1572872 | tf_op jit(solution)/shard_map/ppermute | solution.py:309
  73.0 5.5 %copy-start.12 = (bf16[256,1024]{1,0:T(8,128)(2,1)}, bf16[256,1024]{1,0:T(8,128)(2,1)S(1)}, u32[]{:S(2)}) copy-start(bf16[256,1024]{1,0:T(8,128)(2,1)S(1)} %collective-permute-done.9.refs_7_.refs_12_) | copy-start | bytes 1572868
  73.0 5.4 %collective-permute-start.10 = (bf16[256,1024]{1,0:T(8,128)(2,1)S(1)}, bf16[256,1024]{1,0:T(8,128)(2,1)S(1)}, u32[]{:S(2)}, u32[]{:S(2)}) collective-permute-start(bf16[256,1024]{1,0:T(8,128)(2,1)S(1)} %collective-permute-done.9.refs_7_.refs_12_), channel_id=1, source_target_pairs={{0,1},{1,0},{2,3},{3,2},{4,5},{5,4},{6,7},{7,6},{8,9},{9,8},{10,11... | collective-permute-start | bytes 1572872 | tf_op jit(solution)/shard_map/ppermute | solution.py:277
  73.8 23.7 %all-to-all-start.1 = ((f16[8,64,640]{2,1,0:T(8,128)(2,1)}), f16[8,64,640]{2,1,0:T(8,128)(2,1)S(1)}, u32[]{:S(2)}, u32[]{:S(2)}) async-start(f16[8,64,640]{2,1,0:T(8,128)(2,1)} %pad_maximum_fusion.2), calls=%async_computation.1 | async-start | bytes 1310720 | tf_op jit(solution)/shard_map/all_to_all | solution.py:312
  97.5 24.6 %all-to-all-start.3 = ((f16[8,64,640]{2,1,0:T(8,128)(2,1)}), f16[8,64,640]{2,1,0:T(8,128)(2,1)S(1)}, u32[]{:S(2)}, u32[]{:S(2)}) async-start(f16[8,64,640]{2,1,0:T(8,128)(2,1)} %convert_element_type.80), calls=%async_computation.3 | async-start | bytes 1310720 | tf_op jit(solution)/shard_map/all_to_all | solution.py:312
  122.2 21.1 %all-to-all-start.2 = ((f16[8,64,640]{2,1,0:T(8,128)(2,1)}), f16[8,64,640]{2,1,0:T(8,128)(2,1)S(1)}, u32[]{:S(2)}, u32[]{:S(2)}) async-start(f16[8,64,640]{2,1,0:T(8,128)(2,1)} %convert_element_type.79), calls=%async_computation.2 | async-start | bytes 1310720 | tf_op jit(solution)/shard_map/all_to_all | solution.py:312
  132.3 4.0 %copy-start.5 = (f32[1,64,1024]{2,1,0:T(8,128)S(1)}, f32[1,64,1024]{2,1,0:T(8,128)}, u32[]{:S(2)}) copy-start(f32[1,64,1024]{2,1,0:T(8,128)} %param.16) | copy-start | bytes 786436
  132.3 4.0 %copy-start.7 = (f32[1,64,1024]{2,1,0:T(8,128)S(1)}, f32[1,64,1024]{2,1,0:T(8,128)}, u32[]{:S(2)}) copy-start(f32[1,64,1024]{2,1,0:T(8,128)} %param.11) | copy-start | bytes 786436
  132.3 3.9 %collective-permute-start.11 = (f16[64,512]{1,0:T(8,128)(2,1)S(1)}, f16[64,512]{1,0:T(8,128)(2,1)S(1)}, u32[]{:S(2)}, u32[]{:S(2)}) collective-permute-start(f16[64,512]{1,0:T(8,128)(2,1)S(1)} %fusion.6), channel_id=1, source_target_pairs={{0,1},{1,0},{2,3},{3,2},{4,5},{5,4},{6,7},{7,6},{8,9},{9,8},{10,11... | collective-permute-start | bytes 196616 | tf_op jit(solution)/shard_map/ppermute | solution.py:277
  144.6 4.5 %copy-start.3 = (f32[512,512]{1,0:T(8,128)S(1)}, f32[512,512]{1,0:T(8,128)}, u32[]{:S(2)}) copy-start(f32[512,512]{1,0:T(8,128)} %get-tuple-element.43) | copy-start | bytes 3145732
  146.4 3.9 %collective-permute-start.12 = (f16[64,512]{1,0:T(8,128)(2,1)S(1)}, f16[64,512]{1,0:T(8,128)(2,1)S(1)}, u32[]{:S(2)}, u32[]{:S(2)}) collective-permute-start(f16[64,512]{1,0:T(8,128)(2,1)S(1)} %fusion.7), channel_id=1, source_target_pairs={{0,1},{1,0},{2,3},{3,2},{4,5},{5,4},{6,7},{7,6},{8,9},{9,8},{10,11... | collective-permute-start | bytes 196616 | tf_op jit(solution)/shard_map/ppermute | solution.py:277
  (8 other events, 19.6 us)

commit v10 on v9

--- a/solution.py
+++ b/solution.py
@@ -21,18 +21,27 @@
     return list(range(count))
 
 
+def dense_kernel(cols, live, tiles, out):
+    keep = tiles.shape[1]
+    for r in range(tiles.shape[0]):
+        for c in range(CB_DEV):
+            block = jnp.zeros(tiles.shape[2:], jnp.float32)
+            for k in range(keep):
+                hit = jnp.logical_and(cols[r, k] == c, k < live[r, 0])
+                block += jnp.where(hit, 1.0, 0.0) * tiles[r, k].astype(jnp.float32)
+            side = tiles.shape[2]
+            out[r * side : (r + 1) * side, c * side : (c + 1) * side] = block.astype(jnp.bfloat16)
+
+
 def dense_blocks(kernel_tiles, tile_cols, tile_count):
-    keep = kernel_tiles.shape[1]
-    live = jnp.arange(keep, dtype=jnp.int32)[None, :] < tile_count
-    hits = (tile_cols[:, :, None] == jnp.arange(CB_DEV, dtype=jnp.int32)) & live[:, :, None]
-    blocks = jnp.einsum(
-        "rkc,rkab->racb",
-        hits.astype(jnp.bfloat16),
-        kernel_tiles,
-        preferred_element_type=jnp.float32,
-    )
-    rows, cols = blocks.shape[0] * blocks.shape[1], blocks.shape[2] * blocks.shape[3]
-    return blocks.astype(jnp.bfloat16).reshape(rows, cols)
+    blocks, _, side, _ = kernel_tiles.shape
+    return pl.pallas_call(
+        dense_kernel,
+        out_shape=jax.ShapeDtypeStruct((blocks * side, CB_DEV * side), jnp.bfloat16),
+        in_specs=[pl.BlockSpec(memory_space=pltpu.SMEM)] * 2
+        + [pl.BlockSpec(memory_space=pltpu.VMEM)],
+        out_specs=pl.BlockSpec(memory_space=pltpu.VMEM),
+    )(tile_cols, tile_count, kernel_tiles)
 
 
 def nt(x, y):
@@ -51,21 +60,24 @@
         self.hists = hists
         self.share = share
         self.lanes = rows + 2 * share
-        self.opposite = count // 2
+        self.halves = 2 if count <= 8 else 1
 
 
 class Arrivals:
     def __init__(self, s, table, units, matrix, sems, paired):
         self.count = s.count
-        self.copies = {
-            d: [pltpu.make_async_copy(units[d], matrix.at[d], sems.at[d])]
-            for d in range(s.count - 1)
-        }
+        self.copies = {d: [] for d in range(s.count)}
+        units = iter(units)
+        for d in range(s.count - 1):
+            parts = s.halves if d else 1
+            for part in range(parts):
+                size = s.rows // parts
+                target = matrix.at[d, pl.ds(part * size, size)]
+                self.copies[d].append(pltpu.make_async_copy(next(units), target, sems.at[d]))
         half, d = s.rows // 2, s.count - 1
-        self.copies[d] = []
-        for unit, side in zip(units[d:], (table[s.count], 1 - table[s.count])):
+        for side in (table[s.count], 1 - table[s.count]):
             target = matrix.at[d, pl.ds(pl.multiple_of(side * half, half), half)]
-            self.copies[d].append(pltpu.make_async_copy(unit, target, sems.at[d]))
+            self.copies[d].append(pltpu.make_async_copy(next(units), target, sems.at[d]))
         for d in range(s.count):
             k = table[d]
             for source, target in paired:
@@ -138,7 +150,8 @@
 
 
 def forward_kernel(s, table, mass_in, *refs):
-    units, refs = refs[: s.count + 1], refs[s.count + 1 :]
+    given = 3 + (s.count - 2) * s.halves
+    units, refs = refs[:given], refs[given:]
     thirds, leaving, (mass, matrix, sems, more_sems), state = refs[0], refs[1:6], refs[6:10], refs[10:]
     row_two, row_one, col_one, col_two, col_three = state
     arrived = Arrivals(s, table, units, matrix, sems, [(mass_in, mass)])
@@ -184,7 +197,8 @@
 
 
 def backward_kernel(s, table, mass_in, cot_in, thirds_in, *refs):
-    state_in, units, refs = refs[:5], refs[5 : 6 + s.count], refs[6 + s.count :]
+    given = 3 + (s.count - 2) * s.halves
+    state_in, units, refs = refs[:5], refs[5 : 5 + given], refs[5 + given :]
     out, (mass, matrix, sems, more_sems), state, (cot, thirds) = (
         refs[0],
         refs[1:5],
@@ -265,7 +279,7 @@
             *[pltpu.VMEM(state.shape, state.dtype) for state in scratch],
         ],
         cost_estimate=pl.CostEstimate(
-            flops=products * 2 * s.count * s.rows * 2 * s.cols * 256,
+            flops=products * 2 * s.count * s.rows * 2 * s.cols * s.hists,
             bytes_accessed=s.count * s.rows * 2 * s.cols * 4,
             transcendentals=0,
         ),
@@ -333,22 +347,43 @@
     unit = in_order(mine, swap_cores(mine), 1)
     mass_message = by_histogram(source_mass, target_mass[0])
     cot_message = by_histogram(source_cotangent * COT_SCALE, target_cotangent[0] * COT_SCALE)
+    half = rows // s.halves
+    heads = [unit[k * half : (k + 1) * half] for k in range(s.halves)]
+    came, swapped = {}, {}
+    for step in range(1, last):
+        for k in range(s.halves):
+            if step > 2:
+                heads[k], swapped[step - 2, k] = lax.optimization_barrier(
+                    (heads[k], swapped[step - 2, k])
+                )
+            if step == 2 and k == 0:
+                heads[k], table = lax.optimization_barrier((heads[k], table))
+            came[step, k] = heads[k] = onward(heads[k])
+            leaving = heads[k]
+            if step == last - 1 and k == 0:
+                mass_here = exchange(mass_message)
+                mass = mass_here.astype(jnp.float32)
+                leaving, mass = lax.optimization_barrier((leaving, mass))
+            swapped[step, k] = swap_cores(leaving)
+            if step == 1 and k == 0:
+                swapped[step, k], mass_message = lax.optimization_barrier(
+                    (swapped[step, k], mass_message)
+                )
+    if s.halves == 1:
+        piece = lax.dynamic_slice_in_dim(heads[0], core * (rows // 2), rows // 2, 0)
+    else:
+        piece = jnp.where(core == 0, heads[0], heads[1])
+    due = [swapped[last - 2, k] for k in range(s.halves)]
+    piece, due, cot_message, mass_here = lax.optimization_barrier(
+        (piece, due, cot_message, mass_here)
+    )
+    swapped.update({(last - 2, k): due[k] for k in range(s.halves)})
+    piece = onward(piece)
     units = [unit]
-    for step in range(1, last + 1):
-        if step == 2:
-            unit, table = lax.optimization_barrier((unit, table))
-            units[-1], mass_message = lax.optimization_barrier((units[-1], mass_message))
-        elif step == last:
-            mass = exchange(mass_message).astype(jnp.float32)
-            unit, units[-3], mass, cot_message = lax.optimization_barrier(
-                (unit, units[-3], mass, cot_message)
-            )
-        elif step > 2:
-            unit, units[-3] = lax.optimization_barrier((unit, units[-3]))
-        if step == last:
-            unit = lax.dynamic_slice_in_dim(unit, core * (rows // 2), rows // 2, 0)
-        unit = onward(unit)
-        units += [unit, swap_cores(unit)]
+    for step in range(1, last):
+        for part in (came, swapped):
+            units += [part[step, k] for k in range(s.halves)]
+    units += [piece, swap_cores(piece)]
     cot = exchange(cot_message).astype(jnp.float32)
 
     wide = jax.ShapeDtypeStruct((count, s.hists, s.lanes), jnp.float32)
@@ -362,7 +397,7 @@
     (grads,) = call(
         backward_kernel,
         s,
-        5,
+        20,
         [wide],
         [],
         table,

time: 152 us -> 160 us (1.053)
  starting transfers between devices: 35.5 us -> 58.7 us
  waiting for transfers between devices: 47.6 us -> 25.6 us
  other arithmetic: 20.4 us -> 25.2 us
  Pallas kernels: 31.8 us -> 33.8 us
    ppermute x4 -> x7, waiting for transfers between devices: 39.5 us -> 16.4 us  [onward(): return lax.ppermute(x, ('src', 'tgt'), pairs)]
    all_to_all x4, starting transfers between devices: 20 us -> 31 us  [exchange(): return lax.all_to_all(x, 'src', 0, 0, tiled=True)]
    ppermute x9 -> x12, starting transfers between devices: 8.46 us -> 15 us  [swap_cores(): return lax.ppermute(x, 'tgt', [(0, 1), (1, 0)])]
    ppermute x4 -> x7, starting transfers between devices: 7.02 us -> 12.7 us  [onward(): return lax.ppermute(x, ('src', 'tgt'), pairs)]
    all_to_all x4, waiting for transfers between devices: 6.21 us -> 8.55 us  [exchange(): return lax.all_to_all(x, 'src', 0, 0, tiled=True)]
    concatenate x1 -> x2, other arithmetic: 0.12 us -> 2.27 us  [in_order(): jnp.concatenate([jnp.where(core == 0, mine, other), jnp.where(core == 0,...]
    pallas_call x0 -> x1, Pallas kernels: none -> 2.04 us  [dense_blocks(): pl.pallas_call(dense_kernel, out_shape=jax.ShapeDtypeStruct((blocks * sid...]
    select_n x0 -> x2, other arithmetic: none -> 1.96 us  [the longest x1 1.89 us: local(): piece = jnp.where(core == 0, heads[0], heads[1])]
  transfers between devices with their start and end apart: 17 -> 23, of which waited for: 5 -> 8; matrix products, arithmetic and copies ran while one was open for 18% -> 21% of each run, Pallas kernels for 21% -> 20%
where the time goes in v10:
time: 160 us; the launch traced here: 159 us
  starting transfers between devices  58.7 us (37%)
  Pallas kernels  33.8 us (21%)
  waiting for transfers between devices  25.6 us (16%)
  other arithmetic  25.2 us (16%)
  local copies, waits for them, and re-layouts  14.4 us (9%)
    pallas_call x2, Pallas kernels, call(): pl.pallas_call(functools.partial(kernel, s), out_shape=[*vmem_outs, *hbm_...  31.7 us
    all_to_all x4, starting transfers between devices, exchange(): return lax.all_to_all(x, 'src', 0, 0, tiled=True)  31 us
    ppermute x7, waiting for transfers between devices, onward(): return lax.ppermute(x, ('src', 'tgt'), pairs)  16.4 us
    ppermute x12, starting transfers between devices, swap_cores(): return lax.ppermute(x, 'tgt', [(0, 1), (1, 0)])  15 us
    ppermute x7, starting transfers between devices, onward(): return lax.ppermute(x, ('src', 'tgt'), pairs)  12.7 us
    all_to_all x4, waiting for transfers between devices, exchange(): return lax.all_to_all(x, 'src', 0, 0, tiled=True)  8.55 us
    unnamed x33, local copies, waits for them, and re-layouts  5.11 us
    transpose x4, local copies, waits for them, and re-layouts, by_point(): target = flat[:, rows:].T.reshape(2, share, cols_here)  3.6 us
  transfers between devices with their start and end apart: 23, of which 8 were waited for; matrix products, arithmetic and copies ran while one was open for 21% of the time, Pallas kernels for 20%

profile of v10, /device:TPU:1, one launch (start us, length us, event | category | flops | bytes accessed | tf_op | source)
XLA Modules:
  0.0 158.6 jit_solution(8831281886640245218)
XLA Ops:
  2.0 2.0 %shard_map.129 = bf16[512,512]{1,0:T(8,128)(2,1)} custom-call(s32[2,2]{1,0:T(2,128)} %cols.1, s32[2,1]{1,0:T(2,128)} %copy.27.live, bf16[2,2,256,256]{3,2,1,0:T(8,128)(2,1)} %tiles.1), custom_call_target="tpu_custom_call" | custom-call | tf_op jit(solution)/shard_map/pallas_call | solution.py:38
  9.2 2.7 %collective-permute-start.1 = (bf16[256,1024]{1,0:T(8,128)(2,1)}, bf16[256,1024]{1,0:T(8,128)(2,1)}, u32[]{:S(2)}, u32[]{:S(2)}) collective-permute-start(bf16[256,1024]{1,0:T(8,128)(2,1)} %get-tuple-element.58), channel_id=1, source_target_pairs={{0,4},{1,3},{4,8},{5,1},{8,12},{9,5},{12,14},{13,9},{14,10},{15,13... | collective-permute-start | bytes 1572872 | tf_op jit(solution)/shard_map/ppermute | solution.py:323
  14.6 2.7 %fusion.10 = (f32[512,512]{1,0:T(8,128)}, f16[512,512]{0,1:T(8,128)(2,1)S(1)}, f16[512,512]{0,1:T(8,128)(2,1)}) fusion(f32[512,512]{1,0:T(8,128)} %param.15, f32[512,512]{1,0:T(8,128)S(1)} %copy-done.1), kind=kLoop, calls=%fused_computation.59 | loop fusion | flops 1048576 | bytes 4194304 | tf_op jit(solution)/shard_map/div | solution.py:419
  17.2 1.9 %collective-permute-done.1.refs_1_.refs_6_ = bf16[256,1024]{1,0:T(8,128)(2,1)} collective-permute-done((bf16[256,1024]{1,0:T(8,128)(2,1)}, bf16[256,1024]{1,0:T(8,128)(2,1)}, u32[]{:S(2)}, u32[]{:S(2)}) %collective-permute-start.1) | collective-permute-done | bytes 524320 | tf_op jit(solution)/shard_map/ppermute | solution.py:323
  22.4 1.7 %collective-permute-start.2 = (bf16[256,1024]{1,0:T(8,128)(2,1)}, bf16[256,1024]{1,0:T(8,128)(2,1)}, u32[]{:S(2)}, u32[]{:S(2)}) collective-permute-start(bf16[256,1024]{1,0:T(8,128)(2,1)} %collective-permute-done.1.refs_1_.refs_6_), channel_id=1, source_target_pairs={{0,4},{1,3},{4,8},{5,1},{8,12},{9,5},{12,14},{13,9},{14,10},{15,13... | collective-permute-start | bytes 1572872 | tf_op jit(solution)/shard_map/ppermute | solution.py:323
  25.3 1.7 %collective-permute-start.7 = (bf16[256,1024]{1,0:T(8,128)(2,1)}, bf16[256,1024]{1,0:T(8,128)(2,1)}, u32[]{:S(2)}, u32[]{:S(2)}) collective-permute-start(bf16[256,1024]{1,0:T(8,128)(2,1)} %collective-permute-done.6.refs_2_.refs_7_), channel_id=1, source_target_pairs={{0,4},{1,3},{4,8},{5,1},{8,12},{9,5},{12,14},{13,9},{14,10},{15,13... | collective-permute-start | bytes 1572872 | tf_op jit(solution)/shard_map/ppermute | solution.py:323
  28.3 4.7 %all-to-all-start = ((f16[8,64,640]{2,1,0:T(8,128)(2,1)}), f16[8,64,640]{2,1,0:T(8,128)(2,1)S(1)}, u32[]{:S(2)}, u32[]{:S(2)}) async-start(f16[8,64,640]{2,1,0:T(8,128)(2,1)} %pad_maximum_fusion.1), calls=%async_computation | async-start | bytes 1310720 | tf_op jit(solution)/shard_map/all_to_all | solution.py:326
  33.0 5.8 %collective-permute-done.7.refs_6_.refs_11_ = bf16[256,1024]{1,0:T(8,128)(2,1)} collective-permute-done((bf16[256,1024]{1,0:T(8,128)(2,1)}, bf16[256,1024]{1,0:T(8,128)(2,1)}, u32[]{:S(2)}, u32[]{:S(2)}) %collective-permute-start.7) | collective-permute-done | bytes 524320 | tf_op jit(solution)/shard_map/ppermute | solution.py:323
  38.8 2.2 %collective-permute-start.9 = (bf16[256,1024]{1,0:T(8,128)(2,1)}, bf16[256,1024]{1,0:T(8,128)(2,1)}, u32[]{:S(2)}, u32[]{:S(2)}) collective-permute-start(bf16[256,1024]{1,0:T(8,128)(2,1)} %collective-permute-done.7.refs_6_.refs_11_), channel_id=1, source_target_pairs={{0,4},{1,3},{4,8},{5,1},{8,12},{9,5},{12,14},{13,9},{14,10},{15,13... | collective-permute-start | bytes 1572872 | tf_op jit(solution)/shard_map/ppermute | solution.py:323
  41.0 2.7 %collective-permute-start.5 = (bf16[256,1024]{1,0:T(8,128)(2,1)}, bf16[256,1024]{1,0:T(8,128)(2,1)}, u32[]{:S(2)}, u32[]{:S(2)}) collective-permute-start(bf16[256,1024]{1,0:T(8,128)(2,1)} %collective-permute-done.2.refs_5_.refs_10_), channel_id=1, source_target_pairs={{0,4},{1,3},{4,8},{5,1},{8,12},{9,5},{12,14},{13,9},{14,10},{15,13... | collective-permute-start | bytes 1572872 | tf_op jit(solution)/shard_map/ppermute | solution.py:323
  43.7 5.5 %collective-permute-start.11 = (bf16[256,1024]{1,0:T(8,128)(2,1)}, bf16[256,1024]{1,0:T(8,128)(2,1)}, u32[]{:S(2)}, u32[]{:S(2)}) collective-permute-start(bf16[256,1024]{1,0:T(8,128)(2,1)} %collective-permute-done.7.refs_6_.refs_11_), channel_id=1, source_target_pairs={{0,1},{1,0},{2,3},{3,2},{4,5},{5,4},{6,7},{7,6},{8,9},{9,8},{10,11... | collective-permute-start | bytes 1572872 | tf_op jit(solution)/shard_map/ppermute | solution.py:291
  52.0 1.8 %collective-permute-done.9.refs_10_.refs_15_ = bf16[256,1024]{1,0:T(8,128)(2,1)} collective-permute-done((bf16[256,1024]{1,0:T(8,128)(2,1)}, bf16[256,1024]{1,0:T(8,128)(2,1)}, u32[]{:S(2)}, u32[]{:S(2)}) %collective-permute-start.9) | collective-permute-done | bytes 524320 | tf_op jit(solution)/shard_map/ppermute | solution.py:323
  53.8 5.3 %collective-permute-done.5.refs_9_.refs_14_ = bf16[256,1024]{1,0:T(8,128)(2,1)} collective-permute-done((bf16[256,1024]{1,0:T(8,128)(2,1)}, bf16[256,1024]{1,0:T(8,128)(2,1)}, u32[]{:S(2)}, u32[]{:S(2)}) %collective-permute-start.5) | collective-permute-done | bytes 524320 | tf_op jit(solution)/shard_map/ppermute | solution.py:323
  59.1 1.9 %broadcast_select_fusion = bf16[256,1024]{1,0:T(8,128)(2,1)} fusion(bf16[256,1024]{1,0:T(8,128)(2,1)} %collective-permute-done.5.refs_9_.refs_14_, bf16[256,1024]{1,0:T(8,128)(2,1)} %collective-permute-done.9.refs_10_.refs_15_, pred[]{:T(512)S(6)} %eq.4), kind=kLoop, calls=%fused_computation.18 | loop fusion | flops 262144 | bytes 1572865 | tf_op jit(solution)/shard_map/jit(_where)/select_n | solution.py:375
  61.3 7.7 %all-to-all-start.1 = ((f16[8,64,640]{2,1,0:T(8,128)(2,1)}), f16[8,64,640]{2,1,0:T(8,128)(2,1)S(1)}, u32[]{:S(2)}, u32[]{:S(2)}) async-start(f16[8,64,640]{2,1,0:T(8,128)(2,1)} %pad_maximum_fusion.2), calls=%async_computation.1 | async-start | bytes 1310720 | tf_op jit(solution)/shard_map/all_to_all | solution.py:326
  72.7 3.1 %collective-permute-start.16 = (bf16[256,1024]{1,0:T(8,128)(2,1)}, bf16[256,1024]{1,0:T(8,128)(2,1)S(1)}, u32[]{:S(2)}, u32[]{:S(2)}) collective-permute-start(bf16[256,1024]{1,0:T(8,128)(2,1)} %collective-permute-done.15.refs_13_.refs_18_), channel_id=1, source_target_pairs={{0,1},{1,0},{2,3},{3,2},{4,5},{5,4},{6,7},{7,6},{8,9},{9,8},{10,11... | collective-permute-start | bytes 1572872 | tf_op jit(solution)/shard_map/ppermute | solution.py:291
  78.7 16.0 %shard_map.130 = (f32[8,64,640]{2,1,0:T(8,128)}, f32[8,64,512]{2,1,0:T(8,128)}, f32[8,8,512]{2,1,0:T(8,128)}, f32[64,1024]{1,0:T(8,128)}, f32[64,1024]{1,0:T(8,128)}, /*index=5*/f32[64,1024]{1,0:T(8,128)}) custom-call(s32[9]{0:T(128)} %pad_add_fusion.table, f32[8,64,640]{2,1,0:T(8,128)} %convert_element_type.65.mass_in, ...), custom_call_target="tpu_custom_call" | custom-call | flops 3758096384 | bytes 16777216 | tf_op jit(solution)/shard_map/pallas_call | solution.py:267
  94.6 2.2 %convert_element_type.71 = f16[8,64,640]{2,1,0:T(8,128)(2,1)} convert(f32[8,64,640]{2,1,0:T(8,128)} %get-tuple-element.43.thirds_in) | non-fusion elementwise | flops 327680 | bytes 1966080 | tf_op jit(solution)/shard_map/convert_element_type | solution.py:416
  96.9 13.2 %all-to-all-start.3 = ((f16[8,64,640]{2,1,0:T(8,128)(2,1)}), f16[8,64,640]{2,1,0:T(8,128)(2,1)S(1)}, u32[]{:S(2)}, u32[]{:S(2)}) async-start(f16[8,64,640]{2,1,0:T(8,128)(2,1)} %convert_element_type.71), calls=%async_computation.3 | async-start | bytes 1310720 | tf_op jit(solution)/shard_map/all_to_all | solution.py:326
  111.2 15.8 %shard_map.131 = f32[8,64,640]{2,1,0:T(8,128)} custom-call(s32[9]{0:T(128)} %pad_add_fusion.table, f32[8,64,640]{2,1,0:T(8,128)} %convert_element_type.65.mass_in, f32[8,64,640]{2,1,0:T(8,128)} %convert_element_type.69.cot_in, f32[8,64,640]{2,1,0:T(8,128)} %get-tuple-element.43.thirds_in, f32[8,64,512]{2,1,0:T(8,128)} %get-tuple-element.44.refs_0_, ...), custom_call_target="tpu_custom_call" | custom-call | flops 10737418240 | bytes 16777216 | tf_op jit(solution)/shard_map/pallas_call | solution.py:267
  127.0 2.2 %convert_element_type.70 = f16[8,64,640]{2,1,0:T(8,128)(2,1)} convert(f32[8,64,640]{2,1,0:T(8,128)} %shard_map.131) | non-fusion elementwise | flops 327680 | bytes 1966080 | tf_op jit(solution)/shard_map/convert_element_type | solution.py:423
  129.3 5.4 %all-to-all-start.2 = ((f16[8,64,640]{2,1,0:T(8,128)(2,1)}), f16[8,64,640]{2,1,0:T(8,128)(2,1)}, u32[]{:S(2)}, u32[]{:S(2)}) async-start(f16[8,64,640]{2,1,0:T(8,128)(2,1)} %convert_element_type.70), calls=%async_computation.2 | async-start | bytes 1310720 | tf_op jit(solution)/shard_map/all_to_all | solution.py:326
  142.5 8.5 %all-to-all-done.2 = f16[8,64,640]{2,1,0:T(8,128)(2,1)} async-done(((f16[8,64,640]{2,1,0:T(8,128)(2,1)}), f16[8,64,640]{2,1,0:T(8,128)(2,1)}, u32[]{:S(2)}, u32[]{:S(2)}) %all-to-all-start.2) | async-done | bytes 655392 | tf_op jit(solution)/shard_map/all_to_all | solution.py:326
  154.5 2.1 %collective-permute-start.18 = (f16[64,512]{1,0:T(8,128)(2,1)S(1)}, f16[64,512]{1,0:T(8,128)(2,1)S(1)}, u32[]{:S(2)}, u32[]{:S(2)}) collective-permute-start(f16[64,512]{1,0:T(8,128)(2,1)S(1)} %fusion.8), channel_id=1, source_target_pairs={{0,1},{1,0},{2,3},{3,2},{4,5},{5,4},{6,7},{7,6},{8,9},{9,8},{10,11... | collective-permute-start | bytes 196616 | tf_op jit(solution)/shard_map/ppermute | solution.py:291
  (103 shorter events, 38.6 us)
Async XLA Ops:
  4.0 3.9 %collective-permute-start = (bf16[512,512]{1,0:T(8,128)(2,1)}, bf16[512,512]{1,0:T(8,128)(2,1)S(1)}, u32[]{:S(2)}, u32[]{:S(2)}) collective-permute-start(bf16[512,512]{1,0:T(8,128)(2,1)} %shard_map.129), channel_id=1, source_target_pairs={{0,1},{1,0},{2,3},{3,2},{4,5},{5,4},{6,7},{7,6},{8,9},{9,8},{10,11... | collective-permute-start | bytes 1572872 | tf_op jit(solution)/shard_map/ppermute | solution.py:291
  5.6 15.2 %collective-permute-start.12 = (f16[64,512]{1,0:T(8,128)(2,1)S(1)}, f16[64,512]{1,0:T(8,128)(2,1)S(1)}, u32[]{:S(2)}, u32[]{:S(2)}) collective-permute-start(f16[64,512]{1,0:T(8,128)(2,1)S(1)} %bitcast.77), channel_id=1, source_target_pairs={{0,1},{1,0},{2,3},{3,2},{4,5},{5,4},{6,7},{7,6},{8,9},{9,8},{10,11... | collective-permute-start | bytes 196616 | tf_op jit(solution)/shard_map/ppermute | solution.py:291
  7.2 13.6 %collective-permute-start.4 = (f16[64,512]{1,0:T(8,128)(2,1)}, f16[64,512]{1,0:T(8,128)(2,1)}, u32[]{:S(2)}, u32[]{:S(2)}) collective-permute-start(f16[64,512]{1,0:T(8,128)(2,1)} %bitcast.67), channel_id=1, source_target_pairs={{0,1},{1,0},{2,3},{3,2},{4,5},{5,4},{6,7},{7,6},{8,9},{9,8},{10,11... | collective-permute-start | bytes 196616 | tf_op jit(solution)/shard_map/ppermute | solution.py:291
  9.2 9.9 %collective-permute-start.1 = (bf16[256,1024]{1,0:T(8,128)(2,1)}, bf16[256,1024]{1,0:T(8,128)(2,1)}, u32[]{:S(2)}, u32[]{:S(2)}) collective-permute-start(bf16[256,1024]{1,0:T(8,128)(2,1)} %get-tuple-element.58), channel_id=1, source_target_pairs={{0,4},{1,3},{4,8},{5,1},{8,12},{9,5},{12,14},{13,9},{14,10},{15,13... | collective-permute-start | bytes 1572872 | tf_op jit(solution)/shard_map/ppermute | solution.py:323
  13.2 11.5 %collective-permute-start.6 = (bf16[256,1024]{1,0:T(8,128)(2,1)}, bf16[256,1024]{1,0:T(8,128)(2,1)}, u32[]{:S(2)}, u32[]{:S(2)}) collective-permute-start(bf16[256,1024]{1,0:T(8,128)(2,1)} %get-tuple-element.57), channel_id=1, source_target_pairs={{0,4},{1,3},{4,8},{5,1},{8,12},{9,5},{12,14},{13,9},{14,10},{15,13... | collective-permute-start | bytes 1572872 | tf_op jit(solution)/shard_map/ppermute | solution.py:323
  19.1 9.1 %collective-permute-start.3 = (bf16[256,1024]{1,0:T(8,128)(2,1)}, bf16[256,1024]{1,0:T(8,128)(2,1)}, u32[]{:S(2)}, u32[]{:S(2)}) collective-permute-start(bf16[256,1024]{1,0:T(8,128)(2,1)} %collective-permute-done.1.refs_1_.refs_6_), channel_id=1, source_target_pairs={{0,1},{1,0},{2,3},{3,2},{4,5},{5,4},{6,7},{7,6},{8,9},{9,8},{10,11... | collective-permute-start | bytes 1572872 | tf_op jit(solution)/shard_map/ppermute | solution.py:291
  22.4 18.6 %collective-permute-start.2 = (bf16[256,1024]{1,0:T(8,128)(2,1)}, bf16[256,1024]{1,0:T(8,128)(2,1)}, u32[]{:S(2)}, u32[]{:S(2)}) collective-permute-start(bf16[256,1024]{1,0:T(8,128)(2,1)} %collective-permute-done.1.refs_1_.refs_6_), channel_id=1, source_target_pairs={{0,4},{1,3},{4,8},{5,1},{8,12},{9,5},{12,14},{13,9},{14,10},{15,13... | collective-permute-start | bytes 1572872 | tf_op jit(solution)/shard_map/ppermute | solution.py:323
  24.8 8.2 %collective-permute-start.8 = (bf16[256,1024]{1,0:T(8,128)(2,1)}, bf16[256,1024]{1,0:T(8,128)(2,1)}, u32[]{:S(2)}, u32[]{:S(2)}) collective-permute-start(bf16[256,1024]{1,0:T(8,128)(2,1)} %collective-permute-done.6.refs_2_.refs_7_), channel_id=1, source_target_pairs={{0,1},{1,0},{2,3},{3,2},{4,5},{5,4},{6,7},{7,6},{8,9},{9,8},{10,11... | collective-permute-start | bytes 1572872 | tf_op jit(solution)/shard_map/ppermute | solution.py:291
  25.3 13.5 %collective-permute-start.7 = (bf16[256,1024]{1,0:T(8,128)(2,1)}, bf16[256,1024]{1,0:T(8,128)(2,1)}, u32[]{:S(2)}, u32[]{:S(2)}) collective-permute-start(bf16[256,1024]{1,0:T(8,128)(2,1)} %collective-permute-done.6.refs_2_.refs_7_), channel_id=1, source_target_pairs={{0,4},{1,3},{4,8},{5,1},{8,12},{9,5},{12,14},{13,9},{14,10},{15,13... | collective-permute-start | bytes 1572872 | tf_op jit(solution)/shard_map/ppermute | solution.py:323
  28.3 22.5 %copy-start.8 = (f16[64,512]{1,0:T(8,128)(2,1)S(1)}, f16[64,512]{1,0:T(8,128)(2,1)}, u32[]{:S(2)}) copy-start(f16[64,512]{1,0:T(8,128)(2,1)} %get-tuple-element.68) | copy-start | bytes 196612
  28.3 32.7 %all-to-all-start = ((f16[8,64,640]{2,1,0:T(8,128)(2,1)}), f16[8,64,640]{2,1,0:T(8,128)(2,1)S(1)}, u32[]{:S(2)}, u32[]{:S(2)}) async-start(f16[8,64,640]{2,1,0:T(8,128)(2,1)} %pad_maximum_fusion.1), calls=%async_computation | async-start | bytes 1310720 | tf_op jit(solution)/shard_map/all_to_all | solution.py:326
  38.8 14.9 %collective-permute-start.9 = (bf16[256,1024]{1,0:T(8,128)(2,1)}, bf16[256,1024]{1,0:T(8,128)(2,1)}, u32[]{:S(2)}, u32[]{:S(2)}) collective-permute-start(bf16[256,1024]{1,0:T(8,128)(2,1)} %collective-permute-done.7.refs_6_.refs_11_), channel_id=1, source_target_pairs={{0,4},{1,3},{4,8},{5,1},{8,12},{9,5},{12,14},{13,9},{14,10},{15,13... | collective-permute-start | bytes 1572872 | tf_op jit(solution)/shard_map/ppermute | solution.py:323
  41.0 18.0 %collective-permute-start.5 = (bf16[256,1024]{1,0:T(8,128)(2,1)}, bf16[256,1024]{1,0:T(8,128)(2,1)}, u32[]{:S(2)}, u32[]{:S(2)}) collective-permute-start(bf16[256,1024]{1,0:T(8,128)(2,1)} %collective-permute-done.2.refs_5_.refs_10_), channel_id=1, source_target_pairs={{0,4},{1,3},{4,8},{5,1},{8,12},{9,5},{12,14},{13,9},{14,10},{15,13... | collective-permute-start | bytes 1572872 | tf_op jit(solution)/shard_map/ppermute | solution.py:323
  43.7 17.2 %collective-permute-start.11 = (bf16[256,1024]{1,0:T(8,128)(2,1)}, bf16[256,1024]{1,0:T(8,128)(2,1)}, u32[]{:S(2)}, u32[]{:S(2)}) collective-permute-start(bf16[256,1024]{1,0:T(8,128)(2,1)} %collective-permute-done.7.refs_6_.refs_11_), channel_id=1, source_target_pairs={{0,1},{1,0},{2,3},{3,2},{4,5},{5,4},{6,7},{7,6},{8,9},{9,8},{10,11... | collective-permute-start | bytes 1572872 | tf_op jit(solution)/shard_map/ppermute | solution.py:291
  49.2 11.8 %collective-permute-start.10 = (bf16[256,1024]{1,0:T(8,128)(2,1)}, bf16[256,1024]{1,0:T(8,128)(2,1)}, u32[]{:S(2)}, u32[]{:S(2)}) collective-permute-start(bf16[256,1024]{1,0:T(8,128)(2,1)} %collective-permute-done.2.refs_5_.refs_10_), channel_id=1, source_target_pairs={{0,1},{1,0},{2,3},{3,2},{4,5},{5,4},{6,7},{7,6},{8,9},{9,8},{10,11... | collective-permute-start | bytes 1572872 | tf_op jit(solution)/shard_map/ppermute | solution.py:291
  61.0 11.7 %collective-permute-start.15 = (bf16[256,1024]{1,0:T(8,128)(2,1)}, bf16[256,1024]{1,0:T(8,128)(2,1)}, u32[]{:S(2)}, u32[]{:S(2)}) collective-permute-start(bf16[256,1024]{1,0:T(8,128)(2,1)} %broadcast_select_fusion), channel_id=1, source_target_pairs={{0,4},{1,3},{4,8},{5,1},{8,12},{9,5},{12,14},{13,9},{14,10},{15,13... | collective-permute-start | bytes 1572872 | tf_op jit(solution)/shard_map/ppermute | solution.py:323
  61.3 35.6 %all-to-all-start.1 = ((f16[8,64,640]{2,1,0:T(8,128)(2,1)}), f16[8,64,640]{2,1,0:T(8,128)(2,1)S(1)}, u32[]{:S(2)}, u32[]{:S(2)}) async-start(f16[8,64,640]{2,1,0:T(8,128)(2,1)} %pad_maximum_fusion.2), calls=%async_computation.1 | async-start | bytes 1310720 | tf_op jit(solution)/shard_map/all_to_all | solution.py:326
  68.9 8.0 %collective-permute-start.14 = (bf16[256,1024]{1,0:T(8,128)(2,1)}, bf16[256,1024]{1,0:T(8,128)(2,1)S(1)}, u32[]{:S(2)}, u32[]{:S(2)}) collective-permute-start(bf16[256,1024]{1,0:T(8,128)(2,1)} %collective-permute-done.9.refs_10_.refs_15_), channel_id=1, source_target_pairs={{0,1},{1,0},{2,3},{3,2},{4,5},{5,4},{6,7},{7,6},{8,9},{9,8},{10,11... | collective-permute-start | bytes 1572872 | tf_op jit(solution)/shard_map/ppermute | solution.py:291
  71.7 5.2 %collective-permute-start.13 = (bf16[256,1024]{1,0:T(8,128)(2,1)}, bf16[256,1024]{1,0:T(8,128)(2,1)S(1)}, u32[]{:S(2)}, u32[]{:S(2)}) collective-permute-start(bf16[256,1024]{1,0:T(8,128)(2,1)} %collective-permute-done.5.refs_9_.refs_14_), channel_id=1, source_target_pairs={{0,1},{1,0},{2,3},{3,2},{4,5},{5,4},{6,7},{7,6},{8,9},{9,8},{10,11... | collective-permute-start | bytes 1572872 | tf_op jit(solution)/shard_map/ppermute | solution.py:291
  72.7 4.9 %collective-permute-start.16 = (bf16[256,1024]{1,0:T(8,128)(2,1)}, bf16[256,1024]{1,0:T(8,128)(2,1)S(1)}, u32[]{:S(2)}, u32[]{:S(2)}) collective-permute-start(bf16[256,1024]{1,0:T(8,128)(2,1)} %collective-permute-done.15.refs_13_.refs_18_), channel_id=1, source_target_pairs={{0,1},{1,0},{2,3},{3,2},{4,5},{5,4},{6,7},{7,6},{8,9},{9,8},{10,11... | collective-permute-start | bytes 1572872 | tf_op jit(solution)/shard_map/ppermute | solution.py:291
  96.9 32.4 %all-to-all-start.3 = ((f16[8,64,640]{2,1,0:T(8,128)(2,1)}), f16[8,64,640]{2,1,0:T(8,128)(2,1)S(1)}, u32[]{:S(2)}, u32[]{:S(2)}) async-start(f16[8,64,640]{2,1,0:T(8,128)(2,1)} %convert_element_type.71), calls=%async_computation.3 | async-start | bytes 1310720 | tf_op jit(solution)/shard_map/all_to_all | solution.py:326
  129.3 21.7 %all-to-all-start.2 = ((f16[8,64,640]{2,1,0:T(8,128)(2,1)}), f16[8,64,640]{2,1,0:T(8,128)(2,1)}, u32[]{:S(2)}, u32[]{:S(2)}) async-start(f16[8,64,640]{2,1,0:T(8,128)(2,1)} %convert_element_type.70), calls=%async_computation.2 | async-start | bytes 1310720 | tf_op jit(solution)/shard_map/all_to_all | solution.py:326
  139.4 2.2 %collective-permute-start.17 = (f16[64,512]{1,0:T(8,128)(2,1)S(1)}, f16[64,512]{1,0:T(8,128)(2,1)S(1)}, u32[]{:S(2)}, u32[]{:S(2)}) collective-permute-start(f16[64,512]{1,0:T(8,128)(2,1)S(1)} %fusion.7), channel_id=1, source_target_pairs={{0,1},{1,0},{2,3},{3,2},{4,5},{5,4},{6,7},{7,6},{8,9},{9,8},{10,11... | collective-permute-start | bytes 196616 | tf_op jit(solution)/shard_map/ppermute | solution.py:291
  154.5 3.3 %collective-permute-start.18 = (f16[64,512]{1,0:T(8,128)(2,1)S(1)}, f16[64,512]{1,0:T(8,128)(2,1)S(1)}, u32[]{:S(2)}, u32[]{:S(2)}) collective-permute-start(f16[64,512]{1,0:T(8,128)(2,1)S(1)} %fusion.8), channel_id=1, source_target_pairs={{0,1},{1,0},{2,3},{3,2},{4,5},{5,4},{6,7},{7,6},{8,9},{9,8},{10,11... | collective-permute-start | bytes 196616 | tf_op jit(solution)/shard_map/ppermute | solution.py:291
  (13 other events, 60.6 us)

commit v11 on v10

--- a/solution.py
+++ b/solution.py
@@ -21,27 +21,18 @@
     return list(range(count))
 
 
-def dense_kernel(cols, live, tiles, out):
-    keep = tiles.shape[1]
-    for r in range(tiles.shape[0]):
-        for c in range(CB_DEV):
-            block = jnp.zeros(tiles.shape[2:], jnp.float32)
-            for k in range(keep):
-                hit = jnp.logical_and(cols[r, k] == c, k < live[r, 0])
-                block += jnp.where(hit, 1.0, 0.0) * tiles[r, k].astype(jnp.float32)
-            side = tiles.shape[2]
-            out[r * side : (r + 1) * side, c * side : (c + 1) * side] = block.astype(jnp.bfloat16)
-
-
 def dense_blocks(kernel_tiles, tile_cols, tile_count):
-    blocks, _, side, _ = kernel_tiles.shape
-    return pl.pallas_call(
-        dense_kernel,
-        out_shape=jax.ShapeDtypeStruct((blocks * side, CB_DEV * side), jnp.bfloat16),
-        in_specs=[pl.BlockSpec(memory_space=pltpu.SMEM)] * 2
-        + [pl.BlockSpec(memory_space=pltpu.VMEM)],
-        out_specs=pl.BlockSpec(memory_space=pltpu.VMEM),
-    )(tile_cols, tile_count, kernel_tiles)
+    keep = kernel_tiles.shape[1]
+    live = jnp.arange(keep, dtype=jnp.int32)[None, :] < tile_count
+    hits = (tile_cols[:, :, None] == jnp.arange(CB_DEV, dtype=jnp.int32)) & live[:, :, None]
+    blocks = jnp.einsum(
+        "rkc,rkab->racb",
+        hits.astype(jnp.bfloat16),
+        kernel_tiles,
+        preferred_element_type=jnp.float32,
+    )
+    rows, cols = blocks.shape[0] * blocks.shape[1], blocks.shape[2] * blocks.shape[3]
+    return blocks.astype(jnp.bfloat16).reshape(rows, cols)
 
 
 def nt(x, y):
@@ -155,16 +146,20 @@
     thirds, leaving, (mass, matrix, sems, more_sems), state = refs[0], refs[1:6], refs[6:10], refs[10:]
     row_two, row_one, col_one, col_two, col_three = state
     arrived = Arrivals(s, table, units, matrix, sems, [(mass_in, mass)])
-    ones = jnp.ones((8, 2 * s.cols), jnp.bfloat16)
+    ones = jnp.ones((2 * s.cols, 128), jnp.bfloat16)
     zero = jnp.zeros((s.hists, 2 * s.cols), jnp.float32)
 
     def sums(d):
         arrived(d)
-        return nt(ones, matrix[d])
+        return nn(matrix[d], ones).T[0:8]
+
+    def times(panel):
+        turned = panel.T
+        return lambda d: nn(matrix[d], turned).T
 
     def first(d, row, total):
         row_one[d] = row
-        left = mass[table[d], :, : s.rows] / row[0:1]
+        left = mass[table[d], :, : s.rows] * (1 / row[0:1])
         return total + nn(left.astype(jnp.bfloat16), matrix[d])
 
     total = chain(s.count, sums, first, zero)
@@ -177,7 +172,7 @@
         left = mass[table[d], :, : s.rows] / row
         return total + nn(left.astype(jnp.bfloat16), matrix[d])
 
-    total = chain(s.count, lambda d: nt(panel, matrix[d]), second, zero)
+    total = chain(s.count, times(panel), second, zero)
     col_two[...] = total
     started = load(state[:4], leaving[:4], more_sems)
     last_panel = (target / total).astype(jnp.bfloat16)
@@ -187,7 +182,7 @@
         left = mass[table[d], :, : s.rows] / row
         return total + nn(left.astype(jnp.bfloat16), matrix[d])
 
-    total = chain(s.count, lambda d: nt(last_panel, matrix[d]), third, zero)
+    total = chain(s.count, times(last_panel), third, zero)
     col_three[...] = total
     last = pltpu.make_async_copy(col_three, leaving[4], more_sems.at[4])
     last.start()
@@ -227,11 +222,10 @@
 
     def third(d, grad, total):
         k = table[d]
-        row = thirds[k, :, : s.rows]
-        left = mass[k, :, : s.rows] / row
-        term = grad / row
+        over = 1 / thirds[k, :, : s.rows]
+        term = grad * over
         out[k, :, : s.rows] = term
-        rowgrad = -(cot[k, :, : s.rows] / row + term * left)
+        rowgrad = -over * (cot[k, :, : s.rows] + term * mass[k, :, : s.rows])
         return total + nn(rowgrad.astype(jnp.bfloat16), matrix[d])
 
     total = chain(s.count, first_product, third, zero)
@@ -245,10 +239,10 @@
 
     def second(d, grad, total):
         k = table[d]
-        row = row_two[d]
-        term = grad / row
+        over = 1 / row_two[d]
+        term = grad * over
         out[k, :, : s.rows] += term
-        rowgrad = -term * (mass[k, :, : s.rows] / row)
+        rowgrad = -term * (mass[k, :, : s.rows] * over)
         return total + nn(rowgrad.astype(jnp.bfloat16), matrix[d])
 
     total = chain(s.count, lambda d: nt(panel_two, matrix[d]), second, zero)
@@ -256,7 +250,7 @@
     panel_one = (-term_one * (target / col_one[...])).astype(jnp.bfloat16)
 
     def first(d, grad, carry):
-        out[table[d], :, : s.rows] += grad / row_one[d, 0:1]
+        out[table[d], :, : s.rows] += grad * (1 / row_one[d, 0:1])
         return carry
 
     chain(s.count, lambda d: nt(panel_one, matrix[d]), first, 0)
@@ -279,7 +273,7 @@
             *[pltpu.VMEM(state.shape, state.dtype) for state in scratch],
         ],
         cost_estimate=pl.CostEstimate(
-            flops=products * 2 * s.count * s.rows * 2 * s.cols * s.hists,
+            flops=products * 2 * s.count * s.rows * 2 * s.cols * 256,
             bytes_accessed=s.count * s.rows * 2 * s.cols * 4,
             transcendentals=0,
         ),
@@ -345,8 +339,11 @@
 
     mine = dense_blocks(kernel_tiles, tile_cols, tile_count)
     unit = in_order(mine, swap_cores(mine), 1)
-    mass_message = by_histogram(source_mass, target_mass[0])
-    cot_message = by_histogram(source_cotangent * COT_SCALE, target_cotangent[0] * COT_SCALE)
+    unit, mass_here, points_here, cot_here, cot_points = lax.optimization_barrier(
+        (unit, source_mass, target_mass[0], source_cotangent, target_cotangent[0])
+    )
+    mass_message = by_histogram(mass_here, points_here)
+    cot_message = by_histogram(cot_here * COT_SCALE, cot_points * COT_SCALE)
     half = rows // s.halves
     heads = [unit[k * half : (k + 1) * half] for k in range(s.halves)]
     came, swapped = {}, {}
@@ -397,7 +394,7 @@
     (grads,) = call(
         backward_kernel,
         s,
-        20,
+        5,
         [wide],
         [],
         table,

time: 160 us -> 153 us (0.956)
  starting transfers between devices: 58.7 us -> 51.1 us
  other arithmetic: 25.2 us -> 22.1 us
  waiting for transfers between devices: 25.6 us -> 28.3 us
    all_to_all x4, starting transfers between devices: 31 us -> 21 us  [exchange(): return lax.all_to_all(x, 'src', 0, 0, tiled=True)]
    ppermute x7, waiting for transfers between devices: 16.4 us -> 21.8 us  [onward(): return lax.ppermute(x, ('src', 'tgt'), pairs)]
    transpose x4, local copies, waits for them, and re-layouts: 3.6 us -> 0.29 us  [by_point(): target = flat[:, rows:].T.reshape(2, share, cols_here)]
    pallas_call x2, Pallas kernels: 31.7 us -> 34.2 us  [call(): pl.pallas_call(functools.partial(kernel, s), out_shape=[*vmem_outs, *hbm_...]
    concatenate x2 -> x1, other arithmetic: 2.27 us -> 0.12 us  [in_order(): jnp.concatenate([jnp.where(core == 0, mine, other), jnp.where(core == 0,...]
    pallas_call x1 -> x0, Pallas kernels: 2.04 us -> none  [dense_blocks(): pl.pallas_call(dense_kernel, out_shape=jax.ShapeDtypeStruct((blocks * sid...]
    all_to_all x4, waiting for transfers between devices: 8.55 us -> 6.52 us  [exchange(): return lax.all_to_all(x, 'src', 0, 0, tiled=True)]
    ppermute x7, starting transfers between devices: 12.7 us -> 14.7 us  [onward(): return lax.ppermute(x, ('src', 'tgt'), pairs)]
  transfers between devices with their start and end apart: 23 -> 23, of which waited for: 8 -> 6; matrix products, arithmetic and copies ran while one was open for 21% -> 18% of each run, Pallas kernels for 20% -> 22%
where the time goes in v11:
time: 153 us; the launch traced here: 152 us
  starting transfers between devices  51.1 us (33%)
  Pallas kernels  34.2 us (22%)
  waiting for transfers between devices  28.3 us (18%)
  other arithmetic  22.1 us (14%)
  local copies, waits for them, and re-layouts  13.9 us (9%)
    pallas_call x2, Pallas kernels, call(): pl.pallas_call(functools.partial(kernel, s), out_shape=[*vmem_outs, *hbm_...  34.2 us
    ppermute x7, waiting for transfers between devices, onward(): return lax.ppermute(x, ('src', 'tgt'), pairs)  21.8 us
    all_to_all x4, starting transfers between devices, exchange(): return lax.all_to_all(x, 'src', 0, 0, tiled=True)  21 us
    ppermute x12, starting transfers between devices, swap_cores(): return lax.ppermute(x, 'tgt', [(0, 1), (1, 0)])  15.4 us
    ppermute x7, starting transfers between devices, onward(): return lax.ppermute(x, ('src', 'tgt'), pairs)  14.7 us
    all_to_all x4, waiting for transfers between devices, exchange(): return lax.all_to_all(x, 'src', 0, 0, tiled=True)  6.52 us
    unnamed x35, local copies, waits for them, and re-layouts  5.96 us
  transfers between devices with their start and end apart: 23, of which 6 were waited for; matrix products, arithmetic and copies ran while one was open for 18% of the time, Pallas kernels for 22%

profile of v11, /device:TPU:1, one launch (start us, length us, event | category | flops | bytes accessed | tf_op | source)
XLA Modules:
  0.0 152.2 jit_solution(12907244877186396825)
XLA Ops:
  6.5 2.7 %collective-permute-start.1 = (bf16[256,1024]{1,0:T(8,128)(2,1)}, bf16[256,1024]{1,0:T(8,128)(2,1)}, u32[]{:S(2)}, u32[]{:S(2)}) collective-permute-start(bf16[256,1024]{1,0:T(8,128)(2,1)} %get-tuple-element.67), channel_id=1, source_target_pairs={{0,4},{1,3},{4,8},{5,1},{8,12},{9,5},{12,14},{13,9},{14,10},{15,13... | collective-permute-start | bytes 1572872 | tf_op jit(solution)/shard_map/ppermute | solution.py:317
  13.4 3.0 %collective-permute-done.1.refs_1_.refs_6_ = bf16[256,1024]{1,0:T(8,128)(2,1)} collective-permute-done((bf16[256,1024]{1,0:T(8,128)(2,1)}, bf16[256,1024]{1,0:T(8,128)(2,1)}, u32[]{:S(2)}, u32[]{:S(2)}) %collective-permute-start.1) | collective-permute-done | bytes 524320 | tf_op jit(solution)/shard_map/ppermute | solution.py:317
  19.6 1.6 %broadcast_select_fusion.4 = (f16[64,512]{1,0:T(8,128)(2,1)}, f16[64,512]{1,0:T(8,128)(2,1)}, f16[64,512]{1,0:T(8,128)(2,1)S(1)}, f16[64,512]{1,0:T(8,128)(2,1)S(1)}) fusion(f16[64,512]{1,0:T(8,128)(2,1)} %collective-permute-done.12, pred[]{:T(512)S(6)} %eq.10, f16[64,1,512]{2,1,0:T(2,128)(2,1)S(1)} %get-tuple-element.80, ...), kind=kLoop, calls=%fused_computation.40 | loop fusion | flops 131072 | bytes 524289 | tf_op jit(solution)/shard_map/jit(_where)/select_n | solution.py:324
  21.1 1.7 %collective-permute-start.2 = (bf16[256,1024]{1,0:T(8,128)(2,1)}, bf16[256,1024]{1,0:T(8,128)(2,1)}, u32[]{:S(2)}, u32[]{:S(2)}) collective-permute-start(bf16[256,1024]{1,0:T(8,128)(2,1)} %collective-permute-done.1.refs_1_.refs_6_), channel_id=1, source_target_pairs={{0,4},{1,3},{4,8},{5,1},{8,12},{9,5},{12,14},{13,9},{14,10},{15,13... | collective-permute-start | bytes 1572872 | tf_op jit(solution)/shard_map/ppermute | solution.py:317
  25.6 4.7 %all-to-all-start = ((f16[8,64,640]{2,1,0:T(8,128)(2,1)}), f16[8,64,640]{2,1,0:T(8,128)(2,1)S(1)}, u32[]{:S(2)}, u32[]{:S(2)}) async-start(f16[8,64,640]{2,1,0:T(8,128)(2,1)} %pad_maximum_fusion.1), calls=%async_computation | async-start | bytes 1310720 | tf_op jit(solution)/shard_map/all_to_all | solution.py:320
  30.3 7.1 %collective-permute-done.7.refs_6_.refs_11_ = bf16[256,1024]{1,0:T(8,128)(2,1)} collective-permute-done((bf16[256,1024]{1,0:T(8,128)(2,1)}, bf16[256,1024]{1,0:T(8,128)(2,1)}, u32[]{:S(2)}, u32[]{:S(2)}) %collective-permute-start.7) | collective-permute-done | bytes 524320 | tf_op jit(solution)/shard_map/ppermute | solution.py:317
  37.4 2.8 %collective-permute-start.9 = (bf16[256,1024]{1,0:T(8,128)(2,1)}, bf16[256,1024]{1,0:T(8,128)(2,1)}, u32[]{:S(2)}, u32[]{:S(2)}) collective-permute-start(bf16[256,1024]{1,0:T(8,128)(2,1)} %collective-permute-done.7.refs_6_.refs_11_), channel_id=1, source_target_pairs={{0,4},{1,3},{4,8},{5,1},{8,12},{9,5},{12,14},{13,9},{14,10},{15,13... | collective-permute-start | bytes 1572872 | tf_op jit(solution)/shard_map/ppermute | solution.py:317
  40.2 4.2 %collective-permute-start.5 = (bf16[256,1024]{1,0:T(8,128)(2,1)}, bf16[256,1024]{1,0:T(8,128)(2,1)}, u32[]{:S(2)}, u32[]{:S(2)}) collective-permute-start(bf16[256,1024]{1,0:T(8,128)(2,1)} %collective-permute-done.2.refs_5_.refs_10_), channel_id=1, source_target_pairs={{0,4},{1,3},{4,8},{5,1},{8,12},{9,5},{12,14},{13,9},{14,10},{15,13... | collective-permute-start | bytes 1572872 | tf_op jit(solution)/shard_map/ppermute | solution.py:317
  44.3 4.4 %collective-permute-start.11 = (bf16[256,1024]{1,0:T(8,128)(2,1)}, bf16[256,1024]{1,0:T(8,128)(2,1)}, u32[]{:S(2)}, u32[]{:S(2)}) collective-permute-start(bf16[256,1024]{1,0:T(8,128)(2,1)} %collective-permute-done.7.refs_6_.refs_11_), channel_id=1, source_target_pairs={{0,1},{1,0},{2,3},{3,2},{4,5},{5,4},{6,7},{7,6},{8,9},{9,8},{10,11... | collective-permute-start | bytes 1572872 | tf_op jit(solution)/shard_map/ppermute | solution.py:285
  51.9 5.3 %collective-permute-done.5.refs_9_.refs_14_ = bf16[256,1024]{1,0:T(8,128)(2,1)} collective-permute-done((bf16[256,1024]{1,0:T(8,128)(2,1)}, bf16[256,1024]{1,0:T(8,128)(2,1)}, u32[]{:S(2)}, u32[]{:S(2)}) %collective-permute-start.5) | collective-permute-done | bytes 524320 | tf_op jit(solution)/shard_map/ppermute | solution.py:317
  59.3 4.7 %collective-permute-start.14 = (bf16[256,1024]{1,0:T(8,128)(2,1)}, bf16[256,1024]{1,0:T(8,128)(2,1)}, u32[]{:S(2)}, u32[]{:S(2)}) collective-permute-start(bf16[256,1024]{1,0:T(8,128)(2,1)} %collective-permute-done.9.refs_10_.refs_15_), channel_id=1, source_target_pairs={{0,1},{1,0},{2,3},{3,2},{4,5},{5,4},{6,7},{7,6},{8,9},{9,8},{10,11... | collective-permute-start | bytes 1572872 | tf_op jit(solution)/shard_map/ppermute | solution.py:285
  65.1 4.9 %collective-permute-done.15.refs_13_.refs_18_ = bf16[256,1024]{1,0:T(8,128)(2,1)S(1)} collective-permute-done((bf16[256,1024]{1,0:T(8,128)(2,1)S(1)}, bf16[256,1024]{1,0:T(8,128)(2,1)S(1)}, u32[]{:S(2)}, u32[]{:S(2)}) %collective-permute-start.15) | collective-permute-done | bytes 524320 | tf_op jit(solution)/shard_map/ppermute | solution.py:317
  70.6 5.4 %all-to-all-start.1 = ((f16[8,64,640]{2,1,0:T(8,128)(2,1)}), f16[8,64,640]{2,1,0:T(8,128)(2,1)S(1)}, u32[]{:S(2)}, u32[]{:S(2)}) async-start(f16[8,64,640]{2,1,0:T(8,128)(2,1)} %pad_maximum_fusion.2), calls=%async_computation.1 | async-start | bytes 1310720 | tf_op jit(solution)/shard_map/all_to_all | solution.py:320
  76.9 18.5 %shard_map.132 = (f32[8,64,640]{2,1,0:T(8,128)}, f32[8,64,512]{2,1,0:T(8,128)}, f32[8,8,512]{2,1,0:T(8,128)}, f32[64,1024]{1,0:T(8,128)}, f32[64,1024]{1,0:T(8,128)}, /*index=5*/f32[64,1024]{1,0:T(8,128)}) custom-call(s32[9]{0:T(128)} %pad_add_fusion.table, f32[8,64,640]{2,1,0:T(8,128)} %convert_element_type.65.mass_in, bf16[512,1024]{1,0:T(8,128)(2,1)} %copy-done.4, ...), custom_call_target="tpu_custom_call" | custom-call | flops 15032385536 | bytes 16777216 | tf_op jit(solution)/shard_map/pallas_call | solution.py:261
  95.3 2.3 %convert_element_type.70 = f16[8,64,640]{2,1,0:T(8,128)(2,1)} convert(f32[8,64,640]{2,1,0:T(8,128)} %get-tuple-element.53.thirds_in) | non-fusion elementwise | flops 327680 | bytes 1966080 | tf_op jit(solution)/shard_map/convert_element_type | solution.py:413
  97.6 5.4 %all-to-all-start.3 = ((f16[8,64,640]{2,1,0:T(8,128)(2,1)}), f16[8,64,640]{2,1,0:T(8,128)(2,1)S(1)}, u32[]{:S(2)}, u32[]{:S(2)}) async-start(f16[8,64,640]{2,1,0:T(8,128)(2,1)} %convert_element_type.70), calls=%async_computation.3 | async-start | bytes 1310720 | tf_op jit(solution)/shard_map/all_to_all | solution.py:320
  104.3 15.8 %shard_map.133 = f32[8,64,640]{2,1,0:T(8,128)} custom-call(s32[9]{0:T(128)} %pad_add_fusion.table, f32[8,64,640]{2,1,0:T(8,128)} %convert_element_type.65.mass_in, f32[8,64,640]{2,1,0:T(8,128)} %convert_element_type.68.cot_in, f32[8,64,640]{2,1,0:T(8,128)} %get-tuple-element.53.thirds_in, f32[8,64,512]{2,1,0:T(8,128)} %get-tuple-element.54.refs_0_, ...), custom_call_target="tpu_custom_call" | custom-call | flops 10737418240 | bytes 16777216 | tf_op jit(solution)/shard_map/pallas_call | solution.py:261
  120.0 2.3 %convert_element_type.69 = f16[8,64,640]{2,1,0:T(8,128)(2,1)} convert(f32[8,64,640]{2,1,0:T(8,128)} %shard_map.133) | non-fusion elementwise | flops 327680 | bytes 1966080 | tf_op jit(solution)/shard_map/convert_element_type | solution.py:420
  122.3 5.4 %all-to-all-start.2 = ((f16[8,64,640]{2,1,0:T(8,128)(2,1)}), f16[8,64,640]{2,1,0:T(8,128)(2,1)}, u32[]{:S(2)}, u32[]{:S(2)}) async-start(f16[8,64,640]{2,1,0:T(8,128)(2,1)} %convert_element_type.69), calls=%async_computation.2 | async-start | bytes 1310720 | tf_op jit(solution)/shard_map/all_to_all | solution.py:320
  129.0 2.5 %copy.41 = f32[512,512]{0,1:T(8,128)} copy(f32[512,512]{1,0:T(8,128)} %slice.26) | data formatting | bytes 2097152
  133.2 2.9 %fusion.13 = (f32[512,512]{1,0:T(8,128)S(1)}, f32[512,512]{1,0:T(8,128)}) fusion(f32[512,512]{1,0:T(8,128)S(1)} %copy-done.2, f32[512,512]{1,0:T(8,128)} %param.10, f32[512,512]{0,1:T(8,128)} %copy.41), kind=kLoop, calls=%fused_computation.61 | loop fusion | flops 524288 | bytes 5242880 | tf_op jit(solution)/shard_map/div | solution.py:416
  137.0 6.5 %all-to-all-done.2 = f16[8,64,640]{2,1,0:T(8,128)(2,1)} async-done(((f16[8,64,640]{2,1,0:T(8,128)(2,1)}), f16[8,64,640]{2,1,0:T(8,128)(2,1)}, u32[]{:S(2)}, u32[]{:S(2)}) %all-to-all-start.2) | async-done | bytes 655392 | tf_op jit(solution)/shard_map/all_to_all | solution.py:320
  145.8 1.6 %copy.42 = f32[512,512]{0,1:T(8,128)S(1)} copy(f32[512,512]{1,0:T(8,128)} %slice.28) | data formatting | bytes 2097152
  147.6 2.7 %collective-permute-start.18 = (f16[64,512]{1,0:T(8,128)(2,1)S(1)}, f16[64,512]{1,0:T(8,128)(2,1)S(1)}, u32[]{:S(2)}, u32[]{:S(2)}) collective-permute-start(f16[64,512]{1,0:T(8,128)(2,1)S(1)} %fusion.7), channel_id=1, source_target_pairs={{0,1},{1,0},{2,3},{3,2},{4,5},{5,4},{6,7},{7,6},{8,9},{9,8},{10,11... | collective-permute-start | bytes 196616 | tf_op jit(solution)/shard_map/ppermute | solution.py:285
  (106 shorter events, 32.9 us)
Async XLA Ops:
  3.2 2.0 %collective-permute-start = (bf16[512,512]{1,0:T(8,128)(2,1)S(1)}, bf16[512,512]{1,0:T(8,128)(2,1)S(1)}, u32[]{:S(2)}, u32[]{:S(2)}) collective-permute-start(bf16[512,512]{1,0:T(8,128)(2,1)S(1)} %bitcast.78), channel_id=1, source_target_pairs={{0,1},{1,0},{2,3},{3,2},{4,5},{5,4},{6,7},{7,6},{8,9},{9,8},{10,11... | collective-permute-start | bytes 1572872 | tf_op jit(solution)/shard_map/ppermute | solution.py:285
  6.5 9.9 %collective-permute-start.1 = (bf16[256,1024]{1,0:T(8,128)(2,1)}, bf16[256,1024]{1,0:T(8,128)(2,1)}, u32[]{:S(2)}, u32[]{:S(2)}) collective-permute-start(bf16[256,1024]{1,0:T(8,128)(2,1)} %get-tuple-element.67), channel_id=1, source_target_pairs={{0,4},{1,3},{4,8},{5,1},{8,12},{9,5},{12,14},{13,9},{14,10},{15,13... | collective-permute-start | bytes 1572872 | tf_op jit(solution)/shard_map/ppermute | solution.py:317
  11.2 8.4 %collective-permute-start.12 = (f16[64,512]{1,0:T(8,128)(2,1)}, f16[64,512]{1,0:T(8,128)(2,1)}, u32[]{:S(2)}, u32[]{:S(2)}) collective-permute-start(f16[64,512]{1,0:T(8,128)(2,1)} %bitcast.76), channel_id=1, source_target_pairs={{0,1},{1,0},{2,3},{3,2},{4,5},{5,4},{6,7},{7,6},{8,9},{9,8},{10,11... | collective-permute-start | bytes 196616 | tf_op jit(solution)/shard_map/ppermute | solution.py:285
  11.9 7.6 %collective-permute-start.4 = (f16[64,512]{1,0:T(8,128)(2,1)S(1)}, f16[64,512]{1,0:T(8,128)(2,1)S(1)}, u32[]{:S(2)}, u32[]{:S(2)}) collective-permute-start(f16[64,512]{1,0:T(8,128)(2,1)S(1)} %bitcast.92), channel_id=1, source_target_pairs={{0,1},{1,0},{2,3},{3,2},{4,5},{5,4},{6,7},{7,6},{8,9},{9,8},{10,11... | collective-permute-start | bytes 196616 | tf_op jit(solution)/shard_map/ppermute | solution.py:285
  12.1 10.8 %collective-permute-start.6 = (bf16[256,1024]{1,0:T(8,128)(2,1)}, bf16[256,1024]{1,0:T(8,128)(2,1)}, u32[]{:S(2)}, u32[]{:S(2)}) collective-permute-start(bf16[256,1024]{1,0:T(8,128)(2,1)} %get-tuple-element.66), channel_id=1, source_target_pairs={{0,4},{1,3},{4,8},{5,1},{8,12},{9,5},{12,14},{13,9},{14,10},{15,13... | collective-permute-start | bytes 1572872 | tf_op jit(solution)/shard_map/ppermute | solution.py:317
  16.5 9.1 %collective-permute-start.3 = (bf16[256,1024]{1,0:T(8,128)(2,1)}, bf16[256,1024]{1,0:T(8,128)(2,1)}, u32[]{:S(2)}, u32[]{:S(2)}) collective-permute-start(bf16[256,1024]{1,0:T(8,128)(2,1)} %collective-permute-done.1.refs_1_.refs_6_), channel_id=1, source_target_pairs={{0,1},{1,0},{2,3},{3,2},{4,5},{5,4},{6,7},{7,6},{8,9},{9,8},{10,11... | collective-permute-start | bytes 1572872 | tf_op jit(solution)/shard_map/ppermute | solution.py:285
  21.1 19.0 %collective-permute-start.2 = (bf16[256,1024]{1,0:T(8,128)(2,1)}, bf16[256,1024]{1,0:T(8,128)(2,1)}, u32[]{:S(2)}, u32[]{:S(2)}) collective-permute-start(bf16[256,1024]{1,0:T(8,128)(2,1)} %collective-permute-done.1.refs_1_.refs_6_), channel_id=1, source_target_pairs={{0,4},{1,3},{4,8},{5,1},{8,12},{9,5},{12,14},{13,9},{14,10},{15,13... | collective-permute-start | bytes 1572872 | tf_op jit(solution)/shard_map/ppermute | solution.py:317
  22.9 7.4 %collective-permute-start.8 = (bf16[256,1024]{1,0:T(8,128)(2,1)}, bf16[256,1024]{1,0:T(8,128)(2,1)}, u32[]{:S(2)}, u32[]{:S(2)}) collective-permute-start(bf16[256,1024]{1,0:T(8,128)(2,1)} %collective-permute-done.6.refs_2_.refs_7_), channel_id=1, source_target_pairs={{0,1},{1,0},{2,3},{3,2},{4,5},{5,4},{6,7},{7,6},{8,9},{9,8},{10,11... | collective-permute-start | bytes 1572872 | tf_op jit(solution)/shard_map/ppermute | solution.py:285
  23.2 14.2 %collective-permute-start.7 = (bf16[256,1024]{1,0:T(8,128)(2,1)}, bf16[256,1024]{1,0:T(8,128)(2,1)}, u32[]{:S(2)}, u32[]{:S(2)}) collective-permute-start(bf16[256,1024]{1,0:T(8,128)(2,1)} %collective-permute-done.6.refs_2_.refs_7_), channel_id=1, source_target_pairs={{0,4},{1,3},{4,8},{5,1},{8,12},{9,5},{12,14},{13,9},{14,10},{15,13... | collective-permute-start | bytes 1572872 | tf_op jit(solution)/shard_map/ppermute | solution.py:317
  25.6 23.6 %copy-start.10 = (f16[64,512]{1,0:T(8,128)(2,1)S(1)}, f16[64,512]{1,0:T(8,128)(2,1)}, u32[]{:S(2)}) copy-start(f16[64,512]{1,0:T(8,128)(2,1)} %get-tuple-element.77) | copy-start | bytes 196612
  25.6 32.8 %all-to-all-start = ((f16[8,64,640]{2,1,0:T(8,128)(2,1)}), f16[8,64,640]{2,1,0:T(8,128)(2,1)S(1)}, u32[]{:S(2)}, u32[]{:S(2)}) async-start(f16[8,64,640]{2,1,0:T(8,128)(2,1)} %pad_maximum_fusion.1), calls=%async_computation | async-start | bytes 1310720 | tf_op jit(solution)/shard_map/all_to_all | solution.py:320
  37.4 14.5 %collective-permute-start.9 = (bf16[256,1024]{1,0:T(8,128)(2,1)}, bf16[256,1024]{1,0:T(8,128)(2,1)}, u32[]{:S(2)}, u32[]{:S(2)}) collective-permute-start(bf16[256,1024]{1,0:T(8,128)(2,1)} %collective-permute-done.7.refs_6_.refs_11_), channel_id=1, source_target_pairs={{0,4},{1,3},{4,8},{5,1},{8,12},{9,5},{12,14},{13,9},{14,10},{15,13... | collective-permute-start | bytes 1572872 | tf_op jit(solution)/shard_map/ppermute | solution.py:317
  40.2 17.1 %collective-permute-start.5 = (bf16[256,1024]{1,0:T(8,128)(2,1)}, bf16[256,1024]{1,0:T(8,128)(2,1)}, u32[]{:S(2)}, u32[]{:S(2)}) collective-permute-start(bf16[256,1024]{1,0:T(8,128)(2,1)} %collective-permute-done.2.refs_5_.refs_10_), channel_id=1, source_target_pairs={{0,4},{1,3},{4,8},{5,1},{8,12},{9,5},{12,14},{13,9},{14,10},{15,13... | collective-permute-start | bytes 1572872 | tf_op jit(solution)/shard_map/ppermute | solution.py:317
  44.3 14.0 %collective-permute-start.11 = (bf16[256,1024]{1,0:T(8,128)(2,1)}, bf16[256,1024]{1,0:T(8,128)(2,1)}, u32[]{:S(2)}, u32[]{:S(2)}) collective-permute-start(bf16[256,1024]{1,0:T(8,128)(2,1)} %collective-permute-done.7.refs_6_.refs_11_), channel_id=1, source_target_pairs={{0,1},{1,0},{2,3},{3,2},{4,5},{5,4},{6,7},{7,6},{8,9},{9,8},{10,11... | collective-permute-start | bytes 1572872 | tf_op jit(solution)/shard_map/ppermute | solution.py:285
  48.7 9.7 %collective-permute-start.10 = (bf16[256,1024]{1,0:T(8,128)(2,1)}, bf16[256,1024]{1,0:T(8,128)(2,1)}, u32[]{:S(2)}, u32[]{:S(2)}) collective-permute-start(bf16[256,1024]{1,0:T(8,128)(2,1)} %collective-permute-done.2.refs_5_.refs_10_), channel_id=1, source_target_pairs={{0,1},{1,0},{2,3},{3,2},{4,5},{5,4},{6,7},{7,6},{8,9},{9,8},{10,11... | collective-permute-start | bytes 1572872 | tf_op jit(solution)/shard_map/ppermute | solution.py:285
  58.4 11.6 %collective-permute-start.15 = (bf16[256,1024]{1,0:T(8,128)(2,1)S(1)}, bf16[256,1024]{1,0:T(8,128)(2,1)S(1)}, u32[]{:S(2)}, u32[]{:S(2)}) collective-permute-start(bf16[256,1024]{1,0:T(8,128)(2,1)S(1)} %broadcast_select_fusion), channel_id=1, source_target_pairs={{0,4},{1,3},{4,8},{5,1},{8,12},{9,5},{12,14},{13,9},{14,10},{15,13... | collective-permute-start | bytes 1572872 | tf_op jit(solution)/shard_map/ppermute | solution.py:317
  59.3 16.8 %collective-permute-start.14 = (bf16[256,1024]{1,0:T(8,128)(2,1)}, bf16[256,1024]{1,0:T(8,128)(2,1)}, u32[]{:S(2)}, u32[]{:S(2)}) collective-permute-start(bf16[256,1024]{1,0:T(8,128)(2,1)} %collective-permute-done.9.refs_10_.refs_15_), channel_id=1, source_target_pairs={{0,1},{1,0},{2,3},{3,2},{4,5},{5,4},{6,7},{7,6},{8,9},{9,8},{10,11... | collective-permute-start | bytes 1572872 | tf_op jit(solution)/shard_map/ppermute | solution.py:285
  65.1 10.9 %collective-permute-start.13 = (bf16[256,1024]{1,0:T(8,128)(2,1)}, bf16[256,1024]{1,0:T(8,128)(2,1)}, u32[]{:S(2)}, u32[]{:S(2)}) collective-permute-start(bf16[256,1024]{1,0:T(8,128)(2,1)} %collective-permute-done.5.refs_9_.refs_14_), channel_id=1, source_target_pairs={{0,1},{1,0},{2,3},{3,2},{4,5},{5,4},{6,7},{7,6},{8,9},{9,8},{10,11... | collective-permute-start | bytes 1572872 | tf_op jit(solution)/shard_map/ppermute | solution.py:285
  70.0 6.1 %collective-permute-start.16 = (bf16[256,1024]{1,0:T(8,128)(2,1)S(1)}, bf16[256,1024]{1,0:T(8,128)(2,1)S(1)}, u32[]{:S(2)}, u32[]{:S(2)}) collective-permute-start(bf16[256,1024]{1,0:T(8,128)(2,1)S(1)} %collective-permute-done.15.refs_13_.refs_18_), channel_id=1, source_target_pairs={{0,1},{1,0},{2,3},{3,2},{4,5},{5,4},{6,7},{7,6},{8,9},{9,8},{10,11... | collective-permute-start | bytes 1572872 | tf_op jit(solution)/shard_map/ppermute | solution.py:285
  70.6 27.0 %all-to-all-start.1 = ((f16[8,64,640]{2,1,0:T(8,128)(2,1)}), f16[8,64,640]{2,1,0:T(8,128)(2,1)S(1)}, u32[]{:S(2)}, u32[]{:S(2)}) async-start(f16[8,64,640]{2,1,0:T(8,128)(2,1)} %pad_maximum_fusion.2), calls=%async_computation.1 | async-start | bytes 1310720 | tf_op jit(solution)/shard_map/all_to_all | solution.py:320
  97.6 24.7 %all-to-all-start.3 = ((f16[8,64,640]{2,1,0:T(8,128)(2,1)}), f16[8,64,640]{2,1,0:T(8,128)(2,1)S(1)}, u32[]{:S(2)}, u32[]{:S(2)}) async-start(f16[8,64,640]{2,1,0:T(8,128)(2,1)} %convert_element_type.70), calls=%async_computation.3 | async-start | bytes 1310720 | tf_op jit(solution)/shard_map/all_to_all | solution.py:320
  122.3 21.2 %all-to-all-start.2 = ((f16[8,64,640]{2,1,0:T(8,128)(2,1)}), f16[8,64,640]{2,1,0:T(8,128)(2,1)}, u32[]{:S(2)}, u32[]{:S(2)}) async-start(f16[8,64,640]{2,1,0:T(8,128)(2,1)} %convert_element_type.69), calls=%async_computation.2 | async-start | bytes 1310720 | tf_op jit(solution)/shard_map/all_to_all | solution.py:320
  131.7 4.4 %collective-permute-start.17 = (f16[64,512]{1,0:T(8,128)(2,1)S(1)}, f16[64,512]{1,0:T(8,128)(2,1)S(1)}, u32[]{:S(2)}, u32[]{:S(2)}) collective-permute-start(f16[64,512]{1,0:T(8,128)(2,1)S(1)} %fusion.6), channel_id=1, source_target_pairs={{0,1},{1,0},{2,3},{3,2},{4,5},{5,4},{6,7},{7,6},{8,9},{9,8},{10,11... | collective-permute-start | bytes 196616 | tf_op jit(solution)/shard_map/ppermute | solution.py:285
  147.6 3.9 %collective-permute-start.18 = (f16[64,512]{1,0:T(8,128)(2,1)S(1)}, f16[64,512]{1,0:T(8,128)(2,1)S(1)}, u32[]{:S(2)}, u32[]{:S(2)}) collective-permute-start(f16[64,512]{1,0:T(8,128)(2,1)S(1)} %fusion.7), channel_id=1, source_target_pairs={{0,1},{1,0},{2,3},{3,2},{4,5},{5,4},{6,7},{7,6},{8,9},{9,8},{10,11... | collective-permute-start | bytes 196616 | tf_op jit(solution)/shard_map/ppermute | solution.py:285
  (14 other events, 74.9 us)

commit v12 on v11

--- a/solution.py
+++ b/solution.py
@@ -118,9 +118,9 @@
     )
 
 
-def scatter_targets(s, out, values):
+def scatter_targets(s, out, values, here=0):
     for i in range(s.count):
-        out[i, :, s.rows : s.lanes] = jnp.concatenate(
+        out[i ^ here, :, s.rows : s.lanes] = jnp.concatenate(
             [
                 values[:, t * s.cols + i * s.share : t * s.cols + (i + 1) * s.share]
                 for t in range(2)
@@ -146,16 +146,15 @@
     thirds, leaving, (mass, matrix, sems, more_sems), state = refs[0], refs[1:6], refs[6:10], refs[10:]
     row_two, row_one, col_one, col_two, col_three = state
     arrived = Arrivals(s, table, units, matrix, sems, [(mass_in, mass)])
-    ones = jnp.ones((2 * s.cols, 128), jnp.bfloat16)
+    ones = jnp.ones((8, 2 * s.cols), jnp.bfloat16)
     zero = jnp.zeros((s.hists, 2 * s.cols), jnp.float32)
 
     def sums(d):
         arrived(d)
-        return nn(matrix[d], ones).T[0:8]
+        return nt(ones, matrix[d])
 
     def times(panel):
-        turned = panel.T
-        return lambda d: nn(matrix[d], turned).T
+        return lambda d: nt(panel, matrix[d])
 
     def first(d, row, total):
         row_one[d] = row
@@ -201,6 +200,7 @@
         refs[10:],
     )
     row_two, row_one, col_one, col_two, col_three = state
+    here = table[0]
     early = load([state_in[4], cot_in], [col_three, cot], more_sems)
     paired = [(mass_in, mass), (thirds_in, thirds)]
     arrived = Arrivals(s, table, units, matrix, sems, paired)
@@ -224,7 +224,7 @@
         k = table[d]
         over = 1 / thirds[k, :, : s.rows]
         term = grad * over
-        out[k, :, : s.rows] = term
+        out[k ^ here, :, : s.rows] = term
         rowgrad = -over * (cot[k, :, : s.rows] + term * mass[k, :, : s.rows])
         return total + nn(rowgrad.astype(jnp.bfloat16), matrix[d])
 
@@ -241,7 +241,7 @@
         k = table[d]
         over = 1 / row_two[d]
         term = grad * over
-        out[k, :, : s.rows] += term
+        out[k ^ here, :, : s.rows] += term
         rowgrad = -term * (mass[k, :, : s.rows] * over)
         return total + nn(rowgrad.astype(jnp.bfloat16), matrix[d])
 
@@ -250,11 +250,11 @@
     panel_one = (-term_one * (target / col_one[...])).astype(jnp.bfloat16)
 
     def first(d, grad, carry):
-        out[table[d], :, : s.rows] += grad * (1 / row_one[d, 0:1])
+        out[table[d] ^ here, :, : s.rows] += grad * (1 / row_one[d, 0:1])
         return carry
 
     chain(s.count, lambda d: nt(panel_one, matrix[d]), first, 0)
-    scatter_targets(s, out, term_two + term_one)
+    scatter_targets(s, out, term_two + term_one, here)
 
 
 def call(kernel, s, products, vmem_outs, hbm_outs, table, arrays, scratch):
@@ -402,13 +402,22 @@
         [*states, wide, wide],
     )
 
+    def exchange_by_pairs(x):
+        parts = {0: x[0]}
+        for k in reversed(range(1, count)):
+            parts[k] = lax.ppermute(x[k], "src", [(i, i ^ k) for i in range(count)])
+        whole = jnp.zeros_like(x)
+        for k in (0, *reversed(range(1, count))):
+            whole = lax.dynamic_update_index_in_dim(whole, parts[k], me ^ k, 0)
+        return whole
+
     def by_point(pieces):
-        flat = pieces.reshape(cols_here, s.lanes).astype(jnp.float32)
-        target = flat[:, rows:].T.reshape(2, share, cols_here)
+        turned = pieces.reshape(cols_here, s.lanes).astype(jnp.float32).T
+        target = turned[rows:].reshape(2, share, cols_here)
         own = lax.dynamic_index_in_dim(target, core, 0, keepdims=False)
         other = lax.dynamic_index_in_dim(target, 1 - core, 0, keepdims=False)
         other = swap_cores(other.astype(HALF)).astype(jnp.float32)
-        return flat[:, :rows].T, in_order(own, other, 1)
+        return turned[:rows], in_order(own, other, 1)
 
     row_three, col_three = by_point(exchange(thirds.astype(HALF)))
     source_potential = jnp.log(source_mass / row_three)
@@ -417,7 +426,7 @@
     target_known = target_cotangent[0] / target_mass[0]
     back, source_potential, target_potential, source_known, target_known = lax.optimization_barrier(
         (
-            exchange(grads.astype(HALF)),
+            exchange_by_pairs(grads.astype(HALF)),
             source_potential,
             target_potential,
             source_known,

time: 153 us -> 168 us (1.098)
  waiting for transfers between devices: 28.3 us -> 38.4 us
  local copies, waits for them, and re-layouts: 13.9 us -> 18.1 us
  Pallas kernels: 34.2 us -> 32 us
  starting transfers between devices: 51.1 us -> 52.9 us
    ppermute x0 -> x7, waiting for transfers between devices: none -> 17.2 us  [exchange_by_pairs(): parts[k] = lax.ppermute(x[k], 'src', [(i, i ^ k) for i in range(count)])]
    ppermute x0 -> x7, starting transfers between devices: none -> 11.8 us  [exchange_by_pairs(): parts[k] = lax.ppermute(x[k], 'src', [(i, i ^ k) for i in range(count)])]
    all_to_all x4 -> x3, starting transfers between devices: 21 us -> 13.3 us  [exchange(): return lax.all_to_all(x, 'src', 0, 0, tiled=True)]
    all_to_all x4 -> x3, waiting for transfers between devices: 6.52 us -> 1.14 us  [exchange(): return lax.all_to_all(x, 'src', 0, 0, tiled=True)]
    pallas_call x2, Pallas kernels: 34.2 us -> 32 us  [call(): pl.pallas_call(functools.partial(kernel, s), out_shape=[*vmem_outs, *hbm_...]
    ppermute x7, starting transfers between devices: 14.7 us -> 12.6 us  [onward(): return lax.ppermute(x, ('src', 'tgt'), pairs)]
    slice x2 -> x3, local copies, waits for them, and re-layouts: 2.22 us -> 0.17 us  [by_point(): target = turned[rows:].reshape(2, share, cols_here)]
    ppermute x7, waiting for transfers between devices: 21.8 us -> 20 us  [onward(): return lax.ppermute(x, ('src', 'tgt'), pairs)]
  transfers between devices with their start and end apart: 23 -> 29, of which waited for: 6 -> 9; matrix products, arithmetic and copies ran while one was open for 18% -> 18% of each run, Pallas kernels for 22% -> 10%
where the time goes in v12:
time: 168 us; the launch traced here: 167 us
  starting transfers between devices  52.9 us (31%)
  waiting for transfers between devices  38.4 us (23%)
  Pallas kernels  32 us (19%)
  other arithmetic  22.9 us (14%)
  local copies, waits for them, and re-layouts  18.1 us (11%)
    pallas_call x2, Pallas kernels, call(): pl.pallas_call(functools.partial(kernel, s), out_shape=[*vmem_outs, *hbm_...  32 us
    ppermute x7, waiting for transfers between devices, onward(): return lax.ppermute(x, ('src', 'tgt'), pairs)  20 us
    ppermute x7, waiting for transfers between devices, exchange_by_pairs(): parts[k] = lax.ppermute(x[k], 'src', [(i, i ^ k) for i in range(count)])  17.2 us
    ppermute x12, starting transfers between devices, swap_cores(): return lax.ppermute(x, 'tgt', [(0, 1), (1, 0)])  15.1 us
    all_to_all x3, starting transfers between devices, exchange(): return lax.all_to_all(x, 'src', 0, 0, tiled=True)  13.3 us
    ppermute x7, starting transfers between devices, onward(): return lax.ppermute(x, ('src', 'tgt'), pairs)  12.6 us
    ppermute x7, starting transfers between devices, exchange_by_pairs(): parts[k] = lax.ppermute(x[k], 'src', [(i, i ^ k) for i in range(count)])  11.8 us
    unnamed x46, local copies, waits for them, and re-layouts  7.1 us
  transfers between devices with their start and end apart: 29, of which 9 were waited for; matrix products, arithmetic and copies ran while one was open for 18% of the time, Pallas kernels for 10%

profile of v12, /device:TPU:1, one launch (start us, length us, event | category | flops | bytes accessed | tf_op | source)
XLA Modules:
  0.0 166.7 jit_solution(887577585403693049)
XLA Ops:
  6.5 2.7 %collective-permute-start.1 = (bf16[256,1024]{1,0:T(8,128)(2,1)}, bf16[256,1024]{1,0:T(8,128)(2,1)}, u32[]{:S(2)}, u32[]{:S(2)}) collective-permute-start(bf16[256,1024]{1,0:T(8,128)(2,1)} %get-tuple-element.69), channel_id=1, source_target_pairs={{0,4},{1,3},{4,8},{5,1},{8,12},{9,5},{12,14},{13,9},{14,10},{15,13... | collective-permute-start | bytes 1572872 | tf_op jit(solution)/shard_map/ppermute | solution.py:317
  13.4 3.0 %collective-permute-done.1.refs_1_.refs_6_ = bf16[256,1024]{1,0:T(8,128)(2,1)} collective-permute-done((bf16[256,1024]{1,0:T(8,128)(2,1)}, bf16[256,1024]{1,0:T(8,128)(2,1)}, u32[]{:S(2)}, u32[]{:S(2)}) %collective-permute-start.1) | collective-permute-done | bytes 524320 | tf_op jit(solution)/shard_map/ppermute | solution.py:317
  26.2 4.4 %all-to-all-start = ((f16[8,64,640]{2,1,0:T(8,128)(2,1)}), f16[8,64,640]{2,1,0:T(8,128)(2,1)S(1)}, u32[]{:S(2)}, u32[]{:S(2)}) async-start(f16[8,64,640]{2,1,0:T(8,128)(2,1)} %pad_maximum_fusion.1), calls=%async_computation | async-start | bytes 1310720 | tf_op jit(solution)/shard_map/all_to_all | solution.py:320
  32.1 5.3 %collective-permute-done.7.refs_6_.refs_11_ = bf16[256,1024]{1,0:T(8,128)(2,1)} collective-permute-done((bf16[256,1024]{1,0:T(8,128)(2,1)}, bf16[256,1024]{1,0:T(8,128)(2,1)}, u32[]{:S(2)}, u32[]{:S(2)}) %collective-permute-start.7) | collective-permute-done | bytes 524320 | tf_op jit(solution)/shard_map/ppermute | solution.py:317
  37.4 3.3 %collective-permute-start.9 = (bf16[256,1024]{1,0:T(8,128)(2,1)}, bf16[256,1024]{1,0:T(8,128)(2,1)}, u32[]{:S(2)}, u32[]{:S(2)}) collective-permute-start(bf16[256,1024]{1,0:T(8,128)(2,1)} %collective-permute-done.7.refs_6_.refs_11_), channel_id=1, source_target_pairs={{0,4},{1,3},{4,8},{5,1},{8,12},{9,5},{12,14},{13,9},{14,10},{15,13... | collective-permute-start | bytes 1572872 | tf_op jit(solution)/shard_map/ppermute | solution.py:317
  40.7 5.9 %collective-permute-start.10 = (bf16[256,1024]{1,0:T(8,128)(2,1)}, bf16[256,1024]{1,0:T(8,128)(2,1)}, u32[]{:S(2)}, u32[]{:S(2)}) collective-permute-start(bf16[256,1024]{1,0:T(8,128)(2,1)} %collective-permute-done.2.refs_5_.refs_10_), channel_id=1, source_target_pairs={{0,1},{1,0},{2,3},{3,2},{4,5},{5,4},{6,7},{7,6},{8,9},{9,8},{10,11... | collective-permute-start | bytes 1572872 | tf_op jit(solution)/shard_map/ppermute | solution.py:285
  46.5 2.2 %copy.27 = f16[512,512]{1,0:T(8,128)(2,1)} copy(f16[512,512]{0,1:T(8,128)(2,1)} %get-tuple-element.96) | data formatting | bytes 1048576 | tf_op jit(solution)/shard_map/transpose | solution.py:334
  48.9 2.1 %pad_maximum_fusion.2 = f16[8,64,640]{2,1,0:T(8,128)(2,1)} fusion(f16[8,64,128]{2,1,0:T(8,128)(2,1)S(1)} %bitcast.112, f16[8,64,512]{2,1,0:T(8,128)(2,1)} %bitcast.104), kind=kLoop, calls=%fused_computation.10 | loop fusion | flops 327680 | bytes 1310720 | tf_op jit(solution)/shard_map/concatenate | solution.py:332
  52.1 5.3 %collective-permute-done.9.refs_10_.refs_15_ = bf16[256,1024]{1,0:T(8,128)(2,1)} collective-permute-done((bf16[256,1024]{1,0:T(8,128)(2,1)}, bf16[256,1024]{1,0:T(8,128)(2,1)}, u32[]{:S(2)}, u32[]{:S(2)}) %collective-permute-start.9) | collective-permute-done | bytes 524320 | tf_op jit(solution)/shard_map/ppermute | solution.py:317
  57.4 1.9 %broadcast_select_fusion = bf16[256,1024]{1,0:T(8,128)(2,1)} fusion(bf16[256,1024]{1,0:T(8,128)(2,1)} %collective-permute-done.5.refs_9_.refs_14_, bf16[256,1024]{1,0:T(8,128)(2,1)} %collective-permute-done.9.refs_10_.refs_15_, pred[]{:T(512)S(6)} %eq.10), kind=kLoop, calls=%fused_computation.14 | loop fusion | flops 262144 | bytes 1572865 | tf_op jit(solution)/shard_map/jit(_where)/select_n | solution.py:372
  60.2 4.7 %collective-permute-start.14 = (bf16[256,1024]{1,0:T(8,128)(2,1)}, bf16[256,1024]{1,0:T(8,128)(2,1)}, u32[]{:S(2)}, u32[]{:S(2)}) collective-permute-start(bf16[256,1024]{1,0:T(8,128)(2,1)} %collective-permute-done.9.refs_10_.refs_15_), channel_id=1, source_target_pairs={{0,1},{1,0},{2,3},{3,2},{4,5},{5,4},{6,7},{7,6},{8,9},{9,8},{10,11... | collective-permute-start | bytes 1572872 | tf_op jit(solution)/shard_map/ppermute | solution.py:285
  66.1 5.2 %collective-permute-done.15.refs_13_.refs_18_ = bf16[256,1024]{1,0:T(8,128)(2,1)} collective-permute-done((bf16[256,1024]{1,0:T(8,128)(2,1)}, bf16[256,1024]{1,0:T(8,128)(2,1)}, u32[]{:S(2)}, u32[]{:S(2)}) %collective-permute-start.15) | collective-permute-done | bytes 524320 | tf_op jit(solution)/shard_map/ppermute | solution.py:317
  71.9 5.4 %all-to-all-start.1 = ((f16[8,64,640]{2,1,0:T(8,128)(2,1)}), f16[8,64,640]{2,1,0:T(8,128)(2,1)S(1)}, u32[]{:S(2)}, u32[]{:S(2)}) async-start(f16[8,64,640]{2,1,0:T(8,128)(2,1)} %pad_maximum_fusion.2), calls=%async_computation.1 | async-start | bytes 1310720 | tf_op jit(solution)/shard_map/all_to_all | solution.py:320
  77.4 16.0 %shard_map.132 = (f32[8,64,640]{2,1,0:T(8,128)}, f32[8,64,512]{2,1,0:T(8,128)}, f32[8,8,512]{2,1,0:T(8,128)}, f32[64,1024]{1,0:T(8,128)}, f32[64,1024]{1,0:T(8,128)}, /*index=5*/f32[64,1024]{1,0:T(8,128)}) custom-call(s32[9]{0:T(128)} %pad_add_fusion.table, f32[8,64,640]{2,1,0:T(8,128)} %convert_element_type.61.mass_in, bf16[512,1024]{1,0:T(8,128)(2,1)} %copy-done.6, ...), custom_call_target="tpu_custom_call" | custom-call | flops 15032385536 | bytes 16777216 | tf_op jit(solution)/shard_map/pallas_call | solution.py:261
  95.7 16.0 %shard_map.133 = f32[8,64,640]{2,1,0:T(8,128)} custom-call(s32[9]{0:T(128)} %pad_add_fusion.table, f32[8,64,640]{2,1,0:T(8,128)} %convert_element_type.61.mass_in, f32[8,64,640]{2,1,0:T(8,128)} %convert_element_type.64.cot_in, f32[8,64,640]{2,1,0:T(8,128)} %get-tuple-element.53.thirds_in, f32[8,64,512]{2,1,0:T(8,128)} %get-tuple-element.54.refs_0_, ...), custom_call_target="tpu_custom_call" | custom-call | flops 10737418240 | bytes 16777216 | tf_op jit(solution)/shard_map/pallas_call | solution.py:261
  114.0 3.0 %collective-permute-start.17 = (f16[64,640]{1,0:T(8,128)(2,1)}, f16[64,640]{1,0:T(8,128)(2,1)}, u32[]{:S(2)}, u32[]{:S(2)}) collective-permute-start(f16[64,640]{1,0:T(8,128)(2,1)} %get-tuple-element.78), channel_id=1, source_target_pairs={{0,14},{2,12},{4,10},{6,8},{8,6},{10,4},{12,2},{14,0},{1,15},{3,13... | collective-permute-start | bytes 245768 | tf_op jit(solution)/shard_map/ppermute | solution.py:408
  119.6 2.5 %div.14 = f32[512,512]{0,1:T(8,128)} divide(f32[512,512]{0,1:T(8,128)S(1)} %copy-done.5, f32[512,512]{0,1:T(8,128)} %copy.33) | non-fusion elementwise | flops 262144 | bytes 3145728 | tf_op jit(solution)/shard_map/div | solution.py:425
  123.1 3.5 %all-to-all-start.2 = ((f16[8,64,640]{2,1,0:T(8,128)(2,1)}), f16[8,64,640]{2,1,0:T(8,128)(2,1)S(1)}, u32[]{:S(2)}, u32[]{:S(2)}) async-start(f16[8,64,640]{2,1,0:T(8,128)(2,1)} %convert_element_type.66), calls=%async_computation.2 | async-start | bytes 1310720 | tf_op jit(solution)/shard_map/all_to_all | solution.py:320
  126.7 3.2 %collective-permute-start.18 = (f16[64,640]{1,0:T(8,128)(2,1)S(1)}, f16[64,640]{1,0:T(8,128)(2,1)S(1)}, u32[]{:S(2)}, u32[]{:S(2)}) collective-permute-start(f16[64,640]{1,0:T(8,128)(2,1)S(1)} %copy-done.17), channel_id=1, source_target_pairs={{0,12},{2,14},{4,8},{6,10},{8,4},{10,6},{12,0},{14,2},{1,13},{3,15... | collective-permute-start | bytes 245768 | tf_op jit(solution)/shard_map/ppermute | solution.py:408
  130.1 3.0 %collective-permute-start.20 = (f16[64,640]{1,0:T(8,128)(2,1)S(1)}, f16[64,640]{1,0:T(8,128)(2,1)S(1)}, u32[]{:S(2)}, u32[]{:S(2)}) collective-permute-start(f16[64,640]{1,0:T(8,128)(2,1)S(1)} %copy-done.15), channel_id=1, source_target_pairs={{0,8},{2,10},{4,12},{6,14},{8,0},{10,2},{12,4},{14,6},{1,9},{3,11}... | collective-permute-start | bytes 245768 | tf_op jit(solution)/shard_map/ppermute | solution.py:408
  135.5 6.7 %collective-permute-done.18 = f16[64,640]{1,0:T(8,128)(2,1)S(1)} collective-permute-done((f16[64,640]{1,0:T(8,128)(2,1)S(1)}, f16[64,640]{1,0:T(8,128)(2,1)S(1)}, u32[]{:S(2)}, u32[]{:S(2)}) %collective-permute-start.18) | collective-permute-done | bytes 81952 | tf_op jit(solution)/shard_map/ppermute | solution.py:408
  143.2 9.6 %collective-permute-done.19 = f16[64,640]{1,0:T(8,128)(2,1)S(1)} collective-permute-done((f16[64,640]{1,0:T(8,128)(2,1)S(1)}, f16[64,640]{1,0:T(8,128)(2,1)S(1)}, u32[]{:S(2)}, u32[]{:S(2)}) %collective-permute-start.19) | collective-permute-done | bytes 81952 | tf_op jit(solution)/shard_map/ppermute | solution.py:408
  156.8 1.9 %collective-permute-start.24 = (f16[64,512]{1,0:T(8,128)(2,1)S(1)}, f16[64,512]{1,0:T(8,128)(2,1)S(1)}, u32[]{:S(2)}, u32[]{:S(2)}) collective-permute-start(f16[64,512]{1,0:T(8,128)(2,1)S(1)} %fusion.7), channel_id=1, source_target_pairs={{0,1},{1,0},{2,3},{3,2},{4,5},{5,4},{6,7},{7,6},{8,9},{9,8},{10,11... | collective-permute-start | bytes 196616 | tf_op jit(solution)/shard_map/ppermute | solution.py:285
  163.3 2.6 %copy.35 = f32[512,512]{1,0:T(8,128)} copy(f32[512,512]{0,1:T(8,128)} %fusion) | data formatting | bytes 2097152
  (137 shorter events, 46.1 us)
Async XLA Ops:
  6.5 9.9 %collective-permute-start.1 = (bf16[256,1024]{1,0:T(8,128)(2,1)}, bf16[256,1024]{1,0:T(8,128)(2,1)}, u32[]{:S(2)}, u32[]{:S(2)}) collective-permute-start(bf16[256,1024]{1,0:T(8,128)(2,1)} %get-tuple-element.69), channel_id=1, source_target_pairs={{0,4},{1,3},{4,8},{5,1},{8,12},{9,5},{12,14},{13,9},{14,10},{15,13... | collective-permute-start | bytes 1572872 | tf_op jit(solution)/shard_map/ppermute | solution.py:317
  10.4 9.3 %collective-permute-start.12 = (f16[64,512]{1,0:T(8,128)(2,1)S(1)}, f16[64,512]{1,0:T(8,128)(2,1)S(1)}, u32[]{:S(2)}, u32[]{:S(2)}) collective-permute-start(f16[64,512]{1,0:T(8,128)(2,1)S(1)} %bitcast.115), channel_id=1, source_target_pairs={{0,1},{1,0},{2,3},{3,2},{4,5},{5,4},{6,7},{7,6},{8,9},{9,8},{10,11... | collective-permute-start | bytes 196616 | tf_op jit(solution)/shard_map/ppermute | solution.py:285
  12.1 11.0 %collective-permute-start.6 = (bf16[256,1024]{1,0:T(8,128)(2,1)}, bf16[256,1024]{1,0:T(8,128)(2,1)}, u32[]{:S(2)}, u32[]{:S(2)}) collective-permute-start(bf16[256,1024]{1,0:T(8,128)(2,1)} %get-tuple-element.68), channel_id=1, source_target_pairs={{0,4},{1,3},{4,8},{5,1},{8,12},{9,5},{12,14},{13,9},{14,10},{15,13... | collective-permute-start | bytes 1572872 | tf_op jit(solution)/shard_map/ppermute | solution.py:317
  16.5 9.8 %collective-permute-start.3 = (bf16[256,1024]{1,0:T(8,128)(2,1)}, bf16[256,1024]{1,0:T(8,128)(2,1)}, u32[]{:S(2)}, u32[]{:S(2)}) collective-permute-start(bf16[256,1024]{1,0:T(8,128)(2,1)} %collective-permute-done.1.refs_1_.refs_6_), channel_id=1, source_target_pairs={{0,1},{1,0},{2,3},{3,2},{4,5},{5,4},{6,7},{7,6},{8,9},{9,8},{10,11... | collective-permute-start | bytes 1572872 | tf_op jit(solution)/shard_map/ppermute | solution.py:285
  21.3 9.3 %collective-permute-start.2 = (bf16[256,1024]{1,0:T(8,128)(2,1)}, bf16[256,1024]{1,0:T(8,128)(2,1)}, u32[]{:S(2)}, u32[]{:S(2)}) collective-permute-start(bf16[256,1024]{1,0:T(8,128)(2,1)} %collective-permute-done.1.refs_1_.refs_6_), channel_id=1, source_target_pairs={{0,4},{1,3},{4,8},{5,1},{8,12},{9,5},{12,14},{13,9},{14,10},{15,13... | collective-permute-start | bytes 1572872 | tf_op jit(solution)/shard_map/ppermute | solution.py:317
  23.1 14.3 %collective-permute-start.7 = (bf16[256,1024]{1,0:T(8,128)(2,1)}, bf16[256,1024]{1,0:T(8,128)(2,1)}, u32[]{:S(2)}, u32[]{:S(2)}) collective-permute-start(bf16[256,1024]{1,0:T(8,128)(2,1)} %collective-permute-done.6.refs_2_.refs_7_), channel_id=1, source_target_pairs={{0,4},{1,3},{4,8},{5,1},{8,12},{9,5},{12,14},{13,9},{14,10},{15,13... | collective-permute-start | bytes 1572872 | tf_op jit(solution)/shard_map/ppermute | solution.py:317
  24.4 13.0 %collective-permute-start.8 = (bf16[256,1024]{1,0:T(8,128)(2,1)}, bf16[256,1024]{1,0:T(8,128)(2,1)}, u32[]{:S(2)}, u32[]{:S(2)}) collective-permute-start(bf16[256,1024]{1,0:T(8,128)(2,1)} %collective-permute-done.6.refs_2_.refs_7_), channel_id=1, source_target_pairs={{0,1},{1,0},{2,3},{3,2},{4,5},{5,4},{6,7},{7,6},{8,9},{9,8},{10,11... | collective-permute-start | bytes 1572872 | tf_op jit(solution)/shard_map/ppermute | solution.py:285
  26.2 33.1 %all-to-all-start = ((f16[8,64,640]{2,1,0:T(8,128)(2,1)}), f16[8,64,640]{2,1,0:T(8,128)(2,1)S(1)}, u32[]{:S(2)}, u32[]{:S(2)}) async-start(f16[8,64,640]{2,1,0:T(8,128)(2,1)} %pad_maximum_fusion.1), calls=%async_computation | async-start | bytes 1310720 | tf_op jit(solution)/shard_map/all_to_all | solution.py:320
  30.6 21.5 %collective-permute-start.5 = (bf16[256,1024]{1,0:T(8,128)(2,1)}, bf16[256,1024]{1,0:T(8,128)(2,1)}, u32[]{:S(2)}, u32[]{:S(2)}) collective-permute-start(bf16[256,1024]{1,0:T(8,128)(2,1)} %collective-permute-done.2.refs_5_.refs_10_), channel_id=1, source_target_pairs={{0,4},{1,3},{4,8},{5,1},{8,12},{9,5},{12,14},{13,9},{14,10},{15,13... | collective-permute-start | bytes 1572872 | tf_op jit(solution)/shard_map/ppermute | solution.py:317
  37.4 20.0 %collective-permute-start.9 = (bf16[256,1024]{1,0:T(8,128)(2,1)}, bf16[256,1024]{1,0:T(8,128)(2,1)}, u32[]{:S(2)}, u32[]{:S(2)}) collective-permute-start(bf16[256,1024]{1,0:T(8,128)(2,1)} %collective-permute-done.7.refs_6_.refs_11_), channel_id=1, source_target_pairs={{0,4},{1,3},{4,8},{5,1},{8,12},{9,5},{12,14},{13,9},{14,10},{15,13... | collective-permute-start | bytes 1572872 | tf_op jit(solution)/shard_map/ppermute | solution.py:317
  40.7 18.7 %collective-permute-start.10 = (bf16[256,1024]{1,0:T(8,128)(2,1)}, bf16[256,1024]{1,0:T(8,128)(2,1)}, u32[]{:S(2)}, u32[]{:S(2)}) collective-permute-start(bf16[256,1024]{1,0:T(8,128)(2,1)} %collective-permute-done.2.refs_5_.refs_10_), channel_id=1, source_target_pairs={{0,1},{1,0},{2,3},{3,2},{4,5},{5,4},{6,7},{7,6},{8,9},{9,8},{10,11... | collective-permute-start | bytes 1572872 | tf_op jit(solution)/shard_map/ppermute | solution.py:285
  46.5 12.8 %collective-permute-start.11 = (bf16[256,1024]{1,0:T(8,128)(2,1)}, bf16[256,1024]{1,0:T(8,128)(2,1)}, u32[]{:S(2)}, u32[]{:S(2)}) collective-permute-start(bf16[256,1024]{1,0:T(8,128)(2,1)} %collective-permute-done.7.refs_6_.refs_11_), channel_id=1, source_target_pairs={{0,1},{1,0},{2,3},{3,2},{4,5},{5,4},{6,7},{7,6},{8,9},{9,8},{10,11... | collective-permute-start | bytes 1572872 | tf_op jit(solution)/shard_map/ppermute | solution.py:285
  59.4 11.9 %collective-permute-start.15 = (bf16[256,1024]{1,0:T(8,128)(2,1)}, bf16[256,1024]{1,0:T(8,128)(2,1)}, u32[]{:S(2)}, u32[]{:S(2)}) collective-permute-start(bf16[256,1024]{1,0:T(8,128)(2,1)} %broadcast_select_fusion), channel_id=1, source_target_pairs={{0,4},{1,3},{4,8},{5,1},{8,12},{9,5},{12,14},{13,9},{14,10},{15,13... | collective-permute-start | bytes 1572872 | tf_op jit(solution)/shard_map/ppermute | solution.py:317
  60.2 17.1 %collective-permute-start.14 = (bf16[256,1024]{1,0:T(8,128)(2,1)}, bf16[256,1024]{1,0:T(8,128)(2,1)}, u32[]{:S(2)}, u32[]{:S(2)}) collective-permute-start(bf16[256,1024]{1,0:T(8,128)(2,1)} %collective-permute-done.9.refs_10_.refs_15_), channel_id=1, source_target_pairs={{0,1},{1,0},{2,3},{3,2},{4,5},{5,4},{6,7},{7,6},{8,9},{9,8},{10,11... | collective-permute-start | bytes 1572872 | tf_op jit(solution)/shard_map/ppermute | solution.py:285
  66.1 11.3 %collective-permute-start.13 = (bf16[256,1024]{1,0:T(8,128)(2,1)}, bf16[256,1024]{1,0:T(8,128)(2,1)}, u32[]{:S(2)}, u32[]{:S(2)}) collective-permute-start(bf16[256,1024]{1,0:T(8,128)(2,1)} %collective-permute-done.5.refs_9_.refs_14_), channel_id=1, source_target_pairs={{0,1},{1,0},{2,3},{3,2},{4,5},{5,4},{6,7},{7,6},{8,9},{9,8},{10,11... | collective-permute-start | bytes 1572872 | tf_op jit(solution)/shard_map/ppermute | solution.py:285
  71.9 22.6 %all-to-all-start.1 = ((f16[8,64,640]{2,1,0:T(8,128)(2,1)}), f16[8,64,640]{2,1,0:T(8,128)(2,1)S(1)}, u32[]{:S(2)}, u32[]{:S(2)}) async-start(f16[8,64,640]{2,1,0:T(8,128)(2,1)} %pad_maximum_fusion.2), calls=%async_computation.1 | async-start | bytes 1310720 | tf_op jit(solution)/shard_map/all_to_all | solution.py:320
  114.0 19.1 %collective-permute-start.17 = (f16[64,640]{1,0:T(8,128)(2,1)}, f16[64,640]{1,0:T(8,128)(2,1)}, u32[]{:S(2)}, u32[]{:S(2)}) collective-permute-start(f16[64,640]{1,0:T(8,128)(2,1)} %get-tuple-element.78), channel_id=1, source_target_pairs={{0,14},{2,12},{4,10},{6,8},{8,6},{10,4},{12,2},{14,0},{1,15},{3,13... | collective-permute-start | bytes 245768 | tf_op jit(solution)/shard_map/ppermute | solution.py:408
  123.1 30.7 %all-to-all-start.2 = ((f16[8,64,640]{2,1,0:T(8,128)(2,1)}), f16[8,64,640]{2,1,0:T(8,128)(2,1)S(1)}, u32[]{:S(2)}, u32[]{:S(2)}) async-start(f16[8,64,640]{2,1,0:T(8,128)(2,1)} %convert_element_type.66), calls=%async_computation.2 | async-start | bytes 1310720 | tf_op jit(solution)/shard_map/all_to_all | solution.py:320
  126.7 15.6 %collective-permute-start.18 = (f16[64,640]{1,0:T(8,128)(2,1)S(1)}, f16[64,640]{1,0:T(8,128)(2,1)S(1)}, u32[]{:S(2)}, u32[]{:S(2)}) collective-permute-start(f16[64,640]{1,0:T(8,128)(2,1)S(1)} %copy-done.17), channel_id=1, source_target_pairs={{0,12},{2,14},{4,8},{6,10},{8,4},{10,6},{12,0},{14,2},{1,13},{3,15... | collective-permute-start | bytes 245768 | tf_op jit(solution)/shard_map/ppermute | solution.py:408
  129.8 22.9 %collective-permute-start.19 = (f16[64,640]{1,0:T(8,128)(2,1)S(1)}, f16[64,640]{1,0:T(8,128)(2,1)S(1)}, u32[]{:S(2)}, u32[]{:S(2)}) collective-permute-start(f16[64,640]{1,0:T(8,128)(2,1)S(1)} %copy-done.16), channel_id=1, source_target_pairs={{0,10},{2,8},{4,14},{6,12},{8,2},{10,0},{12,6},{14,4},{1,11},{3,9}... | collective-permute-start | bytes 245768 | tf_op jit(solution)/shard_map/ppermute | solution.py:408
  130.1 23.5 %collective-permute-start.20 = (f16[64,640]{1,0:T(8,128)(2,1)S(1)}, f16[64,640]{1,0:T(8,128)(2,1)S(1)}, u32[]{:S(2)}, u32[]{:S(2)}) collective-permute-start(f16[64,640]{1,0:T(8,128)(2,1)S(1)} %copy-done.15), channel_id=1, source_target_pairs={{0,8},{2,10},{4,12},{6,14},{8,0},{10,2},{12,4},{14,6},{1,9},{3,11}... | collective-permute-start | bytes 245768 | tf_op jit(solution)/shard_map/ppermute | solution.py:408
  133.1 20.5 %collective-permute-start.21 = (f16[64,640]{1,0:T(8,128)(2,1)S(1)}, f16[64,640]{1,0:T(8,128)(2,1)S(1)}, u32[]{:S(2)}, u32[]{:S(2)}) collective-permute-start(f16[64,640]{1,0:T(8,128)(2,1)S(1)} %get-tuple-element.74), channel_id=1, source_target_pairs={{0,6},{2,4},{4,2},{6,0},{8,14},{10,12},{12,10},{14,8},{1,7},{3,5},... | collective-permute-start | bytes 245768 | tf_op jit(solution)/shard_map/ppermute | solution.py:408
  133.1 20.6 %collective-permute-start.22 = (f16[64,640]{1,0:T(8,128)(2,1)S(1)}, f16[64,640]{1,0:T(8,128)(2,1)S(1)}, u32[]{:S(2)}, u32[]{:S(2)}) collective-permute-start(f16[64,640]{1,0:T(8,128)(2,1)S(1)} %get-tuple-element.73), channel_id=1, source_target_pairs={{0,4},{2,6},{4,0},{6,2},{8,12},{10,14},{12,8},{14,10},{1,5},{3,7},... | collective-permute-start | bytes 245768 | tf_op jit(solution)/shard_map/ppermute | solution.py:408
  142.2 11.5 %collective-permute-start.23 = (f16[64,640]{1,0:T(8,128)(2,1)S(1)}, f16[64,640]{1,0:T(8,128)(2,1)S(1)}, u32[]{:S(2)}, u32[]{:S(2)}) collective-permute-start(f16[64,640]{1,0:T(8,128)(2,1)S(1)} %get-tuple-element.72), channel_id=1, source_target_pairs={{0,2},{2,0},{4,6},{6,4},{8,10},{10,8},{12,14},{14,12},{1,3},{3,1},... | collective-permute-start | bytes 245768 | tf_op jit(solution)/shard_map/ppermute | solution.py:408
  (25 other events, 139.2 us)

commit v13 on v11

--- a/solution.py
+++ b/solution.py
@@ -58,17 +58,17 @@
     def __init__(self, s, table, units, matrix, sems, paired):
         self.count = s.count
         self.copies = {d: [] for d in range(s.count)}
+        core = table[s.count]
         units = iter(units)
-        for d in range(s.count - 1):
-            parts = s.halves if d else 1
+        for d in range(s.count):
+            parts = 2 if d == s.count - 1 else s.halves
+            size = s.rows // parts
             for part in range(parts):
-                size = s.rows // parts
-                target = matrix.at[d, pl.ds(part * size, size)]
+                first = 1 - core if d and d % 2 == 0 else core
+                side = first if part == 0 else 1 - first
+                start = pl.multiple_of(side * size, size) if parts > 1 else 0
+                target = matrix.at[d, pl.ds(start, size)]
                 self.copies[d].append(pltpu.make_async_copy(next(units), target, sems.at[d]))
-        half, d = s.rows // 2, s.count - 1
-        for side in (table[s.count], 1 - table[s.count]):
-            target = matrix.at[d, pl.ds(pl.multiple_of(side * half, half), half)]
-            self.copies[d].append(pltpu.make_async_copy(next(units), target, sems.at[d]))
         for d in range(s.count):
             k = table[d]
             for source, target in paired:
@@ -141,21 +141,20 @@
 
 
 def forward_kernel(s, table, mass_in, *refs):
-    given = 3 + (s.count - 2) * s.halves
+    given = 2 + (s.count - 1) * s.halves
     units, refs = refs[:given], refs[given:]
     thirds, leaving, (mass, matrix, sems, more_sems), state = refs[0], refs[1:6], refs[6:10], refs[10:]
     row_two, row_one, col_one, col_two, col_three = state
     arrived = Arrivals(s, table, units, matrix, sems, [(mass_in, mass)])
-    ones = jnp.ones((2 * s.cols, 128), jnp.bfloat16)
+    ones = jnp.ones((8, 2 * s.cols), jnp.bfloat16)
     zero = jnp.zeros((s.hists, 2 * s.cols), jnp.float32)
 
     def sums(d):
         arrived(d)
-        return nn(matrix[d], ones).T[0:8]
+        return nt(ones, matrix[d])
 
     def times(panel):
-        turned = panel.T
-        return lambda d: nn(matrix[d], turned).T
+        return lambda d: nt(panel, matrix[d])
 
     def first(d, row, total):
         row_one[d] = row
@@ -192,7 +191,7 @@
 
 
 def backward_kernel(s, table, mass_in, cot_in, thirds_in, *refs):
-    given = 3 + (s.count - 2) * s.halves
+    given = 2 + (s.count - 1) * s.halves
     state_in, units, refs = refs[:5], refs[5 : 5 + given], refs[5 + given :]
     out, (mass, matrix, sems, more_sems), state, (cot, thirds) = (
         refs[0],
@@ -338,14 +337,19 @@
         )
 
     mine = dense_blocks(kernel_tiles, tile_cols, tile_count)
-    unit = in_order(mine, swap_cores(mine), 1)
-    unit, mass_here, points_here, cot_here, cot_points = lax.optimization_barrier(
-        (unit, source_mass, target_mass[0], source_cotangent, target_cotangent[0])
-    )
+    theirs = swap_cores(mine)
+    half = rows // s.halves
+    heads = []
+    for k in range(s.halves):
+        start = half * jnp.where(core == 0, k, s.halves - 1 - k)
+        both = [lax.dynamic_slice_in_dim(x, start, half, 0) for x in (mine, theirs)]
+        heads.append(in_order(*both, 1))
+    heads, mass_here, points_here, cot_here, cot_points = lax.optimization_barrier(
+        (heads, source_mass, target_mass[0], source_cotangent, target_cotangent[0])
+    )
+    units = list(heads)
     mass_message = by_histogram(mass_here, points_here)
     cot_message = by_histogram(cot_here * COT_SCALE, cot_points * COT_SCALE)
-    half = rows // s.halves
-    heads = [unit[k * half : (k + 1) * half] for k in range(s.halves)]
     came, swapped = {}, {}
     for step in range(1, last):
         for k in range(s.halves):
@@ -369,14 +373,13 @@
     if s.halves == 1:
         piece = lax.dynamic_slice_in_dim(heads[0], core * (rows // 2), rows // 2, 0)
     else:
-        piece = jnp.where(core == 0, heads[0], heads[1])
+        piece = heads[0]
     due = [swapped[last - 2, k] for k in range(s.halves)]
     piece, due, cot_message, mass_here = lax.optimization_barrier(
         (piece, due, cot_message, mass_here)
     )
     swapped.update({(last - 2, k): due[k] for k in range(s.halves)})
     piece = onward(piece)
-    units = [unit]
     for step in range(1, last):
         for part in (came, swapped):
             units += [part[step, k] for k in range(s.halves)]
@@ -403,12 +406,12 @@
     )
 
     def by_point(pieces):
-        flat = pieces.reshape(cols_here, s.lanes).astype(jnp.float32)
-        target = flat[:, rows:].T.reshape(2, share, cols_here)
+        turned = pieces.reshape(cols_here, s.lanes).astype(jnp.float32).T
+        target = turned[rows:].reshape(2, share, cols_here)
         own = lax.dynamic_index_in_dim(target, core, 0, keepdims=False)
         other = lax.dynamic_index_in_dim(target, 1 - core, 0, keepdims=False)
         other = swap_cores(other.astype(HALF)).astype(jnp.float32)
-        return flat[:, :rows].T, in_order(own, other, 1)
+        return turned[:rows], in_order(own, other, 1)
 
     row_three, col_three = by_point(exchange(thirds.astype(HALF)))
     source_potential = jnp.log(source_mass / row_three)

time: 153 us -> 154 us (level)
  waiting for transfers between devices: 28.3 us -> 43.9 us
  starting transfers between devices: 51.1 us -> 43.9 us
  local copies, waits for them, and re-layouts: 13.9 us -> 7.95 us
  Pallas kernels: 34.2 us -> 31.9 us
    ppermute x7, waiting for transfers between devices: 21.8 us -> 33.7 us  [onward(): return lax.ppermute(x, ('src', 'tgt'), pairs)]
    ppermute x12, starting transfers between devices: 15.4 us -> 8.75 us  [swap_cores(): return lax.ppermute(x, 'tgt', [(0, 1), (1, 0)])]
    unnamed x35, local copies, waits for them, and re-layouts: 5.96 us -> 2.7 us
    slice x3 -> x2, local copies, waits for them, and re-layouts: 3.25 us -> 0.04 us  [by_point(): target = turned[rows:].reshape(2, share, cols_here)]
    all_to_all x4, waiting for transfers between devices: 6.52 us -> 9.53 us  [exchange(): return lax.all_to_all(x, 'src', 0, 0, tiled=True)]
    pallas_call x2, Pallas kernels: 34.2 us -> 31.9 us  [call(): pl.pallas_call(functools.partial(kernel, s), out_shape=[*vmem_outs, *hbm_...]
    concatenate x1 -> x2, other arithmetic: 0.12 us -> 1.74 us  [in_order(): jnp.concatenate([jnp.where(core == 0, mine, other), jnp.where(core == 0,...]
  transfers between devices with their start and end apart: 23 -> 23, of which waited for: 6 -> 8; matrix products, arithmetic and copies ran while one was open for 18% -> 16% of each run, Pallas kernels for 22% -> 21%
where the time goes in v13:
time: 154 us; the launch traced here: 153 us
  starting transfers between devices  43.9 us (29%)
  waiting for transfers between devices  43.9 us (29%)
  Pallas kernels  31.9 us (21%)
  other arithmetic  22.8 us (15%)
  local copies, waits for them, and re-layouts  7.95 us (5%)
    ppermute x7, waiting for transfers between devices, onward(): return lax.ppermute(x, ('src', 'tgt'), pairs)  33.7 us
    pallas_call x2, Pallas kernels, call(): pl.pallas_call(functools.partial(kernel, s), out_shape=[*vmem_outs, *hbm_...  31.9 us
    all_to_all x4, starting transfers between devices, exchange(): return lax.all_to_all(x, 'src', 0, 0, tiled=True)  21.3 us
    ppermute x7, starting transfers between devices, onward(): return lax.ppermute(x, ('src', 'tgt'), pairs)  13.8 us
    all_to_all x4, waiting for transfers between devices, exchange(): return lax.all_to_all(x, 'src', 0, 0, tiled=True)  9.53 us
    ppermute x12, starting transfers between devices, swap_cores(): return lax.ppermute(x, 'tgt', [(0, 1), (1, 0)])  8.75 us
    div x1, other arithmetic, local(): source_known = source_cotangent / source_mass  3.27 us
  transfers between devices with their start and end apart: 23, of which 8 were waited for; matrix products, arithmetic and copies ran while one was open for 16% of the time, Pallas kernels for 21%

profile of v13, /device:TPU:1, one launch (start us, length us, event | category | flops | bytes accessed | tf_op | source)
XLA Modules:
  0.0 152.8 jit_solution(13748780681927476563)
XLA Ops:
  7.1 2.4 %collective-permute-start.1 = (bf16[256,1024]{1,0:T(8,128)(2,1)}, bf16[256,1024]{1,0:T(8,128)(2,1)}, u32[]{:S(2)}, u32[]{:S(2)}) collective-permute-start(bf16[256,1024]{1,0:T(8,128)(2,1)} %pad_maximum_fusion.2.refs_0_.refs_5_), channel_id=1, source_target_pairs={{0,4},{1,3},{4,8},{5,1},{8,12},{9,5},{12,14},{13,9},{14,10},{15,13... | collective-permute-start | bytes 1572872 | tf_op jit(solution)/shard_map/ppermute | solution.py:316
  14.3 2.5 %collective-permute-done.1.refs_2_.refs_7_ = bf16[256,1024]{1,0:T(8,128)(2,1)} collective-permute-done((bf16[256,1024]{1,0:T(8,128)(2,1)}, bf16[256,1024]{1,0:T(8,128)(2,1)}, u32[]{:S(2)}, u32[]{:S(2)}) %collective-permute-start.1) | collective-permute-done | bytes 524320 | tf_op jit(solution)/shard_map/ppermute | solution.py:316
  18.7 1.5 copy.22
  21.5 6.1 %all-to-all-start = ((f16[8,64,640]{2,1,0:T(8,128)(2,1)}), f16[8,64,640]{2,1,0:T(8,128)(2,1)S(1)}, u32[]{:S(2)}, u32[]{:S(2)}) async-start(f16[8,64,640]{2,1,0:T(8,128)(2,1)} %pad_maximum_fusion), calls=%async_computation | async-start | bytes 1310720 | tf_op jit(solution)/shard_map/all_to_all | solution.py:319
  28.2 1.5 collective-permute-start.2
  32.0 14.7 %collective-permute-done.2.refs_6_.refs_11_ = bf16[256,1024]{1,0:T(8,128)(2,1)S(1)} collective-permute-done((bf16[256,1024]{1,0:T(8,128)(2,1)}, bf16[256,1024]{1,0:T(8,128)(2,1)S(1)}, u32[]{:S(2)}, u32[]{:S(2)}) %collective-permute-start.2) | collective-permute-done | bytes 524320 | tf_op jit(solution)/shard_map/ppermute | solution.py:316
  46.7 5.3 %collective-permute-done.8.refs_7_.refs_12_ = bf16[256,1024]{1,0:T(8,128)(2,1)S(1)} collective-permute-done((bf16[256,1024]{1,0:T(8,128)(2,1)}, bf16[256,1024]{1,0:T(8,128)(2,1)S(1)}, u32[]{:S(2)}, u32[]{:S(2)}) %collective-permute-start.8) | collective-permute-done | bytes 524320 | tf_op jit(solution)/shard_map/ppermute | solution.py:316
  52.0 1.8 %collective-permute-start.5 = (bf16[256,1024]{1,0:T(8,128)(2,1)S(1)}, bf16[256,1024]{1,0:T(8,128)(2,1)}, u32[]{:S(2)}, u32[]{:S(2)}) collective-permute-start(bf16[256,1024]{1,0:T(8,128)(2,1)S(1)} %collective-permute-done.2.refs_6_.refs_11_), channel_id=1, source_target_pairs={{0,4},{1,3},{4,8},{5,1},{8,12},{9,5},{12,14},{13,9},{14,10},{15,13... | collective-permute-start | bytes 1572872 | tf_op jit(solution)/shard_map/ppermute | solution.py:316
  55.5 4.8 %collective-permute-start.12 = (bf16[256,1024]{1,0:T(8,128)(2,1)S(1)}, bf16[256,1024]{1,0:T(8,128)(2,1)S(1)}, u32[]{:S(2)}, u32[]{:S(2)}) collective-permute-start(bf16[256,1024]{1,0:T(8,128)(2,1)S(1)} %collective-permute-done.8.refs_7_.refs_12_), channel_id=1, source_target_pairs={{0,4},{1,3},{4,8},{5,1},{8,12},{9,5},{12,14},{13,9},{14,10},{15,13... | collective-permute-start | bytes 1572872 | tf_op jit(solution)/shard_map/ppermute | solution.py:316
  60.3 3.3 %collective-permute-done.5.refs_10_.refs_15_ = bf16[256,1024]{1,0:T(8,128)(2,1)} collective-permute-done((bf16[256,1024]{1,0:T(8,128)(2,1)S(1)}, bf16[256,1024]{1,0:T(8,128)(2,1)}, u32[]{:S(2)}, u32[]{:S(2)}) %collective-permute-start.5) | collective-permute-done | bytes 524320 | tf_op jit(solution)/shard_map/ppermute | solution.py:316
  64.7 4.5 %collective-permute-done.12.refs_11_.refs_16_ = bf16[256,1024]{1,0:T(8,128)(2,1)S(1)} collective-permute-done((bf16[256,1024]{1,0:T(8,128)(2,1)S(1)}, bf16[256,1024]{1,0:T(8,128)(2,1)S(1)}, u32[]{:S(2)}, u32[]{:S(2)}) %collective-permute-start.12) | collective-permute-done | bytes 524320 | tf_op jit(solution)/shard_map/ppermute | solution.py:316
  71.1 3.4 %collective-permute-done.15.refs_14_.refs_19_ = bf16[256,1024]{1,0:T(8,128)(2,1)S(1)} collective-permute-done((bf16[256,1024]{1,0:T(8,128)(2,1)}, bf16[256,1024]{1,0:T(8,128)(2,1)S(1)}, u32[]{:S(2)}, u32[]{:S(2)}) %collective-permute-start.15) | collective-permute-done | bytes 524320 | tf_op jit(solution)/shard_map/ppermute | solution.py:316
  75.6 4.4 %all-to-all-start.1 = ((f16[8,64,640]{2,1,0:T(8,128)(2,1)}), f16[8,64,640]{2,1,0:T(8,128)(2,1)S(1)}, u32[]{:S(2)}, u32[]{:S(2)}) async-start(f16[8,64,640]{2,1,0:T(8,128)(2,1)} %pad_maximum_fusion.1), calls=%async_computation.1 | async-start | bytes 1310720 | tf_op jit(solution)/shard_map/all_to_all | solution.py:319
  81.0 16.0 %shard_map.132 = (f32[8,64,640]{2,1,0:T(8,128)}, f32[8,64,512]{2,1,0:T(8,128)}, f32[8,8,512]{2,1,0:T(8,128)}, f32[64,1024]{1,0:T(8,128)}, f32[64,1024]{1,0:T(8,128)}, /*index=5*/f32[64,1024]{1,0:T(8,128)}) custom-call(s32[9]{0:T(128)} %pad_add_fusion.table, f32[8,64,640]{2,1,0:T(8,128)} %convert_element_type.61.mass_in, ...), custom_call_target="tpu_custom_call" | custom-call | flops 15032385536 | bytes 16777216 | tf_op jit(solution)/shard_map/pallas_call | solution.py:260
  97.0 2.2 %convert_element_type.66 = f16[8,64,640]{2,1,0:T(8,128)(2,1)} convert(f32[8,64,640]{2,1,0:T(8,128)} %get-tuple-element.55.thirds_in) | non-fusion elementwise | flops 327680 | bytes 1966080 | tf_op jit(solution)/shard_map/convert_element_type | solution.py:416
  99.3 5.4 %all-to-all-start.3 = ((f16[8,64,640]{2,1,0:T(8,128)(2,1)}), f16[8,64,640]{2,1,0:T(8,128)(2,1)S(1)}, u32[]{:S(2)}, u32[]{:S(2)}) async-start(f16[8,64,640]{2,1,0:T(8,128)(2,1)} %convert_element_type.66), calls=%async_computation.3 | async-start | bytes 1310720 | tf_op jit(solution)/shard_map/all_to_all | solution.py:319
  105.9 15.9 %shard_map.133 = f32[8,64,640]{2,1,0:T(8,128)} custom-call(s32[9]{0:T(128)} %pad_add_fusion.table, f32[8,64,640]{2,1,0:T(8,128)} %convert_element_type.61.mass_in, f32[8,64,640]{2,1,0:T(8,128)} %convert_element_type.64.cot_in, f32[8,64,640]{2,1,0:T(8,128)} %get-tuple-element.55.thirds_in, f32[8,64,512]{2,1,0:T(8,128)} %get-tuple-element.56.refs_0_, ...), custom_call_target="tpu_custom_call" | custom-call | flops 10737418240 | bytes 16777216 | tf_op jit(solution)/shard_map/pallas_call | solution.py:260
  121.8 2.3 %convert_element_type.65 = f16[8,64,640]{2,1,0:T(8,128)(2,1)} convert(f32[8,64,640]{2,1,0:T(8,128)} %shard_map.133) | non-fusion elementwise | flops 327680 | bytes 1966080 | tf_op jit(solution)/shard_map/convert_element_type | solution.py:423
  124.1 5.4 %all-to-all-start.2 = ((f16[8,64,640]{2,1,0:T(8,128)(2,1)}), f16[8,64,640]{2,1,0:T(8,128)(2,1)}, u32[]{:S(2)}, u32[]{:S(2)}) async-start(f16[8,64,640]{2,1,0:T(8,128)(2,1)} %convert_element_type.65), calls=%async_computation.2 | async-start | bytes 1310720 | tf_op jit(solution)/shard_map/all_to_all | solution.py:319
  130.1 1.5 collective-permute-start.17
  131.6 3.3 %fusion.14 = (f32[512,512]{1,0:T(8,128)}, f32[512,512]{1,0:T(8,128)}) fusion(f32[512,512]{1,0:T(8,128)} %param.15, f32[512,512]{1,0:T(8,128)} %param.10, f32[640,512]{1,0:T(8,128)S(1)} %bitcast.71), kind=kLoop, calls=%fused_computation.62 | loop fusion | flops 524288 | bytes 5242880 | tf_op jit(solution)/shard_map/div | solution.py:419
  135.8 9.5 %all-to-all-done.2 = f16[8,64,640]{2,1,0:T(8,128)(2,1)} async-done(((f16[8,64,640]{2,1,0:T(8,128)(2,1)}), f16[8,64,640]{2,1,0:T(8,128)(2,1)}, u32[]{:S(2)}, u32[]{:S(2)}) %all-to-all-start.2) | async-done | bytes 655392 | tf_op jit(solution)/shard_map/all_to_all | solution.py:319
  146.9 2.7 %collective-permute-start.18 = (f16[64,512]{1,0:T(8,128)(2,1)S(1)}, f16[64,512]{1,0:T(8,128)(2,1)S(1)}, u32[]{:S(2)}, u32[]{:S(2)}) collective-permute-start(f16[64,512]{1,0:T(8,128)(2,1)S(1)} %fusion.8), channel_id=1, source_target_pairs={{0,1},{1,0},{2,3},{3,2},{4,5},{5,4},{6,7},{7,6},{8,9},{9,8},{10,11... | collective-permute-start | bytes 196616 | tf_op jit(solution)/shard_map/ppermute | solution.py:284
  149.6 2.4 %fusion = f32[512,512]{1,0:T(8,128)} fusion(f32[512,512]{1,0:T(8,128)} %get-tuple-element.63, f32[640,512]{1,0:T(8,128)S(1)} %bitcast.73), kind=kLoop, calls=%fused_computation.3 | loop fusion | flops 524288 | bytes 3145728 | tf_op jit(solution)/shard_map/add | solution.py:434
  (103 shorter events, 29.0 us)
Async XLA Ops:
  3.2 2.0 %collective-permute-start = (bf16[512,512]{1,0:T(8,128)(2,1)S(1)}, bf16[512,512]{1,0:T(8,128)(2,1)S(1)}, u32[]{:S(2)}, u32[]{:S(2)}) collective-permute-start(bf16[512,512]{1,0:T(8,128)(2,1)S(1)} %bitcast.76), channel_id=1, source_target_pairs={{0,1},{1,0},{2,3},{3,2},{4,5},{5,4},{6,7},{7,6},{8,9},{9,8},{10,11... | collective-permute-start | bytes 1572872 | tf_op jit(solution)/shard_map/ppermute | solution.py:284
  7.1 9.6 %collective-permute-start.1 = (bf16[256,1024]{1,0:T(8,128)(2,1)}, bf16[256,1024]{1,0:T(8,128)(2,1)}, u32[]{:S(2)}, u32[]{:S(2)}) collective-permute-start(bf16[256,1024]{1,0:T(8,128)(2,1)} %pad_maximum_fusion.2.refs_0_.refs_5_), channel_id=1, source_target_pairs={{0,4},{1,3},{4,8},{5,1},{8,12},{9,5},{12,14},{13,9},{14,10},{15,13... | collective-permute-start | bytes 1572872 | tf_op jit(solution)/shard_map/ppermute | solution.py:316
  11.5 8.7 %collective-permute-start.10 = (f16[64,512]{1,0:T(8,128)(2,1)}, f16[64,512]{1,0:T(8,128)(2,1)S(1)}, u32[]{:S(2)}, u32[]{:S(2)}) collective-permute-start(f16[64,512]{1,0:T(8,128)(2,1)} %bitcast.68), channel_id=1, source_target_pairs={{0,1},{1,0},{2,3},{3,2},{4,5},{5,4},{6,7},{7,6},{8,9},{9,8},{10,11... | collective-permute-start | bytes 196616 | tf_op jit(solution)/shard_map/ppermute | solution.py:284
  13.2 7.0 %collective-permute-start.4 = (f16[64,512]{1,0:T(8,128)(2,1)}, f16[64,512]{1,0:T(8,128)(2,1)S(1)}, u32[]{:S(2)}, u32[]{:S(2)}) collective-permute-start(f16[64,512]{1,0:T(8,128)(2,1)} %bitcast.69), channel_id=1, source_target_pairs={{0,1},{1,0},{2,3},{3,2},{4,5},{5,4},{6,7},{7,6},{8,9},{9,8},{10,11... | collective-permute-start | bytes 196616 | tf_op jit(solution)/shard_map/ppermute | solution.py:284
  13.2 16.5 %collective-permute-start.7 = (bf16[256,1024]{1,0:T(8,128)(2,1)}, bf16[256,1024]{1,0:T(8,128)(2,1)}, u32[]{:S(2)}, u32[]{:S(2)}) collective-permute-start(bf16[256,1024]{1,0:T(8,128)(2,1)} %pad_maximum_fusion.3.refs_1_.refs_6_), channel_id=1, source_target_pairs={{0,4},{1,3},{4,8},{5,1},{8,12},{9,5},{12,14},{13,9},{14,10},{15,13... | collective-permute-start | bytes 1572872 | tf_op jit(solution)/shard_map/ppermute | solution.py:316
  16.7 4.8 %collective-permute-start.3 = (bf16[256,1024]{1,0:T(8,128)(2,1)}, bf16[256,1024]{1,0:T(8,128)(2,1)}, u32[]{:S(2)}, u32[]{:S(2)}) collective-permute-start(bf16[256,1024]{1,0:T(8,128)(2,1)} %collective-permute-done.1.refs_2_.refs_7_), channel_id=1, source_target_pairs={{0,1},{1,0},{2,3},{3,2},{4,5},{5,4},{6,7},{7,6},{8,9},{9,8},{10,11... | collective-permute-start | bytes 1572872 | tf_op jit(solution)/shard_map/ppermute | solution.py:284
  21.5 42.1 %all-to-all-start = ((f16[8,64,640]{2,1,0:T(8,128)(2,1)}), f16[8,64,640]{2,1,0:T(8,128)(2,1)S(1)}, u32[]{:S(2)}, u32[]{:S(2)}) async-start(f16[8,64,640]{2,1,0:T(8,128)(2,1)} %pad_maximum_fusion), calls=%async_computation | async-start | bytes 1310720 | tf_op jit(solution)/shard_map/all_to_all | solution.py:319
  28.2 18.4 %collective-permute-start.2 = (bf16[256,1024]{1,0:T(8,128)(2,1)}, bf16[256,1024]{1,0:T(8,128)(2,1)S(1)}, u32[]{:S(2)}, u32[]{:S(2)}) collective-permute-start(bf16[256,1024]{1,0:T(8,128)(2,1)} %collective-permute-done.1.refs_2_.refs_7_), channel_id=1, source_target_pairs={{0,4},{1,3},{4,8},{5,1},{8,12},{9,5},{12,14},{13,9},{14,10},{15,13... | collective-permute-start | bytes 1572872 | tf_op jit(solution)/shard_map/ppermute | solution.py:316
  29.7 22.3 %collective-permute-start.8 = (bf16[256,1024]{1,0:T(8,128)(2,1)}, bf16[256,1024]{1,0:T(8,128)(2,1)S(1)}, u32[]{:S(2)}, u32[]{:S(2)}) collective-permute-start(bf16[256,1024]{1,0:T(8,128)(2,1)} %collective-permute-done.7.refs_3_.refs_8_), channel_id=1, source_target_pairs={{0,4},{1,3},{4,8},{5,1},{8,12},{9,5},{12,14},{13,9},{14,10},{15,13... | collective-permute-start | bytes 1572872 | tf_op jit(solution)/shard_map/ppermute | solution.py:316
  30.9 24.7 %collective-permute-start.11 = (bf16[256,1024]{1,0:T(8,128)(2,1)}, bf16[256,1024]{1,0:T(8,128)(2,1)}, u32[]{:S(2)}, u32[]{:S(2)}) collective-permute-start(bf16[256,1024]{1,0:T(8,128)(2,1)} %collective-permute-done.7.refs_3_.refs_8_), channel_id=1, source_target_pairs={{0,1},{1,0},{2,3},{3,2},{4,5},{5,4},{6,7},{7,6},{8,9},{9,8},{10,11... | collective-permute-start | bytes 1572872 | tf_op jit(solution)/shard_map/ppermute | solution.py:284
  46.7 8.9 %copy-start.9 = (bf16[256,1024]{1,0:T(8,128)(2,1)}, bf16[256,1024]{1,0:T(8,128)(2,1)S(1)}, u32[]{:S(2)}) copy-start(bf16[256,1024]{1,0:T(8,128)(2,1)S(1)} %collective-permute-done.2.refs_6_.refs_11_) | copy-start | bytes 1572868
  46.7 13.7 %collective-permute-start.6 = (bf16[256,1024]{1,0:T(8,128)(2,1)S(1)}, bf16[256,1024]{1,0:T(8,128)(2,1)}, u32[]{:S(2)}, u32[]{:S(2)}) collective-permute-start(bf16[256,1024]{1,0:T(8,128)(2,1)S(1)} %collective-permute-done.2.refs_6_.refs_11_), channel_id=1, source_target_pairs={{0,1},{1,0},{2,3},{3,2},{4,5},{5,4},{6,7},{7,6},{8,9},{9,8},{10,11... | collective-permute-start | bytes 1572872 | tf_op jit(solution)/shard_map/ppermute | solution.py:284
  52.0 8.3 %collective-permute-start.9 = (bf16[256,1024]{1,0:T(8,128)(2,1)S(1)}, bf16[256,1024]{1,0:T(8,128)(2,1)}, u32[]{:S(2)}, u32[]{:S(2)}) collective-permute-start(bf16[256,1024]{1,0:T(8,128)(2,1)S(1)} %collective-permute-done.8.refs_7_.refs_12_), channel_id=1, source_target_pairs={{0,1},{1,0},{2,3},{3,2},{4,5},{5,4},{6,7},{7,6},{8,9},{9,8},{10,11... | collective-permute-start | bytes 1572872 | tf_op jit(solution)/shard_map/ppermute | solution.py:284
  52.0 11.6 %collective-permute-start.5 = (bf16[256,1024]{1,0:T(8,128)(2,1)S(1)}, bf16[256,1024]{1,0:T(8,128)(2,1)}, u32[]{:S(2)}, u32[]{:S(2)}) collective-permute-start(bf16[256,1024]{1,0:T(8,128)(2,1)S(1)} %collective-permute-done.2.refs_6_.refs_11_), channel_id=1, source_target_pairs={{0,4},{1,3},{4,8},{5,1},{8,12},{9,5},{12,14},{13,9},{14,10},{15,13... | collective-permute-start | bytes 1572872 | tf_op jit(solution)/shard_map/ppermute | solution.py:316
  55.5 13.7 %collective-permute-start.12 = (bf16[256,1024]{1,0:T(8,128)(2,1)S(1)}, bf16[256,1024]{1,0:T(8,128)(2,1)S(1)}, u32[]{:S(2)}, u32[]{:S(2)}) collective-permute-start(bf16[256,1024]{1,0:T(8,128)(2,1)S(1)} %collective-permute-done.8.refs_7_.refs_12_), channel_id=1, source_target_pairs={{0,4},{1,3},{4,8},{5,1},{8,12},{9,5},{12,14},{13,9},{14,10},{15,13... | collective-permute-start | bytes 1572872 | tf_op jit(solution)/shard_map/ppermute | solution.py:316
  63.6 10.9 %collective-permute-start.15 = (bf16[256,1024]{1,0:T(8,128)(2,1)}, bf16[256,1024]{1,0:T(8,128)(2,1)S(1)}, u32[]{:S(2)}, u32[]{:S(2)}) collective-permute-start(bf16[256,1024]{1,0:T(8,128)(2,1)} %collective-permute-done.5.refs_10_.refs_15_), channel_id=1, source_target_pairs={{0,4},{1,3},{4,8},{5,1},{8,12},{9,5},{12,14},{13,9},{14,10},{15,13... | collective-permute-start | bytes 1572872 | tf_op jit(solution)/shard_map/ppermute | solution.py:316
  69.2 10.8 %collective-permute-start.14 = (bf16[256,1024]{1,0:T(8,128)(2,1)S(1)}, bf16[256,1024]{1,0:T(8,128)(2,1)S(1)}, u32[]{:S(2)}, u32[]{:S(2)}) collective-permute-start(bf16[256,1024]{1,0:T(8,128)(2,1)S(1)} %collective-permute-done.12.refs_11_.refs_16_), channel_id=1, source_target_pairs={{0,1},{1,0},{2,3},{3,2},{4,5},{5,4},{6,7},{7,6},{8,9},{9,8},{10,11... | collective-permute-start | bytes 1572872 | tf_op jit(solution)/shard_map/ppermute | solution.py:284
  71.0 9.0 %collective-permute-start.13 = (bf16[256,1024]{1,0:T(8,128)(2,1)}, bf16[256,1024]{1,0:T(8,128)(2,1)S(1)}, u32[]{:S(2)}, u32[]{:S(2)}) collective-permute-start(bf16[256,1024]{1,0:T(8,128)(2,1)} %collective-permute-done.5.refs_10_.refs_15_), channel_id=1, source_target_pairs={{0,1},{1,0},{2,3},{3,2},{4,5},{5,4},{6,7},{7,6},{8,9},{9,8},{10,11... | collective-permute-start | bytes 1572872 | tf_op jit(solution)/shard_map/ppermute | solution.py:284
  74.5 5.5 %collective-permute-start.16 = (bf16[256,1024]{1,0:T(8,128)(2,1)S(1)}, bf16[256,1024]{1,0:T(8,128)(2,1)}, u32[]{:S(2)}, u32[]{:S(2)}) collective-permute-start(bf16[256,1024]{1,0:T(8,128)(2,1)S(1)} %collective-permute-done.15.refs_14_.refs_19_), channel_id=1, source_target_pairs={{0,1},{1,0},{2,3},{3,2},{4,5},{5,4},{6,7},{7,6},{8,9},{9,8},{10,11... | collective-permute-start | bytes 1572872 | tf_op jit(solution)/shard_map/ppermute | solution.py:284
  75.6 23.7 %all-to-all-start.1 = ((f16[8,64,640]{2,1,0:T(8,128)(2,1)}), f16[8,64,640]{2,1,0:T(8,128)(2,1)S(1)}, u32[]{:S(2)}, u32[]{:S(2)}) async-start(f16[8,64,640]{2,1,0:T(8,128)(2,1)} %pad_maximum_fusion.1), calls=%async_computation.1 | async-start | bytes 1310720 | tf_op jit(solution)/shard_map/all_to_all | solution.py:319
  99.3 24.8 %all-to-all-start.3 = ((f16[8,64,640]{2,1,0:T(8,128)(2,1)}), f16[8,64,640]{2,1,0:T(8,128)(2,1)S(1)}, u32[]{:S(2)}, u32[]{:S(2)}) async-start(f16[8,64,640]{2,1,0:T(8,128)(2,1)} %convert_element_type.66), calls=%async_computation.3 | async-start | bytes 1310720 | tf_op jit(solution)/shard_map/all_to_all | solution.py:319
  124.1 21.2 %all-to-all-start.2 = ((f16[8,64,640]{2,1,0:T(8,128)(2,1)}), f16[8,64,640]{2,1,0:T(8,128)(2,1)}, u32[]{:S(2)}, u32[]{:S(2)}) async-start(f16[8,64,640]{2,1,0:T(8,128)(2,1)} %convert_element_type.65), calls=%async_computation.2 | async-start | bytes 1310720 | tf_op jit(solution)/shard_map/all_to_all | solution.py:319
  130.1 4.8 %collective-permute-start.17 = (f16[64,512]{1,0:T(8,128)(2,1)S(1)}, f16[64,512]{1,0:T(8,128)(2,1)S(1)}, u32[]{:S(2)}, u32[]{:S(2)}) collective-permute-start(f16[64,512]{1,0:T(8,128)(2,1)S(1)} %fusion.7), channel_id=1, source_target_pairs={{0,1},{1,0},{2,3},{3,2},{4,5},{5,4},{6,7},{7,6},{8,9},{9,8},{10,11... | collective-permute-start | bytes 196616 | tf_op jit(solution)/shard_map/ppermute | solution.py:284
  146.9 5.1 %collective-permute-start.18 = (f16[64,512]{1,0:T(8,128)(2,1)S(1)}, f16[64,512]{1,0:T(8,128)(2,1)S(1)}, u32[]{:S(2)}, u32[]{:S(2)}) collective-permute-start(f16[64,512]{1,0:T(8,128)(2,1)S(1)} %fusion.8), channel_id=1, source_target_pairs={{0,1},{1,0},{2,3},{3,2},{4,5},{5,4},{6,7},{7,6},{8,9},{9,8},{10,11... | collective-permute-start | bytes 196616 | tf_op jit(solution)/shard_map/ppermute | solution.py:284
  (15 other events, 59.7 us)

commit v14 on v13

--- a/solution.py
+++ b/solution.py
@@ -339,11 +339,11 @@
     mine = dense_blocks(kernel_tiles, tile_cols, tile_count)
     theirs = swap_cores(mine)
     half = rows // s.halves
-    heads = []
-    for k in range(s.halves):
-        start = half * jnp.where(core == 0, k, s.halves - 1 - k)
-        both = [lax.dynamic_slice_in_dim(x, start, half, 0) for x in (mine, theirs)]
-        heads.append(in_order(*both, 1))
+    cut = lambda x: [x[k * half : (k + 1) * half] for k in range(s.halves)]
+    heads = [
+        jnp.concatenate([jnp.where(core == 0, a, d), jnp.where(core == 0, b, c)], axis=1)
+        for a, b, c, d in zip(cut(mine), cut(theirs), reversed(cut(mine)), reversed(cut(theirs)))
+    ]
     heads, mass_here, points_here, cot_here, cot_points = lax.optimization_barrier(
         (heads, source_mass, target_mass[0], source_cotangent, target_cotangent[0])
     )
@@ -366,7 +366,7 @@
                 mass = mass_here.astype(jnp.float32)
                 leaving, mass = lax.optimization_barrier((leaving, mass))
             swapped[step, k] = swap_cores(leaving)
-            if step == 1 and k == 0:
+            if step == 1 and k == s.halves - 1:
                 swapped[step, k], mass_message = lax.optimization_barrier(
                     (swapped[step, k], mass_message)
                 )

time: 154 us -> 150 us (0.974)
  waiting for transfers between devices: 43.9 us -> 41.7 us
  starting transfers between devices: 43.9 us -> 42.1 us
    ppermute x7, starting transfers between devices: 13.8 us -> 9.25 us  [onward(): return lax.ppermute(x, ('src', 'tgt'), pairs)]
    ppermute x12, starting transfers between devices: 8.75 us -> 11.7 us  [swap_cores(): return lax.ppermute(x, 'tgt', [(0, 1), (1, 0)])]
    ppermute x7, waiting for transfers between devices: 33.7 us -> 32 us  [onward(): return lax.ppermute(x, ('src', 'tgt'), pairs)]
  transfers between devices with their start and end apart: 23 -> 23, of which waited for: 8 -> 8; matrix products, arithmetic and copies ran while one was open for 16% -> 17% of each run, Pallas kernels for 21% -> 21%
where the time goes in v14:
time: 150 us; the launch traced here: 149 us
  starting transfers between devices  42.1 us (28%)
  waiting for transfers between devices  41.7 us (28%)
  Pallas kernels  31.8 us (21%)
  other arithmetic  22.7 us (15%)
  local copies, waits for them, and re-layouts  8.46 us (6%)
    ppermute x7, waiting for transfers between devices, onward(): return lax.ppermute(x, ('src', 'tgt'), pairs)  32 us
    pallas_call x2, Pallas kernels, call(): pl.pallas_call(functools.partial(kernel, s), out_shape=[*vmem_outs, *hbm_...  31.8 us
    all_to_all x4, starting transfers between devices, exchange(): return lax.all_to_all(x, 'src', 0, 0, tiled=True)  21.2 us
    ppermute x12, starting transfers between devices, swap_cores(): return lax.ppermute(x, 'tgt', [(0, 1), (1, 0)])  11.7 us
    all_to_all x4, waiting for transfers between devices, exchange(): return lax.all_to_all(x, 'src', 0, 0, tiled=True)  9.53 us
    ppermute x7, starting transfers between devices, onward(): return lax.ppermute(x, ('src', 'tgt'), pairs)  9.25 us
    div x1, other arithmetic, local(): source_known = source_cotangent / source_mass  3.27 us
  transfers between devices with their start and end apart: 23, of which 8 were waited for; matrix products, arithmetic and copies ran while one was open for 17% of the time, Pallas kernels for 21%

profile of v14, /device:TPU:1, one launch (start us, length us, event | category | flops | bytes accessed | tf_op | source)
XLA Modules:
  0.0 149.2 jit_solution(4242704971905324335)
XLA Ops:
  7.0 2.6 %collective-permute-start.5 = (bf16[256,1024]{1,0:T(8,128)(2,1)}, bf16[256,1024]{1,0:T(8,128)(2,1)}, u32[]{:S(2)}, u32[]{:S(2)}) collective-permute-start(bf16[256,1024]{1,0:T(8,128)(2,1)} %pad_maximum_fusion.3.refs_1_.refs_6_), channel_id=1, source_target_pairs={{0,4},{1,3},{4,8},{5,1},{8,12},{9,5},{12,14},{13,9},{14,10},{15,13... | collective-permute-start | bytes 1572872 | tf_op jit(solution)/shard_map/ppermute | solution.py:316
  14.3 2.5 %collective-permute-done.5.refs_3_.refs_8_ = bf16[256,1024]{1,0:T(8,128)(2,1)} collective-permute-done((bf16[256,1024]{1,0:T(8,128)(2,1)}, bf16[256,1024]{1,0:T(8,128)(2,1)}, u32[]{:S(2)}, u32[]{:S(2)}) %collective-permute-start.5) | collective-permute-done | bytes 524320 | tf_op jit(solution)/shard_map/ppermute | solution.py:316
  18.5 1.5 %copy.22 = f16[512,512]{1,0:T(8,128)(2,1)S(1)} copy(f16[512,512]{0,1:T(8,128)(2,1)} %get-tuple-element.93) | data formatting | bytes 1048576 | tf_op jit(solution)/shard_map/transpose | solution.py:333
  21.4 6.1 %all-to-all-start = ((f16[8,64,640]{2,1,0:T(8,128)(2,1)}), f16[8,64,640]{2,1,0:T(8,128)(2,1)S(1)}, u32[]{:S(2)}, u32[]{:S(2)}) async-start(f16[8,64,640]{2,1,0:T(8,128)(2,1)} %pad_maximum_fusion), calls=%async_computation | async-start | bytes 1310720 | tf_op jit(solution)/shard_map/all_to_all | solution.py:319
  30.7 15.9 %collective-permute-done.2.refs_6_.refs_11_ = bf16[256,1024]{1,0:T(8,128)(2,1)S(1)} collective-permute-done((bf16[256,1024]{1,0:T(8,128)(2,1)}, bf16[256,1024]{1,0:T(8,128)(2,1)S(1)}, u32[]{:S(2)}, u32[]{:S(2)}) %collective-permute-start.2) | collective-permute-done | bytes 524320 | tf_op jit(solution)/shard_map/ppermute | solution.py:316
  46.7 3.5 %collective-permute-start.8 = (bf16[256,1024]{1,0:T(8,128)(2,1)S(1)}, bf16[256,1024]{1,0:T(8,128)(2,1)}, u32[]{:S(2)}, u32[]{:S(2)}) collective-permute-start(bf16[256,1024]{1,0:T(8,128)(2,1)S(1)} %collective-permute-done.2.refs_6_.refs_11_), channel_id=1, source_target_pairs={{0,1},{1,0},{2,3},{3,2},{4,5},{5,4},{6,7},{7,6},{8,9},{9,8},{10,11... | collective-permute-start | bytes 1572872 | tf_op jit(solution)/shard_map/ppermute | solution.py:284
  50.2 2.1 %collective-permute-done.9.refs_7_.refs_12_ = bf16[256,1024]{1,0:T(8,128)(2,1)} collective-permute-done((bf16[256,1024]{1,0:T(8,128)(2,1)}, bf16[256,1024]{1,0:T(8,128)(2,1)}, u32[]{:S(2)}, u32[]{:S(2)}) %collective-permute-start.9) | collective-permute-done | bytes 524320 | tf_op jit(solution)/shard_map/ppermute | solution.py:316
  54.0 1.5 %collective-permute-start.12 = (bf16[256,1024]{1,0:T(8,128)(2,1)}, bf16[256,1024]{1,0:T(8,128)(2,1)S(1)}, u32[]{:S(2)}, u32[]{:S(2)}) collective-permute-start(bf16[256,1024]{1,0:T(8,128)(2,1)} %collective-permute-done.9.refs_7_.refs_12_), channel_id=1, source_target_pairs={{0,4},{1,3},{4,8},{5,1},{8,12},{9,5},{12,14},{13,9},{14,10},{15,13... | collective-permute-start | bytes 1572872 | tf_op jit(solution)/shard_map/ppermute | solution.py:316
  55.5 2.8 %collective-permute-done.4.refs_10_.refs_15_ = bf16[256,1024]{1,0:T(8,128)(2,1)} collective-permute-done((bf16[256,1024]{1,0:T(8,128)(2,1)S(1)}, bf16[256,1024]{1,0:T(8,128)(2,1)}, u32[]{:S(2)}, u32[]{:S(2)}) %collective-permute-start.4) | collective-permute-done | bytes 524320 | tf_op jit(solution)/shard_map/ppermute | solution.py:316
  58.3 2.0 %collective-permute-start.15 = (bf16[256,1024]{1,0:T(8,128)(2,1)}, bf16[256,1024]{1,0:T(8,128)(2,1)S(1)}, u32[]{:S(2)}, u32[]{:S(2)}) collective-permute-start(bf16[256,1024]{1,0:T(8,128)(2,1)} %collective-permute-done.4.refs_10_.refs_15_), channel_id=1, source_target_pairs={{0,4},{1,3},{4,8},{5,1},{8,12},{9,5},{12,14},{13,9},{14,10},{15,13... | collective-permute-start | bytes 1572872 | tf_op jit(solution)/shard_map/ppermute | solution.py:316
  60.3 5.5 %collective-permute-done.12.refs_11_.refs_16_ = bf16[256,1024]{1,0:T(8,128)(2,1)S(1)} collective-permute-done((bf16[256,1024]{1,0:T(8,128)(2,1)}, bf16[256,1024]{1,0:T(8,128)(2,1)S(1)}, u32[]{:S(2)}, u32[]{:S(2)}) %collective-permute-start.12) | collective-permute-done | bytes 524320 | tf_op jit(solution)/shard_map/ppermute | solution.py:316
  67.8 3.3 %collective-permute-done.15.refs_14_.refs_19_ = bf16[256,1024]{1,0:T(8,128)(2,1)S(1)} collective-permute-done((bf16[256,1024]{1,0:T(8,128)(2,1)}, bf16[256,1024]{1,0:T(8,128)(2,1)S(1)}, u32[]{:S(2)}, u32[]{:S(2)}) %collective-permute-start.15) | collective-permute-done | bytes 524320 | tf_op jit(solution)/shard_map/ppermute | solution.py:316
  72.2 4.3 %all-to-all-start.1 = ((f16[8,64,640]{2,1,0:T(8,128)(2,1)}), f16[8,64,640]{2,1,0:T(8,128)(2,1)S(1)}, u32[]{:S(2)}, u32[]{:S(2)}) async-start(f16[8,64,640]{2,1,0:T(8,128)(2,1)} %pad_maximum_fusion.1), calls=%async_computation.1 | async-start | bytes 1310720 | tf_op jit(solution)/shard_map/all_to_all | solution.py:319
  77.5 16.0 %shard_map.132 = (f32[8,64,640]{2,1,0:T(8,128)}, f32[8,64,512]{2,1,0:T(8,128)}, f32[8,8,512]{2,1,0:T(8,128)}, f32[64,1024]{1,0:T(8,128)}, f32[64,1024]{1,0:T(8,128)}, /*index=5*/f32[64,1024]{1,0:T(8,128)}) custom-call(s32[9]{0:T(128)} %pad_add_fusion.table, f32[8,64,640]{2,1,0:T(8,128)} %convert_element_type.61.mass_in, ...), custom_call_target="tpu_custom_call" | custom-call | flops 15032385536 | bytes 16777216 | tf_op jit(solution)/shard_map/pallas_call | solution.py:260
  93.4 2.2 %convert_element_type.66 = f16[8,64,640]{2,1,0:T(8,128)(2,1)} convert(f32[8,64,640]{2,1,0:T(8,128)} %get-tuple-element.55.thirds_in) | non-fusion elementwise | flops 327680 | bytes 1966080 | tf_op jit(solution)/shard_map/convert_element_type | solution.py:416
  95.7 5.4 %all-to-all-start.3 = ((f16[8,64,640]{2,1,0:T(8,128)(2,1)}), f16[8,64,640]{2,1,0:T(8,128)(2,1)S(1)}, u32[]{:S(2)}, u32[]{:S(2)}) async-start(f16[8,64,640]{2,1,0:T(8,128)(2,1)} %convert_element_type.66), calls=%async_computation.3 | async-start | bytes 1310720 | tf_op jit(solution)/shard_map/all_to_all | solution.py:319
  102.3 15.9 %shard_map.133 = f32[8,64,640]{2,1,0:T(8,128)} custom-call(s32[9]{0:T(128)} %pad_add_fusion.table, f32[8,64,640]{2,1,0:T(8,128)} %convert_element_type.61.mass_in, f32[8,64,640]{2,1,0:T(8,128)} %convert_element_type.64.cot_in, f32[8,64,640]{2,1,0:T(8,128)} %get-tuple-element.55.thirds_in, f32[8,64,512]{2,1,0:T(8,128)} %get-tuple-element.56.refs_0_, ...), custom_call_target="tpu_custom_call" | custom-call | flops 10737418240 | bytes 16777216 | tf_op jit(solution)/shard_map/pallas_call | solution.py:260
  118.2 2.3 %convert_element_type.65 = f16[8,64,640]{2,1,0:T(8,128)(2,1)} convert(f32[8,64,640]{2,1,0:T(8,128)} %shard_map.133) | non-fusion elementwise | flops 327680 | bytes 1966080 | tf_op jit(solution)/shard_map/convert_element_type | solution.py:423
  120.5 5.4 %all-to-all-start.2 = ((f16[8,64,640]{2,1,0:T(8,128)(2,1)}), f16[8,64,640]{2,1,0:T(8,128)(2,1)}, u32[]{:S(2)}, u32[]{:S(2)}) async-start(f16[8,64,640]{2,1,0:T(8,128)(2,1)} %convert_element_type.65), calls=%async_computation.2 | async-start | bytes 1310720 | tf_op jit(solution)/shard_map/all_to_all | solution.py:319
  126.6 1.5 collective-permute-start.17
  128.0 3.3 %fusion.14 = (f32[512,512]{1,0:T(8,128)}, f32[512,512]{1,0:T(8,128)}) fusion(f32[512,512]{1,0:T(8,128)} %param.15, f32[512,512]{1,0:T(8,128)} %param.10, f32[640,512]{1,0:T(8,128)S(1)} %bitcast.77), kind=kLoop, calls=%fused_computation.62 | loop fusion | flops 524288 | bytes 5242880 | tf_op jit(solution)/shard_map/div | solution.py:419
  132.2 9.5 %all-to-all-done.2 = f16[8,64,640]{2,1,0:T(8,128)(2,1)} async-done(((f16[8,64,640]{2,1,0:T(8,128)(2,1)}), f16[8,64,640]{2,1,0:T(8,128)(2,1)}, u32[]{:S(2)}, u32[]{:S(2)}) %all-to-all-start.2) | async-done | bytes 655392 | tf_op jit(solution)/shard_map/all_to_all | solution.py:319
  143.3 2.7 %collective-permute-start.18 = (f16[64,512]{1,0:T(8,128)(2,1)S(1)}, f16[64,512]{1,0:T(8,128)(2,1)S(1)}, u32[]{:S(2)}, u32[]{:S(2)}) collective-permute-start(f16[64,512]{1,0:T(8,128)(2,1)S(1)} %fusion.8), channel_id=1, source_target_pairs={{0,1},{1,0},{2,3},{3,2},{4,5},{5,4},{6,7},{7,6},{8,9},{9,8},{10,11... | collective-permute-start | bytes 196616 | tf_op jit(solution)/shard_map/ppermute | solution.py:284
  146.0 2.4 %fusion = f32[512,512]{1,0:T(8,128)} fusion(f32[512,512]{1,0:T(8,128)} %get-tuple-element.63, f32[640,512]{1,0:T(8,128)S(1)} %bitcast.79), kind=kLoop, calls=%fused_computation.3 | loop fusion | flops 524288 | bytes 3145728 | tf_op jit(solution)/shard_map/add | solution.py:434
  (106 shorter events, 28.1 us)
Async XLA Ops:
  3.2 2.0 %collective-permute-start = (bf16[512,512]{1,0:T(8,128)(2,1)S(1)}, bf16[512,512]{1,0:T(8,128)(2,1)S(1)}, u32[]{:S(2)}, u32[]{:S(2)}) collective-permute-start(bf16[512,512]{1,0:T(8,128)(2,1)S(1)} %bitcast.96), channel_id=1, source_target_pairs={{0,1},{1,0},{2,3},{3,2},{4,5},{5,4},{6,7},{7,6},{8,9},{9,8},{10,11... | collective-permute-start | bytes 1572872 | tf_op jit(solution)/shard_map/ppermute | solution.py:284
  7.0 9.8 %collective-permute-start.5 = (bf16[256,1024]{1,0:T(8,128)(2,1)}, bf16[256,1024]{1,0:T(8,128)(2,1)}, u32[]{:S(2)}, u32[]{:S(2)}) collective-permute-start(bf16[256,1024]{1,0:T(8,128)(2,1)} %pad_maximum_fusion.3.refs_1_.refs_6_), channel_id=1, source_target_pairs={{0,4},{1,3},{4,8},{5,1},{8,12},{9,5},{12,14},{13,9},{14,10},{15,13... | collective-permute-start | bytes 1572872 | tf_op jit(solution)/shard_map/ppermute | solution.py:316
  11.5 8.5 %collective-permute-start.11 = (f16[64,512]{1,0:T(8,128)(2,1)}, f16[64,512]{1,0:T(8,128)(2,1)S(1)}, u32[]{:S(2)}, u32[]{:S(2)}) collective-permute-start(f16[64,512]{1,0:T(8,128)(2,1)} %bitcast.74), channel_id=1, source_target_pairs={{0,1},{1,0},{2,3},{3,2},{4,5},{5,4},{6,7},{7,6},{8,9},{9,8},{10,11... | collective-permute-start | bytes 196616 | tf_op jit(solution)/shard_map/ppermute | solution.py:284
  13.0 7.0 %collective-permute-start.7 = (f16[64,512]{1,0:T(8,128)(2,1)}, f16[64,512]{1,0:T(8,128)(2,1)S(1)}, u32[]{:S(2)}, u32[]{:S(2)}) collective-permute-start(f16[64,512]{1,0:T(8,128)(2,1)} %bitcast.75), channel_id=1, source_target_pairs={{0,1},{1,0},{2,3},{3,2},{4,5},{5,4},{6,7},{7,6},{8,9},{9,8},{10,11... | collective-permute-start | bytes 196616 | tf_op jit(solution)/shard_map/ppermute | solution.py:284
  13.0 15.0 %collective-permute-start.1 = (bf16[256,1024]{1,0:T(8,128)(2,1)}, bf16[256,1024]{1,0:T(8,128)(2,1)}, u32[]{:S(2)}, u32[]{:S(2)}) collective-permute-start(bf16[256,1024]{1,0:T(8,128)(2,1)} %pad_maximum_fusion.2.refs_0_.refs_5_), channel_id=1, source_target_pairs={{0,4},{1,3},{4,8},{5,1},{8,12},{9,5},{12,14},{13,9},{14,10},{15,13... | collective-permute-start | bytes 1572872 | tf_op jit(solution)/shard_map/ppermute | solution.py:316
  16.8 4.6 %collective-permute-start.6 = (bf16[256,1024]{1,0:T(8,128)(2,1)}, bf16[256,1024]{1,0:T(8,128)(2,1)}, u32[]{:S(2)}, u32[]{:S(2)}) collective-permute-start(bf16[256,1024]{1,0:T(8,128)(2,1)} %collective-permute-done.5.refs_3_.refs_8_), channel_id=1, source_target_pairs={{0,1},{1,0},{2,3},{3,2},{4,5},{5,4},{6,7},{7,6},{8,9},{9,8},{10,11... | collective-permute-start | bytes 1572872 | tf_op jit(solution)/shard_map/ppermute | solution.py:284
  21.4 36.9 %all-to-all-start = ((f16[8,64,640]{2,1,0:T(8,128)(2,1)}), f16[8,64,640]{2,1,0:T(8,128)(2,1)S(1)}, u32[]{:S(2)}, u32[]{:S(2)}) async-start(f16[8,64,640]{2,1,0:T(8,128)(2,1)} %pad_maximum_fusion), calls=%async_computation | async-start | bytes 1310720 | tf_op jit(solution)/shard_map/all_to_all | solution.py:319
  28.1 18.6 %collective-permute-start.2 = (bf16[256,1024]{1,0:T(8,128)(2,1)}, bf16[256,1024]{1,0:T(8,128)(2,1)S(1)}, u32[]{:S(2)}, u32[]{:S(2)}) collective-permute-start(bf16[256,1024]{1,0:T(8,128)(2,1)} %collective-permute-done.1.refs_2_.refs_7_), channel_id=1, source_target_pairs={{0,4},{1,3},{4,8},{5,1},{8,12},{9,5},{12,14},{13,9},{14,10},{15,13... | collective-permute-start | bytes 1572872 | tf_op jit(solution)/shard_map/ppermute | solution.py:316
  29.5 17.1 %collective-permute-start.3 = (bf16[256,1024]{1,0:T(8,128)(2,1)}, bf16[256,1024]{1,0:T(8,128)(2,1)S(1)}, u32[]{:S(2)}, u32[]{:S(2)}) collective-permute-start(bf16[256,1024]{1,0:T(8,128)(2,1)} %collective-permute-done.1.refs_2_.refs_7_), channel_id=1, source_target_pairs={{0,1},{1,0},{2,3},{3,2},{4,5},{5,4},{6,7},{7,6},{8,9},{9,8},{10,11... | collective-permute-start | bytes 1572872 | tf_op jit(solution)/shard_map/ppermute | solution.py:284
  30.4 21.9 %collective-permute-start.9 = (bf16[256,1024]{1,0:T(8,128)(2,1)}, bf16[256,1024]{1,0:T(8,128)(2,1)}, u32[]{:S(2)}, u32[]{:S(2)}) collective-permute-start(bf16[256,1024]{1,0:T(8,128)(2,1)} %collective-permute-done.5.refs_3_.refs_8_), channel_id=1, source_target_pairs={{0,4},{1,3},{4,8},{5,1},{8,12},{9,5},{12,14},{13,9},{14,10},{15,13... | collective-permute-start | bytes 1572872 | tf_op jit(solution)/shard_map/ppermute | solution.py:316
  46.6 7.3 %copy-start.9 = (bf16[256,1024]{1,0:T(8,128)(2,1)}, bf16[256,1024]{1,0:T(8,128)(2,1)S(1)}, u32[]{:S(2)}) copy-start(bf16[256,1024]{1,0:T(8,128)(2,1)S(1)} %collective-permute-done.2.refs_6_.refs_11_) | copy-start | bytes 1572868
  46.7 11.7 %collective-permute-start.4 = (bf16[256,1024]{1,0:T(8,128)(2,1)S(1)}, bf16[256,1024]{1,0:T(8,128)(2,1)}, u32[]{:S(2)}, u32[]{:S(2)}) collective-permute-start(bf16[256,1024]{1,0:T(8,128)(2,1)S(1)} %collective-permute-done.2.refs_6_.refs_11_), channel_id=1, source_target_pairs={{0,4},{1,3},{4,8},{5,1},{8,12},{9,5},{12,14},{13,9},{14,10},{15,13... | collective-permute-start | bytes 1572872 | tf_op jit(solution)/shard_map/ppermute | solution.py:316
  46.7 8.8 %collective-permute-start.8 = (bf16[256,1024]{1,0:T(8,128)(2,1)S(1)}, bf16[256,1024]{1,0:T(8,128)(2,1)}, u32[]{:S(2)}, u32[]{:S(2)}) collective-permute-start(bf16[256,1024]{1,0:T(8,128)(2,1)S(1)} %collective-permute-done.2.refs_6_.refs_11_), channel_id=1, source_target_pairs={{0,1},{1,0},{2,3},{3,2},{4,5},{5,4},{6,7},{7,6},{8,9},{9,8},{10,11... | collective-permute-start | bytes 1572872 | tf_op jit(solution)/shard_map/ppermute | solution.py:284
  52.3 6.0 %collective-permute-start.10 = (bf16[256,1024]{1,0:T(8,128)(2,1)}, bf16[256,1024]{1,0:T(8,128)(2,1)}, u32[]{:S(2)}, u32[]{:S(2)}) collective-permute-start(bf16[256,1024]{1,0:T(8,128)(2,1)} %collective-permute-done.9.refs_7_.refs_12_), channel_id=1, source_target_pairs={{0,1},{1,0},{2,3},{3,2},{4,5},{5,4},{6,7},{7,6},{8,9},{9,8},{10,11... | collective-permute-start | bytes 1572872 | tf_op jit(solution)/shard_map/ppermute | solution.py:284
  54.0 11.8 %collective-permute-start.12 = (bf16[256,1024]{1,0:T(8,128)(2,1)}, bf16[256,1024]{1,0:T(8,128)(2,1)S(1)}, u32[]{:S(2)}, u32[]{:S(2)}) collective-permute-start(bf16[256,1024]{1,0:T(8,128)(2,1)} %collective-permute-done.9.refs_7_.refs_12_), channel_id=1, source_target_pairs={{0,4},{1,3},{4,8},{5,1},{8,12},{9,5},{12,14},{13,9},{14,10},{15,13... | collective-permute-start | bytes 1572872 | tf_op jit(solution)/shard_map/ppermute | solution.py:316
  58.3 12.8 %collective-permute-start.15 = (bf16[256,1024]{1,0:T(8,128)(2,1)}, bf16[256,1024]{1,0:T(8,128)(2,1)S(1)}, u32[]{:S(2)}, u32[]{:S(2)}) collective-permute-start(bf16[256,1024]{1,0:T(8,128)(2,1)} %collective-permute-done.4.refs_10_.refs_15_), channel_id=1, source_target_pairs={{0,4},{1,3},{4,8},{5,1},{8,12},{9,5},{12,14},{13,9},{14,10},{15,13... | collective-permute-start | bytes 1572872 | tf_op jit(solution)/shard_map/ppermute | solution.py:316
  65.8 10.6 %collective-permute-start.14 = (bf16[256,1024]{1,0:T(8,128)(2,1)S(1)}, bf16[256,1024]{1,0:T(8,128)(2,1)S(1)}, u32[]{:S(2)}, u32[]{:S(2)}) collective-permute-start(bf16[256,1024]{1,0:T(8,128)(2,1)S(1)} %collective-permute-done.12.refs_11_.refs_16_), channel_id=1, source_target_pairs={{0,1},{1,0},{2,3},{3,2},{4,5},{5,4},{6,7},{7,6},{8,9},{9,8},{10,11... | collective-permute-start | bytes 1572872 | tf_op jit(solution)/shard_map/ppermute | solution.py:284
  67.7 8.7 %collective-permute-start.13 = (bf16[256,1024]{1,0:T(8,128)(2,1)}, bf16[256,1024]{1,0:T(8,128)(2,1)S(1)}, u32[]{:S(2)}, u32[]{:S(2)}) collective-permute-start(bf16[256,1024]{1,0:T(8,128)(2,1)} %collective-permute-done.4.refs_10_.refs_15_), channel_id=1, source_target_pairs={{0,1},{1,0},{2,3},{3,2},{4,5},{5,4},{6,7},{7,6},{8,9},{9,8},{10,11... | collective-permute-start | bytes 1572872 | tf_op jit(solution)/shard_map/ppermute | solution.py:284
  71.1 5.3 %collective-permute-start.16 = (bf16[256,1024]{1,0:T(8,128)(2,1)S(1)}, bf16[256,1024]{1,0:T(8,128)(2,1)}, u32[]{:S(2)}, u32[]{:S(2)}) collective-permute-start(bf16[256,1024]{1,0:T(8,128)(2,1)S(1)} %collective-permute-done.15.refs_14_.refs_19_), channel_id=1, source_target_pairs={{0,1},{1,0},{2,3},{3,2},{4,5},{5,4},{6,7},{7,6},{8,9},{9,8},{10,11... | collective-permute-start | bytes 1572872 | tf_op jit(solution)/shard_map/ppermute | solution.py:284
  72.2 23.5 %all-to-all-start.1 = ((f16[8,64,640]{2,1,0:T(8,128)(2,1)}), f16[8,64,640]{2,1,0:T(8,128)(2,1)S(1)}, u32[]{:S(2)}, u32[]{:S(2)}) async-start(f16[8,64,640]{2,1,0:T(8,128)(2,1)} %pad_maximum_fusion.1), calls=%async_computation.1 | async-start | bytes 1310720 | tf_op jit(solution)/shard_map/all_to_all | solution.py:319
  95.7 24.8 %all-to-all-start.3 = ((f16[8,64,640]{2,1,0:T(8,128)(2,1)}), f16[8,64,640]{2,1,0:T(8,128)(2,1)S(1)}, u32[]{:S(2)}, u32[]{:S(2)}) async-start(f16[8,64,640]{2,1,0:T(8,128)(2,1)} %convert_element_type.66), calls=%async_computation.3 | async-start | bytes 1310720 | tf_op jit(solution)/shard_map/all_to_all | solution.py:319
  120.5 21.2 %all-to-all-start.2 = ((f16[8,64,640]{2,1,0:T(8,128)(2,1)}), f16[8,64,640]{2,1,0:T(8,128)(2,1)}, u32[]{:S(2)}, u32[]{:S(2)}) async-start(f16[8,64,640]{2,1,0:T(8,128)(2,1)} %convert_element_type.65), calls=%async_computation.2 | async-start | bytes 1310720 | tf_op jit(solution)/shard_map/all_to_all | solution.py:319
  126.6 4.8 %collective-permute-start.17 = (f16[64,512]{1,0:T(8,128)(2,1)S(1)}, f16[64,512]{1,0:T(8,128)(2,1)S(1)}, u32[]{:S(2)}, u32[]{:S(2)}) collective-permute-start(f16[64,512]{1,0:T(8,128)(2,1)S(1)} %fusion.7), channel_id=1, source_target_pairs={{0,1},{1,0},{2,3},{3,2},{4,5},{5,4},{6,7},{7,6},{8,9},{9,8},{10,11... | collective-permute-start | bytes 196616 | tf_op jit(solution)/shard_map/ppermute | solution.py:284
  143.3 5.1 %collective-permute-start.18 = (f16[64,512]{1,0:T(8,128)(2,1)S(1)}, f16[64,512]{1,0:T(8,128)(2,1)S(1)}, u32[]{:S(2)}, u32[]{:S(2)}) collective-permute-start(f16[64,512]{1,0:T(8,128)(2,1)S(1)} %fusion.8), channel_id=1, source_target_pairs={{0,1},{1,0},{2,3},{3,2},{4,5},{5,4},{6,7},{7,6},{8,9},{9,8},{10,11... | collective-permute-start | bytes 196616 | tf_op jit(solution)/shard_map/ppermute | solution.py:284
  (15 other events, 61.6 us)

commit v15 on v14

--- a/solution.py
+++ b/solution.py
@@ -357,27 +357,23 @@
                 heads[k], swapped[step - 2, k] = lax.optimization_barrier(
                     (heads[k], swapped[step - 2, k])
                 )
-            if step == 2 and k == 0:
-                heads[k], table = lax.optimization_barrier((heads[k], table))
             came[step, k] = heads[k] = onward(heads[k])
+            if step == min(2, last - 1) and k == 0:
+                heads[k], mass_message, table = lax.optimization_barrier(
+                    (heads[k], mass_message, table)
+                )
+                came[step, k] = heads[k]
             leaving = heads[k]
             if step == last - 1 and k == 0:
-                mass_here = exchange(mass_message)
-                mass = mass_here.astype(jnp.float32)
+                mass = exchange(mass_message).astype(jnp.float32)
                 leaving, mass = lax.optimization_barrier((leaving, mass))
             swapped[step, k] = swap_cores(leaving)
-            if step == 1 and k == s.halves - 1:
-                swapped[step, k], mass_message = lax.optimization_barrier(
-                    (swapped[step, k], mass_message)
-                )
     if s.halves == 1:
         piece = lax.dynamic_slice_in_dim(heads[0], core * (rows // 2), rows // 2, 0)
     else:
         piece = heads[0]
     due = [swapped[last - 2, k] for k in range(s.halves)]
-    piece, due, cot_message, mass_here = lax.optimization_barrier(
-        (piece, due, cot_message, mass_here)
-    )
+    piece, due, cot_message = lax.optimization_barrier((piece, due, cot_message))
     swapped.update({(last - 2, k): due[k] for k in range(s.halves)})
     piece = onward(piece)
     for step in range(1, last):

time: 150 us -> 147 us (0.980)
  waiting for transfers between devices: 41.7 us -> 39.1 us
    ppermute x12, starting transfers between devices: 11.7 us -> 9.28 us  [swap_cores(): return lax.ppermute(x, 'tgt', [(0, 1), (1, 0)])]
    ppermute x7, waiting for transfers between devices: 32 us -> 30 us  [onward(): return lax.ppermute(x, ('src', 'tgt'), pairs)]
    all_to_all x4, starting transfers between devices: 21.2 us -> 23.2 us  [exchange(): return lax.all_to_all(x, 'src', 0, 0, tiled=True)]
  transfers between devices with their start and end apart: 23 -> 23, of which waited for: 8 -> 7; matrix products, arithmetic and copies ran while one was open for 17% -> 17% of each run, Pallas kernels for 21% -> 22%
where the time goes in v15:
time: 147 us; the launch traced here: 146 us
  starting transfers between devices  41.6 us (28%)
  waiting for transfers between devices  39.1 us (27%)
  Pallas kernels  31.9 us (22%)
  other arithmetic  22.7 us (15%)
  local copies, waits for them, and re-layouts  8.25 us (6%)
    pallas_call x2, Pallas kernels, call(): pl.pallas_call(functools.partial(kernel, s), out_shape=[*vmem_outs, *hbm_...  31.9 us
    ppermute x7, waiting for transfers between devices, onward(): return lax.ppermute(x, ('src', 'tgt'), pairs)  30 us
    all_to_all x4, starting transfers between devices, exchange(): return lax.all_to_all(x, 'src', 0, 0, tiled=True)  23.2 us
    ppermute x12, starting transfers between devices, swap_cores(): return lax.ppermute(x, 'tgt', [(0, 1), (1, 0)])  9.28 us
    ppermute x7, starting transfers between devices, onward(): return lax.ppermute(x, ('src', 'tgt'), pairs)  9.11 us
    all_to_all x4, waiting for transfers between devices, exchange(): return lax.all_to_all(x, 'src', 0, 0, tiled=True)  9.09 us
    div x1, other arithmetic, local(): source_known = source_cotangent / source_mass  3.27 us
  transfers between devices with their start and end apart: 23, of which 7 were waited for; matrix products, arithmetic and copies ran while one was open for 17% of the time, Pallas kernels for 22%

profile of v15, /device:TPU:1, one launch (start us, length us, event | category | flops | bytes accessed | tf_op | source)
XLA Modules:
  0.0 145.9 jit_solution(8795961392600901103)
XLA Ops:
  1.7 1.4 convolution_convert_fusion
  7.6 2.7 %collective-permute-start.1 = (bf16[256,1024]{1,0:T(8,128)(2,1)}, bf16[256,1024]{1,0:T(8,128)(2,1)}, u32[]{:S(2)}, u32[]{:S(2)}) collective-permute-start(bf16[256,1024]{1,0:T(8,128)(2,1)} %pad_maximum_fusion.2.refs_0_.refs_5_), channel_id=1, source_target_pairs={{0,4},{1,3},{4,8},{5,1},{8,12},{9,5},{12,14},{13,9},{14,10},{15,13... | collective-permute-start | bytes 1572872 | tf_op jit(solution)/shard_map/ppermute | solution.py:316
  15.2 2.3 %collective-permute-done.1.refs_2_.refs_7_ = bf16[256,1024]{1,0:T(8,128)(2,1)} collective-permute-done((bf16[256,1024]{1,0:T(8,128)(2,1)}, bf16[256,1024]{1,0:T(8,128)(2,1)}, u32[]{:S(2)}, u32[]{:S(2)}) %collective-permute-start.1) | collective-permute-done | bytes 524320 | tf_op jit(solution)/shard_map/ppermute | solution.py:316
  17.5 1.4 collective-permute-start.2
  19.9 1.5 %copy.22 = f16[512,512]{1,0:T(8,128)(2,1)S(1)} copy(f16[512,512]{0,1:T(8,128)(2,1)} %get-tuple-element.91) | data formatting | bytes 1048576 | tf_op jit(solution)/shard_map/transpose | solution.py:333
  23.1 1.4 collective-permute-start.8
  25.8 2.9 %collective-permute-done.2.refs_6_.refs_11_ = bf16[256,1024]{1,0:T(8,128)(2,1)} collective-permute-done((bf16[256,1024]{1,0:T(8,128)(2,1)}, bf16[256,1024]{1,0:T(8,128)(2,1)}, u32[]{:S(2)}, u32[]{:S(2)}) %collective-permute-start.2) | collective-permute-done | bytes 524320 | tf_op jit(solution)/shard_map/ppermute | solution.py:316
  28.7 5.7 %all-to-all-start = ((f16[8,64,640]{2,1,0:T(8,128)(2,1)}), f16[8,64,640]{2,1,0:T(8,128)(2,1)S(1)}, u32[]{:S(2)}, u32[]{:S(2)}) async-start(f16[8,64,640]{2,1,0:T(8,128)(2,1)} %pad_maximum_fusion), calls=%async_computation | async-start | bytes 1310720 | tf_op jit(solution)/shard_map/all_to_all | solution.py:319
  35.7 1.8 %collective-permute-start.5 = (bf16[256,1024]{1,0:T(8,128)(2,1)}, bf16[256,1024]{1,0:T(8,128)(2,1)}, u32[]{:S(2)}, u32[]{:S(2)}) collective-permute-start(bf16[256,1024]{1,0:T(8,128)(2,1)} %collective-permute-done.2.refs_6_.refs_11_), channel_id=1, source_target_pairs={{0,4},{1,3},{4,8},{5,1},{8,12},{9,5},{12,14},{13,9},{14,10},{15,13... | collective-permute-start | bytes 1572872 | tf_op jit(solution)/shard_map/ppermute | solution.py:316
  40.5 12.4 %collective-permute-done.5.refs_10_.refs_15_ = bf16[256,1024]{1,0:T(8,128)(2,1)} collective-permute-done((bf16[256,1024]{1,0:T(8,128)(2,1)}, bf16[256,1024]{1,0:T(8,128)(2,1)}, u32[]{:S(2)}, u32[]{:S(2)}) %collective-permute-start.5) | collective-permute-done | bytes 524320 | tf_op jit(solution)/shard_map/ppermute | solution.py:316
  52.9 6.2 %collective-permute-done.12.refs_11_.refs_16_ = bf16[256,1024]{1,0:T(8,128)(2,1)S(1)} collective-permute-done((bf16[256,1024]{1,0:T(8,128)(2,1)}, bf16[256,1024]{1,0:T(8,128)(2,1)S(1)}, u32[]{:S(2)}, u32[]{:S(2)}) %collective-permute-start.12) | collective-permute-done | bytes 524320 | tf_op jit(solution)/shard_map/ppermute | solution.py:316
  59.1 5.9 %collective-permute-done.15.refs_14_.refs_19_ = bf16[256,1024]{1,0:T(8,128)(2,1)S(1)} collective-permute-done((bf16[256,1024]{1,0:T(8,128)(2,1)}, bf16[256,1024]{1,0:T(8,128)(2,1)S(1)}, u32[]{:S(2)}, u32[]{:S(2)}) %collective-permute-start.15) | collective-permute-done | bytes 524320 | tf_op jit(solution)/shard_map/ppermute | solution.py:316
  66.7 6.6 %all-to-all-start.1 = ((f16[8,64,640]{2,1,0:T(8,128)(2,1)}), f16[8,64,640]{2,1,0:T(8,128)(2,1)S(1)}, u32[]{:S(2)}, u32[]{:S(2)}) async-start(f16[8,64,640]{2,1,0:T(8,128)(2,1)} %pad_maximum_fusion.1), calls=%async_computation.1 | async-start | bytes 1310720 | tf_op jit(solution)/shard_map/all_to_all | solution.py:319
  74.1 16.0 %shard_map.132 = (f32[8,64,640]{2,1,0:T(8,128)}, f32[8,64,512]{2,1,0:T(8,128)}, f32[8,8,512]{2,1,0:T(8,128)}, f32[64,1024]{1,0:T(8,128)}, f32[64,1024]{1,0:T(8,128)}, /*index=5*/f32[64,1024]{1,0:T(8,128)}) custom-call(s32[9]{0:T(128)} %pad_add_fusion.table, f32[8,64,640]{2,1,0:T(8,128)} %convert_element_type.61.mass_in, ...), custom_call_target="tpu_custom_call" | custom-call | flops 15032385536 | bytes 16777216 | tf_op jit(solution)/shard_map/pallas_call | solution.py:260
  90.1 2.2 %convert_element_type.66 = f16[8,64,640]{2,1,0:T(8,128)(2,1)} convert(f32[8,64,640]{2,1,0:T(8,128)} %get-tuple-element.53.thirds_in) | non-fusion elementwise | flops 327680 | bytes 1966080 | tf_op jit(solution)/shard_map/convert_element_type | solution.py:412
  92.3 5.4 %all-to-all-start.3 = ((f16[8,64,640]{2,1,0:T(8,128)(2,1)}), f16[8,64,640]{2,1,0:T(8,128)(2,1)S(1)}, u32[]{:S(2)}, u32[]{:S(2)}) async-start(f16[8,64,640]{2,1,0:T(8,128)(2,1)} %convert_element_type.66), calls=%async_computation.3 | async-start | bytes 1310720 | tf_op jit(solution)/shard_map/all_to_all | solution.py:319
  99.0 15.9 %shard_map.133 = f32[8,64,640]{2,1,0:T(8,128)} custom-call(s32[9]{0:T(128)} %pad_add_fusion.table, f32[8,64,640]{2,1,0:T(8,128)} %convert_element_type.61.mass_in, f32[8,64,640]{2,1,0:T(8,128)} %convert_element_type.64.cot_in, f32[8,64,640]{2,1,0:T(8,128)} %get-tuple-element.53.thirds_in, f32[8,64,512]{2,1,0:T(8,128)} %get-tuple-element.54.refs_0_, ...), custom_call_target="tpu_custom_call" | custom-call | flops 10737418240 | bytes 16777216 | tf_op jit(solution)/shard_map/pallas_call | solution.py:260
  114.9 2.3 %convert_element_type.65 = f16[8,64,640]{2,1,0:T(8,128)(2,1)} convert(f32[8,64,640]{2,1,0:T(8,128)} %shard_map.133) | non-fusion elementwise | flops 327680 | bytes 1966080 | tf_op jit(solution)/shard_map/convert_element_type | solution.py:419
  117.1 5.4 %all-to-all-start.2 = ((f16[8,64,640]{2,1,0:T(8,128)(2,1)}), f16[8,64,640]{2,1,0:T(8,128)(2,1)}, u32[]{:S(2)}, u32[]{:S(2)}) async-start(f16[8,64,640]{2,1,0:T(8,128)(2,1)} %convert_element_type.65), calls=%async_computation.2 | async-start | bytes 1310720 | tf_op jit(solution)/shard_map/all_to_all | solution.py:319
  123.2 1.9 %collective-permute-start.17 = (f16[64,512]{1,0:T(8,128)(2,1)S(1)}, f16[64,512]{1,0:T(8,128)(2,1)S(1)}, u32[]{:S(2)}, u32[]{:S(2)}) collective-permute-start(f16[64,512]{1,0:T(8,128)(2,1)S(1)} %fusion.7), channel_id=1, source_target_pairs={{0,1},{1,0},{2,3},{3,2},{4,5},{5,4},{6,7},{7,6},{8,9},{9,8},{10,11... | collective-permute-start | bytes 196616 | tf_op jit(solution)/shard_map/ppermute | solution.py:284
  125.1 3.3 %fusion.14 = (f32[512,512]{1,0:T(8,128)}, f32[512,512]{1,0:T(8,128)}) fusion(f32[512,512]{1,0:T(8,128)} %param.15, f32[512,512]{1,0:T(8,128)} %param.10, f32[640,512]{1,0:T(8,128)S(1)} %bitcast.77), kind=kLoop, calls=%fused_computation.62 | loop fusion | flops 524288 | bytes 5242880 | tf_op jit(solution)/shard_map/div | solution.py:415
  129.3 9.1 %all-to-all-done.2 = f16[8,64,640]{2,1,0:T(8,128)(2,1)} async-done(((f16[8,64,640]{2,1,0:T(8,128)(2,1)}), f16[8,64,640]{2,1,0:T(8,128)(2,1)}, u32[]{:S(2)}, u32[]{:S(2)}) %all-to-all-start.2) | async-done | bytes 655392 | tf_op jit(solution)/shard_map/all_to_all | solution.py:319
  140.0 2.7 %collective-permute-start.18 = (f16[64,512]{1,0:T(8,128)(2,1)S(1)}, f16[64,512]{1,0:T(8,128)(2,1)S(1)}, u32[]{:S(2)}, u32[]{:S(2)}) collective-permute-start(f16[64,512]{1,0:T(8,128)(2,1)S(1)} %fusion.8), channel_id=1, source_target_pairs={{0,1},{1,0},{2,3},{3,2},{4,5},{5,4},{6,7},{7,6},{8,9},{9,8},{10,11... | collective-permute-start | bytes 196616 | tf_op jit(solution)/shard_map/ppermute | solution.py:284
  142.7 2.4 %fusion = f32[512,512]{1,0:T(8,128)} fusion(f32[512,512]{1,0:T(8,128)} %get-tuple-element.61, f32[640,512]{1,0:T(8,128)S(1)} %bitcast.79), kind=kLoop, calls=%fused_computation.3 | loop fusion | flops 524288 | bytes 3145728 | tf_op jit(solution)/shard_map/add | solution.py:430
  (104 shorter events, 26.2 us)
Async XLA Ops:
  3.2 2.5 %collective-permute-start = (bf16[512,512]{1,0:T(8,128)(2,1)S(1)}, bf16[512,512]{1,0:T(8,128)(2,1)S(1)}, u32[]{:S(2)}, u32[]{:S(2)}) collective-permute-start(bf16[512,512]{1,0:T(8,128)(2,1)S(1)} %bitcast.96), channel_id=1, source_target_pairs={{0,1},{1,0},{2,3},{3,2},{4,5},{5,4},{6,7},{7,6},{8,9},{9,8},{10,11... | collective-permute-start | bytes 1572872 | tf_op jit(solution)/shard_map/ppermute | solution.py:284
  7.6 9.9 %collective-permute-start.1 = (bf16[256,1024]{1,0:T(8,128)(2,1)}, bf16[256,1024]{1,0:T(8,128)(2,1)}, u32[]{:S(2)}, u32[]{:S(2)}) collective-permute-start(bf16[256,1024]{1,0:T(8,128)(2,1)} %pad_maximum_fusion.2.refs_0_.refs_5_), channel_id=1, source_target_pairs={{0,4},{1,3},{4,8},{5,1},{8,12},{9,5},{12,14},{13,9},{14,10},{15,13... | collective-permute-start | bytes 1572872 | tf_op jit(solution)/shard_map/ppermute | solution.py:316
  11.2 11.9 %collective-permute-start.7 = (bf16[256,1024]{1,0:T(8,128)(2,1)}, bf16[256,1024]{1,0:T(8,128)(2,1)}, u32[]{:S(2)}, u32[]{:S(2)}) collective-permute-start(bf16[256,1024]{1,0:T(8,128)(2,1)} %pad_maximum_fusion.3.refs_1_.refs_6_), channel_id=1, source_target_pairs={{0,4},{1,3},{4,8},{5,1},{8,12},{9,5},{12,14},{13,9},{14,10},{15,13... | collective-permute-start | bytes 1572872 | tf_op jit(solution)/shard_map/ppermute | solution.py:316
  13.5 11.0 %collective-permute-start.10 = (f16[64,512]{1,0:T(8,128)(2,1)}, f16[64,512]{1,0:T(8,128)(2,1)S(1)}, u32[]{:S(2)}, u32[]{:S(2)}) collective-permute-start(f16[64,512]{1,0:T(8,128)(2,1)} %bitcast.74), channel_id=1, source_target_pairs={{0,1},{1,0},{2,3},{3,2},{4,5},{5,4},{6,7},{7,6},{8,9},{9,8},{10,11... | collective-permute-start | bytes 196616 | tf_op jit(solution)/shard_map/ppermute | solution.py:284
  15.2 9.3 %collective-permute-start.3 = (f16[64,512]{1,0:T(8,128)(2,1)}, f16[64,512]{1,0:T(8,128)(2,1)S(1)}, u32[]{:S(2)}, u32[]{:S(2)}) collective-permute-start(f16[64,512]{1,0:T(8,128)(2,1)} %bitcast.75), channel_id=1, source_target_pairs={{0,1},{1,0},{2,3},{3,2},{4,5},{5,4},{6,7},{7,6},{8,9},{9,8},{10,11... | collective-permute-start | bytes 196616 | tf_op jit(solution)/shard_map/ppermute | solution.py:284
  17.5 11.2 %collective-permute-start.2 = (bf16[256,1024]{1,0:T(8,128)(2,1)}, bf16[256,1024]{1,0:T(8,128)(2,1)}, u32[]{:S(2)}, u32[]{:S(2)}) collective-permute-start(bf16[256,1024]{1,0:T(8,128)(2,1)} %collective-permute-done.1.refs_2_.refs_7_), channel_id=1, source_target_pairs={{0,4},{1,3},{4,8},{5,1},{8,12},{9,5},{12,14},{13,9},{14,10},{15,13... | collective-permute-start | bytes 1572872 | tf_op jit(solution)/shard_map/ppermute | solution.py:316
  21.4 14.2 %collective-permute-start.4 = (bf16[256,1024]{1,0:T(8,128)(2,1)}, bf16[256,1024]{1,0:T(8,128)(2,1)S(1)}, u32[]{:S(2)}, u32[]{:S(2)}) collective-permute-start(bf16[256,1024]{1,0:T(8,128)(2,1)} %collective-permute-done.1.refs_2_.refs_7_), channel_id=1, source_target_pairs={{0,1},{1,0},{2,3},{3,2},{4,5},{5,4},{6,7},{7,6},{8,9},{9,8},{10,11... | collective-permute-start | bytes 1572872 | tf_op jit(solution)/shard_map/ppermute | solution.py:284
  23.1 12.6 %collective-permute-start.8 = (bf16[256,1024]{1,0:T(8,128)(2,1)}, bf16[256,1024]{1,0:T(8,128)(2,1)}, u32[]{:S(2)}, u32[]{:S(2)}) collective-permute-start(bf16[256,1024]{1,0:T(8,128)(2,1)} %collective-permute-done.7.refs_3_.refs_8_), channel_id=1, source_target_pairs={{0,4},{1,3},{4,8},{5,1},{8,12},{9,5},{12,14},{13,9},{14,10},{15,13... | collective-permute-start | bytes 1572872 | tf_op jit(solution)/shard_map/ppermute | solution.py:316
  28.7 36.3 %all-to-all-start = ((f16[8,64,640]{2,1,0:T(8,128)(2,1)}), f16[8,64,640]{2,1,0:T(8,128)(2,1)S(1)}, u32[]{:S(2)}, u32[]{:S(2)}) async-start(f16[8,64,640]{2,1,0:T(8,128)(2,1)} %pad_maximum_fusion), calls=%async_computation | async-start | bytes 1310720 | tf_op jit(solution)/shard_map/all_to_all | solution.py:319
  34.4 5.5 %collective-permute-start.11 = (bf16[256,1024]{1,0:T(8,128)(2,1)}, bf16[256,1024]{1,0:T(8,128)(2,1)S(1)}, u32[]{:S(2)}, u32[]{:S(2)}) collective-permute-start(bf16[256,1024]{1,0:T(8,128)(2,1)} %collective-permute-done.7.refs_3_.refs_8_), channel_id=1, source_target_pairs={{0,1},{1,0},{2,3},{3,2},{4,5},{5,4},{6,7},{7,6},{8,9},{9,8},{10,11... | collective-permute-start | bytes 1572872 | tf_op jit(solution)/shard_map/ppermute | solution.py:284
  35.6 4.8 %collective-permute-start.9 = (bf16[256,1024]{1,0:T(8,128)(2,1)}, bf16[256,1024]{1,0:T(8,128)(2,1)}, u32[]{:S(2)}, u32[]{:S(2)}) collective-permute-start(bf16[256,1024]{1,0:T(8,128)(2,1)} %collective-permute-done.8.refs_7_.refs_12_), channel_id=1, source_target_pairs={{0,1},{1,0},{2,3},{3,2},{4,5},{5,4},{6,7},{7,6},{8,9},{9,8},{10,11... | collective-permute-start | bytes 1572872 | tf_op jit(solution)/shard_map/ppermute | solution.py:284
  35.7 17.2 %collective-permute-start.5 = (bf16[256,1024]{1,0:T(8,128)(2,1)}, bf16[256,1024]{1,0:T(8,128)(2,1)}, u32[]{:S(2)}, u32[]{:S(2)}) collective-permute-start(bf16[256,1024]{1,0:T(8,128)(2,1)} %collective-permute-done.2.refs_6_.refs_11_), channel_id=1, source_target_pairs={{0,4},{1,3},{4,8},{5,1},{8,12},{9,5},{12,14},{13,9},{14,10},{15,13... | collective-permute-start | bytes 1572872 | tf_op jit(solution)/shard_map/ppermute | solution.py:316
  37.5 15.4 %collective-permute-start.6 = (bf16[256,1024]{1,0:T(8,128)(2,1)}, bf16[256,1024]{1,0:T(8,128)(2,1)}, u32[]{:S(2)}, u32[]{:S(2)}) collective-permute-start(bf16[256,1024]{1,0:T(8,128)(2,1)} %collective-permute-done.2.refs_6_.refs_11_), channel_id=1, source_target_pairs={{0,1},{1,0},{2,3},{3,2},{4,5},{5,4},{6,7},{7,6},{8,9},{9,8},{10,11... | collective-permute-start | bytes 1572872 | tf_op jit(solution)/shard_map/ppermute | solution.py:284
  40.0 26.7 %copy-start.10 = (bf16[256,1024]{1,0:T(8,128)(2,1)}, bf16[256,1024]{1,0:T(8,128)(2,1)S(1)}, u32[]{:S(2)}) copy-start(bf16[256,1024]{1,0:T(8,128)(2,1)S(1)} %collective-permute-done.11.refs_5_.refs_10_) | copy-start | bytes 1572868
  40.0 19.1 %collective-permute-start.12 = (bf16[256,1024]{1,0:T(8,128)(2,1)}, bf16[256,1024]{1,0:T(8,128)(2,1)S(1)}, u32[]{:S(2)}, u32[]{:S(2)}) collective-permute-start(bf16[256,1024]{1,0:T(8,128)(2,1)} %collective-permute-done.8.refs_7_.refs_12_), channel_id=1, source_target_pairs={{0,4},{1,3},{4,8},{5,1},{8,12},{9,5},{12,14},{13,9},{14,10},{15,13... | collective-permute-start | bytes 1572872 | tf_op jit(solution)/shard_map/ppermute | solution.py:316
  52.9 12.0 %collective-permute-start.15 = (bf16[256,1024]{1,0:T(8,128)(2,1)}, bf16[256,1024]{1,0:T(8,128)(2,1)S(1)}, u32[]{:S(2)}, u32[]{:S(2)}) collective-permute-start(bf16[256,1024]{1,0:T(8,128)(2,1)} %collective-permute-done.5.refs_10_.refs_15_), channel_id=1, source_target_pairs={{0,4},{1,3},{4,8},{5,1},{8,12},{9,5},{12,14},{13,9},{14,10},{15,13... | collective-permute-start | bytes 1572872 | tf_op jit(solution)/shard_map/ppermute | solution.py:316
  59.1 14.2 %collective-permute-start.14 = (bf16[256,1024]{1,0:T(8,128)(2,1)S(1)}, bf16[256,1024]{1,0:T(8,128)(2,1)S(1)}, u32[]{:S(2)}, u32[]{:S(2)}) collective-permute-start(bf16[256,1024]{1,0:T(8,128)(2,1)S(1)} %collective-permute-done.12.refs_11_.refs_16_), channel_id=1, source_target_pairs={{0,1},{1,0},{2,3},{3,2},{4,5},{5,4},{6,7},{7,6},{8,9},{9,8},{10,11... | collective-permute-start | bytes 1572872 | tf_op jit(solution)/shard_map/ppermute | solution.py:284
  65.0 8.3 %collective-permute-start.16 = (bf16[256,1024]{1,0:T(8,128)(2,1)S(1)}, bf16[256,1024]{1,0:T(8,128)(2,1)}, u32[]{:S(2)}, u32[]{:S(2)}) collective-permute-start(bf16[256,1024]{1,0:T(8,128)(2,1)S(1)} %collective-permute-done.15.refs_14_.refs_19_), channel_id=1, source_target_pairs={{0,1},{1,0},{2,3},{3,2},{4,5},{5,4},{6,7},{7,6},{8,9},{9,8},{10,11... | collective-permute-start | bytes 1572872 | tf_op jit(solution)/shard_map/ppermute | solution.py:284
  66.2 7.1 %collective-permute-start.13 = (bf16[256,1024]{1,0:T(8,128)(2,1)}, bf16[256,1024]{1,0:T(8,128)(2,1)}, u32[]{:S(2)}, u32[]{:S(2)}) collective-permute-start(bf16[256,1024]{1,0:T(8,128)(2,1)} %collective-permute-done.5.refs_10_.refs_15_), channel_id=1, source_target_pairs={{0,1},{1,0},{2,3},{3,2},{4,5},{5,4},{6,7},{7,6},{8,9},{9,8},{10,11... | collective-permute-start | bytes 1572872 | tf_op jit(solution)/shard_map/ppermute | solution.py:284
  66.7 25.7 %all-to-all-start.1 = ((f16[8,64,640]{2,1,0:T(8,128)(2,1)}), f16[8,64,640]{2,1,0:T(8,128)(2,1)S(1)}, u32[]{:S(2)}, u32[]{:S(2)}) async-start(f16[8,64,640]{2,1,0:T(8,128)(2,1)} %pad_maximum_fusion.1), calls=%async_computation.1 | async-start | bytes 1310720 | tf_op jit(solution)/shard_map/all_to_all | solution.py:319
  92.3 24.8 %all-to-all-start.3 = ((f16[8,64,640]{2,1,0:T(8,128)(2,1)}), f16[8,64,640]{2,1,0:T(8,128)(2,1)S(1)}, u32[]{:S(2)}, u32[]{:S(2)}) async-start(f16[8,64,640]{2,1,0:T(8,128)(2,1)} %convert_element_type.66), calls=%async_computation.3 | async-start | bytes 1310720 | tf_op jit(solution)/shard_map/all_to_all | solution.py:319
  117.1 21.2 %all-to-all-start.2 = ((f16[8,64,640]{2,1,0:T(8,128)(2,1)}), f16[8,64,640]{2,1,0:T(8,128)(2,1)}, u32[]{:S(2)}, u32[]{:S(2)}) async-start(f16[8,64,640]{2,1,0:T(8,128)(2,1)} %convert_element_type.65), calls=%async_computation.2 | async-start | bytes 1310720 | tf_op jit(solution)/shard_map/all_to_all | solution.py:319
  123.2 5.2 %collective-permute-start.17 = (f16[64,512]{1,0:T(8,128)(2,1)S(1)}, f16[64,512]{1,0:T(8,128)(2,1)S(1)}, u32[]{:S(2)}, u32[]{:S(2)}) collective-permute-start(f16[64,512]{1,0:T(8,128)(2,1)S(1)} %fusion.7), channel_id=1, source_target_pairs={{0,1},{1,0},{2,3},{3,2},{4,5},{5,4},{6,7},{7,6},{8,9},{9,8},{10,11... | collective-permute-start | bytes 196616 | tf_op jit(solution)/shard_map/ppermute | solution.py:284
  140.0 5.1 %collective-permute-start.18 = (f16[64,512]{1,0:T(8,128)(2,1)S(1)}, f16[64,512]{1,0:T(8,128)(2,1)S(1)}, u32[]{:S(2)}, u32[]{:S(2)}) collective-permute-start(f16[64,512]{1,0:T(8,128)(2,1)S(1)} %fusion.8), channel_id=1, source_target_pairs={{0,1},{1,0},{2,3},{3,2},{4,5},{5,4},{6,7},{7,6},{8,9},{9,8},{10,11... | collective-permute-start | bytes 196616 | tf_op jit(solution)/shard_map/ppermute | solution.py:284
  (14 other events, 56.0 us)

commit v16 on v15

--- a/solution.py
+++ b/solution.py
@@ -67,13 +67,16 @@
                 first = 1 - core if d and d % 2 == 0 else core
                 side = first if part == 0 else 1 - first
                 start = pl.multiple_of(side * size, size) if parts > 1 else 0
-                target = matrix.at[d, pl.ds(start, size)]
-                self.copies[d].append(pltpu.make_async_copy(next(units), target, sems.at[d]))
+                unit = next(units)
+                for t in range(2):
+                    target = matrix.at[d, pl.ds(start, size), pl.ds(t * s.cols, s.cols)]
+                    self.copies[d].append(pltpu.make_async_copy(unit.at[t], target, sems.at[d]))
         for d in range(s.count):
             k = table[d]
             for source, target in paired:
+                place = (k, slice(None), pl.ds(0, target.shape[2]))
                 self.copies[d].append(
-                    pltpu.make_async_copy(source.at[k], target.at[k], sems.at[d])
+                    pltpu.make_async_copy(source.at[place], target.at[place], sems.at[d])
                 )
         self.ahead = AHEAD if s.count <= 8 else s.count
         for d in range(min(self.ahead, s.count)):
@@ -107,10 +110,10 @@
     return copies
 
 
-def gather_targets(s, pieces):
+def gather_targets(s, pieces, first):
     return jnp.concatenate(
         [
-            pieces[i, :, s.rows + t * s.share : s.rows + (t + 1) * s.share]
+            pieces[i, :, first + t * s.share : first + (t + 1) * s.share]
             for t in range(2)
             for i in range(s.count)
         ],
@@ -163,7 +166,7 @@
 
     total = chain(s.count, sums, first, zero)
     col_one[...] = total
-    target = gather_targets(s, mass)
+    target = gather_targets(s, mass, s.rows)
     panel = (target / total).astype(jnp.bfloat16)
 
     def second(d, row, total):
@@ -193,22 +196,23 @@
 def backward_kernel(s, table, mass_in, cot_in, thirds_in, *refs):
     given = 2 + (s.count - 1) * s.halves
     state_in, units, refs = refs[:5], refs[5 : 5 + given], refs[5 + given :]
-    out, (mass, matrix, sems, more_sems), state, (cot, thirds) = (
+    out, (mass, matrix, sems, more_sems), state, (cot, thirds, cot_points) = (
         refs[0],
         refs[1:5],
         refs[5:10],
         refs[10:],
     )
     row_two, row_one, col_one, col_two, col_three = state
-    early = load([state_in[4], cot_in], [col_three, cot], more_sems)
-    paired = [(mass_in, mass), (thirds_in, thirds)]
+    points = cot_in.at[:, :, pl.ds(s.rows, 2 * s.share)]
+    early = load([state_in[4], points], [col_three, cot_points], more_sems)
+    paired = [(mass_in, mass), (thirds_in, thirds), (cot_in, cot)]
     arrived = Arrivals(s, table, units, matrix, sems, paired)
     late = [
         pltpu.make_async_copy(state_in[k], state[k], more_sems.at[2 + k]) for k in range(4)
     ]
     for copy in early:
         copy.wait()
-    target_cot = gather_targets(s, cot)
+    target_cot = gather_targets(s, cot_points, 0)
     panel = (-target_cot / col_three[...]).astype(jnp.bfloat16)
     zero = jnp.zeros((s.hists, 2 * s.cols), jnp.float32)
 
@@ -232,7 +236,7 @@
         if s.count > 8:
             copy.start()
         copy.wait()
-    target = gather_targets(s, mass)
+    target = gather_targets(s, mass, s.rows)
     term_two = total / col_two[...]
     panel_two = (-term_two * (target / col_two[...])).astype(jnp.bfloat16)
 
@@ -341,7 +345,7 @@
     half = rows // s.halves
     cut = lambda x: [x[k * half : (k + 1) * half] for k in range(s.halves)]
     heads = [
-        jnp.concatenate([jnp.where(core == 0, a, d), jnp.where(core == 0, b, c)], axis=1)
+        jnp.stack([jnp.where(core == 0, a, d), jnp.where(core == 0, b, c)])
         for a, b, c, d in zip(cut(mine), cut(theirs), reversed(cut(mine)), reversed(cut(theirs)))
     ]
     heads, mass_here, points_here, cot_here, cot_points = lax.optimization_barrier(
@@ -363,13 +367,9 @@
                     (heads[k], mass_message, table)
                 )
                 came[step, k] = heads[k]
-            leaving = heads[k]
-            if step == last - 1 and k == 0:
-                mass = exchange(mass_message).astype(jnp.float32)
-                leaving, mass = lax.optimization_barrier((leaving, mass))
-            swapped[step, k] = swap_cores(leaving)
+            swapped[step, k] = swap_cores(heads[k])
     if s.halves == 1:
-        piece = lax.dynamic_slice_in_dim(heads[0], core * (rows // 2), rows // 2, 0)
+        piece = lax.dynamic_slice_in_dim(heads[0], core * (rows // 2), rows // 2, 1)
     else:
         piece = heads[0]
     due = [swapped[last - 2, k] for k in range(s.halves)]
@@ -379,6 +379,8 @@
     for step in range(1, last):
         for part in (came, swapped):
             units += [part[step, k] for k in range(s.halves)]
+    mass = exchange(mass_message).astype(jnp.float32)
+    piece, mass = lax.optimization_barrier((piece, mass))
     units += [piece, swap_cores(piece)]
     cot = exchange(cot_message).astype(jnp.float32)
 
@@ -386,6 +388,7 @@
     panel = jax.ShapeDtypeStruct((count, s.hists, rows), jnp.float32)
     sums = jax.ShapeDtypeStruct((count, 8, rows), jnp.float32)
     column = jax.ShapeDtypeStruct((s.hists, 2 * s.cols), jnp.float32)
+    points = jax.ShapeDtypeStruct((count, s.hists, 2 * share), jnp.float32)
     states = [panel, sums, column, column, column]
     thirds, *state = call(
         forward_kernel, s, 7, [wide], states, table, [mass, *units], states
@@ -398,7 +401,7 @@
         [],
         table,
         [mass, cot, thirds, *state, *units],
-        [*states, wide, wide],
+        [*states, panel, wide, points],
     )
 
     def by_point(pieces):

time: 147 us -> 145 us (0.986)
  waiting for transfers between devices: 39.1 us -> 34.4 us
  starting transfers between devices: 41.6 us -> 45 us
    ppermute x7, waiting for transfers between devices: 30 us -> 24.8 us  [onward(): return lax.ppermute(x, ('src', 'tgt'), pairs)]
    ppermute x12, starting transfers between devices: 9.28 us -> 12.3 us  [swap_cores(): return lax.ppermute(x, 'tgt', [(0, 1), (1, 0)])]
    another operation x0 -> x3, other arithmetic: none -> 1.77 us  [local(): jnp.stack([jnp.where(core == 0, a, d), jnp.where(core == 0, b, c)])]
    concatenate x2 -> x0, other arithmetic: 1.72 us -> none  [local(): jnp.concatenate([jnp.where(core == 0, a, d), jnp.where(core == 0, b, c)],...]
where the time goes in v16:
time: 145 us; the launch traced here: 144 us
  starting transfers between devices  45 us (31%)
  waiting for transfers between devices  34.4 us (24%)
  Pallas kernels  31.6 us (22%)
  other arithmetic  22.7 us (16%)
  local copies, waits for them, and re-layouts  8.23 us (6%)
    pallas_call x2, Pallas kernels, call(): pl.pallas_call(functools.partial(kernel, s), out_shape=[*vmem_outs, *hbm_...  31.6 us
    ppermute x7, waiting for transfers between devices, onward(): return lax.ppermute(x, ('src', 'tgt'), pairs)  24.8 us
    all_to_all x4, starting transfers between devices, exchange(): return lax.all_to_all(x, 'src', 0, 0, tiled=True)  23.6 us
    ppermute x12, starting transfers between devices, swap_cores(): return lax.ppermute(x, 'tgt', [(0, 1), (1, 0)])  12.3 us
    all_to_all x4, waiting for transfers between devices, exchange(): return lax.all_to_all(x, 'src', 0, 0, tiled=True)  9.52 us
    ppermute x7, starting transfers between devices, onward(): return lax.ppermute(x, ('src', 'tgt'), pairs)  9.11 us
    div x1, other arithmetic, local(): source_known = source_cotangent / source_mass  3.27 us
  transfers between devices with their start and end apart: 23, of which 7 were waited for; matrix products, arithmetic and copies ran while one was open for 17% of the time, Pallas kernels for 22%

profile of v16, /device:TPU:1, one launch (start us, length us, event | category | flops | bytes accessed | tf_op | source)
XLA Modules:
  0.0 144.3 jit_solution(13266850126013891863)
XLA Ops:
  7.5 2.7 %collective-permute-start.1 = (bf16[2,256,512]{2,1,0:T(8,128)(2,1)}, bf16[2,256,512]{2,1,0:T(8,128)(2,1)}, u32[]{:S(2)}, u32[]{:S(2)}) collective-permute-start(bf16[2,256,512]{2,1,0:T(8,128)(2,1)} %pad_maximum_fusion.2.refs_0_.refs_5_), channel_id=1, source_target_pairs={{0,4},{1,3},{4,8},{5,1},{8,12},{9,5},{12,14},{13,9},{14,10},{15,13... | collective-permute-start | bytes 1572872 | tf_op jit(solution)/shard_map/ppermute | solution.py:320
  15.2 2.3 %collective-permute-done.1.refs_2_.refs_7_ = bf16[2,256,512]{2,1,0:T(8,128)(2,1)} collective-permute-done((bf16[2,256,512]{2,1,0:T(8,128)(2,1)}, bf16[2,256,512]{2,1,0:T(8,128)(2,1)}, u32[]{:S(2)}, u32[]{:S(2)}) %collective-permute-start.1) | collective-permute-done | bytes 524320 | tf_op jit(solution)/shard_map/ppermute | solution.py:320
  17.4 1.4 collective-permute-start.2
  19.9 1.5 %copy.22 = f16[512,512]{1,0:T(8,128)(2,1)S(1)} copy(f16[512,512]{0,1:T(8,128)(2,1)} %get-tuple-element.91) | data formatting | bytes 1048576 | tf_op jit(solution)/shard_map/transpose | solution.py:337
  23.1 1.4 collective-permute-start.8
  25.8 2.9 %collective-permute-done.2.refs_6_.refs_11_ = bf16[2,256,512]{2,1,0:T(8,128)(2,1)} collective-permute-done((bf16[2,256,512]{2,1,0:T(8,128)(2,1)}, bf16[2,256,512]{2,1,0:T(8,128)(2,1)}, u32[]{:S(2)}, u32[]{:S(2)}) %collective-permute-start.2) | collective-permute-done | bytes 524320 | tf_op jit(solution)/shard_map/ppermute | solution.py:320
  28.7 5.7 %all-to-all-start = ((f16[8,64,640]{2,1,0:T(8,128)(2,1)}), f16[8,64,640]{2,1,0:T(8,128)(2,1)S(1)}, u32[]{:S(2)}, u32[]{:S(2)}) async-start(f16[8,64,640]{2,1,0:T(8,128)(2,1)} %pad_maximum_fusion), calls=%async_computation | async-start | bytes 1310720 | tf_op jit(solution)/shard_map/all_to_all | solution.py:323
  35.7 1.8 %collective-permute-start.5 = (bf16[2,256,512]{2,1,0:T(8,128)(2,1)}, bf16[2,256,512]{2,1,0:T(8,128)(2,1)}, u32[]{:S(2)}, u32[]{:S(2)}) collective-permute-start(bf16[2,256,512]{2,1,0:T(8,128)(2,1)} %collective-permute-done.2.refs_6_.refs_11_), channel_id=1, source_target_pairs={{0,4},{1,3},{4,8},{5,1},{8,12},{9,5},{12,14},{13,9},{14,10},{15,13... | collective-permute-start | bytes 1572872 | tf_op jit(solution)/shard_map/ppermute | solution.py:320
  40.5 12.4 %collective-permute-done.5.refs_10_.refs_15_ = bf16[2,256,512]{2,1,0:T(8,128)(2,1)} collective-permute-done((bf16[2,256,512]{2,1,0:T(8,128)(2,1)}, bf16[2,256,512]{2,1,0:T(8,128)(2,1)}, u32[]{:S(2)}, u32[]{:S(2)}) %collective-permute-start.5) | collective-permute-done | bytes 524320 | tf_op jit(solution)/shard_map/ppermute | solution.py:320
  52.9 3.9 %collective-permute-start.14 = (bf16[2,256,512]{2,1,0:T(8,128)(2,1)}, bf16[2,256,512]{2,1,0:T(8,128)(2,1)S(1)}, u32[]{:S(2)}, u32[]{:S(2)}) collective-permute-start(bf16[2,256,512]{2,1,0:T(8,128)(2,1)} %collective-permute-done.5.refs_10_.refs_15_), channel_id=1, source_target_pairs={{0,1},{1,0},{2,3},{3,2},{4,5},{5,4},{6,7},{7,6},{8,9},{9,8},{10,11... | collective-permute-start | bytes 1572872 | tf_op jit(solution)/shard_map/ppermute | solution.py:288
  56.8 2.3 %collective-permute-done.13.refs_11_.refs_16_ = bf16[2,256,512]{2,1,0:T(8,128)(2,1)S(1)} collective-permute-done((bf16[2,256,512]{2,1,0:T(8,128)(2,1)}, bf16[2,256,512]{2,1,0:T(8,128)(2,1)S(1)}, u32[]{:S(2)}, u32[]{:S(2)}) %collective-permute-start.13) | collective-permute-done | bytes 524320 | tf_op jit(solution)/shard_map/ppermute | solution.py:320
  60.3 4.6 %collective-permute-done.11.refs_14_.refs_19_ = bf16[2,256,512]{2,1,0:T(8,128)(2,1)S(1)} collective-permute-done((bf16[2,256,512]{2,1,0:T(8,128)(2,1)}, bf16[2,256,512]{2,1,0:T(8,128)(2,1)S(1)}, u32[]{:S(2)}, u32[]{:S(2)}) %collective-permute-start.11) | collective-permute-done | bytes 524320 | tf_op jit(solution)/shard_map/ppermute | solution.py:320
  65.0 7.0 %all-to-all-start.1 = ((f16[8,64,640]{2,1,0:T(8,128)(2,1)}), f16[8,64,640]{2,1,0:T(8,128)(2,1)S(1)}, u32[]{:S(2)}, u32[]{:S(2)}) async-start(f16[8,64,640]{2,1,0:T(8,128)(2,1)} %pad_maximum_fusion.1), calls=%async_computation.1 | async-start | bytes 1310720 | tf_op jit(solution)/shard_map/all_to_all | solution.py:323
  72.8 16.0 %shard_map.132 = (f32[8,64,640]{2,1,0:T(8,128)}, f32[8,64,512]{2,1,0:T(8,128)}, f32[8,8,512]{2,1,0:T(8,128)}, f32[64,1024]{1,0:T(8,128)}, f32[64,1024]{1,0:T(8,128)}, /*index=5*/f32[64,1024]{1,0:T(8,128)}) custom-call(s32[9]{0:T(128)} %pad_add_fusion.table, f32[8,64,640]{2,1,0:T(8,128)} %convert_element_type.63.mass_in, ...), custom_call_target="tpu_custom_call" | custom-call | flops 15032385536 | bytes 16777216 | tf_op jit(solution)/shard_map/pallas_call | solution.py:264
  88.8 2.2 %convert_element_type.66 = f16[8,64,640]{2,1,0:T(8,128)(2,1)} convert(f32[8,64,640]{2,1,0:T(8,128)} %get-tuple-element.53.thirds_in) | non-fusion elementwise | flops 327680 | bytes 1966080 | tf_op jit(solution)/shard_map/convert_element_type | solution.py:415
  91.0 5.4 %all-to-all-start.3 = ((f16[8,64,640]{2,1,0:T(8,128)(2,1)}), f16[8,64,640]{2,1,0:T(8,128)(2,1)S(1)}, u32[]{:S(2)}, u32[]{:S(2)}) async-start(f16[8,64,640]{2,1,0:T(8,128)(2,1)} %convert_element_type.66), calls=%async_computation.3 | async-start | bytes 1310720 | tf_op jit(solution)/shard_map/all_to_all | solution.py:323
  97.7 15.6 %shard_map.133 = f32[8,64,640]{2,1,0:T(8,128)} custom-call(s32[9]{0:T(128)} %pad_add_fusion.table, f32[8,64,640]{2,1,0:T(8,128)} %convert_element_type.63.mass_in, f32[8,64,640]{2,1,0:T(8,128)} %convert_element_type.64.cot_in, f32[8,64,640]{2,1,0:T(8,128)} %get-tuple-element.53.thirds_in, f32[8,64,512]{2,1,0:T(8,128)} %get-tuple-element.54.refs_0_, ...), custom_call_target="tpu_custom_call" | custom-call | flops 10737418240 | bytes 16777216 | tf_op jit(solution)/shard_map/pallas_call | solution.py:264
  113.3 2.3 %convert_element_type.65 = f16[8,64,640]{2,1,0:T(8,128)(2,1)} convert(f32[8,64,640]{2,1,0:T(8,128)} %shard_map.133) | non-fusion elementwise | flops 327680 | bytes 1966080 | tf_op jit(solution)/shard_map/convert_element_type | solution.py:422
  115.5 5.4 %all-to-all-start.2 = ((f16[8,64,640]{2,1,0:T(8,128)(2,1)}), f16[8,64,640]{2,1,0:T(8,128)(2,1)}, u32[]{:S(2)}, u32[]{:S(2)}) async-start(f16[8,64,640]{2,1,0:T(8,128)(2,1)} %convert_element_type.65), calls=%async_computation.2 | async-start | bytes 1310720 | tf_op jit(solution)/shard_map/all_to_all | solution.py:323
  121.6 1.5 %collective-permute-start.17 = (f16[64,512]{1,0:T(8,128)(2,1)S(1)}, f16[64,512]{1,0:T(8,128)(2,1)S(1)}, u32[]{:S(2)}, u32[]{:S(2)}) collective-permute-start(f16[64,512]{1,0:T(8,128)(2,1)S(1)} %fusion.7), channel_id=1, source_target_pairs={{0,1},{1,0},{2,3},{3,2},{4,5},{5,4},{6,7},{7,6},{8,9},{9,8},{10,11... | collective-permute-start | bytes 196616 | tf_op jit(solution)/shard_map/ppermute | solution.py:288
  123.1 3.3 %fusion.14 = (f32[512,512]{1,0:T(8,128)}, f32[512,512]{1,0:T(8,128)}) fusion(f32[512,512]{1,0:T(8,128)} %param.15, f32[512,512]{1,0:T(8,128)} %param.10, f32[640,512]{1,0:T(8,128)S(1)} %bitcast.85), kind=kLoop, calls=%fused_computation.62 | loop fusion | flops 524288 | bytes 5242880 | tf_op jit(solution)/shard_map/div | solution.py:418
  127.2 9.5 %all-to-all-done.2 = f16[8,64,640]{2,1,0:T(8,128)(2,1)} async-done(((f16[8,64,640]{2,1,0:T(8,128)(2,1)}), f16[8,64,640]{2,1,0:T(8,128)(2,1)}, u32[]{:S(2)}, u32[]{:S(2)}) %all-to-all-start.2) | async-done | bytes 655392 | tf_op jit(solution)/shard_map/all_to_all | solution.py:323
  138.4 2.7 %collective-permute-start.18 = (f16[64,512]{1,0:T(8,128)(2,1)S(1)}, f16[64,512]{1,0:T(8,128)(2,1)S(1)}, u32[]{:S(2)}, u32[]{:S(2)}) collective-permute-start(f16[64,512]{1,0:T(8,128)(2,1)S(1)} %fusion.8), channel_id=1, source_target_pairs={{0,1},{1,0},{2,3},{3,2},{4,5},{5,4},{6,7},{7,6},{8,9},{9,8},{10,11... | collective-permute-start | bytes 196616 | tf_op jit(solution)/shard_map/ppermute | solution.py:288
  141.1 2.4 %fusion = f32[512,512]{1,0:T(8,128)} fusion(f32[512,512]{1,0:T(8,128)} %get-tuple-element.61, f32[640,512]{1,0:T(8,128)S(1)} %bitcast.87), kind=kLoop, calls=%fused_computation.3 | loop fusion | flops 524288 | bytes 3145728 | tf_op jit(solution)/shard_map/add | solution.py:433
  (104 shorter events, 27.1 us)
Async XLA Ops:
  3.2 2.5 %collective-permute-start = (bf16[512,512]{1,0:T(8,128)(2,1)S(1)}, bf16[512,512]{1,0:T(8,128)(2,1)S(1)}, u32[]{:S(2)}, u32[]{:S(2)}) collective-permute-start(bf16[512,512]{1,0:T(8,128)(2,1)S(1)} %bitcast.104), channel_id=1, source_target_pairs={{0,1},{1,0},{2,3},{3,2},{4,5},{5,4},{6,7},{7,6},{8,9},{9,8},{10,11... | collective-permute-start | bytes 1572872 | tf_op jit(solution)/shard_map/ppermute | solution.py:288
  7.5 9.9 %collective-permute-start.1 = (bf16[2,256,512]{2,1,0:T(8,128)(2,1)}, bf16[2,256,512]{2,1,0:T(8,128)(2,1)}, u32[]{:S(2)}, u32[]{:S(2)}) collective-permute-start(bf16[2,256,512]{2,1,0:T(8,128)(2,1)} %pad_maximum_fusion.2.refs_0_.refs_5_), channel_id=1, source_target_pairs={{0,4},{1,3},{4,8},{5,1},{8,12},{9,5},{12,14},{13,9},{14,10},{15,13... | collective-permute-start | bytes 1572872 | tf_op jit(solution)/shard_map/ppermute | solution.py:320
  11.1 11.9 %collective-permute-start.7 = (bf16[2,256,512]{2,1,0:T(8,128)(2,1)}, bf16[2,256,512]{2,1,0:T(8,128)(2,1)}, u32[]{:S(2)}, u32[]{:S(2)}) collective-permute-start(bf16[2,256,512]{2,1,0:T(8,128)(2,1)} %pad_maximum_fusion.3.refs_1_.refs_6_), channel_id=1, source_target_pairs={{0,4},{1,3},{4,8},{5,1},{8,12},{9,5},{12,14},{13,9},{14,10},{15,13... | collective-permute-start | bytes 1572872 | tf_op jit(solution)/shard_map/ppermute | solution.py:320
  13.5 11.0 %collective-permute-start.10 = (f16[64,512]{1,0:T(8,128)(2,1)}, f16[64,512]{1,0:T(8,128)(2,1)S(1)}, u32[]{:S(2)}, u32[]{:S(2)}) collective-permute-start(f16[64,512]{1,0:T(8,128)(2,1)} %bitcast.82), channel_id=1, source_target_pairs={{0,1},{1,0},{2,3},{3,2},{4,5},{5,4},{6,7},{7,6},{8,9},{9,8},{10,11... | collective-permute-start | bytes 196616 | tf_op jit(solution)/shard_map/ppermute | solution.py:288
  15.2 9.3 %collective-permute-start.3 = (f16[64,512]{1,0:T(8,128)(2,1)}, f16[64,512]{1,0:T(8,128)(2,1)S(1)}, u32[]{:S(2)}, u32[]{:S(2)}) collective-permute-start(f16[64,512]{1,0:T(8,128)(2,1)} %bitcast.83), channel_id=1, source_target_pairs={{0,1},{1,0},{2,3},{3,2},{4,5},{5,4},{6,7},{7,6},{8,9},{9,8},{10,11... | collective-permute-start | bytes 196616 | tf_op jit(solution)/shard_map/ppermute | solution.py:288
  17.4 11.2 %collective-permute-start.2 = (bf16[2,256,512]{2,1,0:T(8,128)(2,1)}, bf16[2,256,512]{2,1,0:T(8,128)(2,1)}, u32[]{:S(2)}, u32[]{:S(2)}) collective-permute-start(bf16[2,256,512]{2,1,0:T(8,128)(2,1)} %collective-permute-done.1.refs_2_.refs_7_), channel_id=1, source_target_pairs={{0,4},{1,3},{4,8},{5,1},{8,12},{9,5},{12,14},{13,9},{14,10},{15,13... | collective-permute-start | bytes 1572872 | tf_op jit(solution)/shard_map/ppermute | solution.py:320
  21.4 14.2 %collective-permute-start.4 = (bf16[2,256,512]{2,1,0:T(8,128)(2,1)}, bf16[2,256,512]{2,1,0:T(8,128)(2,1)S(1)}, u32[]{:S(2)}, u32[]{:S(2)}) collective-permute-start(bf16[2,256,512]{2,1,0:T(8,128)(2,1)} %collective-permute-done.1.refs_2_.refs_7_), channel_id=1, source_target_pairs={{0,1},{1,0},{2,3},{3,2},{4,5},{5,4},{6,7},{7,6},{8,9},{9,8},{10,11... | collective-permute-start | bytes 1572872 | tf_op jit(solution)/shard_map/ppermute | solution.py:288
  23.1 12.6 %collective-permute-start.8 = (bf16[2,256,512]{2,1,0:T(8,128)(2,1)}, bf16[2,256,512]{2,1,0:T(8,128)(2,1)}, u32[]{:S(2)}, u32[]{:S(2)}) collective-permute-start(bf16[2,256,512]{2,1,0:T(8,128)(2,1)} %collective-permute-done.7.refs_3_.refs_8_), channel_id=1, source_target_pairs={{0,4},{1,3},{4,8},{5,1},{8,12},{9,5},{12,14},{13,9},{14,10},{15,13... | collective-permute-start | bytes 1572872 | tf_op jit(solution)/shard_map/ppermute | solution.py:320
  28.7 30.4 %all-to-all-start = ((f16[8,64,640]{2,1,0:T(8,128)(2,1)}), f16[8,64,640]{2,1,0:T(8,128)(2,1)S(1)}, u32[]{:S(2)}, u32[]{:S(2)}) async-start(f16[8,64,640]{2,1,0:T(8,128)(2,1)} %pad_maximum_fusion), calls=%async_computation | async-start | bytes 1310720 | tf_op jit(solution)/shard_map/all_to_all | solution.py:323
  34.4 5.5 %collective-permute-start.12 = (bf16[2,256,512]{2,1,0:T(8,128)(2,1)}, bf16[2,256,512]{2,1,0:T(8,128)(2,1)S(1)}, u32[]{:S(2)}, u32[]{:S(2)}) collective-permute-start(bf16[2,256,512]{2,1,0:T(8,128)(2,1)} %collective-permute-done.7.refs_3_.refs_8_), channel_id=1, source_target_pairs={{0,1},{1,0},{2,3},{3,2},{4,5},{5,4},{6,7},{7,6},{8,9},{9,8},{10,11... | collective-permute-start | bytes 1572872 | tf_op jit(solution)/shard_map/ppermute | solution.py:288
  35.6 4.8 %collective-permute-start.9 = (bf16[2,256,512]{2,1,0:T(8,128)(2,1)}, bf16[2,256,512]{2,1,0:T(8,128)(2,1)}, u32[]{:S(2)}, u32[]{:S(2)}) collective-permute-start(bf16[2,256,512]{2,1,0:T(8,128)(2,1)} %collective-permute-done.8.refs_7_.refs_12_), channel_id=1, source_target_pairs={{0,1},{1,0},{2,3},{3,2},{4,5},{5,4},{6,7},{7,6},{8,9},{9,8},{10,11... | collective-permute-start | bytes 1572872 | tf_op jit(solution)/shard_map/ppermute | solution.py:288
  35.7 17.2 %collective-permute-start.5 = (bf16[2,256,512]{2,1,0:T(8,128)(2,1)}, bf16[2,256,512]{2,1,0:T(8,128)(2,1)}, u32[]{:S(2)}, u32[]{:S(2)}) collective-permute-start(bf16[2,256,512]{2,1,0:T(8,128)(2,1)} %collective-permute-done.2.refs_6_.refs_11_), channel_id=1, source_target_pairs={{0,4},{1,3},{4,8},{5,1},{8,12},{9,5},{12,14},{13,9},{14,10},{15,13... | collective-permute-start | bytes 1572872 | tf_op jit(solution)/shard_map/ppermute | solution.py:320
  37.5 15.4 %collective-permute-start.6 = (bf16[2,256,512]{2,1,0:T(8,128)(2,1)}, bf16[2,256,512]{2,1,0:T(8,128)(2,1)}, u32[]{:S(2)}, u32[]{:S(2)}) collective-permute-start(bf16[2,256,512]{2,1,0:T(8,128)(2,1)} %collective-permute-done.2.refs_6_.refs_11_), channel_id=1, source_target_pairs={{0,1},{1,0},{2,3},{3,2},{4,5},{5,4},{6,7},{7,6},{8,9},{9,8},{10,11... | collective-permute-start | bytes 1572872 | tf_op jit(solution)/shard_map/ppermute | solution.py:288
  39.9 25.0 %copy-start.10 = (bf16[2,256,512]{2,1,0:T(8,128)(2,1)}, bf16[2,256,512]{2,1,0:T(8,128)(2,1)S(1)}, u32[]{:S(2)}) copy-start(bf16[2,256,512]{2,1,0:T(8,128)(2,1)S(1)} %collective-permute-done.12.refs_5_.refs_10_) | copy-start | bytes 1572868
  39.9 19.1 %collective-permute-start.13 = (bf16[2,256,512]{2,1,0:T(8,128)(2,1)}, bf16[2,256,512]{2,1,0:T(8,128)(2,1)S(1)}, u32[]{:S(2)}, u32[]{:S(2)}) collective-permute-start(bf16[2,256,512]{2,1,0:T(8,128)(2,1)} %collective-permute-done.8.refs_7_.refs_12_), channel_id=1, source_target_pairs={{0,4},{1,3},{4,8},{5,1},{8,12},{9,5},{12,14},{13,9},{14,10},{15,13... | collective-permute-start | bytes 1572872 | tf_op jit(solution)/shard_map/ppermute | solution.py:320
  52.9 12.0 %collective-permute-start.11 = (bf16[2,256,512]{2,1,0:T(8,128)(2,1)}, bf16[2,256,512]{2,1,0:T(8,128)(2,1)S(1)}, u32[]{:S(2)}, u32[]{:S(2)}) collective-permute-start(bf16[2,256,512]{2,1,0:T(8,128)(2,1)} %collective-permute-done.5.refs_10_.refs_15_), channel_id=1, source_target_pairs={{0,4},{1,3},{4,8},{5,1},{8,12},{9,5},{12,14},{13,9},{14,10},{15,13... | collective-permute-start | bytes 1572872 | tf_op jit(solution)/shard_map/ppermute | solution.py:320
  52.9 19.1 %collective-permute-start.14 = (bf16[2,256,512]{2,1,0:T(8,128)(2,1)}, bf16[2,256,512]{2,1,0:T(8,128)(2,1)S(1)}, u32[]{:S(2)}, u32[]{:S(2)}) collective-permute-start(bf16[2,256,512]{2,1,0:T(8,128)(2,1)} %collective-permute-done.5.refs_10_.refs_15_), channel_id=1, source_target_pairs={{0,1},{1,0},{2,3},{3,2},{4,5},{5,4},{6,7},{7,6},{8,9},{9,8},{10,11... | collective-permute-start | bytes 1572872 | tf_op jit(solution)/shard_map/ppermute | solution.py:288
  59.1 12.9 %collective-permute-start.15 = (bf16[2,256,512]{2,1,0:T(8,128)(2,1)S(1)}, bf16[2,256,512]{2,1,0:T(8,128)(2,1)}, u32[]{:S(2)}, u32[]{:S(2)}) collective-permute-start(bf16[2,256,512]{2,1,0:T(8,128)(2,1)S(1)} %collective-permute-done.13.refs_11_.refs_16_), channel_id=1, source_target_pairs={{0,1},{1,0},{2,3},{3,2},{4,5},{5,4},{6,7},{7,6},{8,9},{9,8},{10,11... | collective-permute-start | bytes 1572872 | tf_op jit(solution)/shard_map/ppermute | solution.py:288
  64.9 7.1 %collective-permute-start.16 = (bf16[2,256,512]{2,1,0:T(8,128)(2,1)S(1)}, bf16[2,256,512]{2,1,0:T(8,128)(2,1)}, u32[]{:S(2)}, u32[]{:S(2)}) collective-permute-start(bf16[2,256,512]{2,1,0:T(8,128)(2,1)S(1)} %collective-permute-done.11.refs_14_.refs_19_), channel_id=1, source_target_pairs={{0,1},{1,0},{2,3},{3,2},{4,5},{5,4},{6,7},{7,6},{8,9},{9,8},{10,11... | collective-permute-start | bytes 1572872 | tf_op jit(solution)/shard_map/ppermute | solution.py:288
  65.0 26.1 %all-to-all-start.1 = ((f16[8,64,640]{2,1,0:T(8,128)(2,1)}), f16[8,64,640]{2,1,0:T(8,128)(2,1)S(1)}, u32[]{:S(2)}, u32[]{:S(2)}) async-start(f16[8,64,640]{2,1,0:T(8,128)(2,1)} %pad_maximum_fusion.1), calls=%async_computation.1 | async-start | bytes 1310720 | tf_op jit(solution)/shard_map/all_to_all | solution.py:323
  91.0 24.5 %all-to-all-start.3 = ((f16[8,64,640]{2,1,0:T(8,128)(2,1)}), f16[8,64,640]{2,1,0:T(8,128)(2,1)S(1)}, u32[]{:S(2)}, u32[]{:S(2)}) async-start(f16[8,64,640]{2,1,0:T(8,128)(2,1)} %convert_element_type.66), calls=%async_computation.3 | async-start | bytes 1310720 | tf_op jit(solution)/shard_map/all_to_all | solution.py:323
  115.5 21.2 %all-to-all-start.2 = ((f16[8,64,640]{2,1,0:T(8,128)(2,1)}), f16[8,64,640]{2,1,0:T(8,128)(2,1)}, u32[]{:S(2)}, u32[]{:S(2)}) async-start(f16[8,64,640]{2,1,0:T(8,128)(2,1)} %convert_element_type.65), calls=%async_computation.2 | async-start | bytes 1310720 | tf_op jit(solution)/shard_map/all_to_all | solution.py:323
  121.6 4.8 %collective-permute-start.17 = (f16[64,512]{1,0:T(8,128)(2,1)S(1)}, f16[64,512]{1,0:T(8,128)(2,1)S(1)}, u32[]{:S(2)}, u32[]{:S(2)}) collective-permute-start(f16[64,512]{1,0:T(8,128)(2,1)S(1)} %fusion.7), channel_id=1, source_target_pairs={{0,1},{1,0},{2,3},{3,2},{4,5},{5,4},{6,7},{7,6},{8,9},{9,8},{10,11... | collective-permute-start | bytes 196616 | tf_op jit(solution)/shard_map/ppermute | solution.py:288
  138.4 5.1 %collective-permute-start.18 = (f16[64,512]{1,0:T(8,128)(2,1)S(1)}, f16[64,512]{1,0:T(8,128)(2,1)S(1)}, u32[]{:S(2)}, u32[]{:S(2)}) collective-permute-start(f16[64,512]{1,0:T(8,128)(2,1)S(1)} %fusion.8), channel_id=1, source_target_pairs={{0,1},{1,0},{2,3},{3,2},{4,5},{5,4},{6,7},{7,6},{8,9},{9,8},{10,11... | collective-permute-start | bytes 196616 | tf_op jit(solution)/shard_map/ppermute | solution.py:288
  (14 other events, 58.7 us)

commit v17 on v16

--- a/solution.py
+++ b/solution.py
@@ -344,10 +344,9 @@
     theirs = swap_cores(mine)
     half = rows // s.halves
     cut = lambda x: [x[k * half : (k + 1) * half] for k in range(s.halves)]
-    heads = [
-        jnp.stack([jnp.where(core == 0, a, d), jnp.where(core == 0, b, c)])
-        for a, b, c, d in zip(cut(mine), cut(theirs), reversed(cut(mine)), reversed(cut(theirs)))
-    ]
+    own_set = (jnp.arange(2, dtype=jnp.int32) == core)[:, None, None]
+    pick = lambda x: [jnp.where(core == 0, *pair) for pair in zip(cut(x), reversed(cut(x)))]
+    heads = [jnp.where(own_set, a[None], b[None]) for a, b in zip(pick(mine), pick(theirs))]
     heads, mass_here, points_here, cot_here, cot_points = lax.optimization_barrier(
         (heads, source_mass, target_mass[0], source_cotangent, target_cotangent[0])
     )
@@ -362,12 +361,11 @@
                     (heads[k], swapped[step - 2, k])
                 )
             came[step, k] = heads[k] = onward(heads[k])
+            swapped[step, k] = swap_cores(heads[k])
             if step == min(2, last - 1) and k == 0:
-                heads[k], mass_message, table = lax.optimization_barrier(
-                    (heads[k], mass_message, table)
+                swapped[step, k], mass_message, table = lax.optimization_barrier(
+                    (swapped[step, k], mass_message, table)
                 )
-                came[step, k] = heads[k]
-            swapped[step, k] = swap_cores(heads[k])
     if s.halves == 1:
         piece = lax.dynamic_slice_in_dim(heads[0], core * (rows // 2), rows // 2, 1)
     else:

time: 145 us -> 149 us (1.028)
  starting transfers between devices: 45 us -> 50.4 us
    ppermute x12, starting transfers between devices: 12.3 us -> 18 us  [swap_cores(): return lax.ppermute(x, 'tgt', [(0, 1), (1, 0)])]
    ppermute x7, waiting for transfers between devices: 24.8 us -> 22.9 us  [onward(): return lax.ppermute(x, ('src', 'tgt'), pairs)]
    another operation x3 -> x0, other arithmetic: 1.77 us -> none  [local(): jnp.stack([jnp.where(core == 0, a, d), jnp.where(core == 0, b, c)])]
  transfers between devices with their start and end apart: 23 -> 23, of which waited for: 7 -> 8; matrix products, arithmetic and copies ran while one was open for 17% -> 17% of each run, Pallas kernels for 22% -> 21%
where the time goes in v17:
time: 149 us; the launch traced here: 148 us
  starting transfers between devices  50.4 us (34%)
  waiting for transfers between devices  33.8 us (23%)
  Pallas kernels  31.5 us (21%)
  other arithmetic  22.4 us (15%)
  local copies, waits for them, and re-layouts  7.82 us (5%)
    pallas_call x2, Pallas kernels, call(): pl.pallas_call(functools.partial(kernel, s), out_shape=[*vmem_outs, *hbm_...  31.5 us
    ppermute x7, waiting for transfers between devices, onward(): return lax.ppermute(x, ('src', 'tgt'), pairs)  22.9 us
    all_to_all x4, starting transfers between devices, exchange(): return lax.all_to_all(x, 'src', 0, 0, tiled=True)  22.5 us
    ppermute x12, starting transfers between devices, swap_cores(): return lax.ppermute(x, 'tgt', [(0, 1), (1, 0)])  18 us
    ppermute x7, starting transfers between devices, onward(): return lax.ppermute(x, ('src', 'tgt'), pairs)  9.91 us
    all_to_all x4, waiting for transfers between devices, exchange(): return lax.all_to_all(x, 'src', 0, 0, tiled=True)  9.52 us
    div x1, other arithmetic, local(): source_known = source_cotangent / source_mass  3.27 us
  transfers between devices with their start and end apart: 23, of which 8 were waited for; matrix products, arithmetic and copies ran while one was open for 17% of the time, Pallas kernels for 21%

profile of v17, /device:TPU:1, one launch (start us, length us, event | category | flops | bytes accessed | tf_op | source)
XLA Modules:
  0.0 148.3 jit_solution(15547943701396699608)
XLA Ops:
  6.2 2.4 %collective-permute-start.1 = (bf16[2,256,512]{2,1,0:T(8,128)(2,1)S(1)}, bf16[2,256,512]{2,1,0:T(8,128)(2,1)}, u32[]{:S(2)}, u32[]{:S(2)}) collective-permute-start(bf16[2,256,512]{2,1,0:T(8,128)(2,1)S(1)} %get-tuple-element.34.refs_0_.refs_5_), channel_id=1, source_target_pairs={{0,4},{1,3},{4,8},{5,1},{8,12},{9,5},{12,14},{13,9},{14,10},{15,13... | collective-permute-start | bytes 1572872 | tf_op jit(solution)/shard_map/ppermute | solution.py:320
  10.5 5.1 %collective-permute-done.1.refs_2_.refs_7_ = bf16[2,256,512]{2,1,0:T(8,128)(2,1)} collective-permute-done((bf16[2,256,512]{2,1,0:T(8,128)(2,1)S(1)}, bf16[2,256,512]{2,1,0:T(8,128)(2,1)}, u32[]{:S(2)}, u32[]{:S(2)}) %collective-permute-start.1) | collective-permute-done | bytes 524320 | tf_op jit(solution)/shard_map/ppermute | solution.py:320
  20.3 1.8 %collective-permute-start.10 = (f16[64,512]{1,0:T(8,128)(2,1)}, f16[64,512]{1,0:T(8,128)(2,1)S(1)}, u32[]{:S(2)}, u32[]{:S(2)}) collective-permute-start(f16[64,512]{1,0:T(8,128)(2,1)} %bitcast.74), channel_id=1, source_target_pairs={{0,1},{1,0},{2,3},{3,2},{4,5},{5,4},{6,7},{7,6},{8,9},{9,8},{10,11... | collective-permute-start | bytes 196616 | tf_op jit(solution)/shard_map/ppermute | solution.py:288
  24.3 1.7 %collective-permute-start.3 = (bf16[2,256,512]{2,1,0:T(8,128)(2,1)}, bf16[2,256,512]{2,1,0:T(8,128)(2,1)}, u32[]{:S(2)}, u32[]{:S(2)}) collective-permute-start(bf16[2,256,512]{2,1,0:T(8,128)(2,1)} %collective-permute-done.2.refs_6_.refs_11_), channel_id=1, source_target_pairs={{0,1},{1,0},{2,3},{3,2},{4,5},{5,4},{6,7},{7,6},{8,9},{9,8},{10,11... | collective-permute-start | bytes 1572872 | tf_op jit(solution)/shard_map/ppermute | solution.py:288
  27.0 1.5 %copy.22 = f16[512,512]{1,0:T(8,128)(2,1)S(1)} copy(f16[512,512]{0,1:T(8,128)(2,1)} %get-tuple-element.89) | data formatting | bytes 1048576 | tf_op jit(solution)/shard_map/transpose | solution.py:337
  32.6 4.6 %all-to-all-start = ((f16[8,64,640]{2,1,0:T(8,128)(2,1)}), f16[8,64,640]{2,1,0:T(8,128)(2,1)S(1)}, u32[]{:S(2)}, u32[]{:S(2)}) async-start(f16[8,64,640]{2,1,0:T(8,128)(2,1)} %pad_maximum_fusion), calls=%async_computation | async-start | bytes 1310720 | tf_op jit(solution)/shard_map/all_to_all | solution.py:323
  37.2 2.6 %collective-permute-start.12 = (bf16[2,256,512]{2,1,0:T(8,128)(2,1)}, bf16[2,256,512]{2,1,0:T(8,128)(2,1)S(1)}, u32[]{:S(2)}, u32[]{:S(2)}) collective-permute-start(bf16[2,256,512]{2,1,0:T(8,128)(2,1)} %collective-permute-done.7.refs_3_.refs_8_), channel_id=1, source_target_pairs={{0,1},{1,0},{2,3},{3,2},{4,5},{5,4},{6,7},{7,6},{8,9},{9,8},{10,11... | collective-permute-start | bytes 1572872 | tf_op jit(solution)/shard_map/ppermute | solution.py:288
  39.8 1.7 %collective-permute-start.6 = (bf16[2,256,512]{2,1,0:T(8,128)(2,1)}, bf16[2,256,512]{2,1,0:T(8,128)(2,1)}, u32[]{:S(2)}, u32[]{:S(2)}) collective-permute-start(bf16[2,256,512]{2,1,0:T(8,128)(2,1)} %collective-permute-done.2.refs_6_.refs_11_), channel_id=1, source_target_pairs={{0,4},{1,3},{4,8},{5,1},{8,12},{9,5},{12,14},{13,9},{14,10},{15,13... | collective-permute-start | bytes 1572872 | tf_op jit(solution)/shard_map/ppermute | solution.py:320
  44.7 1.6 %collective-permute-start.13 = (bf16[2,256,512]{2,1,0:T(8,128)(2,1)}, bf16[2,256,512]{2,1,0:T(8,128)(2,1)S(1)}, u32[]{:S(2)}, u32[]{:S(2)}) collective-permute-start(bf16[2,256,512]{2,1,0:T(8,128)(2,1)} %collective-permute-done.8.refs_7_.refs_12_), channel_id=1, source_target_pairs={{0,4},{1,3},{4,8},{5,1},{8,12},{9,5},{12,14},{13,9},{14,10},{15,13... | collective-permute-start | bytes 1572872 | tf_op jit(solution)/shard_map/ppermute | solution.py:320
  46.3 10.7 %collective-permute-done.6.refs_10_.refs_15_ = bf16[2,256,512]{2,1,0:T(8,128)(2,1)} collective-permute-done((bf16[2,256,512]{2,1,0:T(8,128)(2,1)}, bf16[2,256,512]{2,1,0:T(8,128)(2,1)}, u32[]{:S(2)}, u32[]{:S(2)}) %collective-permute-start.6) | collective-permute-done | bytes 524320 | tf_op jit(solution)/shard_map/ppermute | solution.py:320
  57.0 5.0 %collective-permute-start.14 = (bf16[2,256,512]{2,1,0:T(8,128)(2,1)}, bf16[2,256,512]{2,1,0:T(8,128)(2,1)S(1)}, u32[]{:S(2)}, u32[]{:S(2)}) collective-permute-start(bf16[2,256,512]{2,1,0:T(8,128)(2,1)} %collective-permute-done.6.refs_10_.refs_15_), channel_id=1, source_target_pairs={{0,1},{1,0},{2,3},{3,2},{4,5},{5,4},{6,7},{7,6},{8,9},{9,8},{10,11... | collective-permute-start | bytes 1572872 | tf_op jit(solution)/shard_map/ppermute | solution.py:288
  64.0 4.0 %collective-permute-done.11.refs_14_.refs_19_ = bf16[2,256,512]{2,1,0:T(8,128)(2,1)S(1)} collective-permute-done((bf16[2,256,512]{2,1,0:T(8,128)(2,1)}, bf16[2,256,512]{2,1,0:T(8,128)(2,1)S(1)}, u32[]{:S(2)}, u32[]{:S(2)}) %collective-permute-start.11) | collective-permute-done | bytes 524320 | tf_op jit(solution)/shard_map/ppermute | solution.py:320
  69.0 7.0 %all-to-all-start.1 = ((f16[8,64,640]{2,1,0:T(8,128)(2,1)}), f16[8,64,640]{2,1,0:T(8,128)(2,1)S(1)}, u32[]{:S(2)}, u32[]{:S(2)}) async-start(f16[8,64,640]{2,1,0:T(8,128)(2,1)} %pad_maximum_fusion.1), calls=%async_computation.1 | async-start | bytes 1310720 | tf_op jit(solution)/shard_map/all_to_all | solution.py:323
  76.9 16.0 %shard_map.132 = (f32[8,64,640]{2,1,0:T(8,128)}, f32[8,64,512]{2,1,0:T(8,128)}, f32[8,8,512]{2,1,0:T(8,128)}, f32[64,1024]{1,0:T(8,128)}, f32[64,1024]{1,0:T(8,128)}, /*index=5*/f32[64,1024]{1,0:T(8,128)}) custom-call(s32[9]{0:T(128)} %pad_add_fusion.table, f32[8,64,640]{2,1,0:T(8,128)} %convert_element_type.63.mass_in, bf16[2,256,512]{2,1,0:T(8,128)(2,1)} %copy-done.8, ...), custom_call_target="tpu_custom_call" | custom-call | flops 15032385536 | bytes 16777216 | tf_op jit(solution)/shard_map/pallas_call | solution.py:264
  92.9 2.2 %convert_element_type.66 = f16[8,64,640]{2,1,0:T(8,128)(2,1)} convert(f32[8,64,640]{2,1,0:T(8,128)} %get-tuple-element.53.thirds_in) | non-fusion elementwise | flops 327680 | bytes 1966080 | tf_op jit(solution)/shard_map/convert_element_type | solution.py:413
  95.1 5.4 %all-to-all-start.3 = ((f16[8,64,640]{2,1,0:T(8,128)(2,1)}), f16[8,64,640]{2,1,0:T(8,128)(2,1)S(1)}, u32[]{:S(2)}, u32[]{:S(2)}) async-start(f16[8,64,640]{2,1,0:T(8,128)(2,1)} %convert_element_type.66), calls=%async_computation.3 | async-start | bytes 1310720 | tf_op jit(solution)/shard_map/all_to_all | solution.py:323
  101.7 15.6 %shard_map.133 = f32[8,64,640]{2,1,0:T(8,128)} custom-call(s32[9]{0:T(128)} %pad_add_fusion.table, f32[8,64,640]{2,1,0:T(8,128)} %convert_element_type.63.mass_in, f32[8,64,640]{2,1,0:T(8,128)} %convert_element_type.64.cot_in, f32[8,64,640]{2,1,0:T(8,128)} %get-tuple-element.53.thirds_in, f32[8,64,512]{2,1,0:T(8,128)} %get-tuple-element.54.refs_0_, ...), custom_call_target="tpu_custom_call" | custom-call | flops 10737418240 | bytes 16777216 | tf_op jit(solution)/shard_map/pallas_call | solution.py:264
  117.3 2.3 %convert_element_type.65 = f16[8,64,640]{2,1,0:T(8,128)(2,1)} convert(f32[8,64,640]{2,1,0:T(8,128)} %shard_map.133) | non-fusion elementwise | flops 327680 | bytes 1966080 | tf_op jit(solution)/shard_map/convert_element_type | solution.py:420
  119.6 5.4 %all-to-all-start.2 = ((f16[8,64,640]{2,1,0:T(8,128)(2,1)}), f16[8,64,640]{2,1,0:T(8,128)(2,1)}, u32[]{:S(2)}, u32[]{:S(2)}) async-start(f16[8,64,640]{2,1,0:T(8,128)(2,1)} %convert_element_type.65), calls=%async_computation.2 | async-start | bytes 1310720 | tf_op jit(solution)/shard_map/all_to_all | solution.py:323
  125.7 1.5 %collective-permute-start.17 = (f16[64,512]{1,0:T(8,128)(2,1)S(1)}, f16[64,512]{1,0:T(8,128)(2,1)S(1)}, u32[]{:S(2)}, u32[]{:S(2)}) collective-permute-start(f16[64,512]{1,0:T(8,128)(2,1)S(1)} %fusion.7), channel_id=1, source_target_pairs={{0,1},{1,0},{2,3},{3,2},{4,5},{5,4},{6,7},{7,6},{8,9},{9,8},{10,11... | collective-permute-start | bytes 196616 | tf_op jit(solution)/shard_map/ppermute | solution.py:288
  127.2 3.3 %fusion.14 = (f32[512,512]{1,0:T(8,128)}, f32[512,512]{1,0:T(8,128)}) fusion(f32[512,512]{1,0:T(8,128)} %param.15, f32[512,512]{1,0:T(8,128)} %param.10, f32[640,512]{1,0:T(8,128)S(1)} %bitcast.77), kind=kLoop, calls=%fused_computation.63 | loop fusion | flops 524288 | bytes 5242880 | tf_op jit(solution)/shard_map/div | solution.py:416
  131.3 9.5 %all-to-all-done.2 = f16[8,64,640]{2,1,0:T(8,128)(2,1)} async-done(((f16[8,64,640]{2,1,0:T(8,128)(2,1)}), f16[8,64,640]{2,1,0:T(8,128)(2,1)}, u32[]{:S(2)}, u32[]{:S(2)}) %all-to-all-start.2) | async-done | bytes 655392 | tf_op jit(solution)/shard_map/all_to_all | solution.py:323
  142.4 2.7 %collective-permute-start.18 = (f16[64,512]{1,0:T(8,128)(2,1)S(1)}, f16[64,512]{1,0:T(8,128)(2,1)S(1)}, u32[]{:S(2)}, u32[]{:S(2)}) collective-permute-start(f16[64,512]{1,0:T(8,128)(2,1)S(1)} %fusion.8), channel_id=1, source_target_pairs={{0,1},{1,0},{2,3},{3,2},{4,5},{5,4},{6,7},{7,6},{8,9},{9,8},{10,11... | collective-permute-start | bytes 196616 | tf_op jit(solution)/shard_map/ppermute | solution.py:288
  145.1 2.4 %fusion = f32[512,512]{1,0:T(8,128)} fusion(f32[512,512]{1,0:T(8,128)} %get-tuple-element.61, f32[640,512]{1,0:T(8,128)S(1)} %bitcast.79), kind=kLoop, calls=%fused_computation.3 | loop fusion | flops 524288 | bytes 3145728 | tf_op jit(solution)/shard_map/add | solution.py:431
  (106 shorter events, 31.1 us)
Async XLA Ops:
  3.2 2.0 %collective-permute-start = (bf16[512,512]{1,0:T(8,128)(2,1)S(1)}, bf16[512,512]{1,0:T(8,128)(2,1)S(1)}, u32[]{:S(2)}, u32[]{:S(2)}) collective-permute-start(bf16[512,512]{1,0:T(8,128)(2,1)S(1)} %bitcast.96), channel_id=1, source_target_pairs={{0,1},{1,0},{2,3},{3,2},{4,5},{5,4},{6,7},{7,6},{8,9},{9,8},{10,11... | collective-permute-start | bytes 1572872 | tf_op jit(solution)/shard_map/ppermute | solution.py:288
  6.2 9.4 %collective-permute-start.1 = (bf16[2,256,512]{2,1,0:T(8,128)(2,1)S(1)}, bf16[2,256,512]{2,1,0:T(8,128)(2,1)}, u32[]{:S(2)}, u32[]{:S(2)}) collective-permute-start(bf16[2,256,512]{2,1,0:T(8,128)(2,1)S(1)} %get-tuple-element.34.refs_0_.refs_5_), channel_id=1, source_target_pairs={{0,4},{1,3},{4,8},{5,1},{8,12},{9,5},{12,14},{13,9},{14,10},{15,13... | collective-permute-start | bytes 1572872 | tf_op jit(solution)/shard_map/ppermute | solution.py:320
  15.6 8.6 %collective-permute-start.2 = (bf16[2,256,512]{2,1,0:T(8,128)(2,1)}, bf16[2,256,512]{2,1,0:T(8,128)(2,1)}, u32[]{:S(2)}, u32[]{:S(2)}) collective-permute-start(bf16[2,256,512]{2,1,0:T(8,128)(2,1)} %collective-permute-done.1.refs_2_.refs_7_), channel_id=1, source_target_pairs={{0,4},{1,3},{4,8},{5,1},{8,12},{9,5},{12,14},{13,9},{14,10},{15,13... | collective-permute-start | bytes 1572872 | tf_op jit(solution)/shard_map/ppermute | solution.py:320
  18.0 11.9 %collective-permute-start.7 = (bf16[2,256,512]{2,1,0:T(8,128)(2,1)}, bf16[2,256,512]{2,1,0:T(8,128)(2,1)}, u32[]{:S(2)}, u32[]{:S(2)}) collective-permute-start(bf16[2,256,512]{2,1,0:T(8,128)(2,1)} %get-tuple-element.40.refs_1_.refs_6_), channel_id=1, source_target_pairs={{0,4},{1,3},{4,8},{5,1},{8,12},{9,5},{12,14},{13,9},{14,10},{15,13... | collective-permute-start | bytes 1572872 | tf_op jit(solution)/shard_map/ppermute | solution.py:320
  20.3 11.0 %collective-permute-start.10 = (f16[64,512]{1,0:T(8,128)(2,1)}, f16[64,512]{1,0:T(8,128)(2,1)S(1)}, u32[]{:S(2)}, u32[]{:S(2)}) collective-permute-start(f16[64,512]{1,0:T(8,128)(2,1)} %bitcast.74), channel_id=1, source_target_pairs={{0,1},{1,0},{2,3},{3,2},{4,5},{5,4},{6,7},{7,6},{8,9},{9,8},{10,11... | collective-permute-start | bytes 196616 | tf_op jit(solution)/shard_map/ppermute | solution.py:288
  23.1 8.1 %collective-permute-start.4 = (f16[64,512]{1,0:T(8,128)(2,1)}, f16[64,512]{1,0:T(8,128)(2,1)S(1)}, u32[]{:S(2)}, u32[]{:S(2)}) collective-permute-start(f16[64,512]{1,0:T(8,128)(2,1)} %bitcast.75), channel_id=1, source_target_pairs={{0,1},{1,0},{2,3},{3,2},{4,5},{5,4},{6,7},{7,6},{8,9},{9,8},{10,11... | collective-permute-start | bytes 196616 | tf_op jit(solution)/shard_map/ppermute | solution.py:288
  24.3 8.3 %collective-permute-start.3 = (bf16[2,256,512]{2,1,0:T(8,128)(2,1)}, bf16[2,256,512]{2,1,0:T(8,128)(2,1)}, u32[]{:S(2)}, u32[]{:S(2)}) collective-permute-start(bf16[2,256,512]{2,1,0:T(8,128)(2,1)} %collective-permute-done.2.refs_6_.refs_11_), channel_id=1, source_target_pairs={{0,1},{1,0},{2,3},{3,2},{4,5},{5,4},{6,7},{7,6},{8,9},{9,8},{10,11... | collective-permute-start | bytes 1572872 | tf_op jit(solution)/shard_map/ppermute | solution.py:288
  28.5 11.3 %collective-permute-start.5 = (bf16[2,256,512]{2,1,0:T(8,128)(2,1)}, bf16[2,256,512]{2,1,0:T(8,128)(2,1)S(1)}, u32[]{:S(2)}, u32[]{:S(2)}) collective-permute-start(bf16[2,256,512]{2,1,0:T(8,128)(2,1)} %collective-permute-done.1.refs_2_.refs_7_), channel_id=1, source_target_pairs={{0,1},{1,0},{2,3},{3,2},{4,5},{5,4},{6,7},{7,6},{8,9},{9,8},{10,11... | collective-permute-start | bytes 1572872 | tf_op jit(solution)/shard_map/ppermute | solution.py:288
  29.9 11.7 %collective-permute-start.8 = (bf16[2,256,512]{2,1,0:T(8,128)(2,1)}, bf16[2,256,512]{2,1,0:T(8,128)(2,1)}, u32[]{:S(2)}, u32[]{:S(2)}) collective-permute-start(bf16[2,256,512]{2,1,0:T(8,128)(2,1)} %collective-permute-done.7.refs_3_.refs_8_), channel_id=1, source_target_pairs={{0,4},{1,3},{4,8},{5,1},{8,12},{9,5},{12,14},{13,9},{14,10},{15,13... | collective-permute-start | bytes 1572872 | tf_op jit(solution)/shard_map/ppermute | solution.py:320
  32.6 30.2 %all-to-all-start = ((f16[8,64,640]{2,1,0:T(8,128)(2,1)}), f16[8,64,640]{2,1,0:T(8,128)(2,1)S(1)}, u32[]{:S(2)}, u32[]{:S(2)}) async-start(f16[8,64,640]{2,1,0:T(8,128)(2,1)} %pad_maximum_fusion), calls=%async_computation | async-start | bytes 1310720 | tf_op jit(solution)/shard_map/all_to_all | solution.py:323
  37.2 7.5 %collective-permute-start.12 = (bf16[2,256,512]{2,1,0:T(8,128)(2,1)}, bf16[2,256,512]{2,1,0:T(8,128)(2,1)S(1)}, u32[]{:S(2)}, u32[]{:S(2)}) collective-permute-start(bf16[2,256,512]{2,1,0:T(8,128)(2,1)} %collective-permute-done.7.refs_3_.refs_8_), channel_id=1, source_target_pairs={{0,1},{1,0},{2,3},{3,2},{4,5},{5,4},{6,7},{7,6},{8,9},{9,8},{10,11... | collective-permute-start | bytes 1572872 | tf_op jit(solution)/shard_map/ppermute | solution.py:288
  39.8 17.1 %collective-permute-start.6 = (bf16[2,256,512]{2,1,0:T(8,128)(2,1)}, bf16[2,256,512]{2,1,0:T(8,128)(2,1)}, u32[]{:S(2)}, u32[]{:S(2)}) collective-permute-start(bf16[2,256,512]{2,1,0:T(8,128)(2,1)} %collective-permute-done.2.refs_6_.refs_11_), channel_id=1, source_target_pairs={{0,4},{1,3},{4,8},{5,1},{8,12},{9,5},{12,14},{13,9},{14,10},{15,13... | collective-permute-start | bytes 1572872 | tf_op jit(solution)/shard_map/ppermute | solution.py:320
  41.6 15.4 %collective-permute-start.9 = (bf16[2,256,512]{2,1,0:T(8,128)(2,1)}, bf16[2,256,512]{2,1,0:T(8,128)(2,1)}, u32[]{:S(2)}, u32[]{:S(2)}) collective-permute-start(bf16[2,256,512]{2,1,0:T(8,128)(2,1)} %collective-permute-done.8.refs_7_.refs_12_), channel_id=1, source_target_pairs={{0,1},{1,0},{2,3},{3,2},{4,5},{5,4},{6,7},{7,6},{8,9},{9,8},{10,11... | collective-permute-start | bytes 1572872 | tf_op jit(solution)/shard_map/ppermute | solution.py:288
  44.7 24.3 %copy-start.11 = (bf16[2,256,512]{2,1,0:T(8,128)(2,1)}, bf16[2,256,512]{2,1,0:T(8,128)(2,1)S(1)}, u32[]{:S(2)}) copy-start(bf16[2,256,512]{2,1,0:T(8,128)(2,1)S(1)} %collective-permute-done.12.refs_5_.refs_10_) | copy-start | bytes 1572868
  44.7 18.1 %collective-permute-start.13 = (bf16[2,256,512]{2,1,0:T(8,128)(2,1)}, bf16[2,256,512]{2,1,0:T(8,128)(2,1)S(1)}, u32[]{:S(2)}, u32[]{:S(2)}) collective-permute-start(bf16[2,256,512]{2,1,0:T(8,128)(2,1)} %collective-permute-done.8.refs_7_.refs_12_), channel_id=1, source_target_pairs={{0,4},{1,3},{4,8},{5,1},{8,12},{9,5},{12,14},{13,9},{14,10},{15,13... | collective-permute-start | bytes 1572872 | tf_op jit(solution)/shard_map/ppermute | solution.py:320
  57.0 11.1 %collective-permute-start.11 = (bf16[2,256,512]{2,1,0:T(8,128)(2,1)}, bf16[2,256,512]{2,1,0:T(8,128)(2,1)S(1)}, u32[]{:S(2)}, u32[]{:S(2)}) collective-permute-start(bf16[2,256,512]{2,1,0:T(8,128)(2,1)} %collective-permute-done.6.refs_10_.refs_15_), channel_id=1, source_target_pairs={{0,4},{1,3},{4,8},{5,1},{8,12},{9,5},{12,14},{13,9},{14,10},{15,13... | collective-permute-start | bytes 1572872 | tf_op jit(solution)/shard_map/ppermute | solution.py:320
  57.0 19.1 %collective-permute-start.14 = (bf16[2,256,512]{2,1,0:T(8,128)(2,1)}, bf16[2,256,512]{2,1,0:T(8,128)(2,1)S(1)}, u32[]{:S(2)}, u32[]{:S(2)}) collective-permute-start(bf16[2,256,512]{2,1,0:T(8,128)(2,1)} %collective-permute-done.6.refs_10_.refs_15_), channel_id=1, source_target_pairs={{0,1},{1,0},{2,3},{3,2},{4,5},{5,4},{6,7},{7,6},{8,9},{9,8},{10,11... | collective-permute-start | bytes 1572872 | tf_op jit(solution)/shard_map/ppermute | solution.py:288
  62.8 13.3 %collective-permute-start.15 = (bf16[2,256,512]{2,1,0:T(8,128)(2,1)S(1)}, bf16[2,256,512]{2,1,0:T(8,128)(2,1)}, u32[]{:S(2)}, u32[]{:S(2)}) collective-permute-start(bf16[2,256,512]{2,1,0:T(8,128)(2,1)S(1)} %collective-permute-done.13.refs_11_.refs_16_), channel_id=1, source_target_pairs={{0,1},{1,0},{2,3},{3,2},{4,5},{5,4},{6,7},{7,6},{8,9},{9,8},{10,11... | collective-permute-start | bytes 1572872 | tf_op jit(solution)/shard_map/ppermute | solution.py:288
  68.1 8.0 %collective-permute-start.16 = (bf16[2,256,512]{2,1,0:T(8,128)(2,1)S(1)}, bf16[2,256,512]{2,1,0:T(8,128)(2,1)}, u32[]{:S(2)}, u32[]{:S(2)}) collective-permute-start(bf16[2,256,512]{2,1,0:T(8,128)(2,1)S(1)} %collective-permute-done.11.refs_14_.refs_19_), channel_id=1, source_target_pairs={{0,1},{1,0},{2,3},{3,2},{4,5},{5,4},{6,7},{7,6},{8,9},{9,8},{10,11... | collective-permute-start | bytes 1572872 | tf_op jit(solution)/shard_map/ppermute | solution.py:288
  69.0 26.1 %all-to-all-start.1 = ((f16[8,64,640]{2,1,0:T(8,128)(2,1)}), f16[8,64,640]{2,1,0:T(8,128)(2,1)S(1)}, u32[]{:S(2)}, u32[]{:S(2)}) async-start(f16[8,64,640]{2,1,0:T(8,128)(2,1)} %pad_maximum_fusion.1), calls=%async_computation.1 | async-start | bytes 1310720 | tf_op jit(solution)/shard_map/all_to_all | solution.py:323
  95.1 24.5 %all-to-all-start.3 = ((f16[8,64,640]{2,1,0:T(8,128)(2,1)}), f16[8,64,640]{2,1,0:T(8,128)(2,1)S(1)}, u32[]{:S(2)}, u32[]{:S(2)}) async-start(f16[8,64,640]{2,1,0:T(8,128)(2,1)} %convert_element_type.66), calls=%async_computation.3 | async-start | bytes 1310720 | tf_op jit(solution)/shard_map/all_to_all | solution.py:323
  119.6 21.2 %all-to-all-start.2 = ((f16[8,64,640]{2,1,0:T(8,128)(2,1)}), f16[8,64,640]{2,1,0:T(8,128)(2,1)}, u32[]{:S(2)}, u32[]{:S(2)}) async-start(f16[8,64,640]{2,1,0:T(8,128)(2,1)} %convert_element_type.65), calls=%async_computation.2 | async-start | bytes 1310720 | tf_op jit(solution)/shard_map/all_to_all | solution.py:323
  125.7 4.8 %collective-permute-start.17 = (f16[64,512]{1,0:T(8,128)(2,1)S(1)}, f16[64,512]{1,0:T(8,128)(2,1)S(1)}, u32[]{:S(2)}, u32[]{:S(2)}) collective-permute-start(f16[64,512]{1,0:T(8,128)(2,1)S(1)} %fusion.7), channel_id=1, source_target_pairs={{0,1},{1,0},{2,3},{3,2},{4,5},{5,4},{6,7},{7,6},{8,9},{9,8},{10,11... | collective-permute-start | bytes 196616 | tf_op jit(solution)/shard_map/ppermute | solution.py:288
  142.4 5.1 %collective-permute-start.18 = (f16[64,512]{1,0:T(8,128)(2,1)S(1)}, f16[64,512]{1,0:T(8,128)(2,1)S(1)}, u32[]{:S(2)}, u32[]{:S(2)}) collective-permute-start(f16[64,512]{1,0:T(8,128)(2,1)S(1)} %fusion.8), channel_id=1, source_target_pairs={{0,1},{1,0},{2,3},{3,2},{4,5},{5,4},{6,7},{7,6},{8,9},{9,8},{10,11... | collective-permute-start | bytes 196616 | tf_op jit(solution)/shard_map/ppermute | solution.py:288
  (15 other events, 95.8 us)

commit v18 on v16

--- a/solution.py
+++ b/solution.py
@@ -344,10 +344,9 @@
     theirs = swap_cores(mine)
     half = rows // s.halves
     cut = lambda x: [x[k * half : (k + 1) * half] for k in range(s.halves)]
-    heads = [
-        jnp.stack([jnp.where(core == 0, a, d), jnp.where(core == 0, b, c)])
-        for a, b, c, d in zip(cut(mine), cut(theirs), reversed(cut(mine)), reversed(cut(theirs)))
-    ]
+    own_set = (jnp.arange(2, dtype=jnp.int32) == core)[:, None, None]
+    pick = lambda x: [jnp.where(core == 0, *pair) for pair in zip(cut(x), reversed(cut(x)))]
+    heads = [jnp.where(own_set, a[None], b[None]) for a, b in zip(pick(mine), pick(theirs))]
     heads, mass_here, points_here, cot_here, cot_points = lax.optimization_barrier(
         (heads, source_mass, target_mass[0], source_cotangent, target_cotangent[0])
     )

time: 145 us -> 144 us (level)
    another operation x3 -> x0, other arithmetic: 1.77 us -> none  [local(): jnp.stack([jnp.where(core == 0, a, d), jnp.where(core == 0, b, c)])]
    select_n x0 -> x3, other arithmetic: none -> 1.6 us  [the longest x1 1.15 us: local(): jnp.where(own_set, a[None], b[None])]
where the time goes in v18:
time: 144 us
  starting transfers between devices  44.8 us (31%)
  waiting for transfers between devices  34.6 us (24%)
  Pallas kernels  31.5 us (22%)
  other arithmetic  22.5 us (16%)
  local copies, waits for them, and re-layouts  7.82 us (5%)
    pallas_call x2, Pallas kernels, call(): pl.pallas_call(functools.partial(kernel, s), out_shape=[*vmem_outs, *hbm_...  31.5 us
    ppermute x7, waiting for transfers between devices, onward(): return lax.ppermute(x, ('src', 'tgt'), pairs)  25 us
    all_to_all x4, starting transfers between devices, exchange(): return lax.all_to_all(x, 'src', 0, 0, tiled=True)  23.6 us
    ppermute x12, starting transfers between devices, swap_cores(): return lax.ppermute(x, 'tgt', [(0, 1), (1, 0)])  12.1 us
    all_to_all x4, waiting for transfers between devices, exchange(): return lax.all_to_all(x, 'src', 0, 0, tiled=True)  9.5 us
    ppermute x7, starting transfers between devices, onward(): return lax.ppermute(x, ('src', 'tgt'), pairs)  9.14 us
    div x1, other arithmetic, local(): source_known = source_cotangent / source_mass  3.27 us
  transfers between devices with their start and end apart: 23, of which 7 were waited for; matrix products, arithmetic and copies ran while one was open for 17% of the time, Pallas kernels for 22%

profile of v18, /device:TPU:1, one launch (start us, length us, event | category | flops | bytes accessed | tf_op | source)
XLA Modules:
  0.0 143.7 jit_solution(10754200648474672006)
XLA Ops:
  7.0 2.7 %collective-permute-start.1 = (bf16[2,256,512]{2,1,0:T(8,128)(2,1)}, bf16[2,256,512]{2,1,0:T(8,128)(2,1)}, u32[]{:S(2)}, u32[]{:S(2)}) collective-permute-start(bf16[2,256,512]{2,1,0:T(8,128)(2,1)} %get-tuple-element.34.refs_0_.refs_5_), channel_id=1, source_target_pairs={{0,4},{1,3},{4,8},{5,1},{8,12},{9,5},{12,14},{13,9},{14,10},{15,13... | collective-permute-start | bytes 1572872 | tf_op jit(solution)/shard_map/ppermute | solution.py:320
  14.6 2.3 %collective-permute-done.1.refs_2_.refs_7_ = bf16[2,256,512]{2,1,0:T(8,128)(2,1)} collective-permute-done((bf16[2,256,512]{2,1,0:T(8,128)(2,1)}, bf16[2,256,512]{2,1,0:T(8,128)(2,1)}, u32[]{:S(2)}, u32[]{:S(2)}) %collective-permute-start.1) | collective-permute-done | bytes 524320 | tf_op jit(solution)/shard_map/ppermute | solution.py:320
  16.9 1.4 collective-permute-start.2
  19.4 1.5 %copy.22 = f16[512,512]{1,0:T(8,128)(2,1)S(1)} copy(f16[512,512]{0,1:T(8,128)(2,1)} %get-tuple-element.89) | data formatting | bytes 1048576 | tf_op jit(solution)/shard_map/transpose | solution.py:337
  22.5 1.4 collective-permute-start.8
  25.3 2.9 %collective-permute-done.2.refs_6_.refs_11_ = bf16[2,256,512]{2,1,0:T(8,128)(2,1)} collective-permute-done((bf16[2,256,512]{2,1,0:T(8,128)(2,1)}, bf16[2,256,512]{2,1,0:T(8,128)(2,1)}, u32[]{:S(2)}, u32[]{:S(2)}) %collective-permute-start.2) | collective-permute-done | bytes 524320 | tf_op jit(solution)/shard_map/ppermute | solution.py:320
  28.2 5.7 %all-to-all-start = ((f16[8,64,640]{2,1,0:T(8,128)(2,1)}), f16[8,64,640]{2,1,0:T(8,128)(2,1)S(1)}, u32[]{:S(2)}, u32[]{:S(2)}) async-start(f16[8,64,640]{2,1,0:T(8,128)(2,1)} %pad_maximum_fusion), calls=%async_computation | async-start | bytes 1310720 | tf_op jit(solution)/shard_map/all_to_all | solution.py:323
  35.2 1.8 %collective-permute-start.5 = (bf16[2,256,512]{2,1,0:T(8,128)(2,1)}, bf16[2,256,512]{2,1,0:T(8,128)(2,1)}, u32[]{:S(2)}, u32[]{:S(2)}) collective-permute-start(bf16[2,256,512]{2,1,0:T(8,128)(2,1)} %collective-permute-done.2.refs_6_.refs_11_), channel_id=1, source_target_pairs={{0,4},{1,3},{4,8},{5,1},{8,12},{9,5},{12,14},{13,9},{14,10},{15,13... | collective-permute-start | bytes 1572872 | tf_op jit(solution)/shard_map/ppermute | solution.py:320
  39.9 12.5 %collective-permute-done.5.refs_10_.refs_15_ = bf16[2,256,512]{2,1,0:T(8,128)(2,1)} collective-permute-done((bf16[2,256,512]{2,1,0:T(8,128)(2,1)}, bf16[2,256,512]{2,1,0:T(8,128)(2,1)}, u32[]{:S(2)}, u32[]{:S(2)}) %collective-permute-start.5) | collective-permute-done | bytes 524320 | tf_op jit(solution)/shard_map/ppermute | solution.py:320
  52.4 3.8 %collective-permute-start.14 = (bf16[2,256,512]{2,1,0:T(8,128)(2,1)}, bf16[2,256,512]{2,1,0:T(8,128)(2,1)S(1)}, u32[]{:S(2)}, u32[]{:S(2)}) collective-permute-start(bf16[2,256,512]{2,1,0:T(8,128)(2,1)} %collective-permute-done.5.refs_10_.refs_15_), channel_id=1, source_target_pairs={{0,1},{1,0},{2,3},{3,2},{4,5},{5,4},{6,7},{7,6},{8,9},{9,8},{10,11... | collective-permute-start | bytes 1572872 | tf_op jit(solution)/shard_map/ppermute | solution.py:288
  56.3 2.3 %collective-permute-done.13.refs_11_.refs_16_ = bf16[2,256,512]{2,1,0:T(8,128)(2,1)S(1)} collective-permute-done((bf16[2,256,512]{2,1,0:T(8,128)(2,1)}, bf16[2,256,512]{2,1,0:T(8,128)(2,1)S(1)}, u32[]{:S(2)}, u32[]{:S(2)}) %collective-permute-start.13) | collective-permute-done | bytes 524320 | tf_op jit(solution)/shard_map/ppermute | solution.py:320
  59.8 4.6 %collective-permute-done.11.refs_14_.refs_19_ = bf16[2,256,512]{2,1,0:T(8,128)(2,1)S(1)} collective-permute-done((bf16[2,256,512]{2,1,0:T(8,128)(2,1)}, bf16[2,256,512]{2,1,0:T(8,128)(2,1)S(1)}, u32[]{:S(2)}, u32[]{:S(2)}) %collective-permute-start.11) | collective-permute-done | bytes 524320 | tf_op jit(solution)/shard_map/ppermute | solution.py:320
  64.4 7.0 %all-to-all-start.1 = ((f16[8,64,640]{2,1,0:T(8,128)(2,1)}), f16[8,64,640]{2,1,0:T(8,128)(2,1)S(1)}, u32[]{:S(2)}, u32[]{:S(2)}) async-start(f16[8,64,640]{2,1,0:T(8,128)(2,1)} %pad_maximum_fusion.1), calls=%async_computation.1 | async-start | bytes 1310720 | tf_op jit(solution)/shard_map/all_to_all | solution.py:323
  72.3 16.0 %shard_map.132 = (f32[8,64,640]{2,1,0:T(8,128)}, f32[8,64,512]{2,1,0:T(8,128)}, f32[8,8,512]{2,1,0:T(8,128)}, f32[64,1024]{1,0:T(8,128)}, f32[64,1024]{1,0:T(8,128)}, /*index=5*/f32[64,1024]{1,0:T(8,128)}) custom-call(s32[9]{0:T(128)} %pad_add_fusion.table, f32[8,64,640]{2,1,0:T(8,128)} %convert_element_type.63.mass_in, ...), custom_call_target="tpu_custom_call" | custom-call | flops 15032385536 | bytes 16777216 | tf_op jit(solution)/shard_map/pallas_call | solution.py:264
  88.2 2.2 %convert_element_type.66 = f16[8,64,640]{2,1,0:T(8,128)(2,1)} convert(f32[8,64,640]{2,1,0:T(8,128)} %get-tuple-element.53.thirds_in) | non-fusion elementwise | flops 327680 | bytes 1966080 | tf_op jit(solution)/shard_map/convert_element_type | solution.py:414
  90.5 5.4 %all-to-all-start.3 = ((f16[8,64,640]{2,1,0:T(8,128)(2,1)}), f16[8,64,640]{2,1,0:T(8,128)(2,1)S(1)}, u32[]{:S(2)}, u32[]{:S(2)}) async-start(f16[8,64,640]{2,1,0:T(8,128)(2,1)} %convert_element_type.66), calls=%async_computation.3 | async-start | bytes 1310720 | tf_op jit(solution)/shard_map/all_to_all | solution.py:323
  97.1 15.6 %shard_map.133 = f32[8,64,640]{2,1,0:T(8,128)} custom-call(s32[9]{0:T(128)} %pad_add_fusion.table, f32[8,64,640]{2,1,0:T(8,128)} %convert_element_type.63.mass_in, f32[8,64,640]{2,1,0:T(8,128)} %convert_element_type.64.cot_in, f32[8,64,640]{2,1,0:T(8,128)} %get-tuple-element.53.thirds_in, f32[8,64,512]{2,1,0:T(8,128)} %get-tuple-element.54.refs_0_, ...), custom_call_target="tpu_custom_call" | custom-call | flops 10737418240 | bytes 16777216 | tf_op jit(solution)/shard_map/pallas_call | solution.py:264
  112.7 2.3 %convert_element_type.65 = f16[8,64,640]{2,1,0:T(8,128)(2,1)} convert(f32[8,64,640]{2,1,0:T(8,128)} %shard_map.133) | non-fusion elementwise | flops 327680 | bytes 1966080 | tf_op jit(solution)/shard_map/convert_element_type | solution.py:421
  115.0 5.4 %all-to-all-start.2 = ((f16[8,64,640]{2,1,0:T(8,128)(2,1)}), f16[8,64,640]{2,1,0:T(8,128)(2,1)}, u32[]{:S(2)}, u32[]{:S(2)}) async-start(f16[8,64,640]{2,1,0:T(8,128)(2,1)} %convert_element_type.65), calls=%async_computation.2 | async-start | bytes 1310720 | tf_op jit(solution)/shard_map/all_to_all | solution.py:323
  121.1 1.5 %collective-permute-start.17 = (f16[64,512]{1,0:T(8,128)(2,1)S(1)}, f16[64,512]{1,0:T(8,128)(2,1)S(1)}, u32[]{:S(2)}, u32[]{:S(2)}) collective-permute-start(f16[64,512]{1,0:T(8,128)(2,1)S(1)} %fusion.7), channel_id=1, source_target_pairs={{0,1},{1,0},{2,3},{3,2},{4,5},{5,4},{6,7},{7,6},{8,9},{9,8},{10,11... | collective-permute-start | bytes 196616 | tf_op jit(solution)/shard_map/ppermute | solution.py:288
  122.6 3.3 %fusion.14 = (f32[512,512]{1,0:T(8,128)}, f32[512,512]{1,0:T(8,128)}) fusion(f32[512,512]{1,0:T(8,128)} %param.15, f32[512,512]{1,0:T(8,128)} %param.10, f32[640,512]{1,0:T(8,128)S(1)} %bitcast.77), kind=kLoop, calls=%fused_computation.63 | loop fusion | flops 524288 | bytes 5242880 | tf_op jit(solution)/shard_map/div | solution.py:417
  126.7 9.5 %all-to-all-done.2 = f16[8,64,640]{2,1,0:T(8,128)(2,1)} async-done(((f16[8,64,640]{2,1,0:T(8,128)(2,1)}), f16[8,64,640]{2,1,0:T(8,128)(2,1)}, u32[]{:S(2)}, u32[]{:S(2)}) %all-to-all-start.2) | async-done | bytes 655392 | tf_op jit(solution)/shard_map/all_to_all | solution.py:323
  137.8 2.7 %collective-permute-start.18 = (f16[64,512]{1,0:T(8,128)(2,1)S(1)}, f16[64,512]{1,0:T(8,128)(2,1)S(1)}, u32[]{:S(2)}, u32[]{:S(2)}) collective-permute-start(f16[64,512]{1,0:T(8,128)(2,1)S(1)} %fusion.8), channel_id=1, source_target_pairs={{0,1},{1,0},{2,3},{3,2},{4,5},{5,4},{6,7},{7,6},{8,9},{9,8},{10,11... | collective-permute-start | bytes 196616 | tf_op jit(solution)/shard_map/ppermute | solution.py:288
  140.5 2.4 %fusion = f32[512,512]{1,0:T(8,128)} fusion(f32[512,512]{1,0:T(8,128)} %get-tuple-element.61, f32[640,512]{1,0:T(8,128)S(1)} %bitcast.79), kind=kLoop, calls=%fused_computation.3 | loop fusion | flops 524288 | bytes 3145728 | tf_op jit(solution)/shard_map/add | solution.py:432
  (104 shorter events, 26.4 us)
Async XLA Ops:
  3.2 2.6 %collective-permute-start = (bf16[512,512]{1,0:T(8,128)(2,1)S(1)}, bf16[512,512]{1,0:T(8,128)(2,1)S(1)}, u32[]{:S(2)}, u32[]{:S(2)}) collective-permute-start(bf16[512,512]{1,0:T(8,128)(2,1)S(1)} %bitcast.96), channel_id=1, source_target_pairs={{0,1},{1,0},{2,3},{3,2},{4,5},{5,4},{6,7},{7,6},{8,9},{9,8},{10,11... | collective-permute-start | bytes 1572872 | tf_op jit(solution)/shard_map/ppermute | solution.py:288
  7.0 9.9 %collective-permute-start.1 = (bf16[2,256,512]{2,1,0:T(8,128)(2,1)}, bf16[2,256,512]{2,1,0:T(8,128)(2,1)}, u32[]{:S(2)}, u32[]{:S(2)}) collective-permute-start(bf16[2,256,512]{2,1,0:T(8,128)(2,1)} %get-tuple-element.34.refs_0_.refs_5_), channel_id=1, source_target_pairs={{0,4},{1,3},{4,8},{5,1},{8,12},{9,5},{12,14},{13,9},{14,10},{15,13... | collective-permute-start | bytes 1572872 | tf_op jit(solution)/shard_map/ppermute | solution.py:320
  10.6 11.9 %collective-permute-start.7 = (bf16[2,256,512]{2,1,0:T(8,128)(2,1)}, bf16[2,256,512]{2,1,0:T(8,128)(2,1)}, u32[]{:S(2)}, u32[]{:S(2)}) collective-permute-start(bf16[2,256,512]{2,1,0:T(8,128)(2,1)} %get-tuple-element.40.refs_1_.refs_6_), channel_id=1, source_target_pairs={{0,4},{1,3},{4,8},{5,1},{8,12},{9,5},{12,14},{13,9},{14,10},{15,13... | collective-permute-start | bytes 1572872 | tf_op jit(solution)/shard_map/ppermute | solution.py:320
  12.9 11.0 %collective-permute-start.10 = (f16[64,512]{1,0:T(8,128)(2,1)}, f16[64,512]{1,0:T(8,128)(2,1)S(1)}, u32[]{:S(2)}, u32[]{:S(2)}) collective-permute-start(f16[64,512]{1,0:T(8,128)(2,1)} %bitcast.74), channel_id=1, source_target_pairs={{0,1},{1,0},{2,3},{3,2},{4,5},{5,4},{6,7},{7,6},{8,9},{9,8},{10,11... | collective-permute-start | bytes 196616 | tf_op jit(solution)/shard_map/ppermute | solution.py:288
  14.6 9.4 %collective-permute-start.3 = (f16[64,512]{1,0:T(8,128)(2,1)}, f16[64,512]{1,0:T(8,128)(2,1)S(1)}, u32[]{:S(2)}, u32[]{:S(2)}) collective-permute-start(f16[64,512]{1,0:T(8,128)(2,1)} %bitcast.75), channel_id=1, source_target_pairs={{0,1},{1,0},{2,3},{3,2},{4,5},{5,4},{6,7},{7,6},{8,9},{9,8},{10,11... | collective-permute-start | bytes 196616 | tf_op jit(solution)/shard_map/ppermute | solution.py:288
  16.9 11.2 %collective-permute-start.2 = (bf16[2,256,512]{2,1,0:T(8,128)(2,1)}, bf16[2,256,512]{2,1,0:T(8,128)(2,1)}, u32[]{:S(2)}, u32[]{:S(2)}) collective-permute-start(bf16[2,256,512]{2,1,0:T(8,128)(2,1)} %collective-permute-done.1.refs_2_.refs_7_), channel_id=1, source_target_pairs={{0,4},{1,3},{4,8},{5,1},{8,12},{9,5},{12,14},{13,9},{14,10},{15,13... | collective-permute-start | bytes 1572872 | tf_op jit(solution)/shard_map/ppermute | solution.py:320
  20.9 14.2 %collective-permute-start.4 = (bf16[2,256,512]{2,1,0:T(8,128)(2,1)}, bf16[2,256,512]{2,1,0:T(8,128)(2,1)S(1)}, u32[]{:S(2)}, u32[]{:S(2)}) collective-permute-start(bf16[2,256,512]{2,1,0:T(8,128)(2,1)} %collective-permute-done.1.refs_2_.refs_7_), channel_id=1, source_target_pairs={{0,1},{1,0},{2,3},{3,2},{4,5},{5,4},{6,7},{7,6},{8,9},{9,8},{10,11... | collective-permute-start | bytes 1572872 | tf_op jit(solution)/shard_map/ppermute | solution.py:288
  22.5 12.5 %collective-permute-start.8 = (bf16[2,256,512]{2,1,0:T(8,128)(2,1)}, bf16[2,256,512]{2,1,0:T(8,128)(2,1)}, u32[]{:S(2)}, u32[]{:S(2)}) collective-permute-start(bf16[2,256,512]{2,1,0:T(8,128)(2,1)} %collective-permute-done.7.refs_3_.refs_8_), channel_id=1, source_target_pairs={{0,4},{1,3},{4,8},{5,1},{8,12},{9,5},{12,14},{13,9},{14,10},{15,13... | collective-permute-start | bytes 1572872 | tf_op jit(solution)/shard_map/ppermute | solution.py:320
  28.2 30.4 %all-to-all-start = ((f16[8,64,640]{2,1,0:T(8,128)(2,1)}), f16[8,64,640]{2,1,0:T(8,128)(2,1)S(1)}, u32[]{:S(2)}, u32[]{:S(2)}) async-start(f16[8,64,640]{2,1,0:T(8,128)(2,1)} %pad_maximum_fusion), calls=%async_computation | async-start | bytes 1310720 | tf_op jit(solution)/shard_map/all_to_all | solution.py:323
  33.9 5.5 %collective-permute-start.12 = (bf16[2,256,512]{2,1,0:T(8,128)(2,1)}, bf16[2,256,512]{2,1,0:T(8,128)(2,1)S(1)}, u32[]{:S(2)}, u32[]{:S(2)}) collective-permute-start(bf16[2,256,512]{2,1,0:T(8,128)(2,1)} %collective-permute-done.7.refs_3_.refs_8_), channel_id=1, source_target_pairs={{0,1},{1,0},{2,3},{3,2},{4,5},{5,4},{6,7},{7,6},{8,9},{9,8},{10,11... | collective-permute-start | bytes 1572872 | tf_op jit(solution)/shard_map/ppermute | solution.py:288
  35.1 4.8 %collective-permute-start.9 = (bf16[2,256,512]{2,1,0:T(8,128)(2,1)}, bf16[2,256,512]{2,1,0:T(8,128)(2,1)}, u32[]{:S(2)}, u32[]{:S(2)}) collective-permute-start(bf16[2,256,512]{2,1,0:T(8,128)(2,1)} %collective-permute-done.8.refs_7_.refs_12_), channel_id=1, source_target_pairs={{0,1},{1,0},{2,3},{3,2},{4,5},{5,4},{6,7},{7,6},{8,9},{9,8},{10,11... | collective-permute-start | bytes 1572872 | tf_op jit(solution)/shard_map/ppermute | solution.py:288
  35.2 17.3 %collective-permute-start.5 = (bf16[2,256,512]{2,1,0:T(8,128)(2,1)}, bf16[2,256,512]{2,1,0:T(8,128)(2,1)}, u32[]{:S(2)}, u32[]{:S(2)}) collective-permute-start(bf16[2,256,512]{2,1,0:T(8,128)(2,1)} %collective-permute-done.2.refs_6_.refs_11_), channel_id=1, source_target_pairs={{0,4},{1,3},{4,8},{5,1},{8,12},{9,5},{12,14},{13,9},{14,10},{15,13... | collective-permute-start | bytes 1572872 | tf_op jit(solution)/shard_map/ppermute | solution.py:320
  36.9 15.5 %collective-permute-start.6 = (bf16[2,256,512]{2,1,0:T(8,128)(2,1)}, bf16[2,256,512]{2,1,0:T(8,128)(2,1)}, u32[]{:S(2)}, u32[]{:S(2)}) collective-permute-start(bf16[2,256,512]{2,1,0:T(8,128)(2,1)} %collective-permute-done.2.refs_6_.refs_11_), channel_id=1, source_target_pairs={{0,1},{1,0},{2,3},{3,2},{4,5},{5,4},{6,7},{7,6},{8,9},{9,8},{10,11... | collective-permute-start | bytes 1572872 | tf_op jit(solution)/shard_map/ppermute | solution.py:288
  39.4 25.1 %copy-start.10 = (bf16[2,256,512]{2,1,0:T(8,128)(2,1)}, bf16[2,256,512]{2,1,0:T(8,128)(2,1)S(1)}, u32[]{:S(2)}) copy-start(bf16[2,256,512]{2,1,0:T(8,128)(2,1)S(1)} %collective-permute-done.12.refs_5_.refs_10_) | copy-start | bytes 1572868
  39.4 19.2 %collective-permute-start.13 = (bf16[2,256,512]{2,1,0:T(8,128)(2,1)}, bf16[2,256,512]{2,1,0:T(8,128)(2,1)S(1)}, u32[]{:S(2)}, u32[]{:S(2)}) collective-permute-start(bf16[2,256,512]{2,1,0:T(8,128)(2,1)} %collective-permute-done.8.refs_7_.refs_12_), channel_id=1, source_target_pairs={{0,4},{1,3},{4,8},{5,1},{8,12},{9,5},{12,14},{13,9},{14,10},{15,13... | collective-permute-start | bytes 1572872 | tf_op jit(solution)/shard_map/ppermute | solution.py:320
  52.4 12.0 %collective-permute-start.11 = (bf16[2,256,512]{2,1,0:T(8,128)(2,1)}, bf16[2,256,512]{2,1,0:T(8,128)(2,1)S(1)}, u32[]{:S(2)}, u32[]{:S(2)}) collective-permute-start(bf16[2,256,512]{2,1,0:T(8,128)(2,1)} %collective-permute-done.5.refs_10_.refs_15_), channel_id=1, source_target_pairs={{0,4},{1,3},{4,8},{5,1},{8,12},{9,5},{12,14},{13,9},{14,10},{15,13... | collective-permute-start | bytes 1572872 | tf_op jit(solution)/shard_map/ppermute | solution.py:320
  52.4 19.0 %collective-permute-start.14 = (bf16[2,256,512]{2,1,0:T(8,128)(2,1)}, bf16[2,256,512]{2,1,0:T(8,128)(2,1)S(1)}, u32[]{:S(2)}, u32[]{:S(2)}) collective-permute-start(bf16[2,256,512]{2,1,0:T(8,128)(2,1)} %collective-permute-done.5.refs_10_.refs_15_), channel_id=1, source_target_pairs={{0,1},{1,0},{2,3},{3,2},{4,5},{5,4},{6,7},{7,6},{8,9},{9,8},{10,11... | collective-permute-start | bytes 1572872 | tf_op jit(solution)/shard_map/ppermute | solution.py:288
  58.6 12.9 %collective-permute-start.15 = (bf16[2,256,512]{2,1,0:T(8,128)(2,1)S(1)}, bf16[2,256,512]{2,1,0:T(8,128)(2,1)}, u32[]{:S(2)}, u32[]{:S(2)}) collective-permute-start(bf16[2,256,512]{2,1,0:T(8,128)(2,1)S(1)} %collective-permute-done.13.refs_11_.refs_16_), channel_id=1, source_target_pairs={{0,1},{1,0},{2,3},{3,2},{4,5},{5,4},{6,7},{7,6},{8,9},{9,8},{10,11... | collective-permute-start | bytes 1572872 | tf_op jit(solution)/shard_map/ppermute | solution.py:288
  64.4 7.1 %collective-permute-start.16 = (bf16[2,256,512]{2,1,0:T(8,128)(2,1)S(1)}, bf16[2,256,512]{2,1,0:T(8,128)(2,1)}, u32[]{:S(2)}, u32[]{:S(2)}) collective-permute-start(bf16[2,256,512]{2,1,0:T(8,128)(2,1)S(1)} %collective-permute-done.11.refs_14_.refs_19_), channel_id=1, source_target_pairs={{0,1},{1,0},{2,3},{3,2},{4,5},{5,4},{6,7},{7,6},{8,9},{9,8},{10,11... | collective-permute-start | bytes 1572872 | tf_op jit(solution)/shard_map/ppermute | solution.py:288
  64.4 26.1 %all-to-all-start.1 = ((f16[8,64,640]{2,1,0:T(8,128)(2,1)}), f16[8,64,640]{2,1,0:T(8,128)(2,1)S(1)}, u32[]{:S(2)}, u32[]{:S(2)}) async-start(f16[8,64,640]{2,1,0:T(8,128)(2,1)} %pad_maximum_fusion.1), calls=%async_computation.1 | async-start | bytes 1310720 | tf_op jit(solution)/shard_map/all_to_all | solution.py:323
  90.5 24.5 %all-to-all-start.3 = ((f16[8,64,640]{2,1,0:T(8,128)(2,1)}), f16[8,64,640]{2,1,0:T(8,128)(2,1)S(1)}, u32[]{:S(2)}, u32[]{:S(2)}) async-start(f16[8,64,640]{2,1,0:T(8,128)(2,1)} %convert_element_type.66), calls=%async_computation.3 | async-start | bytes 1310720 | tf_op jit(solution)/shard_map/all_to_all | solution.py:323
  115.0 21.2 %all-to-all-start.2 = ((f16[8,64,640]{2,1,0:T(8,128)(2,1)}), f16[8,64,640]{2,1,0:T(8,128)(2,1)}, u32[]{:S(2)}, u32[]{:S(2)}) async-start(f16[8,64,640]{2,1,0:T(8,128)(2,1)} %convert_element_type.65), calls=%async_computation.2 | async-start | bytes 1310720 | tf_op jit(solution)/shard_map/all_to_all | solution.py:323
  121.1 4.8 %collective-permute-start.17 = (f16[64,512]{1,0:T(8,128)(2,1)S(1)}, f16[64,512]{1,0:T(8,128)(2,1)S(1)}, u32[]{:S(2)}, u32[]{:S(2)}) collective-permute-start(f16[64,512]{1,0:T(8,128)(2,1)S(1)} %fusion.7), channel_id=1, source_target_pairs={{0,1},{1,0},{2,3},{3,2},{4,5},{5,4},{6,7},{7,6},{8,9},{9,8},{10,11... | collective-permute-start | bytes 196616 | tf_op jit(solution)/shard_map/ppermute | solution.py:288
  137.8 5.1 %collective-permute-start.18 = (f16[64,512]{1,0:T(8,128)(2,1)S(1)}, f16[64,512]{1,0:T(8,128)(2,1)S(1)}, u32[]{:S(2)}, u32[]{:S(2)}) collective-permute-start(f16[64,512]{1,0:T(8,128)(2,1)S(1)} %fusion.8), channel_id=1, source_target_pairs={{0,1},{1,0},{2,3},{3,2},{4,5},{5,4},{6,7},{7,6},{8,9},{9,8},{10,11... | collective-permute-start | bytes 196616 | tf_op jit(solution)/shard_map/ppermute | solution.py:288
  (14 other events, 57.8 us)

commit v19 on v18

--- a/solution.py
+++ b/solution.py
@@ -12,7 +12,7 @@
 HALF = jnp.float16
 COT_SCALE = 256.0
 VMEM = 56 * 1024 * 1024
-AHEAD = 3
+AHEAD = 8
 
 
 def ring_order(count):
@@ -218,7 +218,7 @@
 
     def first_product(d):
         arrived(d)
-        if s.count <= 8 and d == s.count - AHEAD:
+        if s.count <= 8 and d == max(s.count - AHEAD, 0):
             for copy in late:
                 copy.start()
         return nt(panel, matrix[d])

time: 144 us -> 147 us (1.021)
  Pallas kernels: 31.5 us -> 33.7 us
    pallas_call x2, Pallas kernels: 31.5 us -> 33.7 us  [call(): pl.pallas_call(functools.partial(kernel, s), out_shape=[*vmem_outs, *hbm_...]
  transfers between devices with their start and end apart: 23 -> 23, of which waited for: 7 -> 7; matrix products, arithmetic and copies ran while one was open for 17% -> 17% of each run, Pallas kernels for 22% -> 23%
where the time goes in v19:
time: 147 us; the launch traced here: 146 us
  starting transfers between devices  44.8 us (30%)
  waiting for transfers between devices  34.6 us (24%)
  Pallas kernels  33.7 us (23%)
  other arithmetic  22.5 us (15%)
  local copies, waits for them, and re-layouts  7.82 us (5%)
    pallas_call x2, Pallas kernels, call(): pl.pallas_call(functools.partial(kernel, s), out_shape=[*vmem_outs, *hbm_...  33.7 us
    ppermute x7, waiting for transfers between devices, onward(): return lax.ppermute(x, ('src', 'tgt'), pairs)  25 us
    all_to_all x4, starting transfers between devices, exchange(): return lax.all_to_all(x, 'src', 0, 0, tiled=True)  23.6 us
    ppermute x12, starting transfers between devices, swap_cores(): return lax.ppermute(x, 'tgt', [(0, 1), (1, 0)])  12.1 us
    all_to_all x4, waiting for transfers between devices, exchange(): return lax.all_to_all(x, 'src', 0, 0, tiled=True)  9.52 us
    ppermute x7, starting transfers between devices, onward(): return lax.ppermute(x, ('src', 'tgt'), pairs)  9.14 us
    div x1, other arithmetic, local(): source_known = source_cotangent / source_mass  3.27 us
  transfers between devices with their start and end apart: 23, of which 7 were waited for; matrix products, arithmetic and copies ran while one was open for 17% of the time, Pallas kernels for 23%

profile of v19, /device:TPU:1, one launch (start us, length us, event | category | flops | bytes accessed | tf_op | source)
XLA Modules:
  0.0 145.9 jit_solution(11689236308523057321)
XLA Ops:
  7.0 2.7 %collective-permute-start.1 = (bf16[2,256,512]{2,1,0:T(8,128)(2,1)}, bf16[2,256,512]{2,1,0:T(8,128)(2,1)}, u32[]{:S(2)}, u32[]{:S(2)}) collective-permute-start(bf16[2,256,512]{2,1,0:T(8,128)(2,1)} %get-tuple-element.34.refs_0_.refs_5_), channel_id=1, source_target_pairs={{0,4},{1,3},{4,8},{5,1},{8,12},{9,5},{12,14},{13,9},{14,10},{15,13... | collective-permute-start | bytes 1572872 | tf_op jit(solution)/shard_map/ppermute | solution.py:320
  14.6 2.3 %collective-permute-done.1.refs_2_.refs_7_ = bf16[2,256,512]{2,1,0:T(8,128)(2,1)} collective-permute-done((bf16[2,256,512]{2,1,0:T(8,128)(2,1)}, bf16[2,256,512]{2,1,0:T(8,128)(2,1)}, u32[]{:S(2)}, u32[]{:S(2)}) %collective-permute-start.1) | collective-permute-done | bytes 524320 | tf_op jit(solution)/shard_map/ppermute | solution.py:320
  16.9 1.4 collective-permute-start.2
  19.4 1.5 %copy.22 = f16[512,512]{1,0:T(8,128)(2,1)S(1)} copy(f16[512,512]{0,1:T(8,128)(2,1)} %get-tuple-element.89) | data formatting | bytes 1048576 | tf_op jit(solution)/shard_map/transpose | solution.py:337
  22.5 1.4 collective-permute-start.8
  25.3 2.9 %collective-permute-done.2.refs_6_.refs_11_ = bf16[2,256,512]{2,1,0:T(8,128)(2,1)} collective-permute-done((bf16[2,256,512]{2,1,0:T(8,128)(2,1)}, bf16[2,256,512]{2,1,0:T(8,128)(2,1)}, u32[]{:S(2)}, u32[]{:S(2)}) %collective-permute-start.2) | collective-permute-done | bytes 524320 | tf_op jit(solution)/shard_map/ppermute | solution.py:320
  28.2 5.7 %all-to-all-start = ((f16[8,64,640]{2,1,0:T(8,128)(2,1)}), f16[8,64,640]{2,1,0:T(8,128)(2,1)S(1)}, u32[]{:S(2)}, u32[]{:S(2)}) async-start(f16[8,64,640]{2,1,0:T(8,128)(2,1)} %pad_maximum_fusion), calls=%async_computation | async-start | bytes 1310720 | tf_op jit(solution)/shard_map/all_to_all | solution.py:323
  35.2 1.8 %collective-permute-start.5 = (bf16[2,256,512]{2,1,0:T(8,128)(2,1)}, bf16[2,256,512]{2,1,0:T(8,128)(2,1)}, u32[]{:S(2)}, u32[]{:S(2)}) collective-permute-start(bf16[2,256,512]{2,1,0:T(8,128)(2,1)} %collective-permute-done.2.refs_6_.refs_11_), channel_id=1, source_target_pairs={{0,4},{1,3},{4,8},{5,1},{8,12},{9,5},{12,14},{13,9},{14,10},{15,13... | collective-permute-start | bytes 1572872 | tf_op jit(solution)/shard_map/ppermute | solution.py:320
  39.9 12.5 %collective-permute-done.5.refs_10_.refs_15_ = bf16[2,256,512]{2,1,0:T(8,128)(2,1)} collective-permute-done((bf16[2,256,512]{2,1,0:T(8,128)(2,1)}, bf16[2,256,512]{2,1,0:T(8,128)(2,1)}, u32[]{:S(2)}, u32[]{:S(2)}) %collective-permute-start.5) | collective-permute-done | bytes 524320 | tf_op jit(solution)/shard_map/ppermute | solution.py:320
  52.4 3.8 %collective-permute-start.14 = (bf16[2,256,512]{2,1,0:T(8,128)(2,1)}, bf16[2,256,512]{2,1,0:T(8,128)(2,1)S(1)}, u32[]{:S(2)}, u32[]{:S(2)}) collective-permute-start(bf16[2,256,512]{2,1,0:T(8,128)(2,1)} %collective-permute-done.5.refs_10_.refs_15_), channel_id=1, source_target_pairs={{0,1},{1,0},{2,3},{3,2},{4,5},{5,4},{6,7},{7,6},{8,9},{9,8},{10,11... | collective-permute-start | bytes 1572872 | tf_op jit(solution)/shard_map/ppermute | solution.py:288
  56.3 2.3 %collective-permute-done.13.refs_11_.refs_16_ = bf16[2,256,512]{2,1,0:T(8,128)(2,1)S(1)} collective-permute-done((bf16[2,256,512]{2,1,0:T(8,128)(2,1)}, bf16[2,256,512]{2,1,0:T(8,128)(2,1)S(1)}, u32[]{:S(2)}, u32[]{:S(2)}) %collective-permute-start.13) | collective-permute-done | bytes 524320 | tf_op jit(solution)/shard_map/ppermute | solution.py:320
  59.8 4.6 %collective-permute-done.11.refs_14_.refs_19_ = bf16[2,256,512]{2,1,0:T(8,128)(2,1)S(1)} collective-permute-done((bf16[2,256,512]{2,1,0:T(8,128)(2,1)}, bf16[2,256,512]{2,1,0:T(8,128)(2,1)S(1)}, u32[]{:S(2)}, u32[]{:S(2)}) %collective-permute-start.11) | collective-permute-done | bytes 524320 | tf_op jit(solution)/shard_map/ppermute | solution.py:320
  64.4 7.0 %all-to-all-start.1 = ((f16[8,64,640]{2,1,0:T(8,128)(2,1)}), f16[8,64,640]{2,1,0:T(8,128)(2,1)S(1)}, u32[]{:S(2)}, u32[]{:S(2)}) async-start(f16[8,64,640]{2,1,0:T(8,128)(2,1)} %pad_maximum_fusion.1), calls=%async_computation.1 | async-start | bytes 1310720 | tf_op jit(solution)/shard_map/all_to_all | solution.py:323
  72.3 15.9 %shard_map.132 = (f32[8,64,640]{2,1,0:T(8,128)}, f32[8,64,512]{2,1,0:T(8,128)}, f32[8,8,512]{2,1,0:T(8,128)}, f32[64,1024]{1,0:T(8,128)}, f32[64,1024]{1,0:T(8,128)}, /*index=5*/f32[64,1024]{1,0:T(8,128)}) custom-call(s32[9]{0:T(128)} %pad_add_fusion.table, f32[8,64,640]{2,1,0:T(8,128)} %convert_element_type.63.mass_in, ...), custom_call_target="tpu_custom_call" | custom-call | flops 15032385536 | bytes 16777216 | tf_op jit(solution)/shard_map/pallas_call | solution.py:264
  88.2 2.2 %convert_element_type.66 = f16[8,64,640]{2,1,0:T(8,128)(2,1)} convert(f32[8,64,640]{2,1,0:T(8,128)} %get-tuple-element.53.thirds_in) | non-fusion elementwise | flops 327680 | bytes 1966080 | tf_op jit(solution)/shard_map/convert_element_type | solution.py:414
  90.5 5.4 %all-to-all-start.3 = ((f16[8,64,640]{2,1,0:T(8,128)(2,1)}), f16[8,64,640]{2,1,0:T(8,128)(2,1)S(1)}, u32[]{:S(2)}, u32[]{:S(2)}) async-start(f16[8,64,640]{2,1,0:T(8,128)(2,1)} %convert_element_type.66), calls=%async_computation.3 | async-start | bytes 1310720 | tf_op jit(solution)/shard_map/all_to_all | solution.py:323
  97.1 17.8 %shard_map.133 = f32[8,64,640]{2,1,0:T(8,128)} custom-call(s32[9]{0:T(128)} %pad_add_fusion.table, f32[8,64,640]{2,1,0:T(8,128)} %convert_element_type.63.mass_in, f32[8,64,640]{2,1,0:T(8,128)} %convert_element_type.64.cot_in, f32[8,64,640]{2,1,0:T(8,128)} %get-tuple-element.53.thirds_in, f32[8,64,512]{2,1,0:T(8,128)} %get-tuple-element.54.refs_0_, ...), custom_call_target="tpu_custom_call" | custom-call | flops 10737418240 | bytes 16777216 | tf_op jit(solution)/shard_map/pallas_call | solution.py:264
  114.9 2.3 %convert_element_type.65 = f16[8,64,640]{2,1,0:T(8,128)(2,1)} convert(f32[8,64,640]{2,1,0:T(8,128)} %shard_map.133) | non-fusion elementwise | flops 327680 | bytes 1966080 | tf_op jit(solution)/shard_map/convert_element_type | solution.py:421
  117.2 5.4 %all-to-all-start.2 = ((f16[8,64,640]{2,1,0:T(8,128)(2,1)}), f16[8,64,640]{2,1,0:T(8,128)(2,1)}, u32[]{:S(2)}, u32[]{:S(2)}) async-start(f16[8,64,640]{2,1,0:T(8,128)(2,1)} %convert_element_type.65), calls=%async_computation.2 | async-start | bytes 1310720 | tf_op jit(solution)/shard_map/all_to_all | solution.py:323
  123.2 1.5 %collective-permute-start.17 = (f16[64,512]{1,0:T(8,128)(2,1)S(1)}, f16[64,512]{1,0:T(8,128)(2,1)S(1)}, u32[]{:S(2)}, u32[]{:S(2)}) collective-permute-start(f16[64,512]{1,0:T(8,128)(2,1)S(1)} %fusion.7), channel_id=1, source_target_pairs={{0,1},{1,0},{2,3},{3,2},{4,5},{5,4},{6,7},{7,6},{8,9},{9,8},{10,11... | collective-permute-start | bytes 196616 | tf_op jit(solution)/shard_map/ppermute | solution.py:288
  124.7 3.3 %fusion.14 = (f32[512,512]{1,0:T(8,128)}, f32[512,512]{1,0:T(8,128)}) fusion(f32[512,512]{1,0:T(8,128)} %param.15, f32[512,512]{1,0:T(8,128)} %param.10, f32[640,512]{1,0:T(8,128)S(1)} %bitcast.77), kind=kLoop, calls=%fused_computation.63 | loop fusion | flops 524288 | bytes 5242880 | tf_op jit(solution)/shard_map/div | solution.py:417
  128.9 9.5 %all-to-all-done.2 = f16[8,64,640]{2,1,0:T(8,128)(2,1)} async-done(((f16[8,64,640]{2,1,0:T(8,128)(2,1)}), f16[8,64,640]{2,1,0:T(8,128)(2,1)}, u32[]{:S(2)}, u32[]{:S(2)}) %all-to-all-start.2) | async-done | bytes 655392 | tf_op jit(solution)/shard_map/all_to_all | solution.py:323
  140.0 2.7 %collective-permute-start.18 = (f16[64,512]{1,0:T(8,128)(2,1)S(1)}, f16[64,512]{1,0:T(8,128)(2,1)S(1)}, u32[]{:S(2)}, u32[]{:S(2)}) collective-permute-start(f16[64,512]{1,0:T(8,128)(2,1)S(1)} %fusion.8), channel_id=1, source_target_pairs={{0,1},{1,0},{2,3},{3,2},{4,5},{5,4},{6,7},{7,6},{8,9},{9,8},{10,11... | collective-permute-start | bytes 196616 | tf_op jit(solution)/shard_map/ppermute | solution.py:288
  142.7 2.4 %fusion = f32[512,512]{1,0:T(8,128)} fusion(f32[512,512]{1,0:T(8,128)} %get-tuple-element.61, f32[640,512]{1,0:T(8,128)S(1)} %bitcast.79), kind=kLoop, calls=%fused_computation.3 | loop fusion | flops 524288 | bytes 3145728 | tf_op jit(solution)/shard_map/add | solution.py:432
  (104 shorter events, 26.4 us)
Async XLA Ops:
  3.2 2.6 %collective-permute-start = (bf16[512,512]{1,0:T(8,128)(2,1)S(1)}, bf16[512,512]{1,0:T(8,128)(2,1)S(1)}, u32[]{:S(2)}, u32[]{:S(2)}) collective-permute-start(bf16[512,512]{1,0:T(8,128)(2,1)S(1)} %bitcast.96), channel_id=1, source_target_pairs={{0,1},{1,0},{2,3},{3,2},{4,5},{5,4},{6,7},{7,6},{8,9},{9,8},{10,11... | collective-permute-start | bytes 1572872 | tf_op jit(solution)/shard_map/ppermute | solution.py:288
  7.0 9.9 %collective-permute-start.1 = (bf16[2,256,512]{2,1,0:T(8,128)(2,1)}, bf16[2,256,512]{2,1,0:T(8,128)(2,1)}, u32[]{:S(2)}, u32[]{:S(2)}) collective-permute-start(bf16[2,256,512]{2,1,0:T(8,128)(2,1)} %get-tuple-element.34.refs_0_.refs_5_), channel_id=1, source_target_pairs={{0,4},{1,3},{4,8},{5,1},{8,12},{9,5},{12,14},{13,9},{14,10},{15,13... | collective-permute-start | bytes 1572872 | tf_op jit(solution)/shard_map/ppermute | solution.py:320
  10.6 11.9 %collective-permute-start.7 = (bf16[2,256,512]{2,1,0:T(8,128)(2,1)}, bf16[2,256,512]{2,1,0:T(8,128)(2,1)}, u32[]{:S(2)}, u32[]{:S(2)}) collective-permute-start(bf16[2,256,512]{2,1,0:T(8,128)(2,1)} %get-tuple-element.40.refs_1_.refs_6_), channel_id=1, source_target_pairs={{0,4},{1,3},{4,8},{5,1},{8,12},{9,5},{12,14},{13,9},{14,10},{15,13... | collective-permute-start | bytes 1572872 | tf_op jit(solution)/shard_map/ppermute | solution.py:320
  12.9 11.0 %collective-permute-start.10 = (f16[64,512]{1,0:T(8,128)(2,1)}, f16[64,512]{1,0:T(8,128)(2,1)S(1)}, u32[]{:S(2)}, u32[]{:S(2)}) collective-permute-start(f16[64,512]{1,0:T(8,128)(2,1)} %bitcast.74), channel_id=1, source_target_pairs={{0,1},{1,0},{2,3},{3,2},{4,5},{5,4},{6,7},{7,6},{8,9},{9,8},{10,11... | collective-permute-start | bytes 196616 | tf_op jit(solution)/shard_map/ppermute | solution.py:288
  14.6 9.4 %collective-permute-start.3 = (f16[64,512]{1,0:T(8,128)(2,1)}, f16[64,512]{1,0:T(8,128)(2,1)S(1)}, u32[]{:S(2)}, u32[]{:S(2)}) collective-permute-start(f16[64,512]{1,0:T(8,128)(2,1)} %bitcast.75), channel_id=1, source_target_pairs={{0,1},{1,0},{2,3},{3,2},{4,5},{5,4},{6,7},{7,6},{8,9},{9,8},{10,11... | collective-permute-start | bytes 196616 | tf_op jit(solution)/shard_map/ppermute | solution.py:288
  16.9 11.2 %collective-permute-start.2 = (bf16[2,256,512]{2,1,0:T(8,128)(2,1)}, bf16[2,256,512]{2,1,0:T(8,128)(2,1)}, u32[]{:S(2)}, u32[]{:S(2)}) collective-permute-start(bf16[2,256,512]{2,1,0:T(8,128)(2,1)} %collective-permute-done.1.refs_2_.refs_7_), channel_id=1, source_target_pairs={{0,4},{1,3},{4,8},{5,1},{8,12},{9,5},{12,14},{13,9},{14,10},{15,13... | collective-permute-start | bytes 1572872 | tf_op jit(solution)/shard_map/ppermute | solution.py:320
  20.9 14.2 %collective-permute-start.4 = (bf16[2,256,512]{2,1,0:T(8,128)(2,1)}, bf16[2,256,512]{2,1,0:T(8,128)(2,1)S(1)}, u32[]{:S(2)}, u32[]{:S(2)}) collective-permute-start(bf16[2,256,512]{2,1,0:T(8,128)(2,1)} %collective-permute-done.1.refs_2_.refs_7_), channel_id=1, source_target_pairs={{0,1},{1,0},{2,3},{3,2},{4,5},{5,4},{6,7},{7,6},{8,9},{9,8},{10,11... | collective-permute-start | bytes 1572872 | tf_op jit(solution)/shard_map/ppermute | solution.py:288
  22.5 12.5 %collective-permute-start.8 = (bf16[2,256,512]{2,1,0:T(8,128)(2,1)}, bf16[2,256,512]{2,1,0:T(8,128)(2,1)}, u32[]{:S(2)}, u32[]{:S(2)}) collective-permute-start(bf16[2,256,512]{2,1,0:T(8,128)(2,1)} %collective-permute-done.7.refs_3_.refs_8_), channel_id=1, source_target_pairs={{0,4},{1,3},{4,8},{5,1},{8,12},{9,5},{12,14},{13,9},{14,10},{15,13... | collective-permute-start | bytes 1572872 | tf_op jit(solution)/shard_map/ppermute | solution.py:320
  28.2 30.4 %all-to-all-start = ((f16[8,64,640]{2,1,0:T(8,128)(2,1)}), f16[8,64,640]{2,1,0:T(8,128)(2,1)S(1)}, u32[]{:S(2)}, u32[]{:S(2)}) async-start(f16[8,64,640]{2,1,0:T(8,128)(2,1)} %pad_maximum_fusion), calls=%async_computation | async-start | bytes 1310720 | tf_op jit(solution)/shard_map/all_to_all | solution.py:323
  33.9 5.5 %collective-permute-start.12 = (bf16[2,256,512]{2,1,0:T(8,128)(2,1)}, bf16[2,256,512]{2,1,0:T(8,128)(2,1)S(1)}, u32[]{:S(2)}, u32[]{:S(2)}) collective-permute-start(bf16[2,256,512]{2,1,0:T(8,128)(2,1)} %collective-permute-done.7.refs_3_.refs_8_), channel_id=1, source_target_pairs={{0,1},{1,0},{2,3},{3,2},{4,5},{5,4},{6,7},{7,6},{8,9},{9,8},{10,11... | collective-permute-start | bytes 1572872 | tf_op jit(solution)/shard_map/ppermute | solution.py:288
  35.1 4.8 %collective-permute-start.9 = (bf16[2,256,512]{2,1,0:T(8,128)(2,1)}, bf16[2,256,512]{2,1,0:T(8,128)(2,1)}, u32[]{:S(2)}, u32[]{:S(2)}) collective-permute-start(bf16[2,256,512]{2,1,0:T(8,128)(2,1)} %collective-permute-done.8.refs_7_.refs_12_), channel_id=1, source_target_pairs={{0,1},{1,0},{2,3},{3,2},{4,5},{5,4},{6,7},{7,6},{8,9},{9,8},{10,11... | collective-permute-start | bytes 1572872 | tf_op jit(solution)/shard_map/ppermute | solution.py:288
  35.2 17.3 %collective-permute-start.5 = (bf16[2,256,512]{2,1,0:T(8,128)(2,1)}, bf16[2,256,512]{2,1,0:T(8,128)(2,1)}, u32[]{:S(2)}, u32[]{:S(2)}) collective-permute-start(bf16[2,256,512]{2,1,0:T(8,128)(2,1)} %collective-permute-done.2.refs_6_.refs_11_), channel_id=1, source_target_pairs={{0,4},{1,3},{4,8},{5,1},{8,12},{9,5},{12,14},{13,9},{14,10},{15,13... | collective-permute-start | bytes 1572872 | tf_op jit(solution)/shard_map/ppermute | solution.py:320
  36.9 15.5 %collective-permute-start.6 = (bf16[2,256,512]{2,1,0:T(8,128)(2,1)}, bf16[2,256,512]{2,1,0:T(8,128)(2,1)}, u32[]{:S(2)}, u32[]{:S(2)}) collective-permute-start(bf16[2,256,512]{2,1,0:T(8,128)(2,1)} %collective-permute-done.2.refs_6_.refs_11_), channel_id=1, source_target_pairs={{0,1},{1,0},{2,3},{3,2},{4,5},{5,4},{6,7},{7,6},{8,9},{9,8},{10,11... | collective-permute-start | bytes 1572872 | tf_op jit(solution)/shard_map/ppermute | solution.py:288
  39.4 25.1 %copy-start.10 = (bf16[2,256,512]{2,1,0:T(8,128)(2,1)}, bf16[2,256,512]{2,1,0:T(8,128)(2,1)S(1)}, u32[]{:S(2)}) copy-start(bf16[2,256,512]{2,1,0:T(8,128)(2,1)S(1)} %collective-permute-done.12.refs_5_.refs_10_) | copy-start | bytes 1572868
  39.4 19.2 %collective-permute-start.13 = (bf16[2,256,512]{2,1,0:T(8,128)(2,1)}, bf16[2,256,512]{2,1,0:T(8,128)(2,1)S(1)}, u32[]{:S(2)}, u32[]{:S(2)}) collective-permute-start(bf16[2,256,512]{2,1,0:T(8,128)(2,1)} %collective-permute-done.8.refs_7_.refs_12_), channel_id=1, source_target_pairs={{0,4},{1,3},{4,8},{5,1},{8,12},{9,5},{12,14},{13,9},{14,10},{15,13... | collective-permute-start | bytes 1572872 | tf_op jit(solution)/shard_map/ppermute | solution.py:320
  52.4 12.0 %collective-permute-start.11 = (bf16[2,256,512]{2,1,0:T(8,128)(2,1)}, bf16[2,256,512]{2,1,0:T(8,128)(2,1)S(1)}, u32[]{:S(2)}, u32[]{:S(2)}) collective-permute-start(bf16[2,256,512]{2,1,0:T(8,128)(2,1)} %collective-permute-done.5.refs_10_.refs_15_), channel_id=1, source_target_pairs={{0,4},{1,3},{4,8},{5,1},{8,12},{9,5},{12,14},{13,9},{14,10},{15,13... | collective-permute-start | bytes 1572872 | tf_op jit(solution)/shard_map/ppermute | solution.py:320
  52.4 19.0 %collective-permute-start.14 = (bf16[2,256,512]{2,1,0:T(8,128)(2,1)}, bf16[2,256,512]{2,1,0:T(8,128)(2,1)S(1)}, u32[]{:S(2)}, u32[]{:S(2)}) collective-permute-start(bf16[2,256,512]{2,1,0:T(8,128)(2,1)} %collective-permute-done.5.refs_10_.refs_15_), channel_id=1, source_target_pairs={{0,1},{1,0},{2,3},{3,2},{4,5},{5,4},{6,7},{7,6},{8,9},{9,8},{10,11... | collective-permute-start | bytes 1572872 | tf_op jit(solution)/shard_map/ppermute | solution.py:288
  58.6 12.9 %collective-permute-start.15 = (bf16[2,256,512]{2,1,0:T(8,128)(2,1)S(1)}, bf16[2,256,512]{2,1,0:T(8,128)(2,1)}, u32[]{:S(2)}, u32[]{:S(2)}) collective-permute-start(bf16[2,256,512]{2,1,0:T(8,128)(2,1)S(1)} %collective-permute-done.13.refs_11_.refs_16_), channel_id=1, source_target_pairs={{0,1},{1,0},{2,3},{3,2},{4,5},{5,4},{6,7},{7,6},{8,9},{9,8},{10,11... | collective-permute-start | bytes 1572872 | tf_op jit(solution)/shard_map/ppermute | solution.py:288
  64.4 7.1 %collective-permute-start.16 = (bf16[2,256,512]{2,1,0:T(8,128)(2,1)S(1)}, bf16[2,256,512]{2,1,0:T(8,128)(2,1)}, u32[]{:S(2)}, u32[]{:S(2)}) collective-permute-start(bf16[2,256,512]{2,1,0:T(8,128)(2,1)S(1)} %collective-permute-done.11.refs_14_.refs_19_), channel_id=1, source_target_pairs={{0,1},{1,0},{2,3},{3,2},{4,5},{5,4},{6,7},{7,6},{8,9},{9,8},{10,11... | collective-permute-start | bytes 1572872 | tf_op jit(solution)/shard_map/ppermute | solution.py:288
  64.4 26.0 %all-to-all-start.1 = ((f16[8,64,640]{2,1,0:T(8,128)(2,1)}), f16[8,64,640]{2,1,0:T(8,128)(2,1)S(1)}, u32[]{:S(2)}, u32[]{:S(2)}) async-start(f16[8,64,640]{2,1,0:T(8,128)(2,1)} %pad_maximum_fusion.1), calls=%async_computation.1 | async-start | bytes 1310720 | tf_op jit(solution)/shard_map/all_to_all | solution.py:323
  90.5 26.7 %all-to-all-start.3 = ((f16[8,64,640]{2,1,0:T(8,128)(2,1)}), f16[8,64,640]{2,1,0:T(8,128)(2,1)S(1)}, u32[]{:S(2)}, u32[]{:S(2)}) async-start(f16[8,64,640]{2,1,0:T(8,128)(2,1)} %convert_element_type.66), calls=%async_computation.3 | async-start | bytes 1310720 | tf_op jit(solution)/shard_map/all_to_all | solution.py:323
  117.2 21.2 %all-to-all-start.2 = ((f16[8,64,640]{2,1,0:T(8,128)(2,1)}), f16[8,64,640]{2,1,0:T(8,128)(2,1)}, u32[]{:S(2)}, u32[]{:S(2)}) async-start(f16[8,64,640]{2,1,0:T(8,128)(2,1)} %convert_element_type.65), calls=%async_computation.2 | async-start | bytes 1310720 | tf_op jit(solution)/shard_map/all_to_all | solution.py:323
  123.2 4.8 %collective-permute-start.17 = (f16[64,512]{1,0:T(8,128)(2,1)S(1)}, f16[64,512]{1,0:T(8,128)(2,1)S(1)}, u32[]{:S(2)}, u32[]{:S(2)}) collective-permute-start(f16[64,512]{1,0:T(8,128)(2,1)S(1)} %fusion.7), channel_id=1, source_target_pairs={{0,1},{1,0},{2,3},{3,2},{4,5},{5,4},{6,7},{7,6},{8,9},{9,8},{10,11... | collective-permute-start | bytes 196616 | tf_op jit(solution)/shard_map/ppermute | solution.py:288
  140.0 5.1 %collective-permute-start.18 = (f16[64,512]{1,0:T(8,128)(2,1)S(1)}, f16[64,512]{1,0:T(8,128)(2,1)S(1)}, u32[]{:S(2)}, u32[]{:S(2)}) collective-permute-start(f16[64,512]{1,0:T(8,128)(2,1)S(1)} %fusion.8), channel_id=1, source_target_pairs={{0,1},{1,0},{2,3},{3,2},{4,5},{5,4},{6,7},{7,6},{8,9},{9,8},{10,11... | collective-permute-start | bytes 196616 | tf_op jit(solution)/shard_map/ppermute | solution.py:288
  (14 other events, 57.7 us)

commit v20 on v18

--- a/solution.py
+++ b/solution.py
@@ -204,11 +204,11 @@
     )
     row_two, row_one, col_one, col_two, col_three = state
     points = cot_in.at[:, :, pl.ds(s.rows, 2 * s.share)]
-    early = load([state_in[4], points], [col_three, cot_points], more_sems)
+    early = load([state_in[4], points, state_in[3]], [col_three, cot_points, col_two], more_sems)
     paired = [(mass_in, mass), (thirds_in, thirds), (cot_in, cot)]
     arrived = Arrivals(s, table, units, matrix, sems, paired)
     late = [
-        pltpu.make_async_copy(state_in[k], state[k], more_sems.at[2 + k]) for k in range(4)
+        pltpu.make_async_copy(state_in[k], state[k], more_sems.at[3 + k]) for k in range(3)
     ]
     for copy in early:
         copy.wait()
@@ -218,9 +218,6 @@
 
     def first_product(d):
         arrived(d)
-        if s.count <= 8 and d == s.count - AHEAD:
-            for copy in late:
-                copy.start()
         return nt(panel, matrix[d])
 
     def third(d, grad, total):
@@ -233,12 +230,12 @@
 
     total = chain(s.count, first_product, third, zero)
     for copy in late:
-        if s.count > 8:
-            copy.start()
-        copy.wait()
+        copy.start()
     target = gather_targets(s, mass, s.rows)
     term_two = total / col_two[...]
     panel_two = (-term_two * (target / col_two[...])).astype(jnp.bfloat16)
+    for copy in late:
+        copy.wait()
 
     def second(d, grad, total):
         k = table[d]

time: 144 us -> 145 us (level)
  no operation moved by 1% of the time
where the time goes in v20:
time: 145 us; the launch traced here: 144 us
  starting transfers between devices  44.8 us (31%)
  waiting for transfers between devices  34.6 us (24%)
  Pallas kernels  32.1 us (22%)
  other arithmetic  22.5 us (16%)
  local copies, waits for them, and re-layouts  7.82 us (5%)
    pallas_call x2, Pallas kernels, call(): pl.pallas_call(functools.partial(kernel, s), out_shape=[*vmem_outs, *hbm_...  32.1 us
    ppermute x7, waiting for transfers between devices, onward(): return lax.ppermute(x, ('src', 'tgt'), pairs)  25 us
    all_to_all x4, starting transfers between devices, exchange(): return lax.all_to_all(x, 'src', 0, 0, tiled=True)  23.6 us
    ppermute x12, starting transfers between devices, swap_cores(): return lax.ppermute(x, 'tgt', [(0, 1), (1, 0)])  12.1 us
    all_to_all x4, waiting for transfers between devices, exchange(): return lax.all_to_all(x, 'src', 0, 0, tiled=True)  9.52 us
    ppermute x7, starting transfers between devices, onward(): return lax.ppermute(x, ('src', 'tgt'), pairs)  9.14 us
    div x1, other arithmetic, local(): source_known = source_cotangent / source_mass  3.27 us
  transfers between devices with their start and end apart: 23, of which 7 were waited for; matrix products, arithmetic and copies ran while one was open for 17% of the time, Pallas kernels for 22%

profile of v20, /device:TPU:1, one launch (start us, length us, event | category | flops | bytes accessed | tf_op | source)
XLA Modules:
  0.0 144.3 jit_solution(17605630490908022106)
XLA Ops:
  7.0 2.7 %collective-permute-start.1 = (bf16[2,256,512]{2,1,0:T(8,128)(2,1)}, bf16[2,256,512]{2,1,0:T(8,128)(2,1)}, u32[]{:S(2)}, u32[]{:S(2)}) collective-permute-start(bf16[2,256,512]{2,1,0:T(8,128)(2,1)} %get-tuple-element.34.refs_0_.refs_5_), channel_id=1, source_target_pairs={{0,4},{1,3},{4,8},{5,1},{8,12},{9,5},{12,14},{13,9},{14,10},{15,13... | collective-permute-start | bytes 1572872 | tf_op jit(solution)/shard_map/ppermute | solution.py:317
  14.6 2.3 %collective-permute-done.1.refs_2_.refs_7_ = bf16[2,256,512]{2,1,0:T(8,128)(2,1)} collective-permute-done((bf16[2,256,512]{2,1,0:T(8,128)(2,1)}, bf16[2,256,512]{2,1,0:T(8,128)(2,1)}, u32[]{:S(2)}, u32[]{:S(2)}) %collective-permute-start.1) | collective-permute-done | bytes 524320 | tf_op jit(solution)/shard_map/ppermute | solution.py:317
  16.9 1.4 collective-permute-start.2
  19.4 1.5 %copy.22 = f16[512,512]{1,0:T(8,128)(2,1)S(1)} copy(f16[512,512]{0,1:T(8,128)(2,1)} %get-tuple-element.89) | data formatting | bytes 1048576 | tf_op jit(solution)/shard_map/transpose | solution.py:334
  22.5 1.4 collective-permute-start.8
  25.3 2.9 %collective-permute-done.2.refs_6_.refs_11_ = bf16[2,256,512]{2,1,0:T(8,128)(2,1)} collective-permute-done((bf16[2,256,512]{2,1,0:T(8,128)(2,1)}, bf16[2,256,512]{2,1,0:T(8,128)(2,1)}, u32[]{:S(2)}, u32[]{:S(2)}) %collective-permute-start.2) | collective-permute-done | bytes 524320 | tf_op jit(solution)/shard_map/ppermute | solution.py:317
  28.2 5.7 %all-to-all-start = ((f16[8,64,640]{2,1,0:T(8,128)(2,1)}), f16[8,64,640]{2,1,0:T(8,128)(2,1)S(1)}, u32[]{:S(2)}, u32[]{:S(2)}) async-start(f16[8,64,640]{2,1,0:T(8,128)(2,1)} %pad_maximum_fusion), calls=%async_computation | async-start | bytes 1310720 | tf_op jit(solution)/shard_map/all_to_all | solution.py:320
  35.2 1.8 %collective-permute-start.5 = (bf16[2,256,512]{2,1,0:T(8,128)(2,1)}, bf16[2,256,512]{2,1,0:T(8,128)(2,1)}, u32[]{:S(2)}, u32[]{:S(2)}) collective-permute-start(bf16[2,256,512]{2,1,0:T(8,128)(2,1)} %collective-permute-done.2.refs_6_.refs_11_), channel_id=1, source_target_pairs={{0,4},{1,3},{4,8},{5,1},{8,12},{9,5},{12,14},{13,9},{14,10},{15,13... | collective-permute-start | bytes 1572872 | tf_op jit(solution)/shard_map/ppermute | solution.py:317
  39.9 12.5 %collective-permute-done.5.refs_10_.refs_15_ = bf16[2,256,512]{2,1,0:T(8,128)(2,1)} collective-permute-done((bf16[2,256,512]{2,1,0:T(8,128)(2,1)}, bf16[2,256,512]{2,1,0:T(8,128)(2,1)}, u32[]{:S(2)}, u32[]{:S(2)}) %collective-permute-start.5) | collective-permute-done | bytes 524320 | tf_op jit(solution)/shard_map/ppermute | solution.py:317
  52.4 3.8 %collective-permute-start.14 = (bf16[2,256,512]{2,1,0:T(8,128)(2,1)}, bf16[2,256,512]{2,1,0:T(8,128)(2,1)S(1)}, u32[]{:S(2)}, u32[]{:S(2)}) collective-permute-start(bf16[2,256,512]{2,1,0:T(8,128)(2,1)} %collective-permute-done.5.refs_10_.refs_15_), channel_id=1, source_target_pairs={{0,1},{1,0},{2,3},{3,2},{4,5},{5,4},{6,7},{7,6},{8,9},{9,8},{10,11... | collective-permute-start | bytes 1572872 | tf_op jit(solution)/shard_map/ppermute | solution.py:285
  56.3 2.3 %collective-permute-done.13.refs_11_.refs_16_ = bf16[2,256,512]{2,1,0:T(8,128)(2,1)S(1)} collective-permute-done((bf16[2,256,512]{2,1,0:T(8,128)(2,1)}, bf16[2,256,512]{2,1,0:T(8,128)(2,1)S(1)}, u32[]{:S(2)}, u32[]{:S(2)}) %collective-permute-start.13) | collective-permute-done | bytes 524320 | tf_op jit(solution)/shard_map/ppermute | solution.py:317
  59.8 4.6 %collective-permute-done.11.refs_14_.refs_19_ = bf16[2,256,512]{2,1,0:T(8,128)(2,1)S(1)} collective-permute-done((bf16[2,256,512]{2,1,0:T(8,128)(2,1)}, bf16[2,256,512]{2,1,0:T(8,128)(2,1)S(1)}, u32[]{:S(2)}, u32[]{:S(2)}) %collective-permute-start.11) | collective-permute-done | bytes 524320 | tf_op jit(solution)/shard_map/ppermute | solution.py:317
  64.4 7.0 %all-to-all-start.1 = ((f16[8,64,640]{2,1,0:T(8,128)(2,1)}), f16[8,64,640]{2,1,0:T(8,128)(2,1)S(1)}, u32[]{:S(2)}, u32[]{:S(2)}) async-start(f16[8,64,640]{2,1,0:T(8,128)(2,1)} %pad_maximum_fusion.1), calls=%async_computation.1 | async-start | bytes 1310720 | tf_op jit(solution)/shard_map/all_to_all | solution.py:320
  72.3 16.0 %shard_map.132 = (f32[8,64,640]{2,1,0:T(8,128)}, f32[8,64,512]{2,1,0:T(8,128)}, f32[8,8,512]{2,1,0:T(8,128)}, f32[64,1024]{1,0:T(8,128)}, f32[64,1024]{1,0:T(8,128)}, /*index=5*/f32[64,1024]{1,0:T(8,128)}) custom-call(s32[9]{0:T(128)} %pad_add_fusion.table, f32[8,64,640]{2,1,0:T(8,128)} %convert_element_type.63.mass_in, ...), custom_call_target="tpu_custom_call" | custom-call | flops 15032385536 | bytes 16777216 | tf_op jit(solution)/shard_map/pallas_call | solution.py:261
  88.2 2.2 %convert_element_type.66 = f16[8,64,640]{2,1,0:T(8,128)(2,1)} convert(f32[8,64,640]{2,1,0:T(8,128)} %get-tuple-element.53.thirds_in) | non-fusion elementwise | flops 327680 | bytes 1966080 | tf_op jit(solution)/shard_map/convert_element_type | solution.py:411
  90.5 5.4 %all-to-all-start.3 = ((f16[8,64,640]{2,1,0:T(8,128)(2,1)}), f16[8,64,640]{2,1,0:T(8,128)(2,1)S(1)}, u32[]{:S(2)}, u32[]{:S(2)}) async-start(f16[8,64,640]{2,1,0:T(8,128)(2,1)} %convert_element_type.66), calls=%async_computation.3 | async-start | bytes 1310720 | tf_op jit(solution)/shard_map/all_to_all | solution.py:320
  97.1 16.2 %shard_map.133 = f32[8,64,640]{2,1,0:T(8,128)} custom-call(s32[9]{0:T(128)} %pad_add_fusion.table, f32[8,64,640]{2,1,0:T(8,128)} %convert_element_type.63.mass_in, f32[8,64,640]{2,1,0:T(8,128)} %convert_element_type.64.cot_in, f32[8,64,640]{2,1,0:T(8,128)} %get-tuple-element.53.thirds_in, f32[8,64,512]{2,1,0:T(8,128)} %get-tuple-element.54.refs_0_, ...), custom_call_target="tpu_custom_call" | custom-call | flops 10737418240 | bytes 16777216 | tf_op jit(solution)/shard_map/pallas_call | solution.py:261
  113.3 2.3 %convert_element_type.65 = f16[8,64,640]{2,1,0:T(8,128)(2,1)} convert(f32[8,64,640]{2,1,0:T(8,128)} %shard_map.133) | non-fusion elementwise | flops 327680 | bytes 1966080 | tf_op jit(solution)/shard_map/convert_element_type | solution.py:418
  115.6 5.4 %all-to-all-start.2 = ((f16[8,64,640]{2,1,0:T(8,128)(2,1)}), f16[8,64,640]{2,1,0:T(8,128)(2,1)}, u32[]{:S(2)}, u32[]{:S(2)}) async-start(f16[8,64,640]{2,1,0:T(8,128)(2,1)} %convert_element_type.65), calls=%async_computation.2 | async-start | bytes 1310720 | tf_op jit(solution)/shard_map/all_to_all | solution.py:320
  121.7 1.5 %collective-permute-start.17 = (f16[64,512]{1,0:T(8,128)(2,1)S(1)}, f16[64,512]{1,0:T(8,128)(2,1)S(1)}, u32[]{:S(2)}, u32[]{:S(2)}) collective-permute-start(f16[64,512]{1,0:T(8,128)(2,1)S(1)} %fusion.7), channel_id=1, source_target_pairs={{0,1},{1,0},{2,3},{3,2},{4,5},{5,4},{6,7},{7,6},{8,9},{9,8},{10,11... | collective-permute-start | bytes 196616 | tf_op jit(solution)/shard_map/ppermute | solution.py:285
  123.2 3.3 %fusion.14 = (f32[512,512]{1,0:T(8,128)}, f32[512,512]{1,0:T(8,128)}) fusion(f32[512,512]{1,0:T(8,128)} %param.15, f32[512,512]{1,0:T(8,128)} %param.10, f32[640,512]{1,0:T(8,128)S(1)} %bitcast.77), kind=kLoop, calls=%fused_computation.63 | loop fusion | flops 524288 | bytes 5242880 | tf_op jit(solution)/shard_map/div | solution.py:414
  127.3 9.5 %all-to-all-done.2 = f16[8,64,640]{2,1,0:T(8,128)(2,1)} async-done(((f16[8,64,640]{2,1,0:T(8,128)(2,1)}), f16[8,64,640]{2,1,0:T(8,128)(2,1)}, u32[]{:S(2)}, u32[]{:S(2)}) %all-to-all-start.2) | async-done | bytes 655392 | tf_op jit(solution)/shard_map/all_to_all | solution.py:320
  138.4 2.7 %collective-permute-start.18 = (f16[64,512]{1,0:T(8,128)(2,1)S(1)}, f16[64,512]{1,0:T(8,128)(2,1)S(1)}, u32[]{:S(2)}, u32[]{:S(2)}) collective-permute-start(f16[64,512]{1,0:T(8,128)(2,1)S(1)} %fusion.8), channel_id=1, source_target_pairs={{0,1},{1,0},{2,3},{3,2},{4,5},{5,4},{6,7},{7,6},{8,9},{9,8},{10,11... | collective-permute-start | bytes 196616 | tf_op jit(solution)/shard_map/ppermute | solution.py:285
  141.1 2.4 %fusion = f32[512,512]{1,0:T(8,128)} fusion(f32[512,512]{1,0:T(8,128)} %get-tuple-element.61, f32[640,512]{1,0:T(8,128)S(1)} %bitcast.79), kind=kLoop, calls=%fused_computation.3 | loop fusion | flops 524288 | bytes 3145728 | tf_op jit(solution)/shard_map/add | solution.py:429
  (104 shorter events, 26.4 us)
Async XLA Ops:
  3.2 2.6 %collective-permute-start = (bf16[512,512]{1,0:T(8,128)(2,1)S(1)}, bf16[512,512]{1,0:T(8,128)(2,1)S(1)}, u32[]{:S(2)}, u32[]{:S(2)}) collective-permute-start(bf16[512,512]{1,0:T(8,128)(2,1)S(1)} %bitcast.96), channel_id=1, source_target_pairs={{0,1},{1,0},{2,3},{3,2},{4,5},{5,4},{6,7},{7,6},{8,9},{9,8},{10,11... | collective-permute-start | bytes 1572872 | tf_op jit(solution)/shard_map/ppermute | solution.py:285
  7.0 9.9 %collective-permute-start.1 = (bf16[2,256,512]{2,1,0:T(8,128)(2,1)}, bf16[2,256,512]{2,1,0:T(8,128)(2,1)}, u32[]{:S(2)}, u32[]{:S(2)}) collective-permute-start(bf16[2,256,512]{2,1,0:T(8,128)(2,1)} %get-tuple-element.34.refs_0_.refs_5_), channel_id=1, source_target_pairs={{0,4},{1,3},{4,8},{5,1},{8,12},{9,5},{12,14},{13,9},{14,10},{15,13... | collective-permute-start | bytes 1572872 | tf_op jit(solution)/shard_map/ppermute | solution.py:317
  10.6 11.9 %collective-permute-start.7 = (bf16[2,256,512]{2,1,0:T(8,128)(2,1)}, bf16[2,256,512]{2,1,0:T(8,128)(2,1)}, u32[]{:S(2)}, u32[]{:S(2)}) collective-permute-start(bf16[2,256,512]{2,1,0:T(8,128)(2,1)} %get-tuple-element.40.refs_1_.refs_6_), channel_id=1, source_target_pairs={{0,4},{1,3},{4,8},{5,1},{8,12},{9,5},{12,14},{13,9},{14,10},{15,13... | collective-permute-start | bytes 1572872 | tf_op jit(solution)/shard_map/ppermute | solution.py:317
  12.9 11.0 %collective-permute-start.10 = (f16[64,512]{1,0:T(8,128)(2,1)}, f16[64,512]{1,0:T(8,128)(2,1)S(1)}, u32[]{:S(2)}, u32[]{:S(2)}) collective-permute-start(f16[64,512]{1,0:T(8,128)(2,1)} %bitcast.74), channel_id=1, source_target_pairs={{0,1},{1,0},{2,3},{3,2},{4,5},{5,4},{6,7},{7,6},{8,9},{9,8},{10,11... | collective-permute-start | bytes 196616 | tf_op jit(solution)/shard_map/ppermute | solution.py:285
  14.6 9.4 %collective-permute-start.3 = (f16[64,512]{1,0:T(8,128)(2,1)}, f16[64,512]{1,0:T(8,128)(2,1)S(1)}, u32[]{:S(2)}, u32[]{:S(2)}) collective-permute-start(f16[64,512]{1,0:T(8,128)(2,1)} %bitcast.75), channel_id=1, source_target_pairs={{0,1},{1,0},{2,3},{3,2},{4,5},{5,4},{6,7},{7,6},{8,9},{9,8},{10,11... | collective-permute-start | bytes 196616 | tf_op jit(solution)/shard_map/ppermute | solution.py:285
  16.9 11.2 %collective-permute-start.2 = (bf16[2,256,512]{2,1,0:T(8,128)(2,1)}, bf16[2,256,512]{2,1,0:T(8,128)(2,1)}, u32[]{:S(2)}, u32[]{:S(2)}) collective-permute-start(bf16[2,256,512]{2,1,0:T(8,128)(2,1)} %collective-permute-done.1.refs_2_.refs_7_), channel_id=1, source_target_pairs={{0,4},{1,3},{4,8},{5,1},{8,12},{9,5},{12,14},{13,9},{14,10},{15,13... | collective-permute-start | bytes 1572872 | tf_op jit(solution)/shard_map/ppermute | solution.py:317
  20.9 14.2 %collective-permute-start.4 = (bf16[2,256,512]{2,1,0:T(8,128)(2,1)}, bf16[2,256,512]{2,1,0:T(8,128)(2,1)S(1)}, u32[]{:S(2)}, u32[]{:S(2)}) collective-permute-start(bf16[2,256,512]{2,1,0:T(8,128)(2,1)} %collective-permute-done.1.refs_2_.refs_7_), channel_id=1, source_target_pairs={{0,1},{1,0},{2,3},{3,2},{4,5},{5,4},{6,7},{7,6},{8,9},{9,8},{10,11... | collective-permute-start | bytes 1572872 | tf_op jit(solution)/shard_map/ppermute | solution.py:285
  22.5 12.5 %collective-permute-start.8 = (bf16[2,256,512]{2,1,0:T(8,128)(2,1)}, bf16[2,256,512]{2,1,0:T(8,128)(2,1)}, u32[]{:S(2)}, u32[]{:S(2)}) collective-permute-start(bf16[2,256,512]{2,1,0:T(8,128)(2,1)} %collective-permute-done.7.refs_3_.refs_8_), channel_id=1, source_target_pairs={{0,4},{1,3},{4,8},{5,1},{8,12},{9,5},{12,14},{13,9},{14,10},{15,13... | collective-permute-start | bytes 1572872 | tf_op jit(solution)/shard_map/ppermute | solution.py:317
  28.2 30.4 %all-to-all-start = ((f16[8,64,640]{2,1,0:T(8,128)(2,1)}), f16[8,64,640]{2,1,0:T(8,128)(2,1)S(1)}, u32[]{:S(2)}, u32[]{:S(2)}) async-start(f16[8,64,640]{2,1,0:T(8,128)(2,1)} %pad_maximum_fusion), calls=%async_computation | async-start | bytes 1310720 | tf_op jit(solution)/shard_map/all_to_all | solution.py:320
  33.9 5.5 %collective-permute-start.12 = (bf16[2,256,512]{2,1,0:T(8,128)(2,1)}, bf16[2,256,512]{2,1,0:T(8,128)(2,1)S(1)}, u32[]{:S(2)}, u32[]{:S(2)}) collective-permute-start(bf16[2,256,512]{2,1,0:T(8,128)(2,1)} %collective-permute-done.7.refs_3_.refs_8_), channel_id=1, source_target_pairs={{0,1},{1,0},{2,3},{3,2},{4,5},{5,4},{6,7},{7,6},{8,9},{9,8},{10,11... | collective-permute-start | bytes 1572872 | tf_op jit(solution)/shard_map/ppermute | solution.py:285
  35.1 4.8 %collective-permute-start.9 = (bf16[2,256,512]{2,1,0:T(8,128)(2,1)}, bf16[2,256,512]{2,1,0:T(8,128)(2,1)}, u32[]{:S(2)}, u32[]{:S(2)}) collective-permute-start(bf16[2,256,512]{2,1,0:T(8,128)(2,1)} %collective-permute-done.8.refs_7_.refs_12_), channel_id=1, source_target_pairs={{0,1},{1,0},{2,3},{3,2},{4,5},{5,4},{6,7},{7,6},{8,9},{9,8},{10,11... | collective-permute-start | bytes 1572872 | tf_op jit(solution)/shard_map/ppermute | solution.py:285
  35.2 17.3 %collective-permute-start.5 = (bf16[2,256,512]{2,1,0:T(8,128)(2,1)}, bf16[2,256,512]{2,1,0:T(8,128)(2,1)}, u32[]{:S(2)}, u32[]{:S(2)}) collective-permute-start(bf16[2,256,512]{2,1,0:T(8,128)(2,1)} %collective-permute-done.2.refs_6_.refs_11_), channel_id=1, source_target_pairs={{0,4},{1,3},{4,8},{5,1},{8,12},{9,5},{12,14},{13,9},{14,10},{15,13... | collective-permute-start | bytes 1572872 | tf_op jit(solution)/shard_map/ppermute | solution.py:317
  36.9 15.5 %collective-permute-start.6 = (bf16[2,256,512]{2,1,0:T(8,128)(2,1)}, bf16[2,256,512]{2,1,0:T(8,128)(2,1)}, u32[]{:S(2)}, u32[]{:S(2)}) collective-permute-start(bf16[2,256,512]{2,1,0:T(8,128)(2,1)} %collective-permute-done.2.refs_6_.refs_11_), channel_id=1, source_target_pairs={{0,1},{1,0},{2,3},{3,2},{4,5},{5,4},{6,7},{7,6},{8,9},{9,8},{10,11... | collective-permute-start | bytes 1572872 | tf_op jit(solution)/shard_map/ppermute | solution.py:285
  39.4 25.1 %copy-start.10 = (bf16[2,256,512]{2,1,0:T(8,128)(2,1)}, bf16[2,256,512]{2,1,0:T(8,128)(2,1)S(1)}, u32[]{:S(2)}) copy-start(bf16[2,256,512]{2,1,0:T(8,128)(2,1)S(1)} %collective-permute-done.12.refs_5_.refs_10_) | copy-start | bytes 1572868
  39.4 19.2 %collective-permute-start.13 = (bf16[2,256,512]{2,1,0:T(8,128)(2,1)}, bf16[2,256,512]{2,1,0:T(8,128)(2,1)S(1)}, u32[]{:S(2)}, u32[]{:S(2)}) collective-permute-start(bf16[2,256,512]{2,1,0:T(8,128)(2,1)} %collective-permute-done.8.refs_7_.refs_12_), channel_id=1, source_target_pairs={{0,4},{1,3},{4,8},{5,1},{8,12},{9,5},{12,14},{13,9},{14,10},{15,13... | collective-permute-start | bytes 1572872 | tf_op jit(solution)/shard_map/ppermute | solution.py:317
  52.4 12.0 %collective-permute-start.11 = (bf16[2,256,512]{2,1,0:T(8,128)(2,1)}, bf16[2,256,512]{2,1,0:T(8,128)(2,1)S(1)}, u32[]{:S(2)}, u32[]{:S(2)}) collective-permute-start(bf16[2,256,512]{2,1,0:T(8,128)(2,1)} %collective-permute-done.5.refs_10_.refs_15_), channel_id=1, source_target_pairs={{0,4},{1,3},{4,8},{5,1},{8,12},{9,5},{12,14},{13,9},{14,10},{15,13... | collective-permute-start | bytes 1572872 | tf_op jit(solution)/shard_map/ppermute | solution.py:317
  52.4 19.0 %collective-permute-start.14 = (bf16[2,256,512]{2,1,0:T(8,128)(2,1)}, bf16[2,256,512]{2,1,0:T(8,128)(2,1)S(1)}, u32[]{:S(2)}, u32[]{:S(2)}) collective-permute-start(bf16[2,256,512]{2,1,0:T(8,128)(2,1)} %collective-permute-done.5.refs_10_.refs_15_), channel_id=1, source_target_pairs={{0,1},{1,0},{2,3},{3,2},{4,5},{5,4},{6,7},{7,6},{8,9},{9,8},{10,11... | collective-permute-start | bytes 1572872 | tf_op jit(solution)/shard_map/ppermute | solution.py:285
  58.6 12.9 %collective-permute-start.15 = (bf16[2,256,512]{2,1,0:T(8,128)(2,1)S(1)}, bf16[2,256,512]{2,1,0:T(8,128)(2,1)}, u32[]{:S(2)}, u32[]{:S(2)}) collective-permute-start(bf16[2,256,512]{2,1,0:T(8,128)(2,1)S(1)} %collective-permute-done.13.refs_11_.refs_16_), channel_id=1, source_target_pairs={{0,1},{1,0},{2,3},{3,2},{4,5},{5,4},{6,7},{7,6},{8,9},{9,8},{10,11... | collective-permute-start | bytes 1572872 | tf_op jit(solution)/shard_map/ppermute | solution.py:285
  64.4 7.1 %collective-permute-start.16 = (bf16[2,256,512]{2,1,0:T(8,128)(2,1)S(1)}, bf16[2,256,512]{2,1,0:T(8,128)(2,1)}, u32[]{:S(2)}, u32[]{:S(2)}) collective-permute-start(bf16[2,256,512]{2,1,0:T(8,128)(2,1)S(1)} %collective-permute-done.11.refs_14_.refs_19_), channel_id=1, source_target_pairs={{0,1},{1,0},{2,3},{3,2},{4,5},{5,4},{6,7},{7,6},{8,9},{9,8},{10,11... | collective-permute-start | bytes 1572872 | tf_op jit(solution)/shard_map/ppermute | solution.py:285
  64.4 26.1 %all-to-all-start.1 = ((f16[8,64,640]{2,1,0:T(8,128)(2,1)}), f16[8,64,640]{2,1,0:T(8,128)(2,1)S(1)}, u32[]{:S(2)}, u32[]{:S(2)}) async-start(f16[8,64,640]{2,1,0:T(8,128)(2,1)} %pad_maximum_fusion.1), calls=%async_computation.1 | async-start | bytes 1310720 | tf_op jit(solution)/shard_map/all_to_all | solution.py:320
  90.5 25.1 %all-to-all-start.3 = ((f16[8,64,640]{2,1,0:T(8,128)(2,1)}), f16[8,64,640]{2,1,0:T(8,128)(2,1)S(1)}, u32[]{:S(2)}, u32[]{:S(2)}) async-start(f16[8,64,640]{2,1,0:T(8,128)(2,1)} %convert_element_type.66), calls=%async_computation.3 | async-start | bytes 1310720 | tf_op jit(solution)/shard_map/all_to_all | solution.py:320
  115.6 21.2 %all-to-all-start.2 = ((f16[8,64,640]{2,1,0:T(8,128)(2,1)}), f16[8,64,640]{2,1,0:T(8,128)(2,1)}, u32[]{:S(2)}, u32[]{:S(2)}) async-start(f16[8,64,640]{2,1,0:T(8,128)(2,1)} %convert_element_type.65), calls=%async_computation.2 | async-start | bytes 1310720 | tf_op jit(solution)/shard_map/all_to_all | solution.py:320
  121.7 4.8 %collective-permute-start.17 = (f16[64,512]{1,0:T(8,128)(2,1)S(1)}, f16[64,512]{1,0:T(8,128)(2,1)S(1)}, u32[]{:S(2)}, u32[]{:S(2)}) collective-permute-start(f16[64,512]{1,0:T(8,128)(2,1)S(1)} %fusion.7), channel_id=1, source_target_pairs={{0,1},{1,0},{2,3},{3,2},{4,5},{5,4},{6,7},{7,6},{8,9},{9,8},{10,11... | collective-permute-start | bytes 196616 | tf_op jit(solution)/shard_map/ppermute | solution.py:285
  138.4 5.1 %collective-permute-start.18 = (f16[64,512]{1,0:T(8,128)(2,1)S(1)}, f16[64,512]{1,0:T(8,128)(2,1)S(1)}, u32[]{:S(2)}, u32[]{:S(2)}) collective-permute-start(f16[64,512]{1,0:T(8,128)(2,1)S(1)} %fusion.8), channel_id=1, source_target_pairs={{0,1},{1,0},{2,3},{3,2},{4,5},{5,4},{6,7},{7,6},{8,9},{9,8},{10,11... | collective-permute-start | bytes 196616 | tf_op jit(solution)/shard_map/ppermute | solution.py:285
  (14 other events, 57.7 us)

commit v21 on v18

--- a/solution.py
+++ b/solution.py
@@ -361,7 +361,7 @@
                     (heads[k], swapped[step - 2, k])
                 )
             came[step, k] = heads[k] = onward(heads[k])
-            if step == min(2, last - 1) and k == 0:
+            if step == min(2, last - 1) and k == s.halves - 1:
                 heads[k], mass_message, table = lax.optimization_barrier(
                     (heads[k], mass_message, table)
                 )

time: 144 us -> 144 us (level)
  no operation moved by 1% of the time
where the time goes in v21:
time: 144 us
  starting transfers between devices  44.8 us (31%)
  waiting for transfers between devices  34.6 us (24%)
  Pallas kernels  31.5 us (22%)
  other arithmetic  22.5 us (16%)
  local copies, waits for them, and re-layouts  7.81 us (5%)
    pallas_call x2, Pallas kernels, call(): pl.pallas_call(functools.partial(kernel, s), out_shape=[*vmem_outs, *hbm_...  31.5 us
    ppermute x7, waiting for transfers between devices, onward(): return lax.ppermute(x, ('src', 'tgt'), pairs)  25 us
    all_to_all x4, starting transfers between devices, exchange(): return lax.all_to_all(x, 'src', 0, 0, tiled=True)  23.6 us
    ppermute x12, starting transfers between devices, swap_cores(): return lax.ppermute(x, 'tgt', [(0, 1), (1, 0)])  11 us
    ppermute x7, starting transfers between devices, onward(): return lax.ppermute(x, ('src', 'tgt'), pairs)  10.2 us
    all_to_all x4, waiting for transfers between devices, exchange(): return lax.all_to_all(x, 'src', 0, 0, tiled=True)  9.52 us
    div x1, other arithmetic, local(): source_known = source_cotangent / source_mass  3.27 us
  transfers between devices with their start and end apart: 23, of which 7 were waited for; matrix products, arithmetic and copies ran while one was open for 17% of the time, Pallas kernels for 22%

profile of v21, /device:TPU:1, one launch (start us, length us, event | category | flops | bytes accessed | tf_op | source)
XLA Modules:
  0.0 143.7 jit_solution(1945862603479292055)
XLA Ops:
  7.0 2.7 %collective-permute-start.1 = (bf16[2,256,512]{2,1,0:T(8,128)(2,1)}, bf16[2,256,512]{2,1,0:T(8,128)(2,1)}, u32[]{:S(2)}, u32[]{:S(2)}) collective-permute-start(bf16[2,256,512]{2,1,0:T(8,128)(2,1)} %get-tuple-element.34.refs_1_.refs_6_), channel_id=1, source_target_pairs={{0,4},{1,3},{4,8},{5,1},{8,12},{9,5},{12,14},{13,9},{14,10},{15,13... | collective-permute-start | bytes 1572872 | tf_op jit(solution)/shard_map/ppermute | solution.py:320
  14.6 2.3 %collective-permute-done.1.refs_3_.refs_8_ = bf16[2,256,512]{2,1,0:T(8,128)(2,1)} collective-permute-done((bf16[2,256,512]{2,1,0:T(8,128)(2,1)}, bf16[2,256,512]{2,1,0:T(8,128)(2,1)}, u32[]{:S(2)}, u32[]{:S(2)}) %collective-permute-start.1) | collective-permute-done | bytes 524320 | tf_op jit(solution)/shard_map/ppermute | solution.py:320
  19.4 1.5 %copy.22 = f16[512,512]{1,0:T(8,128)(2,1)S(1)} copy(f16[512,512]{0,1:T(8,128)(2,1)} %get-tuple-element.89) | data formatting | bytes 1048576 | tf_op jit(solution)/shard_map/transpose | solution.py:337
  20.9 1.7 %collective-permute-done.4.refs_2_.refs_7_ = bf16[2,256,512]{2,1,0:T(8,128)(2,1)} collective-permute-done((bf16[2,256,512]{2,1,0:T(8,128)(2,1)}, bf16[2,256,512]{2,1,0:T(8,128)(2,1)}, u32[]{:S(2)}, u32[]{:S(2)}) %collective-permute-start.4) | collective-permute-done | bytes 524320 | tf_op jit(solution)/shard_map/ppermute | solution.py:320
  23.1 1.7 %collective-permute-start.5 = (bf16[2,256,512]{2,1,0:T(8,128)(2,1)}, bf16[2,256,512]{2,1,0:T(8,128)(2,1)}, u32[]{:S(2)}, u32[]{:S(2)}) collective-permute-start(bf16[2,256,512]{2,1,0:T(8,128)(2,1)} %collective-permute-done.4.refs_2_.refs_7_), channel_id=1, source_target_pairs={{0,4},{1,3},{4,8},{5,1},{8,12},{9,5},{12,14},{13,9},{14,10},{15,13... | collective-permute-start | bytes 1572872 | tf_op jit(solution)/shard_map/ppermute | solution.py:320
  26.1 2.0 %collective-permute-done.2.refs_7_.refs_12_ = bf16[2,256,512]{2,1,0:T(8,128)(2,1)} collective-permute-done((bf16[2,256,512]{2,1,0:T(8,128)(2,1)}, bf16[2,256,512]{2,1,0:T(8,128)(2,1)}, u32[]{:S(2)}, u32[]{:S(2)}) %collective-permute-start.2) | collective-permute-done | bytes 524320 | tf_op jit(solution)/shard_map/ppermute | solution.py:320
  28.2 5.7 %all-to-all-start = ((f16[8,64,640]{2,1,0:T(8,128)(2,1)}), f16[8,64,640]{2,1,0:T(8,128)(2,1)S(1)}, u32[]{:S(2)}, u32[]{:S(2)}) async-start(f16[8,64,640]{2,1,0:T(8,128)(2,1)} %pad_maximum_fusion), calls=%async_computation | async-start | bytes 1310720 | tf_op jit(solution)/shard_map/all_to_all | solution.py:323
  35.1 1.8 %collective-permute-start.7 = (bf16[2,256,512]{2,1,0:T(8,128)(2,1)}, bf16[2,256,512]{2,1,0:T(8,128)(2,1)}, u32[]{:S(2)}, u32[]{:S(2)}) collective-permute-start(bf16[2,256,512]{2,1,0:T(8,128)(2,1)} %collective-permute-done.5.refs_6_.refs_11_), channel_id=1, source_target_pairs={{0,4},{1,3},{4,8},{5,1},{8,12},{9,5},{12,14},{13,9},{14,10},{15,13... | collective-permute-start | bytes 1572872 | tf_op jit(solution)/shard_map/ppermute | solution.py:320
  40.3 12.1 %collective-permute-done.7.refs_10_.refs_15_ = bf16[2,256,512]{2,1,0:T(8,128)(2,1)} collective-permute-done((bf16[2,256,512]{2,1,0:T(8,128)(2,1)}, bf16[2,256,512]{2,1,0:T(8,128)(2,1)}, u32[]{:S(2)}, u32[]{:S(2)}) %collective-permute-start.7) | collective-permute-done | bytes 524320 | tf_op jit(solution)/shard_map/ppermute | solution.py:320
  52.5 3.8 %collective-permute-start.14 = (bf16[2,256,512]{2,1,0:T(8,128)(2,1)}, bf16[2,256,512]{2,1,0:T(8,128)(2,1)S(1)}, u32[]{:S(2)}, u32[]{:S(2)}) collective-permute-start(bf16[2,256,512]{2,1,0:T(8,128)(2,1)} %collective-permute-done.7.refs_10_.refs_15_), channel_id=1, source_target_pairs={{0,1},{1,0},{2,3},{3,2},{4,5},{5,4},{6,7},{7,6},{8,9},{9,8},{10,11... | collective-permute-start | bytes 1572872 | tf_op jit(solution)/shard_map/ppermute | solution.py:288
  56.3 2.3 %collective-permute-done.13.refs_11_.refs_16_ = bf16[2,256,512]{2,1,0:T(8,128)(2,1)S(1)} collective-permute-done((bf16[2,256,512]{2,1,0:T(8,128)(2,1)}, bf16[2,256,512]{2,1,0:T(8,128)(2,1)S(1)}, u32[]{:S(2)}, u32[]{:S(2)}) %collective-permute-start.13) | collective-permute-done | bytes 524320 | tf_op jit(solution)/shard_map/ppermute | solution.py:320
  59.8 4.6 %collective-permute-done.11.refs_14_.refs_19_ = bf16[2,256,512]{2,1,0:T(8,128)(2,1)S(1)} collective-permute-done((bf16[2,256,512]{2,1,0:T(8,128)(2,1)}, bf16[2,256,512]{2,1,0:T(8,128)(2,1)S(1)}, u32[]{:S(2)}, u32[]{:S(2)}) %collective-permute-start.11) | collective-permute-done | bytes 524320 | tf_op jit(solution)/shard_map/ppermute | solution.py:320
  64.4 7.0 %all-to-all-start.1 = ((f16[8,64,640]{2,1,0:T(8,128)(2,1)}), f16[8,64,640]{2,1,0:T(8,128)(2,1)S(1)}, u32[]{:S(2)}, u32[]{:S(2)}) async-start(f16[8,64,640]{2,1,0:T(8,128)(2,1)} %pad_maximum_fusion.1), calls=%async_computation.1 | async-start | bytes 1310720 | tf_op jit(solution)/shard_map/all_to_all | solution.py:323
  72.3 16.0 %shard_map.132 = (f32[8,64,640]{2,1,0:T(8,128)}, f32[8,64,512]{2,1,0:T(8,128)}, f32[8,8,512]{2,1,0:T(8,128)}, f32[64,1024]{1,0:T(8,128)}, f32[64,1024]{1,0:T(8,128)}, /*index=5*/f32[64,1024]{1,0:T(8,128)}) custom-call(s32[9]{0:T(128)} %pad_add_fusion.table, f32[8,64,640]{2,1,0:T(8,128)} %convert_element_type.63.mass_in, ...), custom_call_target="tpu_custom_call" | custom-call | flops 15032385536 | bytes 16777216 | tf_op jit(solution)/shard_map/pallas_call | solution.py:264
  88.2 2.2 %convert_element_type.66 = f16[8,64,640]{2,1,0:T(8,128)(2,1)} convert(f32[8,64,640]{2,1,0:T(8,128)} %get-tuple-element.53.thirds_in) | non-fusion elementwise | flops 327680 | bytes 1966080 | tf_op jit(solution)/shard_map/convert_element_type | solution.py:414
  90.5 5.4 %all-to-all-start.3 = ((f16[8,64,640]{2,1,0:T(8,128)(2,1)}), f16[8,64,640]{2,1,0:T(8,128)(2,1)S(1)}, u32[]{:S(2)}, u32[]{:S(2)}) async-start(f16[8,64,640]{2,1,0:T(8,128)(2,1)} %convert_element_type.66), calls=%async_computation.3 | async-start | bytes 1310720 | tf_op jit(solution)/shard_map/all_to_all | solution.py:323
  97.1 15.6 %shard_map.133 = f32[8,64,640]{2,1,0:T(8,128)} custom-call(s32[9]{0:T(128)} %pad_add_fusion.table, f32[8,64,640]{2,1,0:T(8,128)} %convert_element_type.63.mass_in, f32[8,64,640]{2,1,0:T(8,128)} %convert_element_type.64.cot_in, f32[8,64,640]{2,1,0:T(8,128)} %get-tuple-element.53.thirds_in, f32[8,64,512]{2,1,0:T(8,128)} %get-tuple-element.54.refs_0_, ...), custom_call_target="tpu_custom_call" | custom-call | flops 10737418240 | bytes 16777216 | tf_op jit(solution)/shard_map/pallas_call | solution.py:264
  112.7 2.3 %convert_element_type.65 = f16[8,64,640]{2,1,0:T(8,128)(2,1)} convert(f32[8,64,640]{2,1,0:T(8,128)} %shard_map.133) | non-fusion elementwise | flops 327680 | bytes 1966080 | tf_op jit(solution)/shard_map/convert_element_type | solution.py:421
  115.0 5.4 %all-to-all-start.2 = ((f16[8,64,640]{2,1,0:T(8,128)(2,1)}), f16[8,64,640]{2,1,0:T(8,128)(2,1)}, u32[]{:S(2)}, u32[]{:S(2)}) async-start(f16[8,64,640]{2,1,0:T(8,128)(2,1)} %convert_element_type.65), calls=%async_computation.2 | async-start | bytes 1310720 | tf_op jit(solution)/shard_map/all_to_all | solution.py:323
  121.1 1.5 %collective-permute-start.17 = (f16[64,512]{1,0:T(8,128)(2,1)S(1)}, f16[64,512]{1,0:T(8,128)(2,1)S(1)}, u32[]{:S(2)}, u32[]{:S(2)}) collective-permute-start(f16[64,512]{1,0:T(8,128)(2,1)S(1)} %fusion.7), channel_id=1, source_target_pairs={{0,1},{1,0},{2,3},{3,2},{4,5},{5,4},{6,7},{7,6},{8,9},{9,8},{10,11... | collective-permute-start | bytes 196616 | tf_op jit(solution)/shard_map/ppermute | solution.py:288
  122.5 3.3 %fusion.14 = (f32[512,512]{1,0:T(8,128)}, f32[512,512]{1,0:T(8,128)}) fusion(f32[512,512]{1,0:T(8,128)} %param.15, f32[512,512]{1,0:T(8,128)} %param.10, f32[640,512]{1,0:T(8,128)S(1)} %bitcast.77), kind=kLoop, calls=%fused_computation.63 | loop fusion | flops 524288 | bytes 5242880 | tf_op jit(solution)/shard_map/div | solution.py:417
  126.7 9.5 %all-to-all-done.2 = f16[8,64,640]{2,1,0:T(8,128)(2,1)} async-done(((f16[8,64,640]{2,1,0:T(8,128)(2,1)}), f16[8,64,640]{2,1,0:T(8,128)(2,1)}, u32[]{:S(2)}, u32[]{:S(2)}) %all-to-all-start.2) | async-done | bytes 655392 | tf_op jit(solution)/shard_map/all_to_all | solution.py:323
  137.8 2.7 %collective-permute-start.18 = (f16[64,512]{1,0:T(8,128)(2,1)S(1)}, f16[64,512]{1,0:T(8,128)(2,1)S(1)}, u32[]{:S(2)}, u32[]{:S(2)}) collective-permute-start(f16[64,512]{1,0:T(8,128)(2,1)S(1)} %fusion.8), channel_id=1, source_target_pairs={{0,1},{1,0},{2,3},{3,2},{4,5},{5,4},{6,7},{7,6},{8,9},{9,8},{10,11... | collective-permute-start | bytes 196616 | tf_op jit(solution)/shard_map/ppermute | solution.py:288
  140.5 2.4 %fusion = f32[512,512]{1,0:T(8,128)} fusion(f32[512,512]{1,0:T(8,128)} %get-tuple-element.61, f32[640,512]{1,0:T(8,128)S(1)} %bitcast.79), kind=kLoop, calls=%fused_computation.3 | loop fusion | flops 524288 | bytes 3145728 | tf_op jit(solution)/shard_map/add | solution.py:432
  (104 shorter events, 27.1 us)
Async XLA Ops:
  3.2 2.6 %collective-permute-start = (bf16[512,512]{1,0:T(8,128)(2,1)S(1)}, bf16[512,512]{1,0:T(8,128)(2,1)S(1)}, u32[]{:S(2)}, u32[]{:S(2)}) collective-permute-start(bf16[512,512]{1,0:T(8,128)(2,1)S(1)} %bitcast.96), channel_id=1, source_target_pairs={{0,1},{1,0},{2,3},{3,2},{4,5},{5,4},{6,7},{7,6},{8,9},{9,8},{10,11... | collective-permute-start | bytes 1572872 | tf_op jit(solution)/shard_map/ppermute | solution.py:288
  7.0 9.9 %collective-permute-start.1 = (bf16[2,256,512]{2,1,0:T(8,128)(2,1)}, bf16[2,256,512]{2,1,0:T(8,128)(2,1)}, u32[]{:S(2)}, u32[]{:S(2)}) collective-permute-start(bf16[2,256,512]{2,1,0:T(8,128)(2,1)} %get-tuple-element.34.refs_1_.refs_6_), channel_id=1, source_target_pairs={{0,4},{1,3},{4,8},{5,1},{8,12},{9,5},{12,14},{13,9},{14,10},{15,13... | collective-permute-start | bytes 1572872 | tf_op jit(solution)/shard_map/ppermute | solution.py:320
  10.6 11.9 %collective-permute-start.4 = (bf16[2,256,512]{2,1,0:T(8,128)(2,1)}, bf16[2,256,512]{2,1,0:T(8,128)(2,1)}, u32[]{:S(2)}, u32[]{:S(2)}) collective-permute-start(bf16[2,256,512]{2,1,0:T(8,128)(2,1)} %get-tuple-element.38.refs_0_.refs_5_), channel_id=1, source_target_pairs={{0,4},{1,3},{4,8},{5,1},{8,12},{9,5},{12,14},{13,9},{14,10},{15,13... | collective-permute-start | bytes 1572872 | tf_op jit(solution)/shard_map/ppermute | solution.py:320
  12.9 11.9 %collective-permute-start.10 = (f16[64,512]{1,0:T(8,128)(2,1)}, f16[64,512]{1,0:T(8,128)(2,1)S(1)}, u32[]{:S(2)}, u32[]{:S(2)}) collective-permute-start(f16[64,512]{1,0:T(8,128)(2,1)} %bitcast.74), channel_id=1, source_target_pairs={{0,1},{1,0},{2,3},{3,2},{4,5},{5,4},{6,7},{7,6},{8,9},{9,8},{10,11... | collective-permute-start | bytes 196616 | tf_op jit(solution)/shard_map/ppermute | solution.py:288
  14.6 10.3 %collective-permute-start.3 = (f16[64,512]{1,0:T(8,128)(2,1)}, f16[64,512]{1,0:T(8,128)(2,1)S(1)}, u32[]{:S(2)}, u32[]{:S(2)}) collective-permute-start(f16[64,512]{1,0:T(8,128)(2,1)} %bitcast.75), channel_id=1, source_target_pairs={{0,1},{1,0},{2,3},{3,2},{4,5},{5,4},{6,7},{7,6},{8,9},{9,8},{10,11... | collective-permute-start | bytes 196616 | tf_op jit(solution)/shard_map/ppermute | solution.py:288
  16.9 11.2 %collective-permute-start.2 = (bf16[2,256,512]{2,1,0:T(8,128)(2,1)}, bf16[2,256,512]{2,1,0:T(8,128)(2,1)}, u32[]{:S(2)}, u32[]{:S(2)}) collective-permute-start(bf16[2,256,512]{2,1,0:T(8,128)(2,1)} %collective-permute-done.1.refs_3_.refs_8_), channel_id=1, source_target_pairs={{0,4},{1,3},{4,8},{5,1},{8,12},{9,5},{12,14},{13,9},{14,10},{15,13... | collective-permute-start | bytes 1572872 | tf_op jit(solution)/shard_map/ppermute | solution.py:320
  22.5 12.5 %collective-permute-start.6 = (bf16[2,256,512]{2,1,0:T(8,128)(2,1)}, bf16[2,256,512]{2,1,0:T(8,128)(2,1)S(1)}, u32[]{:S(2)}, u32[]{:S(2)}) collective-permute-start(bf16[2,256,512]{2,1,0:T(8,128)(2,1)} %collective-permute-done.4.refs_2_.refs_7_), channel_id=1, source_target_pairs={{0,1},{1,0},{2,3},{3,2},{4,5},{5,4},{6,7},{7,6},{8,9},{9,8},{10,11... | collective-permute-start | bytes 1572872 | tf_op jit(solution)/shard_map/ppermute | solution.py:288
  23.1 12.0 %collective-permute-start.5 = (bf16[2,256,512]{2,1,0:T(8,128)(2,1)}, bf16[2,256,512]{2,1,0:T(8,128)(2,1)}, u32[]{:S(2)}, u32[]{:S(2)}) collective-permute-start(bf16[2,256,512]{2,1,0:T(8,128)(2,1)} %collective-permute-done.4.refs_2_.refs_7_), channel_id=1, source_target_pairs={{0,4},{1,3},{4,8},{5,1},{8,12},{9,5},{12,14},{13,9},{14,10},{15,13... | collective-permute-start | bytes 1572872 | tf_op jit(solution)/shard_map/ppermute | solution.py:320
  28.2 30.4 %all-to-all-start = ((f16[8,64,640]{2,1,0:T(8,128)(2,1)}), f16[8,64,640]{2,1,0:T(8,128)(2,1)S(1)}, u32[]{:S(2)}, u32[]{:S(2)}) async-start(f16[8,64,640]{2,1,0:T(8,128)(2,1)} %pad_maximum_fusion), calls=%async_computation | async-start | bytes 1310720 | tf_op jit(solution)/shard_map/all_to_all | solution.py:323
  33.9 5.2 %collective-permute-start.12 = (bf16[2,256,512]{2,1,0:T(8,128)(2,1)}, bf16[2,256,512]{2,1,0:T(8,128)(2,1)S(1)}, u32[]{:S(2)}, u32[]{:S(2)}) collective-permute-start(bf16[2,256,512]{2,1,0:T(8,128)(2,1)} %collective-permute-done.1.refs_3_.refs_8_), channel_id=1, source_target_pairs={{0,1},{1,0},{2,3},{3,2},{4,5},{5,4},{6,7},{7,6},{8,9},{9,8},{10,11... | collective-permute-start | bytes 1572872 | tf_op jit(solution)/shard_map/ppermute | solution.py:288
  35.1 17.4 %collective-permute-start.7 = (bf16[2,256,512]{2,1,0:T(8,128)(2,1)}, bf16[2,256,512]{2,1,0:T(8,128)(2,1)}, u32[]{:S(2)}, u32[]{:S(2)}) collective-permute-start(bf16[2,256,512]{2,1,0:T(8,128)(2,1)} %collective-permute-done.5.refs_6_.refs_11_), channel_id=1, source_target_pairs={{0,4},{1,3},{4,8},{5,1},{8,12},{9,5},{12,14},{13,9},{14,10},{15,13... | collective-permute-start | bytes 1572872 | tf_op jit(solution)/shard_map/ppermute | solution.py:320
  36.9 15.6 %collective-permute-start.8 = (bf16[2,256,512]{2,1,0:T(8,128)(2,1)}, bf16[2,256,512]{2,1,0:T(8,128)(2,1)}, u32[]{:S(2)}, u32[]{:S(2)}) collective-permute-start(bf16[2,256,512]{2,1,0:T(8,128)(2,1)} %collective-permute-done.5.refs_6_.refs_11_), channel_id=1, source_target_pairs={{0,1},{1,0},{2,3},{3,2},{4,5},{5,4},{6,7},{7,6},{8,9},{9,8},{10,11... | collective-permute-start | bytes 1572872 | tf_op jit(solution)/shard_map/ppermute | solution.py:288
  37.2 15.3 %collective-permute-start.9 = (bf16[2,256,512]{2,1,0:T(8,128)(2,1)}, bf16[2,256,512]{2,1,0:T(8,128)(2,1)}, u32[]{:S(2)}, u32[]{:S(2)}) collective-permute-start(bf16[2,256,512]{2,1,0:T(8,128)(2,1)} %collective-permute-done.2.refs_7_.refs_12_), channel_id=1, source_target_pairs={{0,1},{1,0},{2,3},{3,2},{4,5},{5,4},{6,7},{7,6},{8,9},{9,8},{10,11... | collective-permute-start | bytes 1572872 | tf_op jit(solution)/shard_map/ppermute | solution.py:288
  39.1 25.3 %copy-start.10 = (bf16[2,256,512]{2,1,0:T(8,128)(2,1)}, bf16[2,256,512]{2,1,0:T(8,128)(2,1)S(1)}, u32[]{:S(2)}) copy-start(bf16[2,256,512]{2,1,0:T(8,128)(2,1)S(1)} %collective-permute-done.12.refs_5_.refs_10_) | copy-start | bytes 1572868
  39.1 19.5 %collective-permute-start.13 = (bf16[2,256,512]{2,1,0:T(8,128)(2,1)}, bf16[2,256,512]{2,1,0:T(8,128)(2,1)S(1)}, u32[]{:S(2)}, u32[]{:S(2)}) collective-permute-start(bf16[2,256,512]{2,1,0:T(8,128)(2,1)} %collective-permute-done.2.refs_7_.refs_12_), channel_id=1, source_target_pairs={{0,4},{1,3},{4,8},{5,1},{8,12},{9,5},{12,14},{13,9},{14,10},{15,13... | collective-permute-start | bytes 1572872 | tf_op jit(solution)/shard_map/ppermute | solution.py:320
  52.4 12.0 %collective-permute-start.11 = (bf16[2,256,512]{2,1,0:T(8,128)(2,1)}, bf16[2,256,512]{2,1,0:T(8,128)(2,1)S(1)}, u32[]{:S(2)}, u32[]{:S(2)}) collective-permute-start(bf16[2,256,512]{2,1,0:T(8,128)(2,1)} %collective-permute-done.7.refs_10_.refs_15_), channel_id=1, source_target_pairs={{0,4},{1,3},{4,8},{5,1},{8,12},{9,5},{12,14},{13,9},{14,10},{15,13... | collective-permute-start | bytes 1572872 | tf_op jit(solution)/shard_map/ppermute | solution.py:320
  52.5 19.0 %collective-permute-start.14 = (bf16[2,256,512]{2,1,0:T(8,128)(2,1)}, bf16[2,256,512]{2,1,0:T(8,128)(2,1)S(1)}, u32[]{:S(2)}, u32[]{:S(2)}) collective-permute-start(bf16[2,256,512]{2,1,0:T(8,128)(2,1)} %collective-permute-done.7.refs_10_.refs_15_), channel_id=1, source_target_pairs={{0,1},{1,0},{2,3},{3,2},{4,5},{5,4},{6,7},{7,6},{8,9},{9,8},{10,11... | collective-permute-start | bytes 1572872 | tf_op jit(solution)/shard_map/ppermute | solution.py:288
  58.6 12.9 %collective-permute-start.15 = (bf16[2,256,512]{2,1,0:T(8,128)(2,1)S(1)}, bf16[2,256,512]{2,1,0:T(8,128)(2,1)}, u32[]{:S(2)}, u32[]{:S(2)}) collective-permute-start(bf16[2,256,512]{2,1,0:T(8,128)(2,1)S(1)} %collective-permute-done.13.refs_11_.refs_16_), channel_id=1, source_target_pairs={{0,1},{1,0},{2,3},{3,2},{4,5},{5,4},{6,7},{7,6},{8,9},{9,8},{10,11... | collective-permute-start | bytes 1572872 | tf_op jit(solution)/shard_map/ppermute | solution.py:288
  64.4 7.1 %collective-permute-start.16 = (bf16[2,256,512]{2,1,0:T(8,128)(2,1)S(1)}, bf16[2,256,512]{2,1,0:T(8,128)(2,1)}, u32[]{:S(2)}, u32[]{:S(2)}) collective-permute-start(bf16[2,256,512]{2,1,0:T(8,128)(2,1)S(1)} %collective-permute-done.11.refs_14_.refs_19_), channel_id=1, source_target_pairs={{0,1},{1,0},{2,3},{3,2},{4,5},{5,4},{6,7},{7,6},{8,9},{9,8},{10,11... | collective-permute-start | bytes 1572872 | tf_op jit(solution)/shard_map/ppermute | solution.py:288
  64.4 26.0 %all-to-all-start.1 = ((f16[8,64,640]{2,1,0:T(8,128)(2,1)}), f16[8,64,640]{2,1,0:T(8,128)(2,1)S(1)}, u32[]{:S(2)}, u32[]{:S(2)}) async-start(f16[8,64,640]{2,1,0:T(8,128)(2,1)} %pad_maximum_fusion.1), calls=%async_computation.1 | async-start | bytes 1310720 | tf_op jit(solution)/shard_map/all_to_all | solution.py:323
  90.5 24.5 %all-to-all-start.3 = ((f16[8,64,640]{2,1,0:T(8,128)(2,1)}), f16[8,64,640]{2,1,0:T(8,128)(2,1)S(1)}, u32[]{:S(2)}, u32[]{:S(2)}) async-start(f16[8,64,640]{2,1,0:T(8,128)(2,1)} %convert_element_type.66), calls=%async_computation.3 | async-start | bytes 1310720 | tf_op jit(solution)/shard_map/all_to_all | solution.py:323
  115.0 21.2 %all-to-all-start.2 = ((f16[8,64,640]{2,1,0:T(8,128)(2,1)}), f16[8,64,640]{2,1,0:T(8,128)(2,1)}, u32[]{:S(2)}, u32[]{:S(2)}) async-start(f16[8,64,640]{2,1,0:T(8,128)(2,1)} %convert_element_type.65), calls=%async_computation.2 | async-start | bytes 1310720 | tf_op jit(solution)/shard_map/all_to_all | solution.py:323
  121.1 4.8 %collective-permute-start.17 = (f16[64,512]{1,0:T(8,128)(2,1)S(1)}, f16[64,512]{1,0:T(8,128)(2,1)S(1)}, u32[]{:S(2)}, u32[]{:S(2)}) collective-permute-start(f16[64,512]{1,0:T(8,128)(2,1)S(1)} %fusion.7), channel_id=1, source_target_pairs={{0,1},{1,0},{2,3},{3,2},{4,5},{5,4},{6,7},{7,6},{8,9},{9,8},{10,11... | collective-permute-start | bytes 196616 | tf_op jit(solution)/shard_map/ppermute | solution.py:288
  137.8 5.1 %collective-permute-start.18 = (f16[64,512]{1,0:T(8,128)(2,1)S(1)}, f16[64,512]{1,0:T(8,128)(2,1)S(1)}, u32[]{:S(2)}, u32[]{:S(2)}) collective-permute-start(f16[64,512]{1,0:T(8,128)(2,1)S(1)} %fusion.8), channel_id=1, source_target_pairs={{0,1},{1,0},{2,3},{3,2},{4,5},{5,4},{6,7},{7,6},{8,9},{9,8},{10,11... | collective-permute-start | bytes 196616 | tf_op jit(solution)/shard_map/ppermute | solution.py:288
  (14 other events, 57.4 us)
